TPU v7x, 32 devices: a whole 2x2x4 slice. The times are simulated.
32 devices in a mesh: slab: 8 (over z, y), dom: 4 (over x, core).
Axes of the slice: x: 2, y: 2, z: 4, core: 2. Of those that a mesh axis runs over, the one named last changes fastest.
Arguments:
- base_cells: int32 [3, 8192], P(None, ('slab', 'dom')), may hold values from 0 to 511, as said below
- offsets: float32 [3, 8192], P(None, ('slab', 'dom')), may hold values from 0 to 1
- charges: float32 [8192], P(('slab', 'dom')), may hold values from -4 to 4
- bias_coupling: float32 [8192], P(('slab', 'dom')), may hold values from -4 to 4
- counts: int32 [32], P(('slab', 'dom')), may hold values from 128 to 256, as said below
- green: float32 [32, 512, 256], P(None, 'slab', 'dom'), as said below
Outputs:
- potential: float32 [32, 512, 512], P('slab', 'dom')
- gradient: float32 [8192], P(('slab', 'dom'))
Inputs may be any that keep to these rules, and one draw needn't show every extreme that they name: `base_cells`: an atom in slot a belongs to device a // 256, which is slab index (a // 256) // 4 and dom index (a // 256) % 4 of the mesh; its base cell has first coordinate in that slab's 4 planes, second coordinate in that dom index's 128 rows, third coordinate anywhere in 0..511. `counts`: A multiple of 128 of at least half of 256; equal to 256 on at least one device; a device's atoms fill its first slots. `green`: zero at the zero wavenumber and positive elsewhere.
All inputs are finite; a program needn't handle non-finite values.
Results may differ from a plain program's by a relative error of at most 0.000086.
Values sent between devices are 32-bit elements; how exact they have to be, the bound alone decides.
No kernel may reach another device: no remote copies, remote signals or barrier semaphores. Data moves between devices by JAX's collectives and lax.ppermute only.
A program may use at most 64 MiB of HBM per device.

v0:
```python
import functools

import jax
import jax.numpy as jnp
import ml_dtypes
import numpy as np
from jax import lax
from jax.experimental import pallas as pl
from jax.experimental.pallas import tpu as pltpu
from jax.sharding import PartitionSpec as P

XD = 4
NY = 512
NZ = 512
KH = NZ // 2
LANES = 128
SPAN = XD + 3
CHUNKS = 2
DEPTH = XD // CHUNKS
MIB = 1 << 20
BF16 = jnp.bfloat16
F32 = jnp.float32


def polynomial(function, terms):
    nodes = 0.125 * (1.0 - np.cos(np.pi * (np.arange(64) + 0.5) / 64))
    powers = nodes[:, None] ** np.arange(terms)[None, :]
    return [float(v) for v in np.linalg.lstsq(powers, function(np.sqrt(nodes)), rcond=None)[0]]


SINE_TERMS = polynomial(lambda r: np.sin(np.pi * r) / r, 6)
COSINE_TERMS = polynomial(lambda r: np.cos(np.pi * r), 6)


def horner(terms, square):
    total = jnp.full_like(square, terms[-1])
    for term in terms[-2::-1]:
        total = total * square + term
    return total


def turn(fraction):
    left = fraction - jnp.floor(fraction + 0.5)
    square = left * left
    sine = left * horner(SINE_TERMS, square)
    cosine = horner(COSINE_TERMS, square)
    return 1.0 - 2.0 * sine * sine, 2.0 * sine * cosine


def spline(frac):
    inner = 1.0 - frac
    square = frac * frac
    cube = square * frac
    sixth = 1.0 / 6.0
    return (
        inner * inner * inner * sixth,
        (3.0 * cube - 6.0 * square + 4.0) * sixth,
        (-3.0 * cube + 3.0 * square + 3.0 * frac + 1.0) * sixth,
        cube * sixth,
    )


def split(value):
    high = value.astype(BF16)
    return high, (value - high.astype(F32)).astype(BF16)


def iota(shape, axis):
    return lax.broadcasted_iota(jnp.int32, shape, axis).astype(F32)


RADIX = 16
DIGITS = 32
TERMS = 256


def wave_factors(first, rows, length):
    lane = lax.broadcasted_iota(jnp.int32, (rows, TERMS), 1)
    section = lane // DIGITS
    digit = (lane % DIGITS).astype(F32) * jnp.where(section < 2, float(RADIX), 1.0)
    parts = []
    for value in turn((first + iota((rows, TERMS), 0)) * digit * (1.0 / length)):
        high = value.astype(BF16).astype(F32)
        parts.append(jnp.where((section == 1) | (section == 3), value - high, high))
    upper, lower = section < 2, (section >= 2) & (section < 5)
    masked = [jnp.where(mask, part, 0.0) for mask in (upper, lower) for part in parts]
    return jnp.concatenate(masked, 0).astype(BF16)


def wave_kernel(place_ref, out_y_ref, out_z_ref):
    out_y_ref[...] = wave_factors(place_ref[0].astype(F32), out_y_ref.shape[0] // 4, NY)
    out_z_ref[...] = wave_factors(place_ref[1].astype(F32), out_z_ref.shape[0] // 4, NZ)


def atom_waves(base, weights, factors_ref, digits_ref):
    width = base.shape[1]
    high_digit = jnp.floor(base * (1.0 / RADIX))
    row = iota((DIGITS, width), 0)
    chosen = jnp.where(row == high_digit, 1.0, 0.0).astype(BF16)
    step = row - (base - RADIX * high_digit)
    spread = jnp.where(step == 3.0, weights[3], 0.0)
    for r in (2, 1, 0):
        spread = jnp.where(step == float(r), weights[r], spread)
    high, low = split(spread)
    for section, value in enumerate((chosen, chosen, high, high, low)):
        digits_ref[pl.ds(DIGITS * section, DIGITS), :] = value
    product = jnp.dot(factors_ref[...], digits_ref[...], preferred_element_type=F32)
    rows = product.shape[0] // 4
    cos_a, sin_a, cos_b, sin_b = (product[i * rows : (i + 1) * rows] for i in range(4))
    return cos_a * cos_b - sin_a * sin_b, sin_a * cos_b + cos_a * sin_b


def plane_weights(atoms, weights):
    row = iota((8, atoms.shape[1]), 0) - atoms[0:1]
    return sum(weights[r][3:4] * (row == float(r)).astype(F32) for r in range(4))


def swap(value):
    return pltpu.roll(value, LANES // 2, axis=value.ndim - 1)


def half_sign():
    lane = lax.broadcasted_iota(jnp.int32, (1, LANES), 1)
    return jnp.where(lane < LANES // 2, -1.0, 1.0).astype(F32)


def rotate(value, numer, denom, sign, halves):
    if numer == 0:
        return value
    if 4 * numer == denom:
        return swap(value) * (halves * sign)
    angle = 2.0 * np.pi * numer / denom
    return value * float(np.cos(angle)) + swap(value) * (halves * float(sign * np.sin(angle)))


def transform(values, sign, halves):
    count = len(values)
    if count == 1:
        return values
    even = transform(values[0::2], sign, halves)
    odd = transform(values[1::2], sign, halves)
    turned = [rotate(odd[k], k, count, sign, halves) for k in range(count // 2)]
    return [e + t for e, t in zip(even, turned)] + [e - t for e, t in zip(even, turned)]


def pack_kernel(counts_ref, cells_ref, offsets_ref, charges_ref, out_ref):
    width = offsets_ref.shape[1]
    alive = lax.broadcasted_iota(jnp.int32, (1, width), 1) < counts_ref[0]
    atoms = jnp.concatenate(
        [
            lax.bitwise_and(cells_ref[0:1, :], XD - 1).astype(F32),
            cells_ref[1:3, :].astype(F32),
            offsets_ref[...],
            jnp.where(alive, charges_ref[...], 0.0),
            jnp.zeros((1, width), F32),
        ],
        0,
    )
    for copy in range(out_ref.shape[0]):
        out_ref[copy] = atoms


def exchange_order(slabs, doms):
    steps = [("slab", slabs >> (i + 1)) for i in range(slabs.bit_length() - 1)]
    return steps + [("dom", doms >> (i + 1)) for i in range(doms.bit_length() - 2)]


def atoms_of(refs, distance, slot, slabs, doms):
    half = doms // 2
    bits = slabs.bit_length() - 1
    at = sum(((distance >> (bits - 1 - i)) & 1) << i for i in range(bits))
    number = slot % half
    dom_bits = doms.bit_length() - 2
    dom_distance = sum(((number >> i) & 1) * (doms >> (i + 1)) for i in range(dom_bits))
    return refs[slot // half][number * slabs + at], dom_distance ^ (slot // half)


def forward_kernel(
    place_ref,
    same_ref,
    other_ref,
    factors_y,
    factors_z,
    out_ref,
    table_y,
    table_z,
    left_ref,
    right_ref,
    grid_ref,
    digits_y,
    digits_z,
):
    step = pl.program_id(0)
    cells_x = grid_ref.shape[0]
    rows = grid_ref.shape[1] // 2
    ky_local = rows - 8
    width = same_ref.shape[2]
    doms = table_y.shape[2] // width
    slabs = cells_x // XD
    slab = lax.bitwise_xor(place_ref[6], step)
    kept = slab - place_ref[2]
    kept = jnp.where((kept >= 0) & (kept < table_y.shape[0] - 1), kept, table_y.shape[0] - 1)

    @pl.when(step == 0)
    def _():
        grid_ref[...] = jnp.zeros_like(grid_ref)
        digits_y[...] = jnp.zeros_like(digits_y)
        digits_z[...] = jnp.zeros_like(digits_z)

    for slot in range(doms):
        atoms, _ = atoms_of((same_ref, other_ref), step, slot, slabs, doms)
        lanes = pl.ds(slot * width, width)
        weights = spline(atoms)
        along_x = plane_weights(atoms, weights) * atoms[6:7]
        waves = atom_waves(atoms[2:3], [w[5:6] for w in weights], factors_z, digits_z.at[slot])
        waves = jnp.concatenate(waves, 0)
        table_z[kept, :, lanes] = waves
        high, low = split(waves.T)
        right_ref[slot, :, :LANES] = high
        right_ref[slot, :, LANES:] = low
        cosine, sine = atom_waves(atoms[1:2], [w[4:5] for w in weights], factors_y, digits_y.at[slot])
        waves = jnp.concatenate([cosine, sine], 0)
        table_y[kept, :, lanes] = waves
        for plane in range(SPAN):
            first = 4 * rows * plane
            high, low = split(waves * along_x[plane : plane + 1])
            left_ref[slot, pl.ds(first, 2 * rows), :] = high
            left_ref[slot, pl.ds(first + 2 * rows, 2 * rows), :] = low
        product = jnp.dot(left_ref[slot], right_ref[slot], preferred_element_type=F32)
        for plane in range(SPAN):
            first = 4 * rows * plane
            high, low = product[first : first + 2 * rows], product[first + 2 * rows : first + 4 * rows]
            at = lax.rem(slab * XD + plane, cells_x)
            grid_ref[at] += (high[:, :LANES] + high[:, LANES:]) + (low[:, :LANES] + low[:, LANES:])

    @pl.when(step == pl.num_programs(0) - 1)
    def _():
        halves = half_sign()
        quarter_rows = ky_local // 2
        group = min(8, quarter_rows)
        for minus in (0, 1):
            for start in range(0, ky_local, group):
                row = start + minus
                values = []
                for x in range(cells_x):
                    top = grid_ref[x, pl.ds(row, group), :]
                    bottom = swap(grid_ref[x, pl.ds(rows + row, group), :])
                    values.append(bottom - top * halves if minus else -bottom - top * halves)
                at = 2 * minus + start // quarter_rows
                for x, value in enumerate(transform(values, -1.0, halves)):
                    out_ref[at, x, pl.ds(start % quarter_rows, group), :] = value


def inverse_x_kernel(place_ref, spectrum_ref, own_ref, mirrored_ref, *refs):
    *outs, near_ref = refs
    cells_x, quarter_rows = spectrum_ref.shape[1:3]
    group = min(8, quarter_rows)
    halves = half_sign()
    lane = lax.broadcasted_iota(jnp.int32, (1, LANES), 1)
    side = 1.0 - 2.0 * place_ref[3].astype(F32)

    def rows_of(step, carry):
        rows = pl.ds(pl.multiple_of(step * group, group), group)
        for quarter in range(4):
            values = []
            for kx in range(cells_x):
                green = (own_ref if quarter < 2 else mirrored_ref)[kx, rows, :]
                keep = lane < LANES // 2 if quarter % 2 == 0 else lane >= LANES // 2
                values.append(spectrum_ref[quarter, kx, rows, :] * jnp.where(keep, green, swap(green)))
            even = transform(values[0::2], 1.0, halves)
            odd = transform(values[1::2], 1.0, halves)
            for x in range(cells_x // 2):
                turned = rotate(odd[x], x, cells_x, 1.0, halves) * side
                near_ref[x, quarter, rows, :] = even[x] + turned
                if x < 3:
                    near_ref[cells_x // 2 + x, quarter, rows, :] = even[x] - turned
        return carry

    lax.fori_loop(0, quarter_rows // group, rows_of, 0)
    for k, out_ref in enumerate(outs):
        out_ref[...] = near_ref[pl.ds(lax.bitwise_xor(place_ref[4], k) * XD, XD)]


def inverse_y_kernel(sources, chunk, place_ref, *refs):
    ins, (high_ref, low_ref) = refs[:sources], refs[sources : sources + 2]
    outs, (lines_ref, turned_ref) = refs[sources + 2 : -2], refs[-2:]
    for k in range(sources):
        lines_ref[lax.bitwise_xor(place_ref[4], k)] = ins[k][pl.ds(chunk * DEPTH, DEPTH)]
    parts = []
    for x in range(DEPTH):
        lines = jnp.concatenate([lines_ref[source, x] for source in range(sources)], 0)
        pairs = jnp.concatenate([lines, swap(lines) * half_sign()], 0)
        parts.append(split(pairs))
    both = jnp.concatenate([value for part in parts for value in part], 1)
    main = jnp.dot(high_ref[...], both, preferred_element_type=F32)
    high = jnp.concatenate([part[0] for part in parts], 1)
    rest = jnp.dot(low_ref[...], high, preferred_element_type=F32)
    row = lax.broadcasted_iota(jnp.int32, (NY, 1), 0)
    sign = jnp.where((row % 2 == 1) & (place_ref[3] == 1), -1.0, 1.0)
    for x in range(DEPTH):
        total = main[:, 2 * x * LANES : (2 * x + 1) * LANES] + main[:, (2 * x + 1) * LANES : (2 * x + 2) * LANES]
        total = (total + rest[:, x * LANES : (x + 1) * LANES]) * sign
        turned_ref[:, x] = total.reshape(len(outs), -1, LANES)
    for k in range(len(outs)):
        outs[k][...] = turned_ref[lax.bitwise_xor(place_ref[5], k)]


def inverse_z_kernel(sources, place_ref, *refs):
    ins, (high_ref, low_ref) = refs[:sources], refs[sources : sources + 2]
    out_ref, lines_ref = refs[-2:]
    for k in range(sources):
        lines_ref[lax.bitwise_xor(place_ref[5], k)] = ins[k][...]
    for x in range(DEPTH):
        lines = jnp.concatenate([lines_ref[source, x] for source in range(sources)], 1)
        high, low = split(lines)
        total = jnp.dot(high, high_ref[...], preferred_element_type=F32)
        total += jnp.dot(low, high_ref[...], preferred_element_type=F32)
        total += jnp.dot(high, low_ref[...], preferred_element_type=F32)
        out_ref[x] = total


def gather_kernel(
    place_ref, same_ref, other_ref, table_y, table_z, near_ref, out_ref, shift_ref, fields_ref, stack_ref
):
    step = pl.program_id(0)
    half = LANES // 2
    rows = table_y.shape[1] // 2
    ky_local = rows - 8
    width = same_ref.shape[2]
    doms = table_y.shape[2] // width
    planes = near_ref.shape[0]
    slabs = 2 * (planes - 3) // XD
    halves = half_sign()

    @pl.when(step == 0)
    def _():
        stack_ref[...] = jnp.zeros_like(stack_ref)
        shift_ref[...] = jnp.zeros_like(shift_ref)
        row = lax.broadcasted_iota(jnp.int32, (8, LANES), 0)

        def build(x, carry):
            plus = near_ref[x, pl.ds(0, ky_local), :]
            shift_ref[pl.ds(1, ky_local), :] = near_ref[x, pl.ds(ky_local, ky_local), :]
            minus = shift_ref[pl.ds(0, ky_local), :]
            last = shift_ref[pl.ds(ky_local, 8), :][0:1]
            main = [plus + minus, swap(plus - minus) * halves]
            if 2 * ky_local < LANES:
                main.append(jnp.zeros((LANES - 2 * ky_local, LANES), F32))
            rest = jnp.where(row % 2 == 0, last, -swap(jnp.broadcast_to(last, (8, LANES))) * halves)
            rest = jnp.where(row < 6, rest, 0.0)
            rest_high = rest.astype(BF16).astype(F32)
            rest = jnp.where((row == 2) | (row == 3), rest - rest_high, rest_high)
            high, low = split(jnp.concatenate(main, 0).T)
            fields_ref[x, :, pl.ds(0, LANES)] = high
            fields_ref[x, :, pl.ds(LANES, LANES)] = low
            fields_ref[x, :, pl.ds(2 * LANES, LANES)] = high
            rest = jnp.concatenate([rest, jnp.zeros((LANES - 8, LANES), F32)], 0)
            fields_ref[x, :, pl.ds(3 * LANES, LANES)] = rest.T.astype(BF16)
            return carry

        lax.fori_loop(0, planes, build, 0)

    first_z = place_ref[1].astype(F32)
    twice = jnp.where(first_z + iota((half, 1), 0) == 0.0, 1.0, 2.0)
    fields = fields_ref[pl.ds(step * XD, SPAN)].reshape(SPAN * LANES, 4 * LANES)
    distance = lax.bitwise_xor(place_ref[4], step)
    for slot in range(doms):
        lanes = pl.ds(slot * width, width)
        cosine = table_y[step, pl.ds(0, ky_local), lanes]
        sine = table_y[step, pl.ds(rows, ky_local), lanes]
        high, low = split(jnp.concatenate([cosine, sine], 0))
        for part, value in enumerate((high, high, low)):
            stack_ref[pl.ds(LANES * part, 2 * ky_local), lanes] = value
        cosine = table_y[step, pl.ds(ky_local, 8), lanes][0:1]
        sine = table_y[step, pl.ds(rows + ky_local, 8), lanes][0:1]
        row = lax.broadcasted_iota(jnp.int32, (16, width), 0)
        rest = jnp.where(row % 2 == 0, cosine, sine)
        rest_high = rest.astype(BF16).astype(F32)
        rest = jnp.where(row < 4, rest_high, jnp.where(row < 6, rest - rest_high, 0.0))
        stack_ref[pl.ds(3 * LANES, 16), lanes] = rest.astype(BF16)
    product = sum(
        jnp.dot(fields[:, part : part + 2 * LANES], stack_ref[pl.ds(part, 2 * LANES), :], preferred_element_type=F32)
        for part in (0, 2 * LANES)
    )
    for slot in range(doms):
        atoms, dom_distance = atoms_of((same_ref, other_ref), distance, slot, slabs, doms)
        along_x = plane_weights(atoms, spline(atoms))
        lanes = pl.ds(slot * width, width)
        field = product[:, slot * width : (slot + 1) * width]
        total = along_x[0:1] * field[:LANES]
        for plane in range(1, SPAN):
            total += along_x[plane : plane + 1] * field[plane * LANES : (plane + 1) * LANES]
        waves = total * table_z[step, :, lanes]
        sampled = jnp.sum((waves[:half] - waves[half:]) * twice, axis=0, keepdims=True)
        out_ref[step * doms + lax.bitwise_xor(place_ref[5], dom_distance)] = sampled


def bf16_pair(table):
    high = table.astype(ml_dtypes.bfloat16)
    low = (table - high.astype(np.float64)).astype(ml_dtypes.bfloat16)
    return jnp.asarray(high), jnp.asarray(low)


def inverse_y_table(slab_half, ky_local):
    waves = []
    for slab in range(slab_half):
        first = slab * ky_local
        waves += [first + i for i in range(ky_local)] + [-(first + i + 1) for i in range(ky_local)]
    angle = 2.0 * np.pi * (np.outer(np.arange(NY), np.array(waves)) % NY) / NY
    return bf16_pair(np.concatenate([np.cos(angle), np.sin(angle)], 1))


def inverse_z_table(dom_count):
    kz = np.arange(KH)
    angle = 2.0 * np.pi * (np.outer(kz, np.arange(NZ)) % NZ) / NZ
    weight = np.where(kz == 0, 1.0, 2.0)[:, None]
    parts = [weight * np.cos(angle), -weight * np.sin(angle)]
    return bf16_pair(
        np.stack([p.reshape(dom_count, KH // dom_count, NZ) for p in parts], 1).reshape(2 * KH, NZ)
    )


def whole_spec(shape):
    return pl.BlockSpec(shape, lambda *_: (0,) * len(shape))


SMALL = pl.CostEstimate(flops=10**6, bytes_accessed=10**4, transcendentals=0)
SMEM = pl.BlockSpec(memory_space=pltpu.SMEM)


def params(mib):
    return pltpu.CompilerParams(vmem_limit_bytes=mib * MIB)


def swapped(value, axis, distance):
    if distance == 0:
        return value
    return lax.ppermute(value, axis, [(i, i ^ distance) for i in range(lax.axis_size(axis))])


def per_device(base_cells, offsets, charges, bias_coupling, counts, green):
    slabs = lax.axis_size("slab")
    doms = lax.axis_size("dom")
    slab = lax.axis_index("slab")
    dom = lax.axis_index("dom")
    atoms_local = charges.shape[0]
    cells_x = XD * slabs
    ky_local = NY // slabs
    kz_local = KH // doms
    slab_half = slabs // 2
    rows_local = NY // doms
    rows = ky_local + 8
    quarter_rows = ky_local // 2
    normalize = 1.0 / (cells_x * NY * NZ)
    upper = slab // slab_half
    place = jnp.stack(
        [slab * ky_local, dom * kz_local, upper * slab_half, upper, slab % slab_half, dom, slab]
    ).astype(jnp.int32)

    vmem = pl.BlockSpec(memory_space=pltpu.VMEM)
    atoms = pl.pallas_call(
        pack_kernel,
        in_specs=[SMEM, vmem, vmem, vmem],
        out_specs=vmem,
        out_shape=jax.ShapeDtypeStruct((1, 8, atoms_local), F32),
        name="pack",
    )(counts, base_cells, offsets, charges.reshape(1, atoms_local))
    factors_y, factors_z = pl.pallas_call(
        wave_kernel,
        in_specs=[SMEM],
        out_specs=[vmem] * 2,
        out_shape=[jax.ShapeDtypeStruct((4 * count, TERMS), BF16) for count in (rows, LANES // 2)],
        compiler_params=params(8),
        name="waves",
    )(place)
    same = atoms
    for number, (axis, distance) in enumerate(exchange_order(slabs, doms)):
        same = jnp.concatenate([same, swapped(same, axis, distance)], 0)
        if number == 1:
            same, factors_y, factors_z = lax.optimization_barrier((same, factors_y, factors_z))
    other = swapped(same, "dom", 1)

    def halves_beside(value):
        return jnp.concatenate([value[:, :quarter_rows], value[:, quarter_rows:]], 2) * normalize

    own = halves_beside(green)
    same, flipped = lax.optimization_barrier((same, halves_beside(green[:, ::-1])))
    mirrored = lax.ppermute(flipped, "slab", [(s, slabs - 1 - s) for s in range(slabs)])

    atoms_slab = doms * atoms_local
    table_bytes = 4 * (slab_half + 1) * (2 * rows + LANES) * atoms_slab
    spectrum_bytes = 16 * cells_x * max(8, quarter_rows) * LANES
    spectrum, table_y, table_z = pl.pallas_call(
        forward_kernel,
        grid=(slabs,),
        in_specs=[SMEM] + [vmem] * 4,
        out_specs=[vmem] * 3,
        out_shape=[
            jax.ShapeDtypeStruct((4, cells_x, quarter_rows, LANES), F32),
            jax.ShapeDtypeStruct((slab_half + 1, 2 * rows, atoms_slab), F32),
            jax.ShapeDtypeStruct((slab_half + 1, LANES, atoms_slab), F32),
        ],
        scratch_shapes=[
            pltpu.VMEM((doms, SPAN * 4 * rows, atoms_local), BF16),
            pltpu.VMEM((doms, atoms_local, 2 * LANES), BF16),
            pltpu.VMEM((cells_x, 2 * rows, LANES), F32),
            pltpu.VMEM((doms, TERMS, atoms_local), BF16),
            pltpu.VMEM((doms, TERMS, atoms_local), BF16),
        ],
        compiler_params=params(16 + (table_bytes + spectrum_bytes) // MIB),
        cost_estimate=SMALL,
        name="forward",
    )(place, same, other, factors_y, factors_z)

    near_planes = cells_x // 2 + 3
    piece = (XD, 4, quarter_rows, LANES)
    *pieces, near = pl.pallas_call(
        inverse_x_kernel,
        in_specs=[SMEM] + [vmem] * 3,
        out_specs=[vmem] * (slab_half + 1),
        out_shape=[jax.ShapeDtypeStruct(piece, F32)] * slab_half
        + [jax.ShapeDtypeStruct((near_planes, 4, quarter_rows, LANES), F32)],
        compiler_params=params(32),
        cost_estimate=SMALL,
        name="inverse_x",
    )(place, spectrum, own, mirrored)

    partial = pl.pallas_call(
        gather_kernel,
        grid=(slab_half,),
        in_specs=[SMEM] + [vmem] * 5,
        out_specs=vmem,
        out_shape=jax.ShapeDtypeStruct((slab_half * doms, 1, atoms_local), F32),
        scratch_shapes=[
            pltpu.VMEM((rows, LANES), F32),
            pltpu.VMEM((near_planes, LANES, 4 * LANES), BF16),
            pltpu.VMEM((4 * LANES, atoms_slab), BF16),
        ],
        compiler_params=params(12 + (table_bytes + 8 * near_planes * LANES * LANES) // MIB),
        cost_estimate=SMALL,
        name="gather",
    )(place, same, other, table_y, table_z, near.reshape(near_planes, 2 * ky_local, LANES))

    high_y, low_y = inverse_y_table(slab_half, ky_local)
    high_z, low_z = inverse_z_table(doms)
    members = slab_half * doms
    sampled = lax.all_to_all(
        partial.reshape(members, atoms_local),
        ("slab", "dom"),
        0,
        0,
        axis_index_groups=[list(range(members)), list(range(members, 2 * members))],
        tiled=True,
    )
    lines = [swapped(value.reshape(XD, 2 * ky_local, LANES), "slab", k) for k, value in enumerate(pieces)]
    sampled, *lines = lax.optimization_barrier((sampled, *lines))

    potential = None
    for chunk in range(CHUNKS):
        turned = pl.pallas_call(
            functools.partial(inverse_y_kernel, slab_half, chunk),
            in_specs=[SMEM] + [vmem] * (slab_half + 2),
            out_specs=[vmem] * doms,
            out_shape=[jax.ShapeDtypeStruct((DEPTH, rows_local, LANES), F32)] * doms,
            scratch_shapes=[
                pltpu.VMEM((slab_half, DEPTH, 2 * ky_local, LANES), F32),
                pltpu.VMEM((doms, DEPTH, rows_local, LANES), F32),
            ],
            compiler_params=params(24),
            cost_estimate=SMALL,
            name="inverse_y",
        )(place, *lines, high_y, low_y)
        columns = [swapped(value, "dom", k) for k, value in enumerate(turned)]
        earlier = [] if potential is None else [potential]
        potential = pl.pallas_call(
            functools.partial(inverse_z_kernel, doms),
            grid=(1,),
            in_specs=[SMEM]
            + [whole_spec((DEPTH, rows_local, LANES))] * doms
            + [whole_spec((2 * KH, NZ))] * 2
            + [pl.BlockSpec(memory_space=pl.ANY)] * len(earlier),
            out_specs=pl.BlockSpec((DEPTH, rows_local, NZ), lambda _, at=chunk: (at, 0, 0)),
            out_shape=jax.ShapeDtypeStruct((XD, rows_local, NZ), F32),
            scratch_shapes=[pltpu.VMEM((doms, DEPTH, rows_local, LANES), F32)],
            input_output_aliases={doms + 3: 0} if earlier else {},
            compiler_params=params(24),
            cost_estimate=SMALL,
            name="inverse_z",
        )(place, *columns, high_z, low_z, *earlier)

    alive = jnp.arange(atoms_local, dtype=jnp.int32) < counts[0]
    gradient = jnp.where(alive, bias_coupling * jnp.sum(sampled, 0), 0.0)
    return (potential, gradient)


def solution(mesh):
    placed = (
        P(None, ("slab", "dom")),
        P(None, ("slab", "dom")),
        P(("slab", "dom")),
        P(("slab", "dom")),
        P(("slab", "dom")),
        P(None, "slab", "dom"),
    )
    return jax.shard_map(
        per_device,
        mesh=mesh,
        in_specs=placed,
        out_specs=(P("slab", "dom", None), P(("slab", "dom"))),
        check_vma=False,
    )
```

profile of v0, /device:TPU:0, one launch (start us, length us, event | category | flops | bytes accessed | tf_op | source)
XLA Modules:
  0.0 95.4 jit_solution(3141686386213631353)
XLA Ops:
  1.3 1.3 %pack.1 = f32[1,8,256]{2,1,0:T(8,128)} custom-call(s32[1]{0:T(128)} %copy.19.counts_ref, s32[3,256]{1,0:T(4,128)} %cells_ref.1, f32[3,256]{1,0:T(4,128)} %offsets_ref.1, f32[1,256]{1,0:T(1,128)} %bitcast.25), custom_call_target="tpu_custom_call" | custom-call | tf_op jit(solution)/shard_map/pack/pallas_call | solution.py:461
  2.6 4.0 %collective-permute-start = (f32[1,8,256]{2,1,0:T(8,128)}, f32[1,8,256]{2,1,0:T(8,128)S(1)}, u32[]{:S(2)}, u32[]{:S(2)}) collective-permute-start(f32[1,8,256]{2,1,0:T(8,128)} %pack.1), channel_id=1, source_target_pairs={{0,16},{4,20},{8,24},{12,28},{16,0},{20,4},{24,8},{28,12},{1,17},{... | collective-permute-start | bytes 24584 | tf_op jit(solution)/shard_map/ppermute | solution.py:438
  6.6 1.3 %fusion = (f32[32,32,64]{2,1,0:T(8,128)S(1)}, f32[32,32,64]{2,1,0:T(8,128)S(1)}) fusion(f32[32,64,64]{2,1,0:T(8,128)} %param.15), kind=kLoop, calls=%fused_computation.10 | loop fusion | bytes 1048576 | tf_op jit(solution)/shard_map/slice | solution.py:484
  8.5 1.8 %collective-permute-start.1 = (f32[2,8,256]{2,1,0:T(8,128)S(1)}, f32[2,8,256]{2,1,0:T(8,128)S(1)}, u32[]{:S(2)}, u32[]{:S(2)}) collective-permute-start(f32[2,8,256]{2,1,0:T(8,128)S(1)} %pad_maximum_fusion.2), channel_id=1, source_target_pairs={{0,8},{4,12},{8,0},{12,4},{16,24},{20,28},{24,16},{28,20},{1,9},{5... | collective-permute-start | bytes 49160 | tf_op jit(solution)/shard_map/ppermute | solution.py:438
  12.3 1.8 %collective-permute-start.2 = (f32[4,8,256]{2,1,0:T(8,128)S(1)}, f32[4,8,256]{2,1,0:T(8,128)S(1)}, u32[]{:S(2)}, u32[]{:S(2)}) collective-permute-start(f32[4,8,256]{2,1,0:T(8,128)S(1)} %pad_maximum_fusion.1), channel_id=1, source_target_pairs={{0,4},{4,0},{8,12},{12,8},{16,20},{20,16},{24,28},{28,24},{1,5},{5... | collective-permute-start | bytes 98312 | tf_op jit(solution)/shard_map/ppermute | solution.py:438
  14.1 2.1 %collective-permute-done.2 = f32[4,8,256]{2,1,0:T(8,128)S(1)} collective-permute-done((f32[4,8,256]{2,1,0:T(8,128)S(1)}, f32[4,8,256]{2,1,0:T(8,128)S(1)}, u32[]{:S(2)}, u32[]{:S(2)}) %collective-permute-start.2) | collective-permute-done | bytes 32800 | tf_op jit(solution)/shard_map/ppermute | solution.py:438
  16.2 1.8 %collective-permute-start.3 = (f32[8,8,256]{2,1,0:T(8,128)S(1)}, f32[8,8,256]{2,1,0:T(8,128)S(1)}, u32[]{:S(2)}, u32[]{:S(2)}) collective-permute-start(f32[8,8,256]{2,1,0:T(8,128)S(1)} %pad_maximum_fusion), channel_id=1, source_target_pairs={{0,2},{1,3},{2,0},{3,1},{4,6},{5,7},{6,4},{7,5},{8,10},{9,11},{10,... | collective-permute-start | bytes 196616 | tf_op jit(solution)/shard_map/ppermute | solution.py:438
  18.0 2.5 %collective-permute-done.3 = f32[8,8,256]{2,1,0:T(8,128)S(1)} collective-permute-done((f32[8,8,256]{2,1,0:T(8,128)S(1)}, f32[8,8,256]{2,1,0:T(8,128)S(1)}, u32[]{:S(2)}, u32[]{:S(2)}) %collective-permute-start.3) | collective-permute-done | bytes 65568 | tf_op jit(solution)/shard_map/ppermute | solution.py:438
  20.5 4.8 %collective-permute-start.5 = (f32[32,32,128]{2,1,0:T(8,128)S(1)}, f32[32,32,128]{2,1,0:T(8,128)S(1)}, u32[]{:S(2)}, u32[]{:S(2)}) collective-permute-start(f32[32,32,128]{2,1,0:T(8,128)S(1)} %maximum_multiply_fusion), channel_id=1, source_target_pairs={{0,28},{4,24},{8,20},{12,16},{16,12},{20,8},{24,4},{28,0},{1,29},{... | collective-permute-start | bytes 1572872 | tf_op jit(solution)/shard_map/ppermute | solution.py:488
  25.5 1.1 %collective-permute-done.4.other_ref = f32[16,8,256]{2,1,0:T(8,128)S(1)} collective-permute-done((f32[16,8,256]{2,1,0:T(8,128)S(1)}, f32[16,8,256]{2,1,0:T(8,128)S(1)}, u32[]{:S(2)}, u32[]{:S(2)}) %collective-permute-start.4) | collective-permute-done | bytes 131104 | tf_op jit(solution)/shard_map/ppermute | solution.py:438
  26.7 26.2 %forward.1 = (f32[4,32,32,128]{3,2,1,0:T(8,128)S(1)}, f32[5,144,1024]{2,1,0:T(8,128)S(1)}, f32[5,128,1024]{2,1,0:T(8,128)S(1)}) custom-call(s32[7]{0:T(128)S(1)} %stack.31.place_ref, f32[16,8,256]{2,1,0:T(8,128)S(1)} %constant_dynamic-update-slice_fusion.same_ref, f32[16,8,256]{2,1,0:T(8,128)S(1)} %collective-permute-done.4.other_ref, ...), custom_call_target="tpu_custom_call" | custom-call | flops 1000000 | bytes 10000 | tf_op jit(solution)/shard_map/forward/pallas_call | solution.py:493
  52.8 4.1 %inverse_x.1 = (f32[4,4,32,128]{3,2,1,0:T(8,128)S(1)}, f32[4,4,32,128]{3,2,1,0:T(8,128)S(1)}, f32[4,4,32,128]{3,2,1,0:T(8,128)S(1)}, f32[4,4,32,128]{3,2,1,0:T(8,128)S(1)}, f32[19,4,32,128]{3,2,1,0:T(8,128)S(1)}) custom-call(s32[7]{0:T(128)S(1)} %stack.31.place_ref, f32[4,32,32,128]{3,2,1,0:T(8,128)S(1)} %get-tuple-element.38.spectrum_ref, ...), custom_call_target="tpu_custom_call" | custom-call | flops 1000000 | bytes 10000 | tf_op jit(solution)/shard_map/inverse_x/pallas_call | solution.py:517
  57.5 3.0 %collective-permute-start.8 = (f32[4,128,128]{2,1,0:T(8,128)S(1)}, f32[4,128,128]{2,1,0:T(8,128)S(1)}, u32[]{:S(2)}, u32[]{:S(2)}) collective-permute-start(f32[4,128,128]{2,1,0:T(8,128)S(1)} %bitcast.21), channel_id=1, source_target_pairs={{0,12},{4,8},{8,4},{12,0},{16,28},{20,24},{24,20},{28,16},{1,13},{... | collective-permute-start | bytes 786440 | tf_op jit(solution)/shard_map/ppermute | solution.py:438
  60.5 9.0 %gather.1 = f32[16,1,256]{2,1,0:T(1,128)S(1)} custom-call(s32[7]{0:T(128)S(1)} %stack.31.place_ref, f32[16,8,256]{2,1,0:T(8,128)S(1)} %constant_dynamic-update-slice_fusion.same_ref, f32[16,8,256]{2,1,0:T(8,128)S(1)} %collective-permute-done.4.other_ref, f32[5,144,1024]{2,1,0:T(8,128)S(1)} %get-tuple-element.36.table_y, ...), custom_call_target="tpu_custom_call" | custom-call | flops 1000000 | bytes 10000 | tf_op jit(solution)/shard_map/gather/pallas_call | solution.py:528
  69.5 8.2 %all_to_all.9 = f32[16,1,256]{2,1,0:T(1,128)S(1)} all-to-all(f32[16,1,256]{2,1,0:T(1,128)S(1)} %gather.1), channel_id=1, replica_groups={{0,1,2,3,4,5,6,7,8,9,10,11,12,13,14,15},{16,17,18,19,20,21,22,23,24,25,..., dimensions={0} | all-to-all | bytes 32768 | tf_op jit(solution)/shard_map/all_to_all | solution.py:547
  77.8 1.7 %inverse_y.3 = (f32[2,128,128]{2,1,0:T(8,128)S(1)}, f32[2,128,128]{2,1,0:T(8,128)S(1)}, f32[2,128,128]{2,1,0:T(8,128)S(1)}, f32[2,128,128]{2,1,0:T(8,128)S(1)}) custom-call(s32[7]{0:T(128)S(1)} %stack.31.place_ref, f32[4,128,128]{2,1,0:T(8,128)S(1)} %bitcast.19, f32[4,128,128]{2,1,0:T(8,128)S(1)} %collective-permute-done.6.refs_1_, ...), custom_call_target="tpu_custom_call" | custom-call | flops 1000000 | bytes 10000 | tf_op jit(solution)/shard_map/inverse_y/pallas_call | solution.py:560
  80.2 1.2 %collective-permute-start.14 = (f32[2,128,128]{2,1,0:T(8,128)S(1)}, f32[2,128,128]{2,1,0:T(8,128)S(1)}, u32[]{:S(2)}, u32[]{:S(2)}) collective-permute-start(f32[2,128,128]{2,1,0:T(8,128)S(1)} %get-tuple-element.56), channel_id=1, source_target_pairs={{0,3},{1,2},{2,1},{3,0},{4,7},{5,6},{6,5},{7,4},{8,11},{9,10},{10,... | collective-permute-start | bytes 393224 | tf_op jit(solution)/shard_map/ppermute | solution.py:438
  81.4 1.7 %inverse_y.2 = (f32[2,128,128]{2,1,0:T(8,128)S(1)}, f32[2,128,128]{2,1,0:T(8,128)S(1)}, f32[2,128,128]{2,1,0:T(8,128)S(1)}, f32[2,128,128]{2,1,0:T(8,128)S(1)}) custom-call(s32[7]{0:T(128)S(1)} %stack.31.place_ref, f32[4,128,128]{2,1,0:T(8,128)S(1)} %bitcast.20, f32[4,128,128]{2,1,0:T(8,128)S(1)} %collective-permute-done.6.refs_1_, ...), custom_call_target="tpu_custom_call" | custom-call | flops 1000000 | bytes 10000 | tf_op jit(solution)/shard_map/inverse_y/pallas_call | solution.py:560
  84.1 1.0 %collective-permute-start.11 = (f32[2,128,128]{2,1,0:T(8,128)S(1)}, f32[2,128,128]{2,1,0:T(8,128)S(1)}, u32[]{:S(2)}, u32[]{:S(2)}) collective-permute-start(f32[2,128,128]{2,1,0:T(8,128)S(1)} %get-tuple-element.52), channel_id=1, source_target_pairs={{0,3},{1,2},{2,1},{3,0},{4,7},{5,6},{6,5},{7,4},{8,11},{9,10},{10,... | collective-permute-start | bytes 393224 | tf_op jit(solution)/shard_map/ppermute | solution.py:438
  85.9 1.9 %collective-permute-done.14.refs_3_ = f32[2,128,128]{2,1,0:T(8,128)S(1)} collective-permute-done((f32[2,128,128]{2,1,0:T(8,128)S(1)}, f32[2,128,128]{2,1,0:T(8,128)S(1)}, u32[]{:S(2)}, u32[]{:S(2)}) %collective-permute-start.14) | collective-permute-done | bytes 131104 | tf_op jit(solution)/shard_map/ppermute | solution.py:438
  87.8 1.9 %inverse_z.2.refs_6_ = f32[4,128,512]{2,1,0:T(8,128)} custom-call(s32[7]{0:T(128)S(1)} %stack.31.place_ref, f32[2,128,128]{2,1,0:T(8,128)S(1)} %get-tuple-element.53.refs_0_, f32[2,128,128]{2,1,0:T(8,128)S(1)} %collective-permute-done.12.refs_1_, f32[2,128,128]{2,1,0:T(8,128)S(1)} %collective-permute-done.13.refs_2_, ...), custom_call_target="tpu_custom_call" | custom-call | flops 1000000 | bytes 10000 | tf_op jit(solution)/shard_map/inverse_z/pallas_call | solution.py:575
  89.8 1.8 %collective-permute-done.10.refs_2_ = f32[2,128,128]{2,1,0:T(8,128)S(1)} collective-permute-done((f32[2,128,128]{2,1,0:T(8,128)S(1)}, f32[2,128,128]{2,1,0:T(8,128)S(1)}, u32[]{:S(2)}, u32[]{:S(2)}) %collective-permute-start.10) | collective-permute-done | bytes 131104 | tf_op jit(solution)/shard_map/ppermute | solution.py:438
  91.5 1.9 %collective-permute-done.11.refs_3_ = f32[2,128,128]{2,1,0:T(8,128)S(1)} collective-permute-done((f32[2,128,128]{2,1,0:T(8,128)S(1)}, f32[2,128,128]{2,1,0:T(8,128)S(1)}, u32[]{:S(2)}, u32[]{:S(2)}) %collective-permute-start.11) | collective-permute-done | bytes 131104 | tf_op jit(solution)/shard_map/ppermute | solution.py:438
  93.4 1.9 %inverse_z.3 = f32[4,128,512]{2,1,0:T(8,128)} custom-call(s32[7]{0:T(128)S(1)} %stack.31.place_ref, f32[2,128,128]{2,1,0:T(8,128)S(1)} %get-tuple-element.49.refs_0_, f32[2,128,128]{2,1,0:T(8,128)S(1)} %collective-permute-done.9.refs_1_, f32[2,128,128]{2,1,0:T(8,128)S(1)} %collective-permute-done.10.refs_2_, ...), custom_call_target="tpu_custom_call", output_to_operand_aliasing={{}: (7, {})} | custom-call | flops 1000000 | bytes 10000 | tf_op jit(solution)/shard_map/inverse_z/pallas_call | solution.py:575
  (43 shorter events, 5.8 us)
Async XLA Ops:
  2.6 6.0 %copy-start.4 = (f32[1,8,256]{2,1,0:T(8,128)S(1)}, f32[1,8,256]{2,1,0:T(8,128)}, u32[]{:S(2)}) copy-start(f32[1,8,256]{2,1,0:T(8,128)} %pack.1) | copy-start | bytes 24580
  2.6 5.9 %collective-permute-start = (f32[1,8,256]{2,1,0:T(8,128)}, f32[1,8,256]{2,1,0:T(8,128)S(1)}, u32[]{:S(2)}, u32[]{:S(2)}) collective-permute-start(f32[1,8,256]{2,1,0:T(8,128)} %pack.1), channel_id=1, source_target_pairs={{0,16},{4,20},{8,24},{12,28},{16,0},{20,4},{24,8},{28,12},{1,17},{... | collective-permute-start | bytes 24584 | tf_op jit(solution)/shard_map/ppermute | solution.py:438
  8.5 3.7 %collective-permute-start.1 = (f32[2,8,256]{2,1,0:T(8,128)S(1)}, f32[2,8,256]{2,1,0:T(8,128)S(1)}, u32[]{:S(2)}, u32[]{:S(2)}) collective-permute-start(f32[2,8,256]{2,1,0:T(8,128)S(1)} %pad_maximum_fusion.2), channel_id=1, source_target_pairs={{0,8},{4,12},{8,0},{12,4},{16,24},{20,28},{24,16},{28,20},{1,9},{5... | collective-permute-start | bytes 49160 | tf_op jit(solution)/shard_map/ppermute | solution.py:438
  12.3 3.9 %collective-permute-start.2 = (f32[4,8,256]{2,1,0:T(8,128)S(1)}, f32[4,8,256]{2,1,0:T(8,128)S(1)}, u32[]{:S(2)}, u32[]{:S(2)}) collective-permute-start(f32[4,8,256]{2,1,0:T(8,128)S(1)} %pad_maximum_fusion.1), channel_id=1, source_target_pairs={{0,4},{4,0},{8,12},{12,8},{16,20},{20,16},{24,28},{28,24},{1,5},{5... | collective-permute-start | bytes 98312 | tf_op jit(solution)/shard_map/ppermute | solution.py:438
  16.2 4.3 %collective-permute-start.3 = (f32[8,8,256]{2,1,0:T(8,128)S(1)}, f32[8,8,256]{2,1,0:T(8,128)S(1)}, u32[]{:S(2)}, u32[]{:S(2)}) collective-permute-start(f32[8,8,256]{2,1,0:T(8,128)S(1)} %pad_maximum_fusion), channel_id=1, source_target_pairs={{0,2},{1,3},{2,0},{3,1},{4,6},{5,7},{6,4},{7,5},{8,10},{9,11},{10,... | collective-permute-start | bytes 196616 | tf_op jit(solution)/shard_map/ppermute | solution.py:438
  20.5 32.3 %collective-permute-start.5 = (f32[32,32,128]{2,1,0:T(8,128)S(1)}, f32[32,32,128]{2,1,0:T(8,128)S(1)}, u32[]{:S(2)}, u32[]{:S(2)}) collective-permute-start(f32[32,32,128]{2,1,0:T(8,128)S(1)} %maximum_multiply_fusion), channel_id=1, source_target_pairs={{0,28},{4,24},{8,20},{12,16},{16,12},{20,8},{24,4},{28,0},{1,29},{... | collective-permute-start | bytes 1572872 | tf_op jit(solution)/shard_map/ppermute | solution.py:488
  25.3 1.3 %collective-permute-start.4 = (f32[16,8,256]{2,1,0:T(8,128)S(1)}, f32[16,8,256]{2,1,0:T(8,128)S(1)}, u32[]{:S(2)}, u32[]{:S(2)}) collective-permute-start(f32[16,8,256]{2,1,0:T(8,128)S(1)} %constant_dynamic-update-slice_fusion.same_ref), channel_id=1, source_target_pairs={{0,1},{1,0},{2,3},{3,2},{4,5},{5,4},{6,7},{7,6},{8,9},{9,8},{10,11... | collective-permute-start | bytes 393224 | tf_op jit(solution)/shard_map/ppermute | solution.py:438
  56.9 20.8 %collective-permute-start.6 = (f32[4,128,128]{2,1,0:T(8,128)S(1)}, f32[4,128,128]{2,1,0:T(8,128)S(1)}, u32[]{:S(2)}, u32[]{:S(2)}) collective-permute-start(f32[4,128,128]{2,1,0:T(8,128)S(1)} %bitcast.23), channel_id=1, source_target_pairs={{0,4},{4,0},{8,12},{12,8},{16,20},{20,16},{24,28},{28,24},{1,5},{5... | collective-permute-start | bytes 786440 | tf_op jit(solution)/shard_map/ppermute | solution.py:438
  57.5 20.2 %collective-permute-start.7 = (f32[4,128,128]{2,1,0:T(8,128)S(1)}, f32[4,128,128]{2,1,0:T(8,128)S(1)}, u32[]{:S(2)}, u32[]{:S(2)}) collective-permute-start(f32[4,128,128]{2,1,0:T(8,128)S(1)} %bitcast.22), channel_id=1, source_target_pairs={{0,8},{4,12},{8,0},{12,4},{16,24},{20,28},{24,16},{28,20},{1,9},{5... | collective-permute-start | bytes 786440 | tf_op jit(solution)/shard_map/ppermute | solution.py:438
  57.5 20.2 %collective-permute-start.8 = (f32[4,128,128]{2,1,0:T(8,128)S(1)}, f32[4,128,128]{2,1,0:T(8,128)S(1)}, u32[]{:S(2)}, u32[]{:S(2)}) collective-permute-start(f32[4,128,128]{2,1,0:T(8,128)S(1)} %bitcast.21), channel_id=1, source_target_pairs={{0,12},{4,8},{8,4},{12,0},{16,28},{20,24},{24,20},{28,16},{1,13},{... | collective-permute-start | bytes 786440 | tf_op jit(solution)/shard_map/ppermute | solution.py:438
  60.5 17.3 %copy-start = (bf16[512,1024]{1,0:T(8,128)(2,1)S(1)}, bf16[512,1024]{1,0:T(8,128)(2,1)}, u32[]{:S(2)}) copy-start(bf16[512,1024]{1,0:T(8,128)(2,1)} %constant.50.clone.refs_5_) | copy-start | bytes 3145732
  60.5 17.3 %copy-start.1 = (bf16[512,1024]{1,0:T(8,128)(2,1)S(1)}, bf16[512,1024]{1,0:T(8,128)(2,1)}, u32[]{:S(2)}) copy-start(bf16[512,1024]{1,0:T(8,128)(2,1)} %constant.49.clone.refs_4_) | copy-start | bytes 3145732
  77.8 7.4 %copy-start.5 = (f32[256]{0:T(256)S(1)}, f32[256]{0:T(256)}, u32[]{:S(2)}) copy-start(f32[256]{0:T(256)} %param.13) | copy-start | bytes 3076
  77.8 10.1 %copy-start.2 = (bf16[512,512]{1,0:T(8,128)(2,1)S(1)}, bf16[512,512]{1,0:T(8,128)(2,1)}, u32[]{:S(2)}) copy-start(bf16[512,512]{1,0:T(8,128)(2,1)} %constant.52.clone.refs_5_) | copy-start | bytes 1572868
  77.8 10.0 %copy-start.3 = (bf16[512,512]{1,0:T(8,128)(2,1)S(1)}, bf16[512,512]{1,0:T(8,128)(2,1)}, u32[]{:S(2)}) copy-start(bf16[512,512]{1,0:T(8,128)(2,1)} %constant.51.clone.refs_4_) | copy-start | bytes 1572868
  79.5 4.6 %collective-permute-start.12 = (f32[2,128,128]{2,1,0:T(8,128)S(1)}, f32[2,128,128]{2,1,0:T(8,128)S(1)}, u32[]{:S(2)}, u32[]{:S(2)}) collective-permute-start(f32[2,128,128]{2,1,0:T(8,128)S(1)} %get-tuple-element.54), channel_id=1, source_target_pairs={{0,1},{1,0},{2,3},{3,2},{4,5},{5,4},{6,7},{7,6},{8,9},{9,8},{10,11... | collective-permute-start | bytes 393224 | tf_op jit(solution)/shard_map/ppermute | solution.py:438
  79.6 6.4 %collective-permute-start.13 = (f32[2,128,128]{2,1,0:T(8,128)S(1)}, f32[2,128,128]{2,1,0:T(8,128)S(1)}, u32[]{:S(2)}, u32[]{:S(2)}) collective-permute-start(f32[2,128,128]{2,1,0:T(8,128)S(1)} %get-tuple-element.55), channel_id=1, source_target_pairs={{0,2},{1,3},{2,0},{3,1},{4,6},{5,7},{6,4},{7,5},{8,10},{9,11},{10,... | collective-permute-start | bytes 393224 | tf_op jit(solution)/shard_map/ppermute | solution.py:438
  80.2 7.6 %collective-permute-start.14 = (f32[2,128,128]{2,1,0:T(8,128)S(1)}, f32[2,128,128]{2,1,0:T(8,128)S(1)}, u32[]{:S(2)}, u32[]{:S(2)}) collective-permute-start(f32[2,128,128]{2,1,0:T(8,128)S(1)} %get-tuple-element.56), channel_id=1, source_target_pairs={{0,3},{1,2},{2,1},{3,0},{4,7},{5,6},{6,5},{7,4},{8,11},{9,10},{10,... | collective-permute-start | bytes 393224 | tf_op jit(solution)/shard_map/ppermute | solution.py:438
  83.1 6.7 %collective-permute-start.9 = (f32[2,128,128]{2,1,0:T(8,128)S(1)}, f32[2,128,128]{2,1,0:T(8,128)S(1)}, u32[]{:S(2)}, u32[]{:S(2)}) collective-permute-start(f32[2,128,128]{2,1,0:T(8,128)S(1)} %get-tuple-element.50), channel_id=1, source_target_pairs={{0,1},{1,0},{2,3},{3,2},{4,5},{5,4},{6,7},{7,6},{8,9},{9,8},{10,11... | collective-permute-start | bytes 393224 | tf_op jit(solution)/shard_map/ppermute | solution.py:438
  83.5 8.0 %collective-permute-start.10 = (f32[2,128,128]{2,1,0:T(8,128)S(1)}, f32[2,128,128]{2,1,0:T(8,128)S(1)}, u32[]{:S(2)}, u32[]{:S(2)}) collective-permute-start(f32[2,128,128]{2,1,0:T(8,128)S(1)} %get-tuple-element.51), channel_id=1, source_target_pairs={{0,2},{1,3},{2,0},{3,1},{4,6},{5,7},{6,4},{7,5},{8,10},{9,11},{10,... | collective-permute-start | bytes 393224 | tf_op jit(solution)/shard_map/ppermute | solution.py:438
  84.1 9.3 %collective-permute-start.11 = (f32[2,128,128]{2,1,0:T(8,128)S(1)}, f32[2,128,128]{2,1,0:T(8,128)S(1)}, u32[]{:S(2)}, u32[]{:S(2)}) collective-permute-start(f32[2,128,128]{2,1,0:T(8,128)S(1)} %get-tuple-element.52), channel_id=1, source_target_pairs={{0,3},{1,2},{2,1},{3,0},{4,7},{5,6},{6,5},{7,4},{8,11},{9,10},{10,... | collective-permute-start | bytes 393224 | tf_op jit(solution)/shard_map/ppermute | solution.py:438
where the time goes:
time: 95.6 us; the launch traced here: 95.4 us
  Pallas kernels  48.5 us (51%)
  starting transfers between devices  21.7 us (23%)
  waiting for transfers between devices  12.9 us (13%)
  blocking collectives  8.23 us (9%)
  local copies, waits for them, and re-layouts  1.55 us (2%)
  between operations  1.47 us (2%)
  other arithmetic  1 us (1%)
    pallas_call x1, Pallas kernels, per_device(): pl.pallas_call(forward_kernel, grid=(slabs,), in_specs=[SMEM] + [vmem] *...  26.2 us
    ppermute x14, starting transfers between devices, swapped(): lax.ppermute(value, axis, [(i, i ^ distance) for i in range(lax.axis_size...  16.9 us
    ppermute x14, waiting for transfers between devices, swapped(): lax.ppermute(value, axis, [(i, i ^ distance) for i in range(lax.axis_size...  12.9 us
    pallas_call x1, Pallas kernels, per_device(): pl.pallas_call(gather_kernel, grid=(slab_half,), in_specs=[SMEM] + [vmem]...  9 us
    all_to_all x1, blocking collectives, per_device(): lax.all_to_all(partial.reshape(members, atoms_local), ('slab', 'dom'), 0,...  8.23 us
    ppermute x1, starting transfers between devices, per_device(): lax.ppermute(flipped, 'slab', [(s, slabs - 1 - s) for s in range(slabs)])  4.82 us
    pallas_call x1, Pallas kernels, per_device(): pl.pallas_call(inverse_x_kernel, in_specs=[SMEM] + [vmem] * 3, out_specs=...  4.07 us
    pallas_call x2, Pallas kernels, per_device(): pl.pallas_call(functools.partial(inverse_z_kernel, doms), grid=(1,), in_s...  3.89 us
  transfers between devices with their start and end apart: 15, of which 9 were waited for; matrix products, arithmetic and copies ran while one was open for 3% of the time, Pallas kernels for 41%

commit v1 on v0

--- a/solution.py
+++ b/solution.py
@@ -160,25 +160,9 @@
         out_ref[copy] = atoms
 
 
-def exchange_order(slabs, doms):
-    steps = [("slab", slabs >> (i + 1)) for i in range(slabs.bit_length() - 1)]
-    return steps + [("dom", doms >> (i + 1)) for i in range(doms.bit_length() - 2)]
-
-
-def atoms_of(refs, distance, slot, slabs, doms):
-    half = doms // 2
-    bits = slabs.bit_length() - 1
-    at = sum(((distance >> (bits - 1 - i)) & 1) << i for i in range(bits))
-    number = slot % half
-    dom_bits = doms.bit_length() - 2
-    dom_distance = sum(((number >> i) & 1) * (doms >> (i + 1)) for i in range(dom_bits))
-    return refs[slot // half][number * slabs + at], dom_distance ^ (slot // half)
-
-
 def forward_kernel(
     place_ref,
-    same_ref,
-    other_ref,
+    atoms_ref,
     factors_y,
     factors_z,
     out_ref,
@@ -194,11 +178,9 @@
     cells_x = grid_ref.shape[0]
     rows = grid_ref.shape[1] // 2
     ky_local = rows - 8
-    width = same_ref.shape[2]
+    width = atoms_ref.shape[2]
     doms = table_y.shape[2] // width
-    slabs = cells_x // XD
-    slab = lax.bitwise_xor(place_ref[6], step)
-    kept = slab - place_ref[2]
+    kept = step - place_ref[2]
     kept = jnp.where((kept >= 0) & (kept < table_y.shape[0] - 1), kept, table_y.shape[0] - 1)
 
     @pl.when(step == 0)
@@ -208,7 +190,7 @@
         digits_z[...] = jnp.zeros_like(digits_z)
 
     for slot in range(doms):
-        atoms, _ = atoms_of((same_ref, other_ref), step, slot, slabs, doms)
+        atoms = atoms_ref[step * doms + slot]
         lanes = pl.ds(slot * width, width)
         weights = spline(atoms)
         along_x = plane_weights(atoms, weights) * atoms[6:7]
@@ -230,7 +212,7 @@
         for plane in range(SPAN):
             first = 4 * rows * plane
             high, low = product[first : first + 2 * rows], product[first + 2 * rows : first + 4 * rows]
-            at = lax.rem(slab * XD + plane, cells_x)
+            at = lax.rem(step * XD + plane, cells_x)
             grid_ref[at] += (high[:, :LANES] + high[:, LANES:]) + (low[:, :LANES] + low[:, LANES:])
 
     @pl.when(step == pl.num_programs(0) - 1)
@@ -320,16 +302,15 @@
 
 
 def gather_kernel(
-    place_ref, same_ref, other_ref, table_y, table_z, near_ref, out_ref, shift_ref, fields_ref, stack_ref
+    place_ref, atoms_ref, table_y, table_z, near_ref, out_ref, shift_ref, fields_ref, stack_ref
 ):
     step = pl.program_id(0)
     half = LANES // 2
     rows = table_y.shape[1] // 2
     ky_local = rows - 8
-    width = same_ref.shape[2]
+    width = atoms_ref.shape[2]
     doms = table_y.shape[2] // width
     planes = near_ref.shape[0]
-    slabs = 2 * (planes - 3) // XD
     halves = half_sign()
 
     @pl.when(step == 0)
@@ -363,7 +344,6 @@
     first_z = place_ref[1].astype(F32)
     twice = jnp.where(first_z + iota((half, 1), 0) == 0.0, 1.0, 2.0)
     fields = fields_ref[pl.ds(step * XD, SPAN)].reshape(SPAN * LANES, 4 * LANES)
-    distance = lax.bitwise_xor(place_ref[4], step)
     for slot in range(doms):
         lanes = pl.ds(slot * width, width)
         cosine = table_y[step, pl.ds(0, ky_local), lanes]
@@ -383,7 +363,7 @@
         for part in (0, 2 * LANES)
     )
     for slot in range(doms):
-        atoms, dom_distance = atoms_of((same_ref, other_ref), distance, slot, slabs, doms)
+        atoms = atoms_ref[(place_ref[2] + step) * doms + slot]
         along_x = plane_weights(atoms, spline(atoms))
         lanes = pl.ds(slot * width, width)
         field = product[:, slot * width : (slot + 1) * width]
@@ -392,7 +372,7 @@
             total += along_x[plane : plane + 1] * field[plane * LANES : (plane + 1) * LANES]
         waves = total * table_z[step, :, lanes]
         sampled = jnp.sum((waves[:half] - waves[half:]) * twice, axis=0, keepdims=True)
-        out_ref[step * doms + lax.bitwise_xor(place_ref[5], dom_distance)] = sampled
+        out_ref[step * doms + slot] = sampled
 
 
 def bf16_pair(table):
@@ -454,7 +434,7 @@
     normalize = 1.0 / (cells_x * NY * NZ)
     upper = slab // slab_half
     place = jnp.stack(
-        [slab * ky_local, dom * kz_local, upper * slab_half, upper, slab % slab_half, dom, slab]
+        [slab * ky_local, dom * kz_local, upper * slab_half, upper, slab % slab_half, dom]
     ).astype(jnp.int32)
 
     vmem = pl.BlockSpec(memory_space=pltpu.VMEM)
@@ -462,7 +442,7 @@
         pack_kernel,
         in_specs=[SMEM, vmem, vmem, vmem],
         out_specs=vmem,
-        out_shape=jax.ShapeDtypeStruct((1, 8, atoms_local), F32),
+        out_shape=jax.ShapeDtypeStruct((slabs * doms, 8, atoms_local), F32),
         name="pack",
     )(counts, base_cells, offsets, charges.reshape(1, atoms_local))
     factors_y, factors_z = pl.pallas_call(
@@ -473,18 +453,15 @@
         compiler_params=params(8),
         name="waves",
     )(place)
-    same = atoms
-    for number, (axis, distance) in enumerate(exchange_order(slabs, doms)):
-        same = jnp.concatenate([same, swapped(same, axis, distance)], 0)
-        if number == 1:
-            same, factors_y, factors_z = lax.optimization_barrier((same, factors_y, factors_z))
-    other = swapped(same, "dom", 1)
+    gathered = lax.all_to_all(atoms, ("slab", "dom"), 0, 0, tiled=True)
 
     def halves_beside(value):
         return jnp.concatenate([value[:, :quarter_rows], value[:, quarter_rows:]], 2) * normalize
 
     own = halves_beside(green)
-    same, flipped = lax.optimization_barrier((same, halves_beside(green[:, ::-1])))
+    gathered, flipped, factors_y, factors_z = lax.optimization_barrier(
+        (gathered, halves_beside(green[:, ::-1]), factors_y, factors_z)
+    )
     mirrored = lax.ppermute(flipped, "slab", [(s, slabs - 1 - s) for s in range(slabs)])
 
     atoms_slab = doms * atoms_local
@@ -493,7 +470,7 @@
     spectrum, table_y, table_z = pl.pallas_call(
         forward_kernel,
         grid=(slabs,),
-        in_specs=[SMEM] + [vmem] * 4,
+        in_specs=[SMEM] + [vmem] * 3,
         out_specs=[vmem] * 3,
         out_shape=[
             jax.ShapeDtypeStruct((4, cells_x, quarter_rows, LANES), F32),
@@ -510,7 +487,7 @@
         compiler_params=params(16 + (table_bytes + spectrum_bytes) // MIB),
         cost_estimate=SMALL,
         name="forward",
-    )(place, same, other, factors_y, factors_z)
+    )(place, gathered, factors_y, factors_z)
 
     near_planes = cells_x // 2 + 3
     piece = (XD, 4, quarter_rows, LANES)
@@ -528,7 +505,7 @@
     partial = pl.pallas_call(
         gather_kernel,
         grid=(slab_half,),
-        in_specs=[SMEM] + [vmem] * 5,
+        in_specs=[SMEM] + [vmem] * 4,
         out_specs=vmem,
         out_shape=jax.ShapeDtypeStruct((slab_half * doms, 1, atoms_local), F32),
         scratch_shapes=[
@@ -539,21 +516,12 @@
         compiler_params=params(12 + (table_bytes + 8 * near_planes * LANES * LANES) // MIB),
         cost_estimate=SMALL,
         name="gather",
-    )(place, same, other, table_y, table_z, near.reshape(near_planes, 2 * ky_local, LANES))
+    )(place, gathered, table_y, table_z, near.reshape(near_planes, 2 * ky_local, LANES))
 
     high_y, low_y = inverse_y_table(slab_half, ky_local)
     high_z, low_z = inverse_z_table(doms)
-    members = slab_half * doms
-    sampled = lax.all_to_all(
-        partial.reshape(members, atoms_local),
-        ("slab", "dom"),
-        0,
-        0,
-        axis_index_groups=[list(range(members)), list(range(members, 2 * members))],
-        tiled=True,
-    )
     lines = [swapped(value.reshape(XD, 2 * ky_local, LANES), "slab", k) for k, value in enumerate(pieces)]
-    sampled, *lines = lax.optimization_barrier((sampled, *lines))
+    partial, *lines = lax.optimization_barrier((partial, *lines))
 
     potential = None
     for chunk in range(CHUNKS):
@@ -570,6 +538,8 @@
             cost_estimate=SMALL,
             name="inverse_y",
         )(place, *lines, high_y, low_y)
+        if chunk == CHUNKS - 1:
+            partial, *turned = lax.optimization_barrier((partial, *turned))
         columns = [swapped(value, "dom", k) for k, value in enumerate(turned)]
         earlier = [] if potential is None else [potential]
         potential = pl.pallas_call(
@@ -588,6 +558,15 @@
             name="inverse_z",
         )(place, *columns, high_z, low_z, *earlier)
 
+    members = slab_half * doms
+    sampled = lax.all_to_all(
+        partial.reshape(members, atoms_local),
+        ("slab", "dom"),
+        0,
+        0,
+        axis_index_groups=[list(range(members)), list(range(members, 2 * members))],
+        tiled=True,
+    )
     alive = jnp.arange(atoms_local, dtype=jnp.int32) < counts[0]
     gradient = jnp.where(alive, bias_coupling * jnp.sum(sampled, 0), 0.0)
     return (potential, gradient)

time: 95.6 us -> 91.6 us (0.958)
  blocking collectives: 8.23 us -> 0 us
  waiting for transfers between devices: 12.9 us -> 18.6 us
  starting transfers between devices: 21.7 us -> 19.9 us
    all_to_all x0 -> x2, starting transfers between devices: none -> 10.8 us  [the longest x1 7.3 us: per_device(): gathered = lax.all_to_all(atoms, ('slab', 'dom'), 0, 0, tiled=True)]
    all_to_all x0 -> x2, waiting for transfers between devices: none -> 9.93 us  [the longest x1 8.09 us: per_device(): gathered = lax.all_to_all(atoms, ('slab', 'dom'), 0, 0, tiled=True)]
    ppermute x14 -> x9, starting transfers between devices: 16.9 us -> 7.56 us  [swapped(): lax.ppermute(value, axis, [(i, i ^ distance) for i in range(lax.axis_size...]
    all_to_all x1 -> x0, blocking collectives: 8.23 us -> none  [per_device(): lax.all_to_all(partial.reshape(members, atoms_local), ('slab', 'dom'), 0,...]
    ppermute x14 -> x9, waiting for transfers between devices: 12.9 us -> 8.7 us  [swapped(): lax.ppermute(value, axis, [(i, i ^ distance) for i in range(lax.axis_size...]
    ppermute x1, starting transfers between devices: 4.82 us -> 1.53 us  [per_device(): lax.ppermute(flipped, 'slab', [(s, slabs - 1 - s) for s in range(slabs)])]
  transfers between devices with their start and end apart: 15 -> 12, of which waited for: 9 -> 5; matrix products, arithmetic and copies ran while one was open for 3% -> 3% of each run, Pallas kernels for 41% -> 43%
where the time goes in v1:
time: 91.6 us; the launch traced here: 91.1 us
  Pallas kernels  48.6 us (53%)
  starting transfers between devices  19.9 us (22%)
  waiting for transfers between devices  18.6 us (20%)
  local copies, waits for them, and re-layouts  1.53 us (2%)
  between operations  1.43 us (2%)
  other arithmetic  1.01 us (1%)
    pallas_call x1, Pallas kernels, per_device(): pl.pallas_call(forward_kernel, grid=(slabs,), in_specs=[SMEM] + [vmem] *...  25.5 us
    pallas_call x1, Pallas kernels, per_device(): pl.pallas_call(gather_kernel, grid=(slab_half,), in_specs=[SMEM] + [vmem]...  9.67 us
    ppermute x9, waiting for transfers between devices, swapped(): lax.ppermute(value, axis, [(i, i ^ distance) for i in range(lax.axis_size...  8.7 us
    all_to_all x1, waiting for transfers between devices, per_device(): gathered = lax.all_to_all(atoms, ('slab', 'dom'), 0, 0, tiled=True)  8.09 us
    ppermute x9, starting transfers between devices, swapped(): lax.ppermute(value, axis, [(i, i ^ distance) for i in range(lax.axis_size...  7.56 us
    all_to_all x1, starting transfers between devices, per_device(): gathered = lax.all_to_all(atoms, ('slab', 'dom'), 0, 0, tiled=True)  7.3 us
    pallas_call x1, Pallas kernels, per_device(): pl.pallas_call(inverse_x_kernel, in_specs=[SMEM] + [vmem] * 3, out_specs=...  4.07 us
    pallas_call x2, Pallas kernels, per_device(): pl.pallas_call(functools.partial(inverse_z_kernel, doms), grid=(1,), in_s...  3.89 us
  transfers between devices with their start and end apart: 12, of which 5 were waited for; matrix products, arithmetic and copies ran while one was open for 3% of the time, Pallas kernels for 43%

profile of v1, /device:TPU:0, one launch (start us, length us, event | category | flops | bytes accessed | tf_op | source)
XLA Modules:
  0.0 91.1 jit_solution(8631300116282821721)
XLA Ops:
  1.3 1.4 %pack.1 = f32[32,8,256]{2,1,0:T(8,128)} custom-call(s32[1]{0:T(128)} %copy.14.counts_ref, s32[3,256]{1,0:T(4,128)} %cells_ref.1, f32[3,256]{1,0:T(4,128)} %offsets_ref.1, f32[1,256]{1,0:T(1,128)} %bitcast.20), custom_call_target="tpu_custom_call" | custom-call | tf_op jit(solution)/shard_map/pack/pallas_call | solution.py:441
  2.7 7.3 %all-to-all-start = ((f32[32,8,256]{2,1,0:T(8,128)}), f32[32,8,256]{2,1,0:T(8,128)S(1)}, u32[]{:S(2)}, u32[]{:S(2)}) async-start(f32[32,8,256]{2,1,0:T(8,128)} %pack.1), calls=%async_computation | async-start | bytes 524288 | tf_op jit(solution)/shard_map/all_to_all | solution.py:456
  10.1 0.7 waves.1
  10.9 1.3 %fusion = (f32[32,32,64]{2,1,0:T(8,128)S(1)}, f32[32,32,64]{2,1,0:T(8,128)S(1)}) fusion(f32[32,64,64]{2,1,0:T(8,128)} %param.15), kind=kLoop, calls=%fused_computation.3 | loop fusion | bytes 1048576 | tf_op jit(solution)/shard_map/slice | solution.py:459
  12.5 8.1 %all-to-all-done.atoms_ref = f32[32,8,256]{2,1,0:T(8,128)S(1)} async-done(((f32[32,8,256]{2,1,0:T(8,128)}), f32[32,8,256]{2,1,0:T(8,128)S(1)}, u32[]{:S(2)}, u32[]{:S(2)}) %all-to-all-start) | async-done | bytes 262176 | tf_op jit(solution)/shard_map/all_to_all | solution.py:456
  20.6 1.5 %collective-permute-start = (f32[32,32,128]{2,1,0:T(8,128)S(1)}, f32[32,32,128]{2,1,0:T(8,128)S(1)}, u32[]{:S(2)}, u32[]{:S(2)}) collective-permute-start(f32[32,32,128]{2,1,0:T(8,128)S(1)} %maximum_multiply_fusion), channel_id=1, source_target_pairs={{0,28},{4,24},{8,20},{12,16},{16,12},{20,8},{24,4},{28,0},{1,29},{... | collective-permute-start | bytes 1572872 | tf_op jit(solution)/shard_map/ppermute | solution.py:465
  22.4 25.5 %forward.1 = (f32[4,32,32,128]{3,2,1,0:T(8,128)S(1)}, f32[5,144,1024]{2,1,0:T(8,128)S(1)}, f32[5,128,1024]{2,1,0:T(8,128)S(1)}) custom-call(s32[6]{0:T(128)S(1)} %stack.27.place_ref, f32[32,8,256]{2,1,0:T(8,128)S(1)} %all-to-all-done.atoms_ref, bf16[288,256]{1,0:T(8,128)(2,1)S(1)} %get-tuple-element.37.factors_y, ...), custom_call_target="tpu_custom_call" | custom-call | flops 1000000 | bytes 10000 | tf_op jit(solution)/shard_map/forward/pallas_call | solution.py:470
  47.9 4.1 %inverse_x.1 = (f32[4,4,32,128]{3,2,1,0:T(8,128)S(1)}, f32[4,4,32,128]{3,2,1,0:T(8,128)S(1)}, f32[4,4,32,128]{3,2,1,0:T(8,128)S(1)}, f32[4,4,32,128]{3,2,1,0:T(8,128)S(1)}, f32[19,4,32,128]{3,2,1,0:T(8,128)S(1)}) custom-call(s32[6]{0:T(128)S(1)} %stack.27.place_ref, f32[4,32,32,128]{3,2,1,0:T(8,128)S(1)} %get-tuple-element.41.spectrum_ref, ...), custom_call_target="tpu_custom_call" | custom-call | flops 1000000 | bytes 10000 | tf_op jit(solution)/shard_map/inverse_x/pallas_call | solution.py:494
  52.0 1.3 %collective-permute-start.1 = (f32[4,128,128]{2,1,0:T(8,128)S(1)}, f32[4,128,128]{2,1,0:T(8,128)S(1)}, u32[]{:S(2)}, u32[]{:S(2)}) collective-permute-start(f32[4,128,128]{2,1,0:T(8,128)S(1)} %bitcast.19), channel_id=1, source_target_pairs={{0,4},{4,0},{8,12},{12,8},{16,20},{20,16},{24,28},{28,24},{1,5},{5... | collective-permute-start | bytes 786440 | tf_op jit(solution)/shard_map/ppermute | solution.py:418
  53.3 2.2 %collective-permute-start.3 = (f32[4,128,128]{2,1,0:T(8,128)S(1)}, f32[4,128,128]{2,1,0:T(8,128)S(1)}, u32[]{:S(2)}, u32[]{:S(2)}) collective-permute-start(f32[4,128,128]{2,1,0:T(8,128)S(1)} %bitcast.17), channel_id=1, source_target_pairs={{0,12},{4,8},{8,4},{12,0},{16,28},{20,24},{24,20},{28,16},{1,13},{... | collective-permute-start | bytes 786440 | tf_op jit(solution)/shard_map/ppermute | solution.py:418
  55.5 9.7 %gather.1 = f32[16,1,256]{2,1,0:T(1,128)} custom-call(s32[6]{0:T(128)S(1)} %stack.27.place_ref, f32[32,8,256]{2,1,0:T(8,128)S(1)} %all-to-all-done.atoms_ref, f32[5,144,1024]{2,1,0:T(8,128)S(1)} %get-tuple-element.39.table_y, f32[5,128,1024]{2,1,0:T(8,128)S(1)} %get-tuple-element.40.table_z, f32[19,128,128]{2,1,0:T(8,128)S(1)} %bitcast.14), custom_call_target="tpu_custom_call" | custom-call | flops 1000000 | bytes 10000 | tf_op jit(solution)/shard_map/gather/pallas_call | solution.py:505
  65.2 1.3 %collective-permute-done.3.refs_3_ = f32[4,128,128]{2,1,0:T(8,128)S(1)} collective-permute-done((f32[4,128,128]{2,1,0:T(8,128)S(1)}, f32[4,128,128]{2,1,0:T(8,128)S(1)}, u32[]{:S(2)}, u32[]{:S(2)}) %collective-permute-start.3) | collective-permute-done | bytes 262176 | tf_op jit(solution)/shard_map/ppermute | solution.py:418
  66.5 1.7 %inverse_y.3 = (f32[2,128,128]{2,1,0:T(8,128)S(1)}, f32[2,128,128]{2,1,0:T(8,128)S(1)}, f32[2,128,128]{2,1,0:T(8,128)S(1)}, f32[2,128,128]{2,1,0:T(8,128)S(1)}) custom-call(s32[6]{0:T(128)S(1)} %stack.27.place_ref, f32[4,128,128]{2,1,0:T(8,128)S(1)} %bitcast.15, f32[4,128,128]{2,1,0:T(8,128)S(1)} %collective-permute-done.1.refs_1_, ...), custom_call_target="tpu_custom_call" | custom-call | flops 1000000 | bytes 10000 | tf_op jit(solution)/shard_map/inverse_y/pallas_call | solution.py:528
  68.3 1.7 %inverse_y.2 = (f32[2,128,128]{2,1,0:T(8,128)S(1)}, f32[2,128,128]{2,1,0:T(8,128)S(1)}, f32[2,128,128]{2,1,0:T(8,128)S(1)}, f32[2,128,128]{2,1,0:T(8,128)S(1)}) custom-call(s32[6]{0:T(128)S(1)} %stack.27.place_ref, f32[4,128,128]{2,1,0:T(8,128)S(1)} %bitcast.16, f32[4,128,128]{2,1,0:T(8,128)S(1)} %collective-permute-done.1.refs_1_, ...), custom_call_target="tpu_custom_call" | custom-call | flops 1000000 | bytes 10000 | tf_op jit(solution)/shard_map/inverse_y/pallas_call | solution.py:528
  70.0 3.5 %all-to-all-start.1 = ((f32[16,1,256]{2,1,0:T(1,128)}), f32[16,1,256]{2,1,0:T(1,128)S(1)}, u32[]{:S(2)}, u32[]{:S(2)}) async-start(f32[16,1,256]{2,1,0:T(1,128)} %gather.1), calls=%async_computation.1 | async-start | bytes 32768 | tf_op jit(solution)/shard_map/all_to_all | solution.py:562
  73.5 0.5 collective-permute-start.4
  73.9 1.5 %collective-permute-start.5 = (f32[2,128,128]{2,1,0:T(8,128)S(1)}, f32[2,128,128]{2,1,0:T(8,128)S(1)}, u32[]{:S(2)}, u32[]{:S(2)}) collective-permute-start(f32[2,128,128]{2,1,0:T(8,128)S(1)} %get-tuple-element.59), channel_id=1, source_target_pairs={{0,2},{1,3},{2,0},{3,1},{4,6},{5,7},{6,4},{7,5},{8,10},{9,11},{10,... | collective-permute-start | bytes 393224 | tf_op jit(solution)/shard_map/ppermute | solution.py:418
  75.5 1.7 %collective-permute-start.8 = (f32[2,128,128]{2,1,0:T(8,128)S(1)}, f32[2,128,128]{2,1,0:T(8,128)S(1)}, u32[]{:S(2)}, u32[]{:S(2)}) collective-permute-start(f32[2,128,128]{2,1,0:T(8,128)S(1)} %get-tuple-element.63), channel_id=1, source_target_pairs={{0,2},{1,3},{2,0},{3,1},{4,6},{5,7},{6,4},{7,5},{8,10},{9,11},{10,... | collective-permute-start | bytes 393224 | tf_op jit(solution)/shard_map/ppermute | solution.py:418
  77.1 1.8 %all-to-all-done.1 = f32[16,1,256]{2,1,0:T(1,128)S(1)} async-done(((f32[16,1,256]{2,1,0:T(1,128)}), f32[16,1,256]{2,1,0:T(1,128)S(1)}, u32[]{:S(2)}, u32[]{:S(2)}) %all-to-all-start.1) | async-done | bytes 16416 | tf_op jit(solution)/shard_map/all_to_all | solution.py:562
  79.3 0.6 compare_select_fusion
  79.9 6.1 %collective-permute-done.8.refs_2_ = f32[2,128,128]{2,1,0:T(8,128)S(1)} collective-permute-done((f32[2,128,128]{2,1,0:T(8,128)S(1)}, f32[2,128,128]{2,1,0:T(8,128)S(1)}, u32[]{:S(2)}, u32[]{:S(2)}) %collective-permute-start.8) | collective-permute-done | bytes 131104 | tf_op jit(solution)/shard_map/ppermute | solution.py:418
  86.0 1.3 %collective-permute-done.9.refs_3_ = f32[2,128,128]{2,1,0:T(8,128)S(1)} collective-permute-done((f32[2,128,128]{2,1,0:T(8,128)S(1)}, f32[2,128,128]{2,1,0:T(8,128)S(1)}, u32[]{:S(2)}, u32[]{:S(2)}) %collective-permute-start.9) | collective-permute-done | bytes 131104 | tf_op jit(solution)/shard_map/ppermute | solution.py:418
  87.2 1.9 %inverse_z.2.refs_6_ = f32[4,128,512]{2,1,0:T(8,128)} custom-call(s32[6]{0:T(128)S(1)} %stack.27.place_ref, f32[2,128,128]{2,1,0:T(8,128)S(1)} %get-tuple-element.61.refs_0_, f32[2,128,128]{2,1,0:T(8,128)S(1)} %collective-permute-done.7.refs_1_, f32[2,128,128]{2,1,0:T(8,128)S(1)} %collective-permute-done.8.refs_2_, ...), custom_call_target="tpu_custom_call" | custom-call | flops 1000000 | bytes 10000 | tf_op jit(solution)/shard_map/inverse_z/pallas_call | solution.py:545
  89.2 1.9 %inverse_z.3 = f32[4,128,512]{2,1,0:T(8,128)} custom-call(s32[6]{0:T(128)S(1)} %stack.27.place_ref, f32[2,128,128]{2,1,0:T(8,128)S(1)} %get-tuple-element.57.refs_0_, f32[2,128,128]{2,1,0:T(8,128)S(1)} %collective-permute-done.4.refs_1_, f32[2,128,128]{2,1,0:T(8,128)S(1)} %collective-permute-done.5.refs_2_, ...), custom_call_target="tpu_custom_call", output_to_operand_aliasing={{}: (7, {})} | custom-call | flops 1000000 | bytes 10000 | tf_op jit(solution)/shard_map/inverse_z/pallas_call | solution.py:545
  (27 shorter events, 1.0 us)
Async XLA Ops:
  2.7 17.9 %all-to-all-start = ((f32[32,8,256]{2,1,0:T(8,128)}), f32[32,8,256]{2,1,0:T(8,128)S(1)}, u32[]{:S(2)}, u32[]{:S(2)}) async-start(f32[32,8,256]{2,1,0:T(8,128)} %pack.1), calls=%async_computation | async-start | bytes 524288 | tf_op jit(solution)/shard_map/all_to_all | solution.py:456
  20.6 27.3 %collective-permute-start = (f32[32,32,128]{2,1,0:T(8,128)S(1)}, f32[32,32,128]{2,1,0:T(8,128)S(1)}, u32[]{:S(2)}, u32[]{:S(2)}) collective-permute-start(f32[32,32,128]{2,1,0:T(8,128)S(1)} %maximum_multiply_fusion), channel_id=1, source_target_pairs={{0,28},{4,24},{8,20},{12,16},{16,12},{20,8},{24,4},{28,0},{1,29},{... | collective-permute-start | bytes 1572872 | tf_op jit(solution)/shard_map/ppermute | solution.py:465
  52.0 13.2 %collective-permute-start.1 = (f32[4,128,128]{2,1,0:T(8,128)S(1)}, f32[4,128,128]{2,1,0:T(8,128)S(1)}, u32[]{:S(2)}, u32[]{:S(2)}) collective-permute-start(f32[4,128,128]{2,1,0:T(8,128)S(1)} %bitcast.19), channel_id=1, source_target_pairs={{0,4},{4,0},{8,12},{12,8},{16,20},{20,16},{24,28},{28,24},{1,5},{5... | collective-permute-start | bytes 786440 | tf_op jit(solution)/shard_map/ppermute | solution.py:418
  53.3 11.9 %collective-permute-start.2 = (f32[4,128,128]{2,1,0:T(8,128)S(1)}, f32[4,128,128]{2,1,0:T(8,128)S(1)}, u32[]{:S(2)}, u32[]{:S(2)}) collective-permute-start(f32[4,128,128]{2,1,0:T(8,128)S(1)} %bitcast.18), channel_id=1, source_target_pairs={{0,8},{4,12},{8,0},{12,4},{16,24},{20,28},{24,16},{28,20},{1,9},{5... | collective-permute-start | bytes 786440 | tf_op jit(solution)/shard_map/ppermute | solution.py:418
  53.3 13.2 %collective-permute-start.3 = (f32[4,128,128]{2,1,0:T(8,128)S(1)}, f32[4,128,128]{2,1,0:T(8,128)S(1)}, u32[]{:S(2)}, u32[]{:S(2)}) collective-permute-start(f32[4,128,128]{2,1,0:T(8,128)S(1)} %bitcast.17), channel_id=1, source_target_pairs={{0,12},{4,8},{8,4},{12,0},{16,28},{20,24},{24,20},{28,16},{1,13},{... | collective-permute-start | bytes 786440 | tf_op jit(solution)/shard_map/ppermute | solution.py:418
  55.5 11.0 %copy-start = (bf16[512,1024]{1,0:T(8,128)(2,1)S(1)}, bf16[512,1024]{1,0:T(8,128)(2,1)}, u32[]{:S(2)}) copy-start(bf16[512,1024]{1,0:T(8,128)(2,1)} %constant.50.clone.refs_5_) | copy-start | bytes 3145732
  55.5 11.0 %copy-start.1 = (bf16[512,1024]{1,0:T(8,128)(2,1)S(1)}, bf16[512,1024]{1,0:T(8,128)(2,1)}, u32[]{:S(2)}) copy-start(bf16[512,1024]{1,0:T(8,128)(2,1)} %constant.49.clone.refs_4_) | copy-start | bytes 3145732
  66.5 12.8 %copy-start.4 = (f32[256]{0:T(256)S(1)}, f32[256]{0:T(256)}, u32[]{:S(2)}) copy-start(f32[256]{0:T(256)} %param.13) | copy-start | bytes 3076
  66.5 20.7 %copy-start.2 = (bf16[512,512]{1,0:T(8,128)(2,1)S(1)}, bf16[512,512]{1,0:T(8,128)(2,1)}, u32[]{:S(2)}) copy-start(bf16[512,512]{1,0:T(8,128)(2,1)} %constant.52.clone.refs_5_) | copy-start | bytes 1572868
  66.5 20.7 %copy-start.3 = (bf16[512,512]{1,0:T(8,128)(2,1)S(1)}, bf16[512,512]{1,0:T(8,128)(2,1)}, u32[]{:S(2)}) copy-start(bf16[512,512]{1,0:T(8,128)(2,1)} %constant.51.clone.refs_4_) | copy-start | bytes 1572868
  68.2 10.8 %collective-permute-start.7 = (f32[2,128,128]{2,1,0:T(8,128)S(1)}, f32[2,128,128]{2,1,0:T(8,128)S(1)}, u32[]{:S(2)}, u32[]{:S(2)}) collective-permute-start(f32[2,128,128]{2,1,0:T(8,128)S(1)} %get-tuple-element.62), channel_id=1, source_target_pairs={{0,1},{1,0},{2,3},{3,2},{4,5},{5,4},{6,7},{7,6},{8,9},{9,8},{10,11... | collective-permute-start | bytes 393224 | tf_op jit(solution)/shard_map/ppermute | solution.py:418
  70.0 9.0 %all-to-all-start.1 = ((f32[16,1,256]{2,1,0:T(1,128)}), f32[16,1,256]{2,1,0:T(1,128)S(1)}, u32[]{:S(2)}, u32[]{:S(2)}) async-start(f32[16,1,256]{2,1,0:T(1,128)} %gather.1), calls=%async_computation.1 | async-start | bytes 32768 | tf_op jit(solution)/shard_map/all_to_all | solution.py:562
  73.5 15.7 %collective-permute-start.4 = (f32[2,128,128]{2,1,0:T(8,128)S(1)}, f32[2,128,128]{2,1,0:T(8,128)S(1)}, u32[]{:S(2)}, u32[]{:S(2)}) collective-permute-start(f32[2,128,128]{2,1,0:T(8,128)S(1)} %get-tuple-element.58), channel_id=1, source_target_pairs={{0,1},{1,0},{2,3},{3,2},{4,5},{5,4},{6,7},{7,6},{8,9},{9,8},{10,11... | collective-permute-start | bytes 393224 | tf_op jit(solution)/shard_map/ppermute | solution.py:418
  73.9 15.3 %collective-permute-start.5 = (f32[2,128,128]{2,1,0:T(8,128)S(1)}, f32[2,128,128]{2,1,0:T(8,128)S(1)}, u32[]{:S(2)}, u32[]{:S(2)}) collective-permute-start(f32[2,128,128]{2,1,0:T(8,128)S(1)} %get-tuple-element.59), channel_id=1, source_target_pairs={{0,2},{1,3},{2,0},{3,1},{4,6},{5,7},{6,4},{7,5},{8,10},{9,11},{10,... | collective-permute-start | bytes 393224 | tf_op jit(solution)/shard_map/ppermute | solution.py:418
  75.4 13.7 %collective-permute-start.6 = (f32[2,128,128]{2,1,0:T(8,128)S(1)}, f32[2,128,128]{2,1,0:T(8,128)S(1)}, u32[]{:S(2)}, u32[]{:S(2)}) collective-permute-start(f32[2,128,128]{2,1,0:T(8,128)S(1)} %get-tuple-element.60), channel_id=1, source_target_pairs={{0,3},{1,2},{2,1},{3,0},{4,7},{5,6},{6,5},{7,4},{8,11},{9,10},{10,... | collective-permute-start | bytes 393224 | tf_op jit(solution)/shard_map/ppermute | solution.py:418
  75.5 10.5 %collective-permute-start.8 = (f32[2,128,128]{2,1,0:T(8,128)S(1)}, f32[2,128,128]{2,1,0:T(8,128)S(1)}, u32[]{:S(2)}, u32[]{:S(2)}) collective-permute-start(f32[2,128,128]{2,1,0:T(8,128)S(1)} %get-tuple-element.63), channel_id=1, source_target_pairs={{0,2},{1,3},{2,0},{3,1},{4,6},{5,7},{6,4},{7,5},{8,10},{9,11},{10,... | collective-permute-start | bytes 393224 | tf_op jit(solution)/shard_map/ppermute | solution.py:418
  79.0 8.2 %collective-permute-start.9 = (f32[2,128,128]{2,1,0:T(8,128)S(1)}, f32[2,128,128]{2,1,0:T(8,128)S(1)}, u32[]{:S(2)}, u32[]{:S(2)}) collective-permute-start(f32[2,128,128]{2,1,0:T(8,128)S(1)} %get-tuple-element.64), channel_id=1, source_target_pairs={{0,3},{1,2},{2,1},{3,0},{4,7},{5,6},{6,5},{7,4},{8,11},{9,10},{10,... | collective-permute-start | bytes 393224 | tf_op jit(solution)/shard_map/ppermute | solution.py:418

commit v2 on v1

--- a/solution.py
+++ b/solution.py
@@ -15,7 +15,7 @@
 KH = NZ // 2
 LANES = 128
 SPAN = XD + 3
-CHUNKS = 2
+CHUNKS = 1
 DEPTH = XD // CHUNKS
 MIB = 1 << 20
 BF16 = jnp.bfloat16
@@ -124,23 +124,42 @@
     return jnp.where(lane < LANES // 2, -1.0, 1.0).astype(F32)
 
 
-def rotate(value, numer, denom, sign, halves):
+def rotate(value, numer, denom, sign):
+    real, imag = value
     if numer == 0:
         return value
     if 4 * numer == denom:
-        return swap(value) * (halves * sign)
+        return (-imag, real) if sign > 0 else (imag, -real)
     angle = 2.0 * np.pi * numer / denom
-    return value * float(np.cos(angle)) + swap(value) * (halves * float(sign * np.sin(angle)))
-
-
-def transform(values, sign, halves):
+    cosine, sine = float(np.cos(angle)), float(sign * np.sin(angle))
+    if 8 * numer in (denom, 3 * denom):
+        size = abs(cosine)
+        cos_sign, sin_sign = (1 if cosine > 0 else -1), (1 if sine > 0 else -1)
+        if cos_sign == sin_sign:
+            return ((real - imag) * (cos_sign * size), (real + imag) * (cos_sign * size))
+        return ((real + imag) * (cos_sign * size), (imag - real) * (cos_sign * size))
+    return real * cosine - imag * sine, imag * cosine + real * sine
+
+
+def butterfly(even, turned):
+    plus = (even[0] + turned[0], even[1] + turned[1])
+    return plus, (even[0] - turned[0], even[1] - turned[1])
+
+
+def transform(values, sign):
     count = len(values)
     if count == 1:
         return values
-    even = transform(values[0::2], sign, halves)
-    odd = transform(values[1::2], sign, halves)
-    turned = [rotate(odd[k], k, count, sign, halves) for k in range(count // 2)]
-    return [e + t for e, t in zip(even, turned)] + [e - t for e, t in zip(even, turned)]
+    even = transform(values[0::2], sign)
+    odd = transform(values[1::2], sign)
+    both = [butterfly(even[k], rotate(odd[k], k, count, sign)) for k in range(count // 2)]
+    return [pair[0] for pair in both] + [pair[1] for pair in both]
+
+
+def regroup(low, high):
+    first = lax.broadcasted_iota(jnp.int32, low.shape, 1) < LANES // 2
+    crossed = swap(jnp.where(first, high, low))
+    return jnp.where(first, low, crossed), jnp.where(first, crossed, high)
 
 
 def pack_kernel(counts_ref, cells_ref, offsets_ref, charges_ref, out_ref):
@@ -217,45 +236,49 @@
 
     @pl.when(step == pl.num_programs(0) - 1)
     def _():
-        halves = half_sign()
         quarter_rows = ky_local // 2
         group = min(8, quarter_rows)
         for minus in (0, 1):
-            for start in range(0, ky_local, group):
-                row = start + minus
+            for start in range(0, quarter_rows, group):
                 values = []
                 for x in range(cells_x):
-                    top = grid_ref[x, pl.ds(row, group), :]
-                    bottom = swap(grid_ref[x, pl.ds(rows + row, group), :])
-                    values.append(bottom - top * halves if minus else -bottom - top * halves)
-                at = 2 * minus + start // quarter_rows
-                for x, value in enumerate(transform(values, -1.0, halves)):
-                    out_ref[at, x, pl.ds(start % quarter_rows, group), :] = value
+                    parts = [
+                        grid_ref[x, pl.ds(minus + start + offset, group), :]
+                        for offset in (0, quarter_rows, rows, rows + quarter_rows)
+                    ]
+                    cos_cos, cos_sin = regroup(parts[0], parts[1])
+                    sin_cos, sin_sin = regroup(parts[2], parts[3])
+                    if minus:
+                        values.append((cos_cos + sin_sin, sin_cos - cos_sin))
+                    else:
+                        values.append((cos_cos - sin_sin, -cos_sin - sin_cos))
+                for x, value in enumerate(transform(values, -1)):
+                    for part in (0, 1):
+                        out_ref[2 * minus + part, x, pl.ds(start, group), :] = value[part]
 
 
 def inverse_x_kernel(place_ref, spectrum_ref, own_ref, mirrored_ref, *refs):
     *outs, near_ref = refs
     cells_x, quarter_rows = spectrum_ref.shape[1:3]
     group = min(8, quarter_rows)
-    halves = half_sign()
-    lane = lax.broadcasted_iota(jnp.int32, (1, LANES), 1)
     side = 1.0 - 2.0 * place_ref[3].astype(F32)
 
     def rows_of(step, carry):
         rows = pl.ds(pl.multiple_of(step * group, group), group)
-        for quarter in range(4):
+        for minus, green_ref in enumerate((own_ref, mirrored_ref)):
             values = []
             for kx in range(cells_x):
-                green = (own_ref if quarter < 2 else mirrored_ref)[kx, rows, :]
-                keep = lane < LANES // 2 if quarter % 2 == 0 else lane >= LANES // 2
-                values.append(spectrum_ref[quarter, kx, rows, :] * jnp.where(keep, green, swap(green)))
-            even = transform(values[0::2], 1.0, halves)
-            odd = transform(values[1::2], 1.0, halves)
+                green = green_ref[kx, rows, :]
+                values.append(tuple(spectrum_ref[2 * minus + part, kx, rows, :] * green for part in (0, 1)))
+            even = transform(values[0::2], 1)
+            odd = transform([(value[0] * side, value[1] * side) for value in values[1::2]], 1)
             for x in range(cells_x // 2):
-                turned = rotate(odd[x], x, cells_x, 1.0, halves) * side
-                near_ref[x, quarter, rows, :] = even[x] + turned
-                if x < 3:
-                    near_ref[cells_x // 2 + x, quarter, rows, :] = even[x] - turned
+                here, there = butterfly(even[x], rotate(odd[x], x, cells_x, 1))
+                wanted = [(x, here)] + ([(cells_x // 2 + x, there)] if x < 3 else [])
+                for plane, value in wanted:
+                    low, high = regroup(value[0], value[1])
+                    near_ref[plane, 2 * minus, rows, :] = low
+                    near_ref[plane, 2 * minus + 1, rows, :] = high
         return carry
 
     lax.fori_loop(0, quarter_rows // group, rows_of, 0)
@@ -534,13 +557,13 @@
                 pltpu.VMEM((slab_half, DEPTH, 2 * ky_local, LANES), F32),
                 pltpu.VMEM((doms, DEPTH, rows_local, LANES), F32),
             ],
-            compiler_params=params(24),
+            compiler_params=params(32),
             cost_estimate=SMALL,
             name="inverse_y",
         )(place, *lines, high_y, low_y)
+        columns = [swapped(value, "dom", k) for k, value in enumerate(turned)]
         if chunk == CHUNKS - 1:
-            partial, *turned = lax.optimization_barrier((partial, *turned))
-        columns = [swapped(value, "dom", k) for k, value in enumerate(turned)]
+            partial, columns[1] = lax.optimization_barrier((partial, columns[1]))
         earlier = [] if potential is None else [potential]
         potential = pl.pallas_call(
             functools.partial(inverse_z_kernel, doms),

time: 91.6 us -> 81.7 us (0.89)
  Pallas kernels: 48.6 us -> 37.8 us
  starting transfers between devices: 19.9 us -> 22.5 us
  waiting for transfers between devices: 18.6 us -> 17.1 us
    pallas_call x1, Pallas kernels: 25.5 us -> 19.1 us  [per_device(): pl.pallas_call(forward_kernel, grid=(slabs,), in_specs=[SMEM] + [vmem] *...]
    pallas_call x1, Pallas kernels: 4.07 us -> 1.85 us  [per_device(): pl.pallas_call(inverse_x_kernel, in_specs=[SMEM] + [vmem] * 3, out_specs=...]
    ppermute x9 -> x6, starting transfers between devices: 7.56 us -> 9.42 us  [swapped(): lax.ppermute(value, axis, [(i, i ^ distance) for i in range(lax.axis_size...]
    all_to_all x1, waiting for transfers between devices: 1.84 us -> 0.01 us  [per_device(): lax.all_to_all(partial.reshape(members, atoms_local), ('slab', 'dom'), 0,...]
    pallas_call x2 -> x1, Pallas kernels: 3.89 us -> 2.58 us  [per_device(): pl.pallas_call(functools.partial(inverse_z_kernel, doms), grid=(1,), in_s...]
    pallas_call x2 -> x1, Pallas kernels: 3.31 us -> 2.48 us  [per_device(): pl.pallas_call(functools.partial(inverse_y_kernel, slab_half, chunk), in_...]
    ppermute x9 -> x6, waiting for transfers between devices: 8.7 us -> 9.01 us  [swapped(): lax.ppermute(value, axis, [(i, i ^ distance) for i in range(lax.axis_size...]
  transfers between devices with their start and end apart: 12 -> 9, of which waited for: 5 -> 4; matrix products, arithmetic and copies ran while one was open for 3% -> 2% of each run, Pallas kernels for 43% -> 39%
where the time goes in v2:
time: 81.7 us; the launch traced here: 81.4 us
  Pallas kernels  37.8 us (46%)
  starting transfers between devices  22.5 us (28%)
  waiting for transfers between devices  17.1 us (21%)
  local copies, waits for them, and re-layouts  1.53 us (2%)
  between operations  1.41 us (2%)
  other arithmetic  1.01 us (1%)
    pallas_call x1, Pallas kernels, per_device(): pl.pallas_call(forward_kernel, grid=(slabs,), in_specs=[SMEM] + [vmem] *...  19.1 us
    pallas_call x1, Pallas kernels, per_device(): pl.pallas_call(gather_kernel, grid=(slab_half,), in_specs=[SMEM] + [vmem]...  9.67 us
    ppermute x6, starting transfers between devices, swapped(): lax.ppermute(value, axis, [(i, i ^ distance) for i in range(lax.axis_size...  9.42 us
    ppermute x6, waiting for transfers between devices, swapped(): lax.ppermute(value, axis, [(i, i ^ distance) for i in range(lax.axis_size...  9.01 us
    all_to_all x1, waiting for transfers between devices, per_device(): gathered = lax.all_to_all(atoms, ('slab', 'dom'), 0, 0, tiled=True)  8.09 us
    all_to_all x1, starting transfers between devices, per_device(): gathered = lax.all_to_all(atoms, ('slab', 'dom'), 0, 0, tiled=True)  7.3 us
    all_to_all x1, starting transfers between devices, per_device(): lax.all_to_all(partial.reshape(members, atoms_local), ('slab', 'dom'), 0,...  4.29 us
    pallas_call x1, Pallas kernels, per_device(): pl.pallas_call(functools.partial(inverse_z_kernel, doms), grid=(1,), in_s...  2.58 us
  transfers between devices with their start and end apart: 9, of which 4 were waited for; matrix products, arithmetic and copies ran while one was open for 2% of the time, Pallas kernels for 39%

profile of v2, /device:TPU:0, one launch (start us, length us, event | category | flops | bytes accessed | tf_op | source)
XLA Modules:
  0.0 81.4 jit_solution(13326337626893654315)
XLA Ops:
  1.3 1.4 %pack.1 = f32[32,8,256]{2,1,0:T(8,128)} custom-call(s32[1]{0:T(128)} %copy.12.counts_ref, s32[3,256]{1,0:T(4,128)} %cells_ref.1, f32[3,256]{1,0:T(4,128)} %offsets_ref.1, f32[1,256]{1,0:T(1,128)} %bitcast.19), custom_call_target="tpu_custom_call" | custom-call | tf_op jit(solution)/shard_map/pack/pallas_call | solution.py:464
  2.7 7.3 %all-to-all-start = ((f32[32,8,256]{2,1,0:T(8,128)}), f32[32,8,256]{2,1,0:T(8,128)S(1)}, u32[]{:S(2)}, u32[]{:S(2)}) async-start(f32[32,8,256]{2,1,0:T(8,128)} %pack.1), calls=%async_computation | async-start | bytes 524288 | tf_op jit(solution)/shard_map/all_to_all | solution.py:479
  10.0 0.1 stack.27.place_ref
  10.1 0.7 waves.1
  10.9 1.3 %fusion = (f32[32,32,64]{2,1,0:T(8,128)S(1)}, f32[32,32,64]{2,1,0:T(8,128)S(1)}) fusion(f32[32,64,64]{2,1,0:T(8,128)} %param.15), kind=kLoop, calls=%fused_computation.3 | loop fusion | bytes 1048576 | tf_op jit(solution)/shard_map/slice | solution.py:482
  12.2 0.1 slice.17
  12.3 0.2 maximum_multiply_fusion
  12.5 8.1 %all-to-all-done.atoms_ref = f32[32,8,256]{2,1,0:T(8,128)S(1)} async-done(((f32[32,8,256]{2,1,0:T(8,128)}), f32[32,8,256]{2,1,0:T(8,128)S(1)}, u32[]{:S(2)}, u32[]{:S(2)}) %all-to-all-start) | async-done | bytes 262176 | tf_op jit(solution)/shard_map/all_to_all | solution.py:479
  20.6 1.5 %collective-permute-start = (f32[32,32,128]{2,1,0:T(8,128)S(1)}, f32[32,32,128]{2,1,0:T(8,128)S(1)}, u32[]{:S(2)}, u32[]{:S(2)}) collective-permute-start(f32[32,32,128]{2,1,0:T(8,128)S(1)} %maximum_multiply_fusion), channel_id=1, source_target_pairs={{0,28},{4,24},{8,20},{12,16},{16,12},{20,8},{24,4},{28,0},{1,29},{... | collective-permute-start | bytes 1572872 | tf_op jit(solution)/shard_map/ppermute | solution.py:488
  22.1 0.2 maximum_multiply_fusion.1.own_ref
  22.4 19.1 %forward.1 = (f32[4,32,32,128]{3,2,1,0:T(8,128)S(1)}, f32[5,144,1024]{2,1,0:T(8,128)S(1)}, f32[5,128,1024]{2,1,0:T(8,128)S(1)}) custom-call(s32[6]{0:T(128)S(1)} %stack.27.place_ref, f32[32,8,256]{2,1,0:T(8,128)S(1)} %all-to-all-done.atoms_ref, bf16[288,256]{1,0:T(8,128)(2,1)S(1)} %get-tuple-element.30.factors_y, ...), custom_call_target="tpu_custom_call" | custom-call | flops 1000000 | bytes 10000 | tf_op jit(solution)/shard_map/forward/pallas_call | solution.py:493
  41.4 1.9 %inverse_x.1 = (f32[4,4,32,128]{3,2,1,0:T(8,128)S(1)}, f32[4,4,32,128]{3,2,1,0:T(8,128)S(1)}, f32[4,4,32,128]{3,2,1,0:T(8,128)S(1)}, f32[4,4,32,128]{3,2,1,0:T(8,128)S(1)}, f32[19,4,32,128]{3,2,1,0:T(8,128)S(1)}) custom-call(s32[6]{0:T(128)S(1)} %stack.27.place_ref, f32[4,32,32,128]{3,2,1,0:T(8,128)S(1)} %get-tuple-element.34.spectrum_ref, ...), custom_call_target="tpu_custom_call" | custom-call | flops 1000000 | bytes 10000 | tf_op jit(solution)/shard_map/inverse_x/pallas_call | solution.py:517
  43.3 1.3 %collective-permute-start.1 = (f32[4,128,128]{2,1,0:T(8,128)S(1)}, f32[4,128,128]{2,1,0:T(8,128)S(1)}, u32[]{:S(2)}, u32[]{:S(2)}) collective-permute-start(f32[4,128,128]{2,1,0:T(8,128)S(1)} %bitcast.18), channel_id=1, source_target_pairs={{0,4},{4,0},{8,12},{12,8},{16,20},{20,16},{24,28},{28,24},{1,5},{5... | collective-permute-start | bytes 786440 | tf_op jit(solution)/shard_map/ppermute | solution.py:441
  44.6 5.4 %collective-permute-start.2 = (f32[4,128,128]{2,1,0:T(8,128)S(1)}, f32[4,128,128]{2,1,0:T(8,128)S(1)}, u32[]{:S(2)}, u32[]{:S(2)}) collective-permute-start(f32[4,128,128]{2,1,0:T(8,128)S(1)} %bitcast.17), channel_id=1, source_target_pairs={{0,8},{4,12},{8,0},{12,4},{16,24},{20,28},{24,16},{28,20},{1,9},{5... | collective-permute-start | bytes 786440 | tf_op jit(solution)/shard_map/ppermute | solution.py:441
  50.0 9.7 %gather.1 = f32[16,1,256]{2,1,0:T(1,128)} custom-call(s32[6]{0:T(128)S(1)} %stack.27.place_ref, f32[32,8,256]{2,1,0:T(8,128)S(1)} %all-to-all-done.atoms_ref, f32[5,144,1024]{2,1,0:T(8,128)S(1)} %get-tuple-element.32.table_y, f32[5,128,1024]{2,1,0:T(8,128)S(1)} %get-tuple-element.33.table_z, f32[19,128,128]{2,1,0:T(8,128)S(1)} %bitcast.14), custom_call_target="tpu_custom_call" | custom-call | flops 1000000 | bytes 10000 | tf_op jit(solution)/shard_map/gather/pallas_call | solution.py:528
  59.7 1.0 %collective-permute-done.3.refs_3_ = f32[4,128,128]{2,1,0:T(8,128)S(1)} collective-permute-done((f32[4,128,128]{2,1,0:T(8,128)S(1)}, f32[4,128,128]{2,1,0:T(8,128)S(1)}, u32[]{:S(2)}, u32[]{:S(2)}) %collective-permute-start.3) | collective-permute-done | bytes 262176 | tf_op jit(solution)/shard_map/ppermute | solution.py:441
  60.7 2.5 %inverse_y.1 = (f32[4,128,128]{2,1,0:T(8,128)S(1)}, f32[4,128,128]{2,1,0:T(8,128)S(1)}, f32[4,128,128]{2,1,0:T(8,128)S(1)}, f32[4,128,128]{2,1,0:T(8,128)S(1)}) custom-call(s32[6]{0:T(128)S(1)} %stack.27.place_ref, f32[4,128,128]{2,1,0:T(8,128)S(1)} %bitcast.15, f32[4,128,128]{2,1,0:T(8,128)S(1)} %collective-permute-done.1.refs_1_, ...), custom_call_target="tpu_custom_call" | custom-call | flops 1000000 | bytes 10000 | tf_op jit(solution)/shard_map/inverse_y/pallas_call | solution.py:551
  63.2 0.1 collective-permute-start.4
  63.3 2.6 %collective-permute-start.5 = (f32[4,128,128]{2,1,0:T(8,128)S(1)}, f32[4,128,128]{2,1,0:T(8,128)S(1)}, u32[]{:S(2)}, u32[]{:S(2)}) collective-permute-start(f32[4,128,128]{2,1,0:T(8,128)S(1)} %get-tuple-element.49), channel_id=1, source_target_pairs={{0,2},{1,3},{2,0},{3,1},{4,6},{5,7},{6,4},{7,5},{8,10},{9,11},{10,... | collective-permute-start | bytes 786440 | tf_op jit(solution)/shard_map/ppermute | solution.py:441
  65.9 4.3 %all-to-all-start.1 = ((f32[16,1,256]{2,1,0:T(1,128)}), f32[16,1,256]{2,1,0:T(1,128)S(1)}, u32[]{:S(2)}, u32[]{:S(2)}) async-start(f32[16,1,256]{2,1,0:T(1,128)} %gather.1), calls=%async_computation.1 | async-start | bytes 32768 | tf_op jit(solution)/shard_map/all_to_all | solution.py:585
  70.2 2.8 %collective-permute-done.5.refs_2_ = f32[4,128,128]{2,1,0:T(8,128)S(1)} collective-permute-done((f32[4,128,128]{2,1,0:T(8,128)S(1)}, f32[4,128,128]{2,1,0:T(8,128)S(1)}, u32[]{:S(2)}, u32[]{:S(2)}) %collective-permute-start.5) | collective-permute-done | bytes 262176 | tf_op jit(solution)/shard_map/ppermute | solution.py:441
  73.0 5.2 %collective-permute-done.6.refs_3_ = f32[4,128,128]{2,1,0:T(8,128)S(1)} collective-permute-done((f32[4,128,128]{2,1,0:T(8,128)S(1)}, f32[4,128,128]{2,1,0:T(8,128)S(1)}, u32[]{:S(2)}, u32[]{:S(2)}) %collective-permute-start.6) | collective-permute-done | bytes 262176 | tf_op jit(solution)/shard_map/ppermute | solution.py:441
  78.2 2.6 %inverse_z.1 = f32[4,128,512]{2,1,0:T(8,128)} custom-call(s32[6]{0:T(128)S(1)} %stack.27.place_ref, f32[4,128,128]{2,1,0:T(8,128)S(1)} %get-tuple-element.45.refs_0_, f32[4,128,128]{2,1,0:T(8,128)S(1)} %collective-permute-done.4.refs_1_, f32[4,128,128]{2,1,0:T(8,128)S(1)} %collective-permute-done.5.refs_2_, ...), custom_call_target="tpu_custom_call" | custom-call | flops 1000000 | bytes 10000 | tf_op jit(solution)/shard_map/inverse_z/pallas_call | solution.py:568
  80.8 0.6 compare_select_fusion
  (19 shorter events, 0.2 us)
Async XLA Ops:
  2.7 17.9 %all-to-all-start = ((f32[32,8,256]{2,1,0:T(8,128)}), f32[32,8,256]{2,1,0:T(8,128)S(1)}, u32[]{:S(2)}, u32[]{:S(2)}) async-start(f32[32,8,256]{2,1,0:T(8,128)} %pack.1), calls=%async_computation | async-start | bytes 524288 | tf_op jit(solution)/shard_map/all_to_all | solution.py:479
  20.6 20.8 %collective-permute-start = (f32[32,32,128]{2,1,0:T(8,128)S(1)}, f32[32,32,128]{2,1,0:T(8,128)S(1)}, u32[]{:S(2)}, u32[]{:S(2)}) collective-permute-start(f32[32,32,128]{2,1,0:T(8,128)S(1)} %maximum_multiply_fusion), channel_id=1, source_target_pairs={{0,28},{4,24},{8,20},{12,16},{16,12},{20,8},{24,4},{28,0},{1,29},{... | collective-permute-start | bytes 1572872 | tf_op jit(solution)/shard_map/ppermute | solution.py:488
  43.3 16.4 %collective-permute-start.1 = (f32[4,128,128]{2,1,0:T(8,128)S(1)}, f32[4,128,128]{2,1,0:T(8,128)S(1)}, u32[]{:S(2)}, u32[]{:S(2)}) collective-permute-start(f32[4,128,128]{2,1,0:T(8,128)S(1)} %bitcast.18), channel_id=1, source_target_pairs={{0,4},{4,0},{8,12},{12,8},{16,20},{20,16},{24,28},{28,24},{1,5},{5... | collective-permute-start | bytes 786440 | tf_op jit(solution)/shard_map/ppermute | solution.py:441
  44.6 15.1 %collective-permute-start.2 = (f32[4,128,128]{2,1,0:T(8,128)S(1)}, f32[4,128,128]{2,1,0:T(8,128)S(1)}, u32[]{:S(2)}, u32[]{:S(2)}) collective-permute-start(f32[4,128,128]{2,1,0:T(8,128)S(1)} %bitcast.17), channel_id=1, source_target_pairs={{0,8},{4,12},{8,0},{12,4},{16,24},{20,28},{24,16},{28,20},{1,9},{5... | collective-permute-start | bytes 786440 | tf_op jit(solution)/shard_map/ppermute | solution.py:441
  50.0 10.7 %collective-permute-start.3 = (f32[4,128,128]{2,1,0:T(8,128)S(1)}, f32[4,128,128]{2,1,0:T(8,128)S(1)}, u32[]{:S(2)}, u32[]{:S(2)}) collective-permute-start(f32[4,128,128]{2,1,0:T(8,128)S(1)} %bitcast.16), channel_id=1, source_target_pairs={{0,12},{4,8},{8,4},{12,0},{16,28},{20,24},{24,20},{28,16},{1,13},{... | collective-permute-start | bytes 786440 | tf_op jit(solution)/shard_map/ppermute | solution.py:441
  50.0 10.7 %copy-start = (bf16[512,1024]{1,0:T(8,128)(2,1)S(1)}, bf16[512,1024]{1,0:T(8,128)(2,1)}, u32[]{:S(2)}) copy-start(bf16[512,1024]{1,0:T(8,128)(2,1)} %constant.50.clone.refs_5_) | copy-start | bytes 3145732
  50.0 10.7 %copy-start.1 = (bf16[512,1024]{1,0:T(8,128)(2,1)S(1)}, bf16[512,1024]{1,0:T(8,128)(2,1)}, u32[]{:S(2)}) copy-start(bf16[512,1024]{1,0:T(8,128)(2,1)} %constant.49.clone.refs_4_) | copy-start | bytes 3145732
  59.7 18.5 %copy-start.2 = (bf16[512,512]{1,0:T(8,128)(2,1)S(1)}, bf16[512,512]{1,0:T(8,128)(2,1)}, u32[]{:S(2)}) copy-start(bf16[512,512]{1,0:T(8,128)(2,1)} %constant.52.clone.refs_5_) | copy-start | bytes 1572868
  59.7 18.5 %copy-start.3 = (bf16[512,512]{1,0:T(8,128)(2,1)S(1)}, bf16[512,512]{1,0:T(8,128)(2,1)}, u32[]{:S(2)}) copy-start(bf16[512,512]{1,0:T(8,128)(2,1)} %constant.51.clone.refs_4_) | copy-start | bytes 1572868
  60.7 20.1 %copy-start.4 = (f32[256]{0:T(256)S(1)}, f32[256]{0:T(256)}, u32[]{:S(2)}) copy-start(f32[256]{0:T(256)} %param.13) | copy-start | bytes 3076
  63.2 2.7 %collective-permute-start.4 = (f32[4,128,128]{2,1,0:T(8,128)S(1)}, f32[4,128,128]{2,1,0:T(8,128)S(1)}, u32[]{:S(2)}, u32[]{:S(2)}) collective-permute-start(f32[4,128,128]{2,1,0:T(8,128)S(1)} %get-tuple-element.47), channel_id=1, source_target_pairs={{0,1},{1,0},{2,3},{3,2},{4,5},{5,4},{6,7},{7,6},{8,9},{9,8},{10,11... | collective-permute-start | bytes 786440 | tf_op jit(solution)/shard_map/ppermute | solution.py:441
  63.3 9.7 %collective-permute-start.5 = (f32[4,128,128]{2,1,0:T(8,128)S(1)}, f32[4,128,128]{2,1,0:T(8,128)S(1)}, u32[]{:S(2)}, u32[]{:S(2)}) collective-permute-start(f32[4,128,128]{2,1,0:T(8,128)S(1)} %get-tuple-element.49), channel_id=1, source_target_pairs={{0,2},{1,3},{2,0},{3,1},{4,6},{5,7},{6,4},{7,5},{8,10},{9,11},{10,... | collective-permute-start | bytes 786440 | tf_op jit(solution)/shard_map/ppermute | solution.py:441
  65.9 12.3 %collective-permute-start.6 = (f32[4,128,128]{2,1,0:T(8,128)S(1)}, f32[4,128,128]{2,1,0:T(8,128)S(1)}, u32[]{:S(2)}, u32[]{:S(2)}) collective-permute-start(f32[4,128,128]{2,1,0:T(8,128)S(1)} %get-tuple-element.50), channel_id=1, source_target_pairs={{0,3},{1,2},{2,1},{3,0},{4,7},{5,6},{6,5},{7,4},{8,11},{9,10},{10,... | collective-permute-start | bytes 786440 | tf_op jit(solution)/shard_map/ppermute | solution.py:441
  65.9 14.9 %all-to-all-start.1 = ((f32[16,1,256]{2,1,0:T(1,128)}), f32[16,1,256]{2,1,0:T(1,128)S(1)}, u32[]{:S(2)}, u32[]{:S(2)}) async-start(f32[16,1,256]{2,1,0:T(1,128)} %gather.1), calls=%async_computation.1 | async-start | bytes 32768 | tf_op jit(solution)/shard_map/all_to_all | solution.py:585

commit v3 on v2

--- a/solution.py
+++ b/solution.py
@@ -179,12 +179,19 @@
         out_ref[copy] = atoms
 
 
+def atoms_of(same_ref, other_ref, slab, slot, doms):
+    half = doms // 2
+    return (same_ref, other_ref)[slot // half][slab * half + slot % half]
+
+
 def forward_kernel(
     place_ref,
-    atoms_ref,
+    same_ref,
+    other_ref,
     factors_y,
     factors_z,
-    out_ref,
+    plus_ref,
+    minus_ref,
     table_y,
     table_z,
     left_ref,
@@ -197,7 +204,7 @@
     cells_x = grid_ref.shape[0]
     rows = grid_ref.shape[1] // 2
     ky_local = rows - 8
-    width = atoms_ref.shape[2]
+    width = same_ref.shape[2]
     doms = table_y.shape[2] // width
     kept = step - place_ref[2]
     kept = jnp.where((kept >= 0) & (kept < table_y.shape[0] - 1), kept, table_y.shape[0] - 1)
@@ -209,16 +216,16 @@
         digits_z[...] = jnp.zeros_like(digits_z)
 
     for slot in range(doms):
-        atoms = atoms_ref[step * doms + slot]
+        atoms = atoms_of(same_ref, other_ref, step, slot, doms)
         lanes = pl.ds(slot * width, width)
         weights = spline(atoms)
         along_x = plane_weights(atoms, weights) * atoms[6:7]
         waves = atom_waves(atoms[2:3], [w[5:6] for w in weights], factors_z, digits_z.at[slot])
         waves = jnp.concatenate(waves, 0)
         table_z[kept, :, lanes] = waves
-        high, low = split(waves.T)
-        right_ref[slot, :, :LANES] = high
-        right_ref[slot, :, LANES:] = low
+        high, low = split(waves)
+        right_ref[slot, pl.ds(0, LANES), :] = high
+        right_ref[slot, pl.ds(LANES, LANES), :] = low
         cosine, sine = atom_waves(atoms[1:2], [w[4:5] for w in weights], factors_y, digits_y.at[slot])
         waves = jnp.concatenate([cosine, sine], 0)
         table_y[kept, :, lanes] = waves
@@ -227,7 +234,9 @@
             high, low = split(waves * along_x[plane : plane + 1])
             left_ref[slot, pl.ds(first, 2 * rows), :] = high
             left_ref[slot, pl.ds(first + 2 * rows, 2 * rows), :] = low
-        product = jnp.dot(left_ref[slot], right_ref[slot], preferred_element_type=F32)
+        product = lax.dot_general(
+            left_ref[slot], right_ref[slot], (((1,), (1,)), ((), ())), preferred_element_type=F32
+        )
         for plane in range(SPAN):
             first = 4 * rows * plane
             high, low = product[first : first + 2 * rows], product[first + 2 * rows : first + 4 * rows]
@@ -238,7 +247,7 @@
     def _():
         quarter_rows = ky_local // 2
         group = min(8, quarter_rows)
-        for minus in (0, 1):
+        for minus, out_ref in enumerate((plus_ref, minus_ref)):
             for start in range(0, quarter_rows, group):
                 values = []
                 for x in range(cells_x):
@@ -254,10 +263,10 @@
                         values.append((cos_cos - sin_sin, -cos_sin - sin_cos))
                 for x, value in enumerate(transform(values, -1)):
                     for part in (0, 1):
-                        out_ref[2 * minus + part, x, pl.ds(start, group), :] = value[part]
-
-
-def inverse_x_kernel(place_ref, spectrum_ref, own_ref, mirrored_ref, *refs):
+                        out_ref[part, x, pl.ds(start, group), :] = value[part]
+
+
+def inverse_x_kernel(place_ref, spectrum_ref, green_ref, *refs):
     *outs, near_ref = refs
     cells_x, quarter_rows = spectrum_ref.shape[1:3]
     group = min(8, quarter_rows)
@@ -265,20 +274,18 @@
 
     def rows_of(step, carry):
         rows = pl.ds(pl.multiple_of(step * group, group), group)
-        for minus, green_ref in enumerate((own_ref, mirrored_ref)):
-            values = []
-            for kx in range(cells_x):
-                green = green_ref[kx, rows, :]
-                values.append(tuple(spectrum_ref[2 * minus + part, kx, rows, :] * green for part in (0, 1)))
-            even = transform(values[0::2], 1)
-            odd = transform([(value[0] * side, value[1] * side) for value in values[1::2]], 1)
-            for x in range(cells_x // 2):
-                here, there = butterfly(even[x], rotate(odd[x], x, cells_x, 1))
-                wanted = [(x, here)] + ([(cells_x // 2 + x, there)] if x < 3 else [])
-                for plane, value in wanted:
-                    low, high = regroup(value[0], value[1])
-                    near_ref[plane, 2 * minus, rows, :] = low
-                    near_ref[plane, 2 * minus + 1, rows, :] = high
+        values = []
+        for kx in range(cells_x):
+            green = green_ref[kx, rows, :]
+            values.append(tuple(spectrum_ref[part, kx, rows, :] * green for part in (0, 1)))
+        even = transform(values[0::2], 1)
+        odd = transform([(value[0] * side, value[1] * side) for value in values[1::2]], 1)
+        for x in range(cells_x // 2):
+            here, there = butterfly(even[x], rotate(odd[x], x, cells_x, 1))
+            wanted = [(x, here)] + ([(cells_x // 2 + x, there)] if x < 3 else [])
+            for plane, value in wanted:
+                for part, row_group in enumerate(regroup(value[0], value[1])):
+                    near_ref[plane, part, rows, :] = row_group
         return carry
 
     lax.fori_loop(0, quarter_rows // group, rows_of, 0)
@@ -287,10 +294,13 @@
 
 
 def inverse_y_kernel(sources, chunk, place_ref, *refs):
-    ins, (high_ref, low_ref) = refs[:sources], refs[sources : sources + 2]
-    outs, (lines_ref, turned_ref) = refs[sources + 2 : -2], refs[-2:]
-    for k in range(sources):
-        lines_ref[lax.bitwise_xor(place_ref[4], k)] = ins[k][pl.ds(chunk * DEPTH, DEPTH)]
+    ins, (high_ref, low_ref) = refs[: 2 * sources], refs[2 * sources : 2 * sources + 2]
+    outs, (lines_ref, turned_ref) = refs[2 * sources + 2 : -2], refs[-2:]
+    for number, in_ref in enumerate(ins):
+        source = lax.bitwise_xor(place_ref[4], number % sources)
+        half = in_ref.shape[1]
+        rows = pl.ds(half * (number // sources), half)
+        lines_ref[source, :, rows, :] = in_ref[pl.ds(chunk * DEPTH, DEPTH)]
     parts = []
     for x in range(DEPTH):
         lines = jnp.concatenate([lines_ref[source, x] for source in range(sources)], 0)
@@ -325,15 +335,15 @@
 
 
 def gather_kernel(
-    place_ref, atoms_ref, table_y, table_z, near_ref, out_ref, shift_ref, fields_ref, stack_ref
+    place_ref, same_ref, other_ref, table_y, table_z, plus_ref, minus_ref, out_ref, shift_ref, fields_ref, stack_ref
 ):
     step = pl.program_id(0)
     half = LANES // 2
     rows = table_y.shape[1] // 2
     ky_local = rows - 8
-    width = atoms_ref.shape[2]
+    width = same_ref.shape[2]
     doms = table_y.shape[2] // width
-    planes = near_ref.shape[0]
+    planes = plus_ref.shape[0]
     halves = half_sign()
 
     @pl.when(step == 0)
@@ -343,8 +353,8 @@
         row = lax.broadcasted_iota(jnp.int32, (8, LANES), 0)
 
         def build(x, carry):
-            plus = near_ref[x, pl.ds(0, ky_local), :]
-            shift_ref[pl.ds(1, ky_local), :] = near_ref[x, pl.ds(ky_local, ky_local), :]
+            plus = plus_ref[x]
+            shift_ref[pl.ds(1, ky_local), :] = minus_ref[x]
             minus = shift_ref[pl.ds(0, ky_local), :]
             last = shift_ref[pl.ds(ky_local, 8), :][0:1]
             main = [plus + minus, swap(plus - minus) * halves]
@@ -386,7 +396,7 @@
         for part in (0, 2 * LANES)
     )
     for slot in range(doms):
-        atoms = atoms_ref[(place_ref[2] + step) * doms + slot]
+        atoms = atoms_of(same_ref, other_ref, place_ref[2] + step, slot, doms)
         along_x = plane_weights(atoms, spline(atoms))
         lanes = pl.ds(slot * width, width)
         field = product[:, slot * width : (slot + 1) * width]
@@ -395,7 +405,8 @@
             total += along_x[plane : plane + 1] * field[plane * LANES : (plane + 1) * LANES]
         waves = total * table_z[step, :, lanes]
         sampled = jnp.sum((waves[:half] - waves[half:]) * twice, axis=0, keepdims=True)
-        out_ref[step * doms + slot] = sampled
+        core = place_ref[5] % 2 if slot < doms // 2 else 1 - place_ref[5] % 2
+        out_ref[step * doms + 2 * (slot % (doms // 2)) + core] = sampled
 
 
 def bf16_pair(table):
@@ -465,7 +476,7 @@
         pack_kernel,
         in_specs=[SMEM, vmem, vmem, vmem],
         out_specs=vmem,
-        out_shape=jax.ShapeDtypeStruct((slabs * doms, 8, atoms_local), F32),
+        out_shape=jax.ShapeDtypeStruct((slabs * doms // 2, 8, atoms_local), F32),
         name="pack",
     )(counts, base_cells, offsets, charges.reshape(1, atoms_local))
     factors_y, factors_z = pl.pallas_call(
@@ -476,33 +487,38 @@
         compiler_params=params(8),
         name="waves",
     )(place)
-    gathered = lax.all_to_all(atoms, ("slab", "dom"), 0, 0, tiled=True)
+    everyone = list(range(slabs * doms))
+    same = lax.all_to_all(
+        atoms, ("slab", "dom"), 0, 0, axis_index_groups=[everyone[0::2], everyone[1::2]], tiled=True
+    )
 
     def halves_beside(value):
         return jnp.concatenate([value[:, :quarter_rows], value[:, quarter_rows:]], 2) * normalize
 
     own = halves_beside(green)
-    gathered, flipped, factors_y, factors_z = lax.optimization_barrier(
-        (gathered, halves_beside(green[:, ::-1]), factors_y, factors_z)
-    )
+    same, flipped, factors_y, factors_z = lax.optimization_barrier(
+        (same, halves_beside(green[:, ::-1]), factors_y, factors_z)
+    )
+    other = swapped(same, "dom", 1)
     mirrored = lax.ppermute(flipped, "slab", [(s, slabs - 1 - s) for s in range(slabs)])
 
     atoms_slab = doms * atoms_local
     table_bytes = 4 * (slab_half + 1) * (2 * rows + LANES) * atoms_slab
     spectrum_bytes = 16 * cells_x * max(8, quarter_rows) * LANES
-    spectrum, table_y, table_z = pl.pallas_call(
+    plus, minus, table_y, table_z = pl.pallas_call(
         forward_kernel,
         grid=(slabs,),
-        in_specs=[SMEM] + [vmem] * 3,
-        out_specs=[vmem] * 3,
+        in_specs=[SMEM] + [vmem] * 4,
+        out_specs=[vmem] * 4,
         out_shape=[
-            jax.ShapeDtypeStruct((4, cells_x, quarter_rows, LANES), F32),
+            jax.ShapeDtypeStruct((2, cells_x, quarter_rows, LANES), F32),
+            jax.ShapeDtypeStruct((2, cells_x, quarter_rows, LANES), F32),
             jax.ShapeDtypeStruct((slab_half + 1, 2 * rows, atoms_slab), F32),
             jax.ShapeDtypeStruct((slab_half + 1, LANES, atoms_slab), F32),
         ],
         scratch_shapes=[
             pltpu.VMEM((doms, SPAN * 4 * rows, atoms_local), BF16),
-            pltpu.VMEM((doms, atoms_local, 2 * LANES), BF16),
+            pltpu.VMEM((doms, 2 * LANES, atoms_local), BF16),
             pltpu.VMEM((cells_x, 2 * rows, LANES), F32),
             pltpu.VMEM((doms, TERMS, atoms_local), BF16),
             pltpu.VMEM((doms, TERMS, atoms_local), BF16),
@@ -510,25 +526,28 @@
         compiler_params=params(16 + (table_bytes + spectrum_bytes) // MIB),
         cost_estimate=SMALL,
         name="forward",
-    )(place, gathered, factors_y, factors_z)
+    )(place, same, other, factors_y, factors_z)
 
     near_planes = cells_x // 2 + 3
-    piece = (XD, 4, quarter_rows, LANES)
-    *pieces, near = pl.pallas_call(
-        inverse_x_kernel,
-        in_specs=[SMEM] + [vmem] * 3,
-        out_specs=[vmem] * (slab_half + 1),
-        out_shape=[jax.ShapeDtypeStruct(piece, F32)] * slab_half
-        + [jax.ShapeDtypeStruct((near_planes, 4, quarter_rows, LANES), F32)],
-        compiler_params=params(32),
-        cost_estimate=SMALL,
-        name="inverse_x",
-    )(place, spectrum, own, mirrored)
+    lines, near = [], []
+    for spectrum, influence in ((plus, own), (minus, mirrored)):
+        *pieces, planes = pl.pallas_call(
+            inverse_x_kernel,
+            in_specs=[SMEM] + [vmem] * 2,
+            out_specs=[vmem] * (slab_half + 1),
+            out_shape=[jax.ShapeDtypeStruct((XD, 2, quarter_rows, LANES), F32)] * slab_half
+            + [jax.ShapeDtypeStruct((near_planes, 2, quarter_rows, LANES), F32)],
+            compiler_params=params(24),
+            cost_estimate=SMALL,
+            name="inverse_x",
+        )(place, spectrum, influence)
+        near.append(planes.reshape(near_planes, ky_local, LANES))
+        lines += [swapped(value.reshape(XD, ky_local, LANES), "slab", k) for k, value in enumerate(pieces)]
 
     partial = pl.pallas_call(
         gather_kernel,
         grid=(slab_half,),
-        in_specs=[SMEM] + [vmem] * 4,
+        in_specs=[SMEM] + [vmem] * 6,
         out_specs=vmem,
         out_shape=jax.ShapeDtypeStruct((slab_half * doms, 1, atoms_local), F32),
         scratch_shapes=[
@@ -539,18 +558,17 @@
         compiler_params=params(12 + (table_bytes + 8 * near_planes * LANES * LANES) // MIB),
         cost_estimate=SMALL,
         name="gather",
-    )(place, gathered, table_y, table_z, near.reshape(near_planes, 2 * ky_local, LANES))
+    )(place, same, other, table_y, table_z, *near)
 
     high_y, low_y = inverse_y_table(slab_half, ky_local)
     high_z, low_z = inverse_z_table(doms)
-    lines = [swapped(value.reshape(XD, 2 * ky_local, LANES), "slab", k) for k, value in enumerate(pieces)]
     partial, *lines = lax.optimization_barrier((partial, *lines))
 
     potential = None
     for chunk in range(CHUNKS):
         turned = pl.pallas_call(
             functools.partial(inverse_y_kernel, slab_half, chunk),
-            in_specs=[SMEM] + [vmem] * (slab_half + 2),
+            in_specs=[SMEM] + [vmem] * (2 * slab_half + 2),
             out_specs=[vmem] * doms,
             out_shape=[jax.ShapeDtypeStruct((DEPTH, rows_local, LANES), F32)] * doms,
             scratch_shapes=[

time: 81.7 us -> 80.9 us (level)
  waiting for transfers between devices: 17.1 us -> 15.1 us
  Pallas kernels: 37.8 us -> 39.1 us
    all_to_all x1, waiting for transfers between devices: 8.09 us -> 5.29 us  [per_device(): lax.all_to_all(atoms, ('slab', 'dom'), 0, 0, axis_index_groups=[everyone[...]
    all_to_all x1, starting transfers between devices: 7.3 us -> 8.31 us  [per_device(): lax.all_to_all(atoms, ('slab', 'dom'), 0, 0, axis_index_groups=[everyone[...]
    pallas_call x1 -> x2, Pallas kernels: 1.85 us -> 2.68 us  [per_device(): pl.pallas_call(inverse_x_kernel, in_specs=[SMEM] + [vmem] * 2, out_specs=...]
    ppermute x6 -> x10, waiting for transfers between devices: 9.01 us -> 9.77 us  [swapped(): lax.ppermute(value, axis, [(i, i ^ distance) for i in range(lax.axis_size...]
    ppermute x6 -> x10, starting transfers between devices: 9.42 us -> 9.04 us  [swapped(): lax.ppermute(value, axis, [(i, i ^ distance) for i in range(lax.axis_size...]
  transfers between devices with their start and end apart: 9 -> 13, of which waited for: 4 -> 4; matrix products, arithmetic and copies ran while one was open for 2% -> 2% of each run, Pallas kernels for 39% -> 44%
where the time goes in v3:
time: 80.9 us; the launch traced here: 80.4 us
  Pallas kernels  39.1 us (48%)
  starting transfers between devices  22.3 us (28%)
  waiting for transfers between devices  15.1 us (19%)
  local copies, waits for them, and re-layouts  1.53 us (2%)
  between operations  1.45 us (2%)
  other arithmetic  1.01 us (1%)
    pallas_call x1, Pallas kernels, per_device(): pl.pallas_call(forward_kernel, grid=(slabs,), in_specs=[SMEM] + [vmem] *...  19.6 us
    ppermute x10, waiting for transfers between devices, swapped(): lax.ppermute(value, axis, [(i, i ^ distance) for i in range(lax.axis_size...  9.77 us
    pallas_call x1, Pallas kernels, per_device(): pl.pallas_call(gather_kernel, grid=(slab_half,), in_specs=[SMEM] + [vmem]...  9.61 us
    ppermute x10, starting transfers between devices, swapped(): lax.ppermute(value, axis, [(i, i ^ distance) for i in range(lax.axis_size...  9.04 us
    all_to_all x1, starting transfers between devices, per_device(): lax.all_to_all(atoms, ('slab', 'dom'), 0, 0, axis_index_groups=[everyone[...  8.31 us
    all_to_all x1, waiting for transfers between devices, per_device(): lax.all_to_all(atoms, ('slab', 'dom'), 0, 0, axis_index_groups=[everyone[...  5.29 us
    all_to_all x1, starting transfers between devices, per_device(): lax.all_to_all(partial.reshape(members, atoms_local), ('slab', 'dom'), 0,...  3.48 us
    pallas_call x2, Pallas kernels, per_device(): pl.pallas_call(inverse_x_kernel, in_specs=[SMEM] + [vmem] * 2, out_specs=...  2.68 us
  transfers between devices with their start and end apart: 13, of which 4 were waited for; matrix products, arithmetic and copies ran while one was open for 2% of the time, Pallas kernels for 44%

profile of v3, /device:TPU:0, one launch (start us, length us, event | category | flops | bytes accessed | tf_op | source)
XLA Modules:
  0.0 80.4 jit_solution(436465568897536508)
XLA Ops:
  1.3 1.4 %pack.1 = f32[16,8,256]{2,1,0:T(8,128)} custom-call(s32[1]{0:T(128)} %copy.12.counts_ref, s32[3,256]{1,0:T(4,128)} %cells_ref.1, f32[3,256]{1,0:T(4,128)} %offsets_ref.1, f32[1,256]{1,0:T(1,128)} %bitcast.29), custom_call_target="tpu_custom_call" | custom-call | tf_op jit(solution)/shard_map/pack/pallas_call | solution.py:475
  2.7 8.3 %all-to-all-start = ((f32[16,8,256]{2,1,0:T(8,128)}), f32[16,8,256]{2,1,0:T(8,128)S(1)}, u32[]{:S(2)}, u32[]{:S(2)}) async-start(f32[16,8,256]{2,1,0:T(8,128)} %pack.1), calls=%async_computation | async-start | bytes 262144 | tf_op jit(solution)/shard_map/all_to_all | solution.py:491
  11.0 1.3 %fusion = (f32[32,32,64]{2,1,0:T(8,128)S(1)}, f32[32,32,64]{2,1,0:T(8,128)S(1)}) fusion(f32[32,64,64]{2,1,0:T(8,128)} %param.15), kind=kLoop, calls=%fused_computation.3 | loop fusion | bytes 1048576 | tf_op jit(solution)/shard_map/slice | solution.py:496
  12.4 0.7 waves.1
  13.5 5.3 %all-to-all-done.same_ref = f32[16,8,256]{2,1,0:T(8,128)S(1)} async-done(((f32[16,8,256]{2,1,0:T(8,128)}), f32[16,8,256]{2,1,0:T(8,128)S(1)}, u32[]{:S(2)}, u32[]{:S(2)}) %all-to-all-start) | async-done | bytes 131104 | tf_op jit(solution)/shard_map/all_to_all | solution.py:491
  18.8 1.4 %collective-permute-start.1 = (f32[32,32,128]{2,1,0:T(8,128)S(1)}, f32[32,32,128]{2,1,0:T(8,128)S(1)}, u32[]{:S(2)}, u32[]{:S(2)}) collective-permute-start(f32[32,32,128]{2,1,0:T(8,128)S(1)} %maximum_multiply_fusion), channel_id=1, source_target_pairs={{0,28},{4,24},{8,20},{12,16},{16,12},{20,8},{24,4},{28,0},{1,29},{... | collective-permute-start | bytes 1572872 | tf_op jit(solution)/shard_map/ppermute | solution.py:503
  20.4 1.1 %collective-permute-done.other_ref = f32[16,8,256]{2,1,0:T(8,128)S(1)} collective-permute-done((f32[16,8,256]{2,1,0:T(8,128)S(1)}, f32[16,8,256]{2,1,0:T(8,128)S(1)}, u32[]{:S(2)}, u32[]{:S(2)}) %collective-permute-start) | collective-permute-done | bytes 131104 | tf_op jit(solution)/shard_map/ppermute | solution.py:452
  21.6 19.6 %forward.1 = (f32[2,32,32,128]{3,2,1,0:T(8,128)S(1)}, f32[2,32,32,128]{3,2,1,0:T(8,128)S(1)}, f32[5,144,1024]{2,1,0:T(8,128)S(1)}, f32[5,128,1024]{2,1,0:T(8,128)S(1)}) custom-call(s32[6]{0:T(128)S(1)} %stack.27.place_ref, f32[16,8,256]{2,1,0:T(8,128)S(1)} %all-to-all-done.same_ref, f32[16,8,256]{2,1,0:T(8,128)S(1)} %collective-permute-done.other_ref, ...), custom_call_target="tpu_custom_call" | custom-call | flops 1000000 | bytes 10000 | tf_op jit(solution)/shard_map/forward/pallas_call | solution.py:508
  41.2 1.3 %inverse_x.2 = (f32[4,2,32,128]{3,2,1,0:T(8,128)S(1)}, f32[4,2,32,128]{3,2,1,0:T(8,128)S(1)}, f32[4,2,32,128]{3,2,1,0:T(8,128)S(1)}, f32[4,2,32,128]{3,2,1,0:T(8,128)S(1)}, f32[19,2,32,128]{3,2,1,0:T(8,128)S(1)}) custom-call(s32[6]{0:T(128)S(1)} %stack.27.place_ref, f32[2,32,32,128]{3,2,1,0:T(8,128)S(1)} %get-tuple-element.44.spectrum_ref, ...), custom_call_target="tpu_custom_call" | custom-call | flops 1000000 | bytes 10000 | tf_op jit(solution)/shard_map/inverse_x/pallas_call | solution.py:534
  42.5 1.3 %collective-permute-start.2 = (f32[4,64,128]{2,1,0:T(8,128)S(1)}, f32[4,64,128]{2,1,0:T(8,128)S(1)}, u32[]{:S(2)}, u32[]{:S(2)}) collective-permute-start(f32[4,64,128]{2,1,0:T(8,128)S(1)} %bitcast.27), channel_id=1, source_target_pairs={{0,4},{4,0},{8,12},{12,8},{16,20},{20,16},{24,28},{28,24},{1,5},{5... | collective-permute-start | bytes 393224 | tf_op jit(solution)/shard_map/ppermute | solution.py:452
  44.1 2.0 %collective-permute-start.4 = (f32[4,64,128]{2,1,0:T(8,128)S(1)}, f32[4,64,128]{2,1,0:T(8,128)S(1)}, u32[]{:S(2)}, u32[]{:S(2)}) collective-permute-start(f32[4,64,128]{2,1,0:T(8,128)S(1)} %bitcast.23), channel_id=1, source_target_pairs={{0,12},{4,8},{8,4},{12,0},{16,28},{20,24},{24,20},{28,16},{1,13},{... | collective-permute-start | bytes 393224 | tf_op jit(solution)/shard_map/ppermute | solution.py:452
  46.1 1.3 %inverse_x.3 = (f32[4,2,32,128]{3,2,1,0:T(8,128)S(1)}, f32[4,2,32,128]{3,2,1,0:T(8,128)S(1)}, f32[4,2,32,128]{3,2,1,0:T(8,128)S(1)}, f32[4,2,32,128]{3,2,1,0:T(8,128)S(1)}, f32[19,2,32,128]{3,2,1,0:T(8,128)S(1)}) custom-call(s32[6]{0:T(128)S(1)} %stack.27.place_ref, f32[2,32,32,128]{3,2,1,0:T(8,128)S(1)} %get-tuple-element.46.spectrum_ref, ...), custom_call_target="tpu_custom_call" | custom-call | flops 1000000 | bytes 10000 | tf_op jit(solution)/shard_map/inverse_x/pallas_call | solution.py:534
  47.4 1.3 %collective-permute-start.5 = (f32[4,64,128]{2,1,0:T(8,128)S(1)}, f32[4,64,128]{2,1,0:T(8,128)S(1)}, u32[]{:S(2)}, u32[]{:S(2)}) collective-permute-start(f32[4,64,128]{2,1,0:T(8,128)S(1)} %bitcast.28), channel_id=1, source_target_pairs={{0,4},{4,0},{8,12},{12,8},{16,20},{20,16},{24,28},{28,24},{1,5},{5... | collective-permute-start | bytes 393224 | tf_op jit(solution)/shard_map/ppermute | solution.py:452
  48.8 0.2 collective-permute-start.6
  49.0 2.0 %collective-permute-start.7 = (f32[4,64,128]{2,1,0:T(8,128)S(1)}, f32[4,64,128]{2,1,0:T(8,128)S(1)}, u32[]{:S(2)}, u32[]{:S(2)}) collective-permute-start(f32[4,64,128]{2,1,0:T(8,128)S(1)} %bitcast.25), channel_id=1, source_target_pairs={{0,12},{4,8},{8,4},{12,0},{16,28},{20,24},{24,20},{28,16},{1,13},{... | collective-permute-start | bytes 393224 | tf_op jit(solution)/shard_map/ppermute | solution.py:452
  51.0 9.6 %gather.1 = f32[16,1,256]{2,1,0:T(1,128)} custom-call(s32[6]{0:T(128)S(1)} %stack.27.place_ref, f32[16,8,256]{2,1,0:T(8,128)S(1)} %all-to-all-done.same_ref, f32[16,8,256]{2,1,0:T(8,128)S(1)} %collective-permute-done.other_ref, f32[5,144,1024]{2,1,0:T(8,128)S(1)} %get-tuple-element.42.table_y, f32[5,128,1024]{2,1,0:T(8,128)S(1)} %get-tuple-element.43.table_z, ...), custom_call_target="tpu_custom_call" | custom-call | flops 1000000 | bytes 10000 | tf_op jit(solution)/shard_map/gather/pallas_call | solution.py:547
  60.7 2.5 %inverse_y.1 = (f32[4,128,128]{2,1,0:T(8,128)S(1)}, f32[4,128,128]{2,1,0:T(8,128)S(1)}, f32[4,128,128]{2,1,0:T(8,128)S(1)}, f32[4,128,128]{2,1,0:T(8,128)S(1)}) custom-call(s32[6]{0:T(128)S(1)} %stack.27.place_ref, f32[4,64,128]{2,1,0:T(8,128)S(1)} %bitcast.21, f32[4,64,128]{2,1,0:T(8,128)S(1)} %collective-permute-done.2.refs_1_, ...), custom_call_target="tpu_custom_call" | custom-call | flops 1000000 | bytes 10000 | tf_op jit(solution)/shard_map/inverse_y/pallas_call | solution.py:569
  63.3 0.5 collective-permute-start.9
  63.8 1.3 %collective-permute-start.10 = (f32[4,128,128]{2,1,0:T(8,128)S(1)}, f32[4,128,128]{2,1,0:T(8,128)S(1)}, u32[]{:S(2)}, u32[]{:S(2)}) collective-permute-start(f32[4,128,128]{2,1,0:T(8,128)S(1)} %get-tuple-element.70), channel_id=1, source_target_pairs={{0,3},{1,2},{2,1},{3,0},{4,7},{5,6},{6,5},{7,4},{8,11},{9,10},{10,... | collective-permute-start | bytes 786440 | tf_op jit(solution)/shard_map/ppermute | solution.py:452
  65.1 3.5 %all-to-all-start.1 = ((f32[16,1,256]{2,1,0:T(1,128)}), f32[16,1,256]{2,1,0:T(1,128)S(1)}, u32[]{:S(2)}, u32[]{:S(2)}) async-start(f32[16,1,256]{2,1,0:T(1,128)} %gather.1), calls=%async_computation.1 | async-start | bytes 32768 | tf_op jit(solution)/shard_map/all_to_all | solution.py:603
  68.6 3.8 %collective-permute-done.9.refs_2_ = f32[4,128,128]{2,1,0:T(8,128)S(1)} collective-permute-done((f32[4,128,128]{2,1,0:T(8,128)S(1)}, f32[4,128,128]{2,1,0:T(8,128)S(1)}, u32[]{:S(2)}, u32[]{:S(2)}) %collective-permute-start.9) | collective-permute-done | bytes 262176 | tf_op jit(solution)/shard_map/ppermute | solution.py:452
  72.4 4.8 %collective-permute-done.10.refs_3_ = f32[4,128,128]{2,1,0:T(8,128)S(1)} collective-permute-done((f32[4,128,128]{2,1,0:T(8,128)S(1)}, f32[4,128,128]{2,1,0:T(8,128)S(1)}, u32[]{:S(2)}, u32[]{:S(2)}) %collective-permute-start.10) | collective-permute-done | bytes 262176 | tf_op jit(solution)/shard_map/ppermute | solution.py:452
  77.2 2.6 %inverse_z.1 = f32[4,128,512]{2,1,0:T(8,128)} custom-call(s32[6]{0:T(128)S(1)} %stack.27.place_ref, f32[4,128,128]{2,1,0:T(8,128)S(1)} %get-tuple-element.65.refs_0_, f32[4,128,128]{2,1,0:T(8,128)S(1)} %collective-permute-done.8.refs_1_, f32[4,128,128]{2,1,0:T(8,128)S(1)} %collective-permute-done.9.refs_2_, ...), custom_call_target="tpu_custom_call" | custom-call | flops 1000000 | bytes 10000 | tf_op jit(solution)/shard_map/inverse_z/pallas_call | solution.py:586
  79.9 0.6 compare_select_fusion
  (28 shorter events, 1.0 us)
Async XLA Ops:
  2.7 16.1 %all-to-all-start = ((f32[16,8,256]{2,1,0:T(8,128)}), f32[16,8,256]{2,1,0:T(8,128)S(1)}, u32[]{:S(2)}, u32[]{:S(2)}) async-start(f32[16,8,256]{2,1,0:T(8,128)} %pack.1), calls=%async_computation | async-start | bytes 262144 | tf_op jit(solution)/shard_map/all_to_all | solution.py:491
  18.8 27.3 %collective-permute-start.1 = (f32[32,32,128]{2,1,0:T(8,128)S(1)}, f32[32,32,128]{2,1,0:T(8,128)S(1)}, u32[]{:S(2)}, u32[]{:S(2)}) collective-permute-start(f32[32,32,128]{2,1,0:T(8,128)S(1)} %maximum_multiply_fusion), channel_id=1, source_target_pairs={{0,28},{4,24},{8,20},{12,16},{16,12},{20,8},{24,4},{28,0},{1,29},{... | collective-permute-start | bytes 1572872 | tf_op jit(solution)/shard_map/ppermute | solution.py:503
  20.2 1.3 %collective-permute-start = (f32[16,8,256]{2,1,0:T(8,128)S(1)}, f32[16,8,256]{2,1,0:T(8,128)S(1)}, u32[]{:S(2)}, u32[]{:S(2)}) collective-permute-start(f32[16,8,256]{2,1,0:T(8,128)S(1)} %all-to-all-done.same_ref), channel_id=1, source_target_pairs={{0,1},{1,0},{2,3},{3,2},{4,5},{5,4},{6,7},{7,6},{8,9},{9,8},{10,11... | collective-permute-start | bytes 393224 | tf_op jit(solution)/shard_map/ppermute | solution.py:452
  42.5 6.5 %collective-permute-start.2 = (f32[4,64,128]{2,1,0:T(8,128)S(1)}, f32[4,64,128]{2,1,0:T(8,128)S(1)}, u32[]{:S(2)}, u32[]{:S(2)}) collective-permute-start(f32[4,64,128]{2,1,0:T(8,128)S(1)} %bitcast.27), channel_id=1, source_target_pairs={{0,4},{4,0},{8,12},{12,8},{16,20},{20,16},{24,28},{28,24},{1,5},{5... | collective-permute-start | bytes 393224 | tf_op jit(solution)/shard_map/ppermute | solution.py:452
  43.9 16.7 %collective-permute-start.3 = (f32[4,64,128]{2,1,0:T(8,128)S(1)}, f32[4,64,128]{2,1,0:T(8,128)S(1)}, u32[]{:S(2)}, u32[]{:S(2)}) collective-permute-start(f32[4,64,128]{2,1,0:T(8,128)S(1)} %bitcast.24), channel_id=1, source_target_pairs={{0,8},{4,12},{8,0},{12,4},{16,24},{20,28},{24,16},{28,20},{1,9},{5... | collective-permute-start | bytes 393224 | tf_op jit(solution)/shard_map/ppermute | solution.py:452
  44.1 16.5 %collective-permute-start.4 = (f32[4,64,128]{2,1,0:T(8,128)S(1)}, f32[4,64,128]{2,1,0:T(8,128)S(1)}, u32[]{:S(2)}, u32[]{:S(2)}) collective-permute-start(f32[4,64,128]{2,1,0:T(8,128)S(1)} %bitcast.23), channel_id=1, source_target_pairs={{0,12},{4,8},{8,4},{12,0},{16,28},{20,24},{24,20},{28,16},{1,13},{... | collective-permute-start | bytes 393224 | tf_op jit(solution)/shard_map/ppermute | solution.py:452
  47.4 13.2 %collective-permute-start.5 = (f32[4,64,128]{2,1,0:T(8,128)S(1)}, f32[4,64,128]{2,1,0:T(8,128)S(1)}, u32[]{:S(2)}, u32[]{:S(2)}) collective-permute-start(f32[4,64,128]{2,1,0:T(8,128)S(1)} %bitcast.28), channel_id=1, source_target_pairs={{0,4},{4,0},{8,12},{12,8},{16,20},{20,16},{24,28},{28,24},{1,5},{5... | collective-permute-start | bytes 393224 | tf_op jit(solution)/shard_map/ppermute | solution.py:452
  48.8 11.8 %collective-permute-start.6 = (f32[4,64,128]{2,1,0:T(8,128)S(1)}, f32[4,64,128]{2,1,0:T(8,128)S(1)}, u32[]{:S(2)}, u32[]{:S(2)}) collective-permute-start(f32[4,64,128]{2,1,0:T(8,128)S(1)} %bitcast.26), channel_id=1, source_target_pairs={{0,8},{4,12},{8,0},{12,4},{16,24},{20,28},{24,16},{28,20},{1,9},{5... | collective-permute-start | bytes 393224 | tf_op jit(solution)/shard_map/ppermute | solution.py:452
  49.0 11.6 %collective-permute-start.7 = (f32[4,64,128]{2,1,0:T(8,128)S(1)}, f32[4,64,128]{2,1,0:T(8,128)S(1)}, u32[]{:S(2)}, u32[]{:S(2)}) collective-permute-start(f32[4,64,128]{2,1,0:T(8,128)S(1)} %bitcast.25), channel_id=1, source_target_pairs={{0,12},{4,8},{8,4},{12,0},{16,28},{20,24},{24,20},{28,16},{1,13},{... | collective-permute-start | bytes 393224 | tf_op jit(solution)/shard_map/ppermute | solution.py:452
  51.0 9.7 %copy-start = (bf16[512,1024]{1,0:T(8,128)(2,1)S(1)}, bf16[512,1024]{1,0:T(8,128)(2,1)}, u32[]{:S(2)}) copy-start(bf16[512,1024]{1,0:T(8,128)(2,1)} %constant.50.clone.refs_9_) | copy-start | bytes 3145732
  51.0 9.7 %copy-start.1 = (bf16[512,1024]{1,0:T(8,128)(2,1)S(1)}, bf16[512,1024]{1,0:T(8,128)(2,1)}, u32[]{:S(2)}) copy-start(bf16[512,1024]{1,0:T(8,128)(2,1)} %constant.49.clone.refs_8_) | copy-start | bytes 3145732
  60.6 16.6 %copy-start.2 = (bf16[512,512]{1,0:T(8,128)(2,1)S(1)}, bf16[512,512]{1,0:T(8,128)(2,1)}, u32[]{:S(2)}) copy-start(bf16[512,512]{1,0:T(8,128)(2,1)} %constant.52.clone.refs_5_) | copy-start | bytes 1572868
  60.6 16.6 %copy-start.3 = (bf16[512,512]{1,0:T(8,128)(2,1)S(1)}, bf16[512,512]{1,0:T(8,128)(2,1)}, u32[]{:S(2)}) copy-start(bf16[512,512]{1,0:T(8,128)(2,1)} %constant.51.clone.refs_4_) | copy-start | bytes 1572868
  60.7 19.2 %copy-start.4 = (f32[256]{0:T(256)S(1)}, f32[256]{0:T(256)}, u32[]{:S(2)}) copy-start(f32[256]{0:T(256)} %param.13) | copy-start | bytes 3076
  63.2 1.9 %collective-permute-start.8 = (f32[4,128,128]{2,1,0:T(8,128)S(1)}, f32[4,128,128]{2,1,0:T(8,128)S(1)}, u32[]{:S(2)}, u32[]{:S(2)}) collective-permute-start(f32[4,128,128]{2,1,0:T(8,128)S(1)} %get-tuple-element.67), channel_id=1, source_target_pairs={{0,1},{1,0},{2,3},{3,2},{4,5},{5,4},{6,7},{7,6},{8,9},{9,8},{10,11... | collective-permute-start | bytes 786440 | tf_op jit(solution)/shard_map/ppermute | solution.py:452
  63.3 9.2 %collective-permute-start.9 = (f32[4,128,128]{2,1,0:T(8,128)S(1)}, f32[4,128,128]{2,1,0:T(8,128)S(1)}, u32[]{:S(2)}, u32[]{:S(2)}) collective-permute-start(f32[4,128,128]{2,1,0:T(8,128)S(1)} %get-tuple-element.69), channel_id=1, source_target_pairs={{0,2},{1,3},{2,0},{3,1},{4,6},{5,7},{6,4},{7,5},{8,10},{9,11},{10,... | collective-permute-start | bytes 786440 | tf_op jit(solution)/shard_map/ppermute | solution.py:452
  63.8 13.4 %collective-permute-start.10 = (f32[4,128,128]{2,1,0:T(8,128)S(1)}, f32[4,128,128]{2,1,0:T(8,128)S(1)}, u32[]{:S(2)}, u32[]{:S(2)}) collective-permute-start(f32[4,128,128]{2,1,0:T(8,128)S(1)} %get-tuple-element.70), channel_id=1, source_target_pairs={{0,3},{1,2},{2,1},{3,0},{4,7},{5,6},{6,5},{7,4},{8,11},{9,10},{10,... | collective-permute-start | bytes 786440 | tf_op jit(solution)/shard_map/ppermute | solution.py:452
  65.1 14.7 %all-to-all-start.1 = ((f32[16,1,256]{2,1,0:T(1,128)}), f32[16,1,256]{2,1,0:T(1,128)S(1)}, u32[]{:S(2)}, u32[]{:S(2)}) async-start(f32[16,1,256]{2,1,0:T(1,128)} %gather.1), calls=%async_computation.1 | async-start | bytes 32768 | tf_op jit(solution)/shard_map/all_to_all | solution.py:603

commit v4 on v3

--- a/solution.py
+++ b/solution.py
@@ -15,8 +15,8 @@
 KH = NZ // 2
 LANES = 128
 SPAN = XD + 3
-CHUNKS = 1
-DEPTH = XD // CHUNKS
+DEPTH = 2
+GATHERS = 2
 MIB = 1 << 20
 BF16 = jnp.bfloat16
 F32 = jnp.float32
@@ -293,16 +293,16 @@
         out_ref[...] = near_ref[pl.ds(lax.bitwise_xor(place_ref[4], k) * XD, XD)]
 
 
-def inverse_y_kernel(sources, chunk, place_ref, *refs):
+def inverse_y_kernel(sources, place_ref, *refs):
     ins, (high_ref, low_ref) = refs[: 2 * sources], refs[2 * sources : 2 * sources + 2]
     outs, (lines_ref, turned_ref) = refs[2 * sources + 2 : -2], refs[-2:]
     for number, in_ref in enumerate(ins):
         source = lax.bitwise_xor(place_ref[4], number % sources)
         half = in_ref.shape[1]
         rows = pl.ds(half * (number // sources), half)
-        lines_ref[source, :, rows, :] = in_ref[pl.ds(chunk * DEPTH, DEPTH)]
+        lines_ref[source, :, rows, :] = in_ref[...]
     parts = []
-    for x in range(DEPTH):
+    for x in range(XD):
         lines = jnp.concatenate([lines_ref[source, x] for source in range(sources)], 0)
         pairs = jnp.concatenate([lines, swap(lines) * half_sign()], 0)
         parts.append(split(pairs))
@@ -312,7 +312,7 @@
     rest = jnp.dot(low_ref[...], high, preferred_element_type=F32)
     row = lax.broadcasted_iota(jnp.int32, (NY, 1), 0)
     sign = jnp.where((row % 2 == 1) & (place_ref[3] == 1), -1.0, 1.0)
-    for x in range(DEPTH):
+    for x in range(XD):
         total = main[:, 2 * x * LANES : (2 * x + 1) * LANES] + main[:, (2 * x + 1) * LANES : (2 * x + 2) * LANES]
         total = (total + rest[:, x * LANES : (x + 1) * LANES]) * sign
         turned_ref[:, x] = total.reshape(len(outs), -1, LANES)
@@ -323,19 +323,20 @@
 def inverse_z_kernel(sources, place_ref, *refs):
     ins, (high_ref, low_ref) = refs[:sources], refs[sources : sources + 2]
     out_ref, lines_ref = refs[-2:]
+    first = pl.program_id(0) * DEPTH
     for k in range(sources):
-        lines_ref[lax.bitwise_xor(place_ref[5], k)] = ins[k][...]
-    for x in range(DEPTH):
-        lines = jnp.concatenate([lines_ref[source, x] for source in range(sources)], 1)
-        high, low = split(lines)
-        total = jnp.dot(high, high_ref[...], preferred_element_type=F32)
-        total += jnp.dot(low, high_ref[...], preferred_element_type=F32)
-        total += jnp.dot(high, low_ref[...], preferred_element_type=F32)
-        out_ref[x] = total
+        lines_ref[lax.bitwise_xor(place_ref[5], k)] = ins[k][pl.ds(first, DEPTH)]
+    rows = DEPTH * lines_ref.shape[2]
+    lines = jnp.concatenate([lines_ref[source].reshape(rows, LANES) for source in range(sources)], 1)
+    high, low = split(lines)
+    total = jnp.dot(high, high_ref[...], preferred_element_type=F32)
+    total += jnp.dot(low, high_ref[...], preferred_element_type=F32)
+    total += jnp.dot(high, low_ref[...], preferred_element_type=F32)
+    out_ref[...] = total.reshape(out_ref.shape)
 
 
 def gather_kernel(
-    place_ref, same_ref, other_ref, table_y, table_z, plus_ref, minus_ref, out_ref, shift_ref, fields_ref, stack_ref
+    first, place_ref, same_ref, other_ref, table_y, table_z, plus_ref, minus_ref, out_ref, shift_ref, fields_ref, stack_ref
 ):
     step = pl.program_id(0)
     half = LANES // 2
@@ -343,7 +344,7 @@
     ky_local = rows - 8
     width = same_ref.shape[2]
     doms = table_y.shape[2] // width
-    planes = plus_ref.shape[0]
+    planes = fields_ref.shape[0]
     halves = half_sign()
 
     @pl.when(step == 0)
@@ -353,8 +354,8 @@
         row = lax.broadcasted_iota(jnp.int32, (8, LANES), 0)
 
         def build(x, carry):
-            plus = plus_ref[x]
-            shift_ref[pl.ds(1, ky_local), :] = minus_ref[x]
+            plus = plus_ref[first * XD + x]
+            shift_ref[pl.ds(1, ky_local), :] = minus_ref[first * XD + x]
             minus = shift_ref[pl.ds(0, ky_local), :]
             last = shift_ref[pl.ds(ky_local, 8), :][0:1]
             main = [plus + minus, swap(plus - minus) * halves]
@@ -379,13 +380,13 @@
     fields = fields_ref[pl.ds(step * XD, SPAN)].reshape(SPAN * LANES, 4 * LANES)
     for slot in range(doms):
         lanes = pl.ds(slot * width, width)
-        cosine = table_y[step, pl.ds(0, ky_local), lanes]
-        sine = table_y[step, pl.ds(rows, ky_local), lanes]
+        cosine = table_y[first + step, pl.ds(0, ky_local), lanes]
+        sine = table_y[first + step, pl.ds(rows, ky_local), lanes]
         high, low = split(jnp.concatenate([cosine, sine], 0))
         for part, value in enumerate((high, high, low)):
             stack_ref[pl.ds(LANES * part, 2 * ky_local), lanes] = value
-        cosine = table_y[step, pl.ds(ky_local, 8), lanes][0:1]
-        sine = table_y[step, pl.ds(rows + ky_local, 8), lanes][0:1]
+        cosine = table_y[first + step, pl.ds(ky_local, 8), lanes][0:1]
+        sine = table_y[first + step, pl.ds(rows + ky_local, 8), lanes][0:1]
         row = lax.broadcasted_iota(jnp.int32, (16, width), 0)
         rest = jnp.where(row % 2 == 0, cosine, sine)
         rest_high = rest.astype(BF16).astype(F32)
@@ -396,14 +397,14 @@
         for part in (0, 2 * LANES)
     )
     for slot in range(doms):
-        atoms = atoms_of(same_ref, other_ref, place_ref[2] + step, slot, doms)
+        atoms = atoms_of(same_ref, other_ref, place_ref[2] + first + step, slot, doms)
         along_x = plane_weights(atoms, spline(atoms))
         lanes = pl.ds(slot * width, width)
         field = product[:, slot * width : (slot + 1) * width]
         total = along_x[0:1] * field[:LANES]
         for plane in range(1, SPAN):
             total += along_x[plane : plane + 1] * field[plane * LANES : (plane + 1) * LANES]
-        waves = total * table_z[step, :, lanes]
+        waves = total * table_z[first + step, :, lanes]
         sampled = jnp.sum((waves[:half] - waves[half:]) * twice, axis=0, keepdims=True)
         core = place_ref[5] % 2 if slot < doms // 2 else 1 - place_ref[5] % 2
         out_ref[step * doms + 2 * (slot % (doms // 2)) + core] = sampled
@@ -544,61 +545,47 @@
         near.append(planes.reshape(near_planes, ky_local, LANES))
         lines += [swapped(value.reshape(XD, ky_local, LANES), "slab", k) for k, value in enumerate(pieces)]
 
-    partial = pl.pallas_call(
-        gather_kernel,
-        grid=(slab_half,),
-        in_specs=[SMEM] + [vmem] * 6,
-        out_specs=vmem,
-        out_shape=jax.ShapeDtypeStruct((slab_half * doms, 1, atoms_local), F32),
-        scratch_shapes=[
-            pltpu.VMEM((rows, LANES), F32),
-            pltpu.VMEM((near_planes, LANES, 4 * LANES), BF16),
-            pltpu.VMEM((4 * LANES, atoms_slab), BF16),
-        ],
-        compiler_params=params(12 + (table_bytes + 8 * near_planes * LANES * LANES) // MIB),
-        cost_estimate=SMALL,
-        name="gather",
-    )(place, same, other, table_y, table_z, *near)
+    steps = slab_half // GATHERS
+
+    def gather(part, place):
+        return pl.pallas_call(
+            functools.partial(gather_kernel, part * steps),
+            grid=(steps,),
+            in_specs=[SMEM] + [vmem] * 6,
+            out_specs=vmem,
+            out_shape=jax.ShapeDtypeStruct((steps * doms, 1, atoms_local), F32),
+            scratch_shapes=[
+                pltpu.VMEM((rows, LANES), F32),
+                pltpu.VMEM((steps * XD + 3, LANES, 4 * LANES), BF16),
+                pltpu.VMEM((4 * LANES, atoms_slab), BF16),
+            ],
+            compiler_params=params(12 + (table_bytes + 8 * near_planes * LANES * LANES) // MIB),
+            cost_estimate=SMALL,
+            name="gather",
+        )(place, same, other, table_y, table_z, *near)
+
+    earlier, *lines = lax.optimization_barrier((gather(0, place), *lines))
 
     high_y, low_y = inverse_y_table(slab_half, ky_local)
     high_z, low_z = inverse_z_table(doms)
-    partial, *lines = lax.optimization_barrier((partial, *lines))
-
-    potential = None
-    for chunk in range(CHUNKS):
-        turned = pl.pallas_call(
-            functools.partial(inverse_y_kernel, slab_half, chunk),
-            in_specs=[SMEM] + [vmem] * (2 * slab_half + 2),
-            out_specs=[vmem] * doms,
-            out_shape=[jax.ShapeDtypeStruct((DEPTH, rows_local, LANES), F32)] * doms,
-            scratch_shapes=[
-                pltpu.VMEM((slab_half, DEPTH, 2 * ky_local, LANES), F32),
-                pltpu.VMEM((doms, DEPTH, rows_local, LANES), F32),
-            ],
-            compiler_params=params(32),
-            cost_estimate=SMALL,
-            name="inverse_y",
-        )(place, *lines, high_y, low_y)
-        columns = [swapped(value, "dom", k) for k, value in enumerate(turned)]
-        if chunk == CHUNKS - 1:
-            partial, columns[1] = lax.optimization_barrier((partial, columns[1]))
-        earlier = [] if potential is None else [potential]
-        potential = pl.pallas_call(
-            functools.partial(inverse_z_kernel, doms),
-            grid=(1,),
-            in_specs=[SMEM]
-            + [whole_spec((DEPTH, rows_local, LANES))] * doms
-            + [whole_spec((2 * KH, NZ))] * 2
-            + [pl.BlockSpec(memory_space=pl.ANY)] * len(earlier),
-            out_specs=pl.BlockSpec((DEPTH, rows_local, NZ), lambda _, at=chunk: (at, 0, 0)),
-            out_shape=jax.ShapeDtypeStruct((XD, rows_local, NZ), F32),
-            scratch_shapes=[pltpu.VMEM((doms, DEPTH, rows_local, LANES), F32)],
-            input_output_aliases={doms + 3: 0} if earlier else {},
-            compiler_params=params(24),
-            cost_estimate=SMALL,
-            name="inverse_z",
-        )(place, *columns, high_z, low_z, *earlier)
-
+
+    turned = pl.pallas_call(
+        functools.partial(inverse_y_kernel, slab_half),
+        in_specs=[SMEM] + [vmem] * (2 * slab_half + 2),
+        out_specs=[vmem] * doms,
+        out_shape=[jax.ShapeDtypeStruct((XD, rows_local, LANES), F32)] * doms,
+        scratch_shapes=[
+            pltpu.VMEM((slab_half, XD, 2 * ky_local, LANES), F32),
+            pltpu.VMEM((doms, XD, rows_local, LANES), F32),
+        ],
+        compiler_params=params(32),
+        cost_estimate=SMALL,
+        name="inverse_y",
+    )(place, *lines, high_y, low_y)
+    columns = [swapped(value, "dom", k) for k, value in enumerate(turned)]
+
+    columns[1], late_place = lax.optimization_barrier((columns[1], place))
+    partial = jnp.concatenate([earlier] + [gather(part, late_place) for part in range(1, GATHERS)], 0)
     members = slab_half * doms
     sampled = lax.all_to_all(
         partial.reshape(members, atoms_local),
@@ -610,6 +597,19 @@
     )
     alive = jnp.arange(atoms_local, dtype=jnp.int32) < counts[0]
     gradient = jnp.where(alive, bias_coupling * jnp.sum(sampled, 0), 0.0)
+    gradient, *columns = lax.optimization_barrier((gradient, *columns))
+
+    potential = pl.pallas_call(
+        functools.partial(inverse_z_kernel, doms),
+        grid=(XD // DEPTH,),
+        in_specs=[SMEM] + [vmem] * (doms + 2),
+        out_specs=pl.BlockSpec((DEPTH, rows_local, NZ), lambda step: (step, 0, 0)),
+        out_shape=jax.ShapeDtypeStruct((XD, rows_local, NZ), F32),
+        scratch_shapes=[pltpu.VMEM((doms, DEPTH, rows_local, LANES), F32)],
+        compiler_params=params(24),
+        cost_estimate=SMALL,
+        name="inverse_z",
+    )(place, *columns, high_z, low_z)
     return (potential, gradient)
 
 

time: 80.9 us -> 79.1 us (0.978)
  blocking collectives: 0 us -> 8.23 us
  waiting for transfers between devices: 15.1 us -> 8.1 us
  starting transfers between devices: 22.3 us -> 18.8 us
    all_to_all x0 -> x1, blocking collectives: none -> 8.23 us  [per_device(): lax.all_to_all(partial.reshape(members, atoms_local), ('slab', 'dom'), 0,...]
    ppermute x10, waiting for transfers between devices: 9.77 us -> 2.81 us  [swapped(): lax.ppermute(value, axis, [(i, i ^ distance) for i in range(lax.axis_size...]
    all_to_all x1 -> x0, starting transfers between devices: 3.48 us -> none  [per_device(): lax.all_to_all(partial.reshape(members, atoms_local), ('slab', 'dom'), 0,...]
    pallas_call x3 -> x4, Pallas kernels: 14.7 us -> 15.2 us  [the longest x2 10.1 us: gather(): pl.pallas_call(functools.partial(gather_kernel, part * steps), grid=(step...]
  transfers between devices with their start and end apart: 13 -> 12, of which waited for: 4 -> 3; matrix products, arithmetic and copies ran while one was open for 2% -> 3% of each run, Pallas kernels for 44% -> 42%
where the time goes in v4:
time: 79.1 us; the launch traced here: 78.7 us
  Pallas kernels  39.6 us (50%)
  starting transfers between devices  18.8 us (24%)
  blocking collectives  8.23 us (10%)
  waiting for transfers between devices  8.1 us (10%)
  local copies, waits for them, and re-layouts  1.53 us (2%)
  between operations  1.46 us (2%)
  other arithmetic  1.03 us (1%)
    pallas_call x1, Pallas kernels, per_device(): pl.pallas_call(forward_kernel, grid=(slabs,), in_specs=[SMEM] + [vmem] *...  19.6 us
    pallas_call x2, Pallas kernels, gather(): pl.pallas_call(functools.partial(gather_kernel, part * steps), grid=(step...  10.1 us
    ppermute x10, starting transfers between devices, swapped(): lax.ppermute(value, axis, [(i, i ^ distance) for i in range(lax.axis_size...  9.04 us
    all_to_all x1, starting transfers between devices, per_device(): lax.all_to_all(atoms, ('slab', 'dom'), 0, 0, axis_index_groups=[everyone[...  8.31 us
    all_to_all x1, blocking collectives, per_device(): lax.all_to_all(partial.reshape(members, atoms_local), ('slab', 'dom'), 0,...  8.23 us
    all_to_all x1, waiting for transfers between devices, per_device(): lax.all_to_all(atoms, ('slab', 'dom'), 0, 0, axis_index_groups=[everyone[...  5.29 us
    ppermute x10, waiting for transfers between devices, swapped(): lax.ppermute(value, axis, [(i, i ^ distance) for i in range(lax.axis_size...  2.81 us
    pallas_call x2, Pallas kernels, per_device(): pl.pallas_call(inverse_x_kernel, in_specs=[SMEM] + [vmem] * 2, out_specs=...  2.68 us
  transfers between devices with their start and end apart: 12, of which 3 were waited for; matrix products, arithmetic and copies ran while one was open for 3% of the time, Pallas kernels for 42%

profile of v4, /device:TPU:0, one launch (start us, length us, event | category | flops | bytes accessed | tf_op | source)
XLA Modules:
  0.0 78.7 jit_solution(3186304934036097309)
XLA Ops:
  1.3 1.4 %pack.1 = f32[16,8,256]{2,1,0:T(8,128)} custom-call(s32[1]{0:T(128)} %copy.12.counts_ref, s32[3,256]{1,0:T(4,128)} %cells_ref.1, f32[3,256]{1,0:T(4,128)} %offsets_ref.1, f32[1,256]{1,0:T(1,128)} %bitcast.31), custom_call_target="tpu_custom_call" | custom-call | tf_op jit(solution)/shard_map/pack/pallas_call | solution.py:476
  2.7 8.3 %all-to-all-start = ((f32[16,8,256]{2,1,0:T(8,128)}), f32[16,8,256]{2,1,0:T(8,128)S(1)}, u32[]{:S(2)}, u32[]{:S(2)}) async-start(f32[16,8,256]{2,1,0:T(8,128)} %pack.1), calls=%async_computation | async-start | bytes 262144 | tf_op jit(solution)/shard_map/all_to_all | solution.py:492
  11.0 1.3 %fusion = (f32[32,32,64]{2,1,0:T(8,128)S(1)}, f32[32,32,64]{2,1,0:T(8,128)S(1)}) fusion(f32[32,64,64]{2,1,0:T(8,128)} %param.15), kind=kLoop, calls=%fused_computation.4 | loop fusion | bytes 1048576 | tf_op jit(solution)/shard_map/slice | solution.py:497
  12.4 0.7 waves.1
  13.5 5.3 %all-to-all-done.same_ref = f32[16,8,256]{2,1,0:T(8,128)S(1)} async-done(((f32[16,8,256]{2,1,0:T(8,128)}), f32[16,8,256]{2,1,0:T(8,128)S(1)}, u32[]{:S(2)}, u32[]{:S(2)}) %all-to-all-start) | async-done | bytes 131104 | tf_op jit(solution)/shard_map/all_to_all | solution.py:492
  18.8 1.4 %collective-permute-start.1 = (f32[32,32,128]{2,1,0:T(8,128)S(1)}, f32[32,32,128]{2,1,0:T(8,128)S(1)}, u32[]{:S(2)}, u32[]{:S(2)}) collective-permute-start(f32[32,32,128]{2,1,0:T(8,128)S(1)} %maximum_multiply_fusion), channel_id=1, source_target_pairs={{0,28},{4,24},{8,20},{12,16},{16,12},{20,8},{24,4},{28,0},{1,29},{... | collective-permute-start | bytes 1572872 | tf_op jit(solution)/shard_map/ppermute | solution.py:504
  20.4 1.1 %collective-permute-done.other_ref = f32[16,8,256]{2,1,0:T(8,128)S(1)} collective-permute-done((f32[16,8,256]{2,1,0:T(8,128)S(1)}, f32[16,8,256]{2,1,0:T(8,128)S(1)}, u32[]{:S(2)}, u32[]{:S(2)}) %collective-permute-start) | collective-permute-done | bytes 131104 | tf_op jit(solution)/shard_map/ppermute | solution.py:453
  21.6 19.6 %forward.1 = (f32[2,32,32,128]{3,2,1,0:T(8,128)S(1)}, f32[2,32,32,128]{3,2,1,0:T(8,128)S(1)}, f32[5,144,1024]{2,1,0:T(8,128)S(1)}, f32[5,128,1024]{2,1,0:T(8,128)S(1)}) custom-call(s32[6]{0:T(128)S(1)} %stack.27.place_ref, f32[16,8,256]{2,1,0:T(8,128)S(1)} %all-to-all-done.same_ref, f32[16,8,256]{2,1,0:T(8,128)S(1)} %collective-permute-done.other_ref, ...), custom_call_target="tpu_custom_call" | custom-call | flops 1000000 | bytes 10000 | tf_op jit(solution)/shard_map/forward/pallas_call | solution.py:509
  41.2 1.3 %inverse_x.2 = (f32[4,2,32,128]{3,2,1,0:T(8,128)S(1)}, f32[4,2,32,128]{3,2,1,0:T(8,128)S(1)}, f32[4,2,32,128]{3,2,1,0:T(8,128)S(1)}, f32[4,2,32,128]{3,2,1,0:T(8,128)S(1)}, f32[19,2,32,128]{3,2,1,0:T(8,128)S(1)}) custom-call(s32[6]{0:T(128)S(1)} %stack.27.place_ref, f32[2,32,32,128]{3,2,1,0:T(8,128)S(1)} %get-tuple-element.49.spectrum_ref, ...), custom_call_target="tpu_custom_call" | custom-call | flops 1000000 | bytes 10000 | tf_op jit(solution)/shard_map/inverse_x/pallas_call | solution.py:535
  42.5 1.3 %collective-permute-start.2 = (f32[4,64,128]{2,1,0:T(8,128)S(1)}, f32[4,64,128]{2,1,0:T(8,128)S(1)}, u32[]{:S(2)}, u32[]{:S(2)}) collective-permute-start(f32[4,64,128]{2,1,0:T(8,128)S(1)} %bitcast.27), channel_id=1, source_target_pairs={{0,4},{4,0},{8,12},{12,8},{16,20},{20,16},{24,28},{28,24},{1,5},{5... | collective-permute-start | bytes 393224 | tf_op jit(solution)/shard_map/ppermute | solution.py:453
  44.1 2.0 %collective-permute-start.4 = (f32[4,64,128]{2,1,0:T(8,128)S(1)}, f32[4,64,128]{2,1,0:T(8,128)S(1)}, u32[]{:S(2)}, u32[]{:S(2)}) collective-permute-start(f32[4,64,128]{2,1,0:T(8,128)S(1)} %bitcast.25), channel_id=1, source_target_pairs={{0,12},{4,8},{8,4},{12,0},{16,28},{20,24},{24,20},{28,16},{1,13},{... | collective-permute-start | bytes 393224 | tf_op jit(solution)/shard_map/ppermute | solution.py:453
  46.1 1.3 %inverse_x.3 = (f32[4,2,32,128]{3,2,1,0:T(8,128)S(1)}, f32[4,2,32,128]{3,2,1,0:T(8,128)S(1)}, f32[4,2,32,128]{3,2,1,0:T(8,128)S(1)}, f32[4,2,32,128]{3,2,1,0:T(8,128)S(1)}, f32[19,2,32,128]{3,2,1,0:T(8,128)S(1)}) custom-call(s32[6]{0:T(128)S(1)} %stack.27.place_ref, f32[2,32,32,128]{3,2,1,0:T(8,128)S(1)} %get-tuple-element.51.spectrum_ref, ...), custom_call_target="tpu_custom_call" | custom-call | flops 1000000 | bytes 10000 | tf_op jit(solution)/shard_map/inverse_x/pallas_call | solution.py:535
  47.4 1.3 %collective-permute-start.5 = (f32[4,64,128]{2,1,0:T(8,128)S(1)}, f32[4,64,128]{2,1,0:T(8,128)S(1)}, u32[]{:S(2)}, u32[]{:S(2)}) collective-permute-start(f32[4,64,128]{2,1,0:T(8,128)S(1)} %bitcast.30), channel_id=1, source_target_pairs={{0,4},{4,0},{8,12},{12,8},{16,20},{20,16},{24,28},{28,24},{1,5},{5... | collective-permute-start | bytes 393224 | tf_op jit(solution)/shard_map/ppermute | solution.py:453
  48.8 0.2 collective-permute-start.6
  49.0 2.0 %collective-permute-start.7 = (f32[4,64,128]{2,1,0:T(8,128)S(1)}, f32[4,64,128]{2,1,0:T(8,128)S(1)}, u32[]{:S(2)}, u32[]{:S(2)}) collective-permute-start(f32[4,64,128]{2,1,0:T(8,128)S(1)} %bitcast.28), channel_id=1, source_target_pairs={{0,12},{4,8},{8,4},{12,0},{16,28},{20,24},{24,20},{28,16},{1,13},{... | collective-permute-start | bytes 393224 | tf_op jit(solution)/shard_map/ppermute | solution.py:453
  51.0 5.1 %gather.2 = f32[8,1,256]{2,1,0:T(1,128)S(1)} custom-call(s32[6]{0:T(128)S(1)} %stack.27.place_ref, f32[16,8,256]{2,1,0:T(8,128)S(1)} %all-to-all-done.same_ref, f32[16,8,256]{2,1,0:T(8,128)S(1)} %collective-permute-done.other_ref, f32[5,144,1024]{2,1,0:T(8,128)S(1)} %get-tuple-element.47.table_y, f32[5,128,1024]{2,1,0:T(8,128)S(1)} %get-tuple-element.48.table_z, ...), custom_call_target="tpu_custom_call" | custom-call | flops 1000000 | bytes 10000 | tf_op jit(solution)/shard_map/gather/pallas_call | solution.py:551
  56.1 1.7 %collective-permute-done.7.refs_7_ = f32[4,64,128]{2,1,0:T(8,128)S(1)} collective-permute-done((f32[4,64,128]{2,1,0:T(8,128)S(1)}, f32[4,64,128]{2,1,0:T(8,128)S(1)}, u32[]{:S(2)}, u32[]{:S(2)}) %collective-permute-start.7) | collective-permute-done | bytes 131104 | tf_op jit(solution)/shard_map/ppermute | solution.py:453
  57.7 2.5 %inverse_y.1 = (f32[4,128,128]{2,1,0:T(8,128)S(1)}, f32[4,128,128]{2,1,0:T(8,128)S(1)}, f32[4,128,128]{2,1,0:T(8,128)S(1)}, f32[4,128,128]{2,1,0:T(8,128)S(1)}) custom-call(s32[6]{0:T(128)S(1)} %stack.27.place_ref, f32[4,64,128]{2,1,0:T(8,128)S(1)} %bitcast.23, f32[4,64,128]{2,1,0:T(8,128)S(1)} %collective-permute-done.2.refs_1_, ...), custom_call_target="tpu_custom_call" | custom-call | flops 1000000 | bytes 10000 | tf_op jit(solution)/shard_map/inverse_y/pallas_call | solution.py:572
  60.3 0.5 collective-permute-start.9
  60.9 1.3 %collective-permute-start.10 = (f32[4,128,128]{2,1,0:T(8,128)S(1)}, f32[4,128,128]{2,1,0:T(8,128)S(1)}, u32[]{:S(2)}, u32[]{:S(2)}) collective-permute-start(f32[4,128,128]{2,1,0:T(8,128)S(1)} %get-tuple-element.76), channel_id=1, source_target_pairs={{0,3},{1,2},{2,1},{3,0},{4,7},{5,6},{6,5},{7,4},{8,11},{9,10},{10,... | collective-permute-start | bytes 786440 | tf_op jit(solution)/shard_map/ppermute | solution.py:453
  62.2 5.1 %gather.3 = f32[8,1,256]{2,1,0:T(1,128)S(1)} custom-call(s32[6]{0:T(128)S(1)} %stack.27.place_ref, f32[16,8,256]{2,1,0:T(8,128)S(1)} %all-to-all-done.same_ref, f32[16,8,256]{2,1,0:T(8,128)S(1)} %collective-permute-done.other_ref, f32[5,144,1024]{2,1,0:T(8,128)S(1)} %get-tuple-element.47.table_y, f32[5,128,1024]{2,1,0:T(8,128)S(1)} %get-tuple-element.48.table_z, ...), custom_call_target="tpu_custom_call" | custom-call | flops 1000000 | bytes 10000 | tf_op jit(solution)/shard_map/gather/pallas_call | solution.py:551
  67.3 8.2 %all_to_all.11 = f32[16,1,256]{2,1,0:T(1,128)S(1)} all-to-all(f32[16,1,256]{2,1,0:T(1,128)S(1)} %pad_maximum_fusion), channel_id=1, replica_groups={{0,1,2,3,4,5,6,7,8,9,10,11,12,13,14,15},{16,17,18,19,20,21,22,23,24,25,..., dimensions={0} | all-to-all | bytes 32768 | tf_op jit(solution)/shard_map/all_to_all | solution.py:590
  75.6 0.6 compare_select_fusion
  76.2 2.6 %inverse_z.1 = f32[4,128,512]{2,1,0:T(8,128)} custom-call(s32[6]{0:T(128)S(1)} %stack.27.place_ref, f32[4,128,128]{2,1,0:T(8,128)S(1)} %get-tuple-element.77.refs_0_, f32[4,128,128]{2,1,0:T(8,128)S(1)} %collective-permute-done.8.refs_1_, f32[4,128,128]{2,1,0:T(8,128)S(1)} %collective-permute-done.9.refs_2_, ...), custom_call_target="tpu_custom_call" | custom-call | flops 1000000 | bytes 10000 | tf_op jit(solution)/shard_map/inverse_z/pallas_call | solution.py:602
  (29 shorter events, 1.0 us)
Async XLA Ops:
  2.7 16.1 %all-to-all-start = ((f32[16,8,256]{2,1,0:T(8,128)}), f32[16,8,256]{2,1,0:T(8,128)S(1)}, u32[]{:S(2)}, u32[]{:S(2)}) async-start(f32[16,8,256]{2,1,0:T(8,128)} %pack.1), calls=%async_computation | async-start | bytes 262144 | tf_op jit(solution)/shard_map/all_to_all | solution.py:492
  18.8 27.3 %collective-permute-start.1 = (f32[32,32,128]{2,1,0:T(8,128)S(1)}, f32[32,32,128]{2,1,0:T(8,128)S(1)}, u32[]{:S(2)}, u32[]{:S(2)}) collective-permute-start(f32[32,32,128]{2,1,0:T(8,128)S(1)} %maximum_multiply_fusion), channel_id=1, source_target_pairs={{0,28},{4,24},{8,20},{12,16},{16,12},{20,8},{24,4},{28,0},{1,29},{... | collective-permute-start | bytes 1572872 | tf_op jit(solution)/shard_map/ppermute | solution.py:504
  20.2 1.3 %collective-permute-start = (f32[16,8,256]{2,1,0:T(8,128)S(1)}, f32[16,8,256]{2,1,0:T(8,128)S(1)}, u32[]{:S(2)}, u32[]{:S(2)}) collective-permute-start(f32[16,8,256]{2,1,0:T(8,128)S(1)} %all-to-all-done.same_ref), channel_id=1, source_target_pairs={{0,1},{1,0},{2,3},{3,2},{4,5},{5,4},{6,7},{7,6},{8,9},{9,8},{10,11... | collective-permute-start | bytes 393224 | tf_op jit(solution)/shard_map/ppermute | solution.py:453
  42.5 6.5 %collective-permute-start.2 = (f32[4,64,128]{2,1,0:T(8,128)S(1)}, f32[4,64,128]{2,1,0:T(8,128)S(1)}, u32[]{:S(2)}, u32[]{:S(2)}) collective-permute-start(f32[4,64,128]{2,1,0:T(8,128)S(1)} %bitcast.27), channel_id=1, source_target_pairs={{0,4},{4,0},{8,12},{12,8},{16,20},{20,16},{24,28},{28,24},{1,5},{5... | collective-permute-start | bytes 393224 | tf_op jit(solution)/shard_map/ppermute | solution.py:453
  43.9 12.2 %collective-permute-start.3 = (f32[4,64,128]{2,1,0:T(8,128)S(1)}, f32[4,64,128]{2,1,0:T(8,128)S(1)}, u32[]{:S(2)}, u32[]{:S(2)}) collective-permute-start(f32[4,64,128]{2,1,0:T(8,128)S(1)} %bitcast.26), channel_id=1, source_target_pairs={{0,8},{4,12},{8,0},{12,4},{16,24},{20,28},{24,16},{28,20},{1,9},{5... | collective-permute-start | bytes 393224 | tf_op jit(solution)/shard_map/ppermute | solution.py:453
  44.1 12.0 %collective-permute-start.4 = (f32[4,64,128]{2,1,0:T(8,128)S(1)}, f32[4,64,128]{2,1,0:T(8,128)S(1)}, u32[]{:S(2)}, u32[]{:S(2)}) collective-permute-start(f32[4,64,128]{2,1,0:T(8,128)S(1)} %bitcast.25), channel_id=1, source_target_pairs={{0,12},{4,8},{8,4},{12,0},{16,28},{20,24},{24,20},{28,16},{1,13},{... | collective-permute-start | bytes 393224 | tf_op jit(solution)/shard_map/ppermute | solution.py:453
  47.4 8.7 %collective-permute-start.5 = (f32[4,64,128]{2,1,0:T(8,128)S(1)}, f32[4,64,128]{2,1,0:T(8,128)S(1)}, u32[]{:S(2)}, u32[]{:S(2)}) collective-permute-start(f32[4,64,128]{2,1,0:T(8,128)S(1)} %bitcast.30), channel_id=1, source_target_pairs={{0,4},{4,0},{8,12},{12,8},{16,20},{20,16},{24,28},{28,24},{1,5},{5... | collective-permute-start | bytes 393224 | tf_op jit(solution)/shard_map/ppermute | solution.py:453
  48.8 7.3 %collective-permute-start.6 = (f32[4,64,128]{2,1,0:T(8,128)S(1)}, f32[4,64,128]{2,1,0:T(8,128)S(1)}, u32[]{:S(2)}, u32[]{:S(2)}) collective-permute-start(f32[4,64,128]{2,1,0:T(8,128)S(1)} %bitcast.29), channel_id=1, source_target_pairs={{0,8},{4,12},{8,0},{12,4},{16,24},{20,28},{24,16},{28,20},{1,9},{5... | collective-permute-start | bytes 393224 | tf_op jit(solution)/shard_map/ppermute | solution.py:453
  49.0 8.7 %collective-permute-start.7 = (f32[4,64,128]{2,1,0:T(8,128)S(1)}, f32[4,64,128]{2,1,0:T(8,128)S(1)}, u32[]{:S(2)}, u32[]{:S(2)}) collective-permute-start(f32[4,64,128]{2,1,0:T(8,128)S(1)} %bitcast.28), channel_id=1, source_target_pairs={{0,12},{4,8},{8,4},{12,0},{16,28},{20,24},{24,20},{28,16},{1,13},{... | collective-permute-start | bytes 393224 | tf_op jit(solution)/shard_map/ppermute | solution.py:453
  51.0 6.8 %copy-start = (bf16[512,1024]{1,0:T(8,128)(2,1)S(1)}, bf16[512,1024]{1,0:T(8,128)(2,1)}, u32[]{:S(2)}) copy-start(bf16[512,1024]{1,0:T(8,128)(2,1)} %constant.50.clone.refs_9_) | copy-start | bytes 3145732
  51.0 6.8 %copy-start.1 = (bf16[512,1024]{1,0:T(8,128)(2,1)S(1)}, bf16[512,1024]{1,0:T(8,128)(2,1)}, u32[]{:S(2)}) copy-start(bf16[512,1024]{1,0:T(8,128)(2,1)} %constant.49.clone.refs_8_) | copy-start | bytes 3145732
  60.3 2.0 %collective-permute-start.8 = (f32[4,128,128]{2,1,0:T(8,128)S(1)}, f32[4,128,128]{2,1,0:T(8,128)S(1)}, u32[]{:S(2)}, u32[]{:S(2)}) collective-permute-start(f32[4,128,128]{2,1,0:T(8,128)S(1)} %get-tuple-element.71), channel_id=1, source_target_pairs={{0,1},{1,0},{2,3},{3,2},{4,5},{5,4},{6,7},{7,6},{8,9},{9,8},{10,11... | collective-permute-start | bytes 786440 | tf_op jit(solution)/shard_map/ppermute | solution.py:453
  60.3 15.8 %collective-permute-start.9 = (f32[4,128,128]{2,1,0:T(8,128)S(1)}, f32[4,128,128]{2,1,0:T(8,128)S(1)}, u32[]{:S(2)}, u32[]{:S(2)}) collective-permute-start(f32[4,128,128]{2,1,0:T(8,128)S(1)} %get-tuple-element.75), channel_id=1, source_target_pairs={{0,2},{1,3},{2,0},{3,1},{4,6},{5,7},{6,4},{7,5},{8,10},{9,11},{10,... | collective-permute-start | bytes 786440 | tf_op jit(solution)/shard_map/ppermute | solution.py:453
  60.9 14.7 %copy-start.4 = (f32[256]{0:T(256)S(1)}, f32[256]{0:T(256)}, u32[]{:S(2)}) copy-start(f32[256]{0:T(256)} %param.13) | copy-start | bytes 3076
  60.9 15.3 %copy-start.2 = (bf16[512,512]{1,0:T(8,128)(2,1)S(1)}, bf16[512,512]{1,0:T(8,128)(2,1)}, u32[]{:S(2)}) copy-start(bf16[512,512]{1,0:T(8,128)(2,1)} %constant.52.clone.refs_5_) | copy-start | bytes 1572868
  60.9 15.3 %copy-start.3 = (bf16[512,512]{1,0:T(8,128)(2,1)S(1)}, bf16[512,512]{1,0:T(8,128)(2,1)}, u32[]{:S(2)}) copy-start(bf16[512,512]{1,0:T(8,128)(2,1)} %constant.51.clone.refs_4_) | copy-start | bytes 1572868
  60.9 15.3 %collective-permute-start.10 = (f32[4,128,128]{2,1,0:T(8,128)S(1)}, f32[4,128,128]{2,1,0:T(8,128)S(1)}, u32[]{:S(2)}, u32[]{:S(2)}) collective-permute-start(f32[4,128,128]{2,1,0:T(8,128)S(1)} %get-tuple-element.76), channel_id=1, source_target_pairs={{0,3},{1,2},{2,1},{3,0},{4,7},{5,6},{6,5},{7,4},{8,11},{9,10},{10,... | collective-permute-start | bytes 786440 | tf_op jit(solution)/shard_map/ppermute | solution.py:453

commit v5 on v4

--- a/solution.py
+++ b/solution.py
@@ -171,7 +171,7 @@
             cells_ref[1:3, :].astype(F32),
             offsets_ref[...],
             jnp.where(alive, charges_ref[...], 0.0),
-            jnp.zeros((1, width), F32),
+            jnp.full((1, width), counts_ref[0].astype(F32)),
         ],
         0,
     )
@@ -186,6 +186,7 @@
 
 def forward_kernel(
     place_ref,
+    live_ref,
     same_ref,
     other_ref,
     factors_y,
@@ -197,6 +198,7 @@
     left_ref,
     right_ref,
     grid_ref,
+    atoms_ref,
     digits_y,
     digits_z,
 ):
@@ -204,8 +206,8 @@
     cells_x = grid_ref.shape[0]
     rows = grid_ref.shape[1] // 2
     ky_local = rows - 8
-    width = same_ref.shape[2]
-    doms = table_y.shape[2] // width
+    half_slot = same_ref.shape[2] // 2
+    doms = table_y.shape[2] // (2 * half_slot)
     kept = step - place_ref[2]
     kept = jnp.where((kept >= 0) & (kept < table_y.shape[0] - 1), kept, table_y.shape[0] - 1)
 
@@ -216,32 +218,54 @@
         digits_z[...] = jnp.zeros_like(digits_z)
 
     for slot in range(doms):
-        atoms = atoms_of(same_ref, other_ref, step, slot, doms)
-        lanes = pl.ds(slot * width, width)
+        atoms_ref[slot] = atoms_of(same_ref, other_ref, step, slot, doms)
+
+    def add_tile(tile, halves):
+        atoms = jnp.concatenate([atoms_ref[slot, :, pl.ds(part * half_slot, half_slot)] for slot, part, _ in halves], 1)
+        counted = jnp.concatenate([jnp.full((1, half_slot), weight) for _, _, weight in halves], 1)
         weights = spline(atoms)
-        along_x = plane_weights(atoms, weights) * atoms[6:7]
-        waves = atom_waves(atoms[2:3], [w[5:6] for w in weights], factors_z, digits_z.at[slot])
-        waves = jnp.concatenate(waves, 0)
-        table_z[kept, :, lanes] = waves
-        high, low = split(waves)
-        right_ref[slot, pl.ds(0, LANES), :] = high
-        right_ref[slot, pl.ds(LANES, LANES), :] = low
-        cosine, sine = atom_waves(atoms[1:2], [w[4:5] for w in weights], factors_y, digits_y.at[slot])
-        waves = jnp.concatenate([cosine, sine], 0)
-        table_y[kept, :, lanes] = waves
+        along_x = plane_weights(atoms, weights) * (atoms[6:7] * counted)
+        waves_z = atom_waves(atoms[2:3], [w[5:6] for w in weights], factors_z, digits_z.at[tile])
+        waves_z = jnp.concatenate(waves_z, 0)
+        waves_y = atom_waves(atoms[1:2], [w[4:5] for w in weights], factors_y, digits_y.at[tile])
+        waves_y = jnp.concatenate(waves_y, 0)
+        for number, (slot, part, _) in enumerate(halves):
+            lanes = slice(number * half_slot, (number + 1) * half_slot)
+            start = pl.multiple_of((2 * slot + part) * half_slot, half_slot)
+            table_z[kept, :, pl.ds(start, half_slot)] = waves_z[:, lanes]
+            table_y[kept, :, pl.ds(start, half_slot)] = waves_y[:, lanes]
+        high, low = split(waves_z)
+        right_ref[tile, pl.ds(0, LANES), :] = high
+        right_ref[tile, pl.ds(LANES, LANES), :] = low
         for plane in range(SPAN):
             first = 4 * rows * plane
-            high, low = split(waves * along_x[plane : plane + 1])
-            left_ref[slot, pl.ds(first, 2 * rows), :] = high
-            left_ref[slot, pl.ds(first + 2 * rows, 2 * rows), :] = low
+            high, low = split(waves_y * along_x[plane : plane + 1])
+            left_ref[tile, pl.ds(first, 2 * rows), :] = high
+            left_ref[tile, pl.ds(first + 2 * rows, 2 * rows), :] = low
         product = lax.dot_general(
-            left_ref[slot], right_ref[slot], (((1,), (1,)), ((), ())), preferred_element_type=F32
+            left_ref[tile], right_ref[tile], (((1,), (1,)), ((), ())), preferred_element_type=F32
         )
         for plane in range(SPAN):
             first = 4 * rows * plane
             high, low = product[first : first + 2 * rows], product[first + 2 * rows : first + 4 * rows]
             at = lax.rem(step * XD + plane, cells_x)
             grid_ref[at] += (high[:, :LANES] + high[:, LANES:]) + (low[:, :LANES] + low[:, LANES:])
+
+    for tile in range(doms // 2):
+        add_tile(tile, [(2 * tile, 0, 1.0), (2 * tile + 1, 0, 1.0)])
+
+    reach = [live_ref[step * doms + slot] for slot in range(doms)]
+    reach = [sum(reach[: slot + 1]) for slot in range(doms)]
+    for tile in range(doms // 2):
+
+        @pl.when(reach[-1] > 2 * tile)
+        def _(tile=tile):
+            chosen = []
+            for place in (2 * tile, 2 * tile + 1):
+                slot = sum((total <= place).astype(jnp.int32) for total in reach)
+                weight = jnp.where(slot < doms, 1.0, 0.0).astype(F32)
+                chosen.append((jnp.minimum(slot, doms - 1), 1, weight))
+            add_tile(doms // 2 + tile, chosen)
 
     @pl.when(step == pl.num_programs(0) - 1)
     def _():
@@ -503,13 +527,15 @@
     other = swapped(same, "dom", 1)
     mirrored = lax.ppermute(flipped, "slab", [(s, slabs - 1 - s) for s in range(slabs)])
 
+    reaches = [value[:, 7, 0].reshape(slabs, doms // 2) for value in (same, other)]
+    live = (jnp.concatenate(reaches, 1).reshape(-1) > atoms_local // 2).astype(jnp.int32)
     atoms_slab = doms * atoms_local
     table_bytes = 4 * (slab_half + 1) * (2 * rows + LANES) * atoms_slab
     spectrum_bytes = 16 * cells_x * max(8, quarter_rows) * LANES
     plus, minus, table_y, table_z = pl.pallas_call(
         forward_kernel,
         grid=(slabs,),
-        in_specs=[SMEM] + [vmem] * 4,
+        in_specs=[SMEM] * 2 + [vmem] * 4,
         out_specs=[vmem] * 4,
         out_shape=[
             jax.ShapeDtypeStruct((2, cells_x, quarter_rows, LANES), F32),
@@ -521,13 +547,14 @@
             pltpu.VMEM((doms, SPAN * 4 * rows, atoms_local), BF16),
             pltpu.VMEM((doms, 2 * LANES, atoms_local), BF16),
             pltpu.VMEM((cells_x, 2 * rows, LANES), F32),
+            pltpu.VMEM((doms, 8, atoms_local), F32),
             pltpu.VMEM((doms, TERMS, atoms_local), BF16),
             pltpu.VMEM((doms, TERMS, atoms_local), BF16),
         ],
         compiler_params=params(16 + (table_bytes + spectrum_bytes) // MIB),
         cost_estimate=SMALL,
         name="forward",
-    )(place, same, other, factors_y, factors_z)
+    )(place, live, same, other, factors_y, factors_z)
 
     near_planes = cells_x // 2 + 3
     lines, near = [], []

time: 79.1 us -> 79.2 us (level)
  waiting for transfers between devices: 8.1 us -> 7.01 us
    ppermute x10, waiting for transfers between devices: 2.81 us -> 1.72 us  [swapped(): lax.ppermute(value, axis, [(i, i ^ distance) for i in range(lax.axis_size...]
  transfers between devices with their start and end apart: 12 -> 12, of which waited for: 3 -> 2; matrix products, arithmetic and copies ran while one was open for 3% -> 4% of each run, Pallas kernels for 42% -> 43%
where the time goes in v5:
time: 79.2 us; the launch traced here: 78.8 us
  Pallas kernels  40.1 us (51%)
  starting transfers between devices  18.8 us (24%)
  blocking collectives  8.2 us (10%)
  waiting for transfers between devices  7.01 us (9%)
  local copies, waits for them, and re-layouts  2.18 us (3%)
  between operations  1.46 us (2%)
  other arithmetic  1.1 us (1%)
    pallas_call x1, Pallas kernels, per_device(): pl.pallas_call(forward_kernel, grid=(slabs,), in_specs=[SMEM] * 2 + [vmem...  20 us
    pallas_call x2, Pallas kernels, gather(): pl.pallas_call(functools.partial(gather_kernel, part * steps), grid=(step...  10.2 us
    ppermute x10, starting transfers between devices, swapped(): lax.ppermute(value, axis, [(i, i ^ distance) for i in range(lax.axis_size...  9.04 us
    all_to_all x1, starting transfers between devices, per_device(): lax.all_to_all(atoms, ('slab', 'dom'), 0, 0, axis_index_groups=[everyone[...  8.31 us
    all_to_all x1, blocking collectives, per_device(): lax.all_to_all(partial.reshape(members, atoms_local), ('slab', 'dom'), 0,...  8.2 us
    all_to_all x1, waiting for transfers between devices, per_device(): lax.all_to_all(atoms, ('slab', 'dom'), 0, 0, axis_index_groups=[everyone[...  5.29 us
    pallas_call x2, Pallas kernels, per_device(): pl.pallas_call(inverse_x_kernel, in_specs=[SMEM] + [vmem] * 2, out_specs=...  2.68 us
    pallas_call x1, Pallas kernels, per_device(): pl.pallas_call(functools.partial(inverse_z_kernel, doms), grid=(XD // DEP...  2.59 us
  transfers between devices with their start and end apart: 12, of which 2 were waited for; matrix products, arithmetic and copies ran while one was open for 4% of the time, Pallas kernels for 43%

profile of v5, /device:TPU:0, one launch (start us, length us, event | category | flops | bytes accessed | tf_op | source)
XLA Modules:
  0.0 78.8 jit_solution(8907100976958795181)
XLA Ops:
  1.3 1.4 %pack.1 = f32[16,8,256]{2,1,0:T(8,128)} custom-call(s32[1]{0:T(128)} %copy.12.counts_ref, s32[3,256]{1,0:T(4,128)} %cells_ref.1, f32[3,256]{1,0:T(4,128)} %offsets_ref.1, f32[1,256]{1,0:T(1,128)} %bitcast.31), custom_call_target="tpu_custom_call" | custom-call | tf_op jit(solution)/shard_map/pack/pallas_call | solution.py:500
  2.7 8.3 %all-to-all-start = ((f32[16,8,256]{2,1,0:T(8,128)}), f32[16,8,256]{2,1,0:T(8,128)S(1)}, u32[]{:S(2)}, u32[]{:S(2)}) async-start(f32[16,8,256]{2,1,0:T(8,128)} %pack.1), calls=%async_computation | async-start | bytes 262144 | tf_op jit(solution)/shard_map/all_to_all | solution.py:516
  11.0 1.3 %fusion.1 = (f32[32,32,64]{2,1,0:T(8,128)S(1)}, f32[32,32,64]{2,1,0:T(8,128)S(1)}) fusion(f32[32,64,64]{2,1,0:T(8,128)} %param.15), kind=kLoop, calls=%fused_computation.8 | loop fusion | bytes 1048576 | tf_op jit(solution)/shard_map/slice | solution.py:521
  12.4 0.7 waves.1
  13.5 5.3 %all-to-all-done.same_ref = f32[16,8,256]{2,1,0:T(8,128)S(1)} async-done(((f32[16,8,256]{2,1,0:T(8,128)}), f32[16,8,256]{2,1,0:T(8,128)S(1)}, u32[]{:S(2)}, u32[]{:S(2)}) %all-to-all-start) | async-done | bytes 131104 | tf_op jit(solution)/shard_map/all_to_all | solution.py:516
  18.8 1.4 %collective-permute-start.1 = (f32[32,32,128]{2,1,0:T(8,128)S(1)}, f32[32,32,128]{2,1,0:T(8,128)S(1)}, u32[]{:S(2)}, u32[]{:S(2)}) collective-permute-start(f32[32,32,128]{2,1,0:T(8,128)S(1)} %maximum_multiply_fusion), channel_id=1, source_target_pairs={{0,28},{4,24},{8,20},{12,16},{16,12},{20,8},{24,4},{28,0},{1,29},{... | collective-permute-start | bytes 1572872 | tf_op jit(solution)/shard_map/ppermute | solution.py:528
  21.2 20.0 %forward.1 = (f32[2,32,32,128]{3,2,1,0:T(8,128)S(1)}, f32[2,32,32,128]{3,2,1,0:T(8,128)S(1)}, f32[5,144,1024]{2,1,0:T(8,128)S(1)}, f32[5,128,1024]{2,1,0:T(8,128)S(1)}) custom-call(s32[6]{0:T(128)S(1)} %stack.27.place_ref, s32[32]{0:T(128)S(1)} %reshape.57.live_ref, f32[16,8,256]{2,1,0:T(8,128)S(1)} %all-to-all-done.same_ref, ...), custom_call_target="tpu_custom_call" | custom-call | flops 1000000 | bytes 10000 | tf_op jit(solution)/shard_map/forward/pallas_call | solution.py:535
  41.2 1.3 %inverse_x.2 = (f32[4,2,32,128]{3,2,1,0:T(8,128)S(1)}, f32[4,2,32,128]{3,2,1,0:T(8,128)S(1)}, f32[4,2,32,128]{3,2,1,0:T(8,128)S(1)}, f32[4,2,32,128]{3,2,1,0:T(8,128)S(1)}, f32[19,2,32,128]{3,2,1,0:T(8,128)S(1)}) custom-call(s32[6]{0:T(128)S(1)} %stack.27.place_ref, f32[2,32,32,128]{3,2,1,0:T(8,128)S(1)} %get-tuple-element.49.spectrum_ref, ...), custom_call_target="tpu_custom_call" | custom-call | flops 1000000 | bytes 10000 | tf_op jit(solution)/shard_map/inverse_x/pallas_call | solution.py:562
  42.5 1.4 %collective-permute-start.2 = (f32[4,64,128]{2,1,0:T(8,128)S(1)}, f32[4,64,128]{2,1,0:T(8,128)S(1)}, u32[]{:S(2)}, u32[]{:S(2)}) collective-permute-start(f32[4,64,128]{2,1,0:T(8,128)S(1)} %bitcast.27), channel_id=1, source_target_pairs={{0,4},{4,0},{8,12},{12,8},{16,20},{20,16},{24,28},{28,24},{1,5},{5... | collective-permute-start | bytes 393224 | tf_op jit(solution)/shard_map/ppermute | solution.py:477
  43.9 0.2 collective-permute-start.3
  44.1 2.0 %collective-permute-start.4 = (f32[4,64,128]{2,1,0:T(8,128)S(1)}, f32[4,64,128]{2,1,0:T(8,128)S(1)}, u32[]{:S(2)}, u32[]{:S(2)}) collective-permute-start(f32[4,64,128]{2,1,0:T(8,128)S(1)} %bitcast.25), channel_id=1, source_target_pairs={{0,12},{4,8},{8,4},{12,0},{16,28},{20,24},{24,20},{28,16},{1,13},{... | collective-permute-start | bytes 393224 | tf_op jit(solution)/shard_map/ppermute | solution.py:477
  46.1 1.3 %inverse_x.3 = (f32[4,2,32,128]{3,2,1,0:T(8,128)S(1)}, f32[4,2,32,128]{3,2,1,0:T(8,128)S(1)}, f32[4,2,32,128]{3,2,1,0:T(8,128)S(1)}, f32[4,2,32,128]{3,2,1,0:T(8,128)S(1)}, f32[19,2,32,128]{3,2,1,0:T(8,128)S(1)}) custom-call(s32[6]{0:T(128)S(1)} %stack.27.place_ref, f32[2,32,32,128]{3,2,1,0:T(8,128)S(1)} %get-tuple-element.51.spectrum_ref, ...), custom_call_target="tpu_custom_call" | custom-call | flops 1000000 | bytes 10000 | tf_op jit(solution)/shard_map/inverse_x/pallas_call | solution.py:562
  47.4 1.4 %collective-permute-start.5 = (f32[4,64,128]{2,1,0:T(8,128)S(1)}, f32[4,64,128]{2,1,0:T(8,128)S(1)}, u32[]{:S(2)}, u32[]{:S(2)}) collective-permute-start(f32[4,64,128]{2,1,0:T(8,128)S(1)} %bitcast.30), channel_id=1, source_target_pairs={{0,4},{4,0},{8,12},{12,8},{16,20},{20,16},{24,28},{28,24},{1,5},{5... | collective-permute-start | bytes 393224 | tf_op jit(solution)/shard_map/ppermute | solution.py:477
  48.8 0.2 collective-permute-start.6
  49.0 2.0 %collective-permute-start.7 = (f32[4,64,128]{2,1,0:T(8,128)S(1)}, f32[4,64,128]{2,1,0:T(8,128)S(1)}, u32[]{:S(2)}, u32[]{:S(2)}) collective-permute-start(f32[4,64,128]{2,1,0:T(8,128)S(1)} %bitcast.28), channel_id=1, source_target_pairs={{0,12},{4,8},{8,4},{12,0},{16,28},{20,24},{24,20},{28,16},{1,13},{... | collective-permute-start | bytes 393224 | tf_op jit(solution)/shard_map/ppermute | solution.py:477
  51.0 5.1 %gather.2 = f32[8,1,256]{2,1,0:T(1,128)S(1)} custom-call(s32[6]{0:T(128)S(1)} %stack.27.place_ref, f32[16,8,256]{2,1,0:T(8,128)S(1)} %all-to-all-done.same_ref, f32[16,8,256]{2,1,0:T(8,128)S(1)} %collective-permute-done.other_ref, f32[5,144,1024]{2,1,0:T(8,128)S(1)} %get-tuple-element.47.table_y, f32[5,128,1024]{2,1,0:T(8,128)S(1)} %get-tuple-element.48.table_z, ...), custom_call_target="tpu_custom_call" | custom-call | flops 1000000 | bytes 10000 | tf_op jit(solution)/shard_map/gather/pallas_call | solution.py:578
  56.1 1.7 %collective-permute-done.7.refs_7_ = f32[4,64,128]{2,1,0:T(8,128)S(1)} collective-permute-done((f32[4,64,128]{2,1,0:T(8,128)S(1)}, f32[4,64,128]{2,1,0:T(8,128)S(1)}, u32[]{:S(2)}, u32[]{:S(2)}) %collective-permute-start.7) | collective-permute-done | bytes 131104 | tf_op jit(solution)/shard_map/ppermute | solution.py:477
  57.8 2.5 %inverse_y.1 = (f32[4,128,128]{2,1,0:T(8,128)S(1)}, f32[4,128,128]{2,1,0:T(8,128)S(1)}, f32[4,128,128]{2,1,0:T(8,128)S(1)}, f32[4,128,128]{2,1,0:T(8,128)S(1)}) custom-call(s32[6]{0:T(128)S(1)} %stack.27.place_ref, f32[4,64,128]{2,1,0:T(8,128)S(1)} %bitcast.23, f32[4,64,128]{2,1,0:T(8,128)S(1)} %collective-permute-done.2.refs_1_, ...), custom_call_target="tpu_custom_call" | custom-call | flops 1000000 | bytes 10000 | tf_op jit(solution)/shard_map/inverse_y/pallas_call | solution.py:599
  60.4 0.5 collective-permute-start.9
  61.0 1.3 %collective-permute-start.10 = (f32[4,128,128]{2,1,0:T(8,128)S(1)}, f32[4,128,128]{2,1,0:T(8,128)S(1)}, u32[]{:S(2)}, u32[]{:S(2)}) collective-permute-start(f32[4,128,128]{2,1,0:T(8,128)S(1)} %get-tuple-element.76), channel_id=1, source_target_pairs={{0,3},{1,2},{2,1},{3,0},{4,7},{5,6},{6,5},{7,4},{8,11},{9,10},{10,... | collective-permute-start | bytes 786440 | tf_op jit(solution)/shard_map/ppermute | solution.py:477
  62.3 5.1 %gather.3 = f32[8,1,256]{2,1,0:T(1,128)S(1)} custom-call(s32[6]{0:T(128)S(1)} %stack.27.place_ref, f32[16,8,256]{2,1,0:T(8,128)S(1)} %all-to-all-done.same_ref, f32[16,8,256]{2,1,0:T(8,128)S(1)} %collective-permute-done.other_ref, f32[5,144,1024]{2,1,0:T(8,128)S(1)} %get-tuple-element.47.table_y, f32[5,128,1024]{2,1,0:T(8,128)S(1)} %get-tuple-element.48.table_z, ...), custom_call_target="tpu_custom_call" | custom-call | flops 1000000 | bytes 10000 | tf_op jit(solution)/shard_map/gather/pallas_call | solution.py:578
  67.4 8.2 %all_to_all.11 = f32[16,1,256]{2,1,0:T(1,128)S(1)} all-to-all(f32[16,1,256]{2,1,0:T(1,128)S(1)} %pad_maximum_fusion), channel_id=1, replica_groups={{0,1,2,3,4,5,6,7,8,9,10,11,12,13,14,15},{16,17,18,19,20,21,22,23,24,25,..., dimensions={0} | all-to-all | bytes 32768 | tf_op jit(solution)/shard_map/all_to_all | solution.py:617
  75.7 0.6 compare_select_fusion
  76.2 2.6 %inverse_z.1 = f32[4,128,512]{2,1,0:T(8,128)} custom-call(s32[6]{0:T(128)S(1)} %stack.27.place_ref, f32[4,128,128]{2,1,0:T(8,128)S(1)} %get-tuple-element.77.refs_0_, f32[4,128,128]{2,1,0:T(8,128)S(1)} %collective-permute-done.8.refs_1_, f32[4,128,128]{2,1,0:T(8,128)S(1)} %collective-permute-done.9.refs_2_, ...), custom_call_target="tpu_custom_call" | custom-call | flops 1000000 | bytes 10000 | tf_op jit(solution)/shard_map/inverse_z/pallas_call | solution.py:629
  (35 shorter events, 1.5 us)
Async XLA Ops:
  2.7 16.1 %all-to-all-start = ((f32[16,8,256]{2,1,0:T(8,128)}), f32[16,8,256]{2,1,0:T(8,128)S(1)}, u32[]{:S(2)}, u32[]{:S(2)}) async-start(f32[16,8,256]{2,1,0:T(8,128)} %pack.1), calls=%async_computation | async-start | bytes 262144 | tf_op jit(solution)/shard_map/all_to_all | solution.py:516
  18.8 1.9 %collective-permute-start = (f32[16,8,256]{2,1,0:T(8,128)S(1)}, f32[16,8,256]{2,1,0:T(8,128)S(1)}, u32[]{:S(2)}, u32[]{:S(2)}) collective-permute-start(f32[16,8,256]{2,1,0:T(8,128)S(1)} %all-to-all-done.same_ref), channel_id=1, source_target_pairs={{0,1},{1,0},{2,3},{3,2},{4,5},{5,4},{6,7},{7,6},{8,9},{9,8},{10,11... | collective-permute-start | bytes 393224 | tf_op jit(solution)/shard_map/ppermute | solution.py:477
  18.8 27.3 %collective-permute-start.1 = (f32[32,32,128]{2,1,0:T(8,128)S(1)}, f32[32,32,128]{2,1,0:T(8,128)S(1)}, u32[]{:S(2)}, u32[]{:S(2)}) collective-permute-start(f32[32,32,128]{2,1,0:T(8,128)S(1)} %maximum_multiply_fusion), channel_id=1, source_target_pairs={{0,28},{4,24},{8,20},{12,16},{16,12},{20,8},{24,4},{28,0},{1,29},{... | collective-permute-start | bytes 1572872 | tf_op jit(solution)/shard_map/ppermute | solution.py:528
  42.5 6.5 %collective-permute-start.2 = (f32[4,64,128]{2,1,0:T(8,128)S(1)}, f32[4,64,128]{2,1,0:T(8,128)S(1)}, u32[]{:S(2)}, u32[]{:S(2)}) collective-permute-start(f32[4,64,128]{2,1,0:T(8,128)S(1)} %bitcast.27), channel_id=1, source_target_pairs={{0,4},{4,0},{8,12},{12,8},{16,20},{20,16},{24,28},{28,24},{1,5},{5... | collective-permute-start | bytes 393224 | tf_op jit(solution)/shard_map/ppermute | solution.py:477
  43.9 12.2 %collective-permute-start.3 = (f32[4,64,128]{2,1,0:T(8,128)S(1)}, f32[4,64,128]{2,1,0:T(8,128)S(1)}, u32[]{:S(2)}, u32[]{:S(2)}) collective-permute-start(f32[4,64,128]{2,1,0:T(8,128)S(1)} %bitcast.26), channel_id=1, source_target_pairs={{0,8},{4,12},{8,0},{12,4},{16,24},{20,28},{24,16},{28,20},{1,9},{5... | collective-permute-start | bytes 393224 | tf_op jit(solution)/shard_map/ppermute | solution.py:477
  44.1 12.0 %collective-permute-start.4 = (f32[4,64,128]{2,1,0:T(8,128)S(1)}, f32[4,64,128]{2,1,0:T(8,128)S(1)}, u32[]{:S(2)}, u32[]{:S(2)}) collective-permute-start(f32[4,64,128]{2,1,0:T(8,128)S(1)} %bitcast.25), channel_id=1, source_target_pairs={{0,12},{4,8},{8,4},{12,0},{16,28},{20,24},{24,20},{28,16},{1,13},{... | collective-permute-start | bytes 393224 | tf_op jit(solution)/shard_map/ppermute | solution.py:477
  47.4 8.7 %collective-permute-start.5 = (f32[4,64,128]{2,1,0:T(8,128)S(1)}, f32[4,64,128]{2,1,0:T(8,128)S(1)}, u32[]{:S(2)}, u32[]{:S(2)}) collective-permute-start(f32[4,64,128]{2,1,0:T(8,128)S(1)} %bitcast.30), channel_id=1, source_target_pairs={{0,4},{4,0},{8,12},{12,8},{16,20},{20,16},{24,28},{28,24},{1,5},{5... | collective-permute-start | bytes 393224 | tf_op jit(solution)/shard_map/ppermute | solution.py:477
  48.8 7.3 %collective-permute-start.6 = (f32[4,64,128]{2,1,0:T(8,128)S(1)}, f32[4,64,128]{2,1,0:T(8,128)S(1)}, u32[]{:S(2)}, u32[]{:S(2)}) collective-permute-start(f32[4,64,128]{2,1,0:T(8,128)S(1)} %bitcast.29), channel_id=1, source_target_pairs={{0,8},{4,12},{8,0},{12,4},{16,24},{20,28},{24,16},{28,20},{1,9},{5... | collective-permute-start | bytes 393224 | tf_op jit(solution)/shard_map/ppermute | solution.py:477
  49.0 8.8 %collective-permute-start.7 = (f32[4,64,128]{2,1,0:T(8,128)S(1)}, f32[4,64,128]{2,1,0:T(8,128)S(1)}, u32[]{:S(2)}, u32[]{:S(2)}) collective-permute-start(f32[4,64,128]{2,1,0:T(8,128)S(1)} %bitcast.28), channel_id=1, source_target_pairs={{0,12},{4,8},{8,4},{12,0},{16,28},{20,24},{24,20},{28,16},{1,13},{... | collective-permute-start | bytes 393224 | tf_op jit(solution)/shard_map/ppermute | solution.py:477
  51.0 6.9 %copy-start = (bf16[512,1024]{1,0:T(8,128)(2,1)S(1)}, bf16[512,1024]{1,0:T(8,128)(2,1)}, u32[]{:S(2)}) copy-start(bf16[512,1024]{1,0:T(8,128)(2,1)} %constant.52.clone.refs_9_) | copy-start | bytes 3145732
  51.0 6.9 %copy-start.1 = (bf16[512,1024]{1,0:T(8,128)(2,1)S(1)}, bf16[512,1024]{1,0:T(8,128)(2,1)}, u32[]{:S(2)}) copy-start(bf16[512,1024]{1,0:T(8,128)(2,1)} %constant.51.clone.refs_8_) | copy-start | bytes 3145732
  60.3 2.0 %collective-permute-start.8 = (f32[4,128,128]{2,1,0:T(8,128)S(1)}, f32[4,128,128]{2,1,0:T(8,128)S(1)}, u32[]{:S(2)}, u32[]{:S(2)}) collective-permute-start(f32[4,128,128]{2,1,0:T(8,128)S(1)} %get-tuple-element.71), channel_id=1, source_target_pairs={{0,1},{1,0},{2,3},{3,2},{4,5},{5,4},{6,7},{7,6},{8,9},{9,8},{10,11... | collective-permute-start | bytes 786440 | tf_op jit(solution)/shard_map/ppermute | solution.py:477
  60.4 15.8 %collective-permute-start.9 = (f32[4,128,128]{2,1,0:T(8,128)S(1)}, f32[4,128,128]{2,1,0:T(8,128)S(1)}, u32[]{:S(2)}, u32[]{:S(2)}) collective-permute-start(f32[4,128,128]{2,1,0:T(8,128)S(1)} %get-tuple-element.75), channel_id=1, source_target_pairs={{0,2},{1,3},{2,0},{3,1},{4,6},{5,7},{6,4},{7,5},{8,10},{9,11},{10,... | collective-permute-start | bytes 786440 | tf_op jit(solution)/shard_map/ppermute | solution.py:477
  61.0 14.7 %copy-start.4 = (f32[256]{0:T(256)S(1)}, f32[256]{0:T(256)}, u32[]{:S(2)}) copy-start(f32[256]{0:T(256)} %param.13) | copy-start | bytes 3076
  61.0 15.3 %copy-start.2 = (bf16[512,512]{1,0:T(8,128)(2,1)S(1)}, bf16[512,512]{1,0:T(8,128)(2,1)}, u32[]{:S(2)}) copy-start(bf16[512,512]{1,0:T(8,128)(2,1)} %constant.54.clone.refs_5_) | copy-start | bytes 1572868
  61.0 15.3 %copy-start.3 = (bf16[512,512]{1,0:T(8,128)(2,1)S(1)}, bf16[512,512]{1,0:T(8,128)(2,1)}, u32[]{:S(2)}) copy-start(bf16[512,512]{1,0:T(8,128)(2,1)} %constant.53.clone.refs_4_) | copy-start | bytes 1572868
  61.0 15.3 %collective-permute-start.10 = (f32[4,128,128]{2,1,0:T(8,128)S(1)}, f32[4,128,128]{2,1,0:T(8,128)S(1)}, u32[]{:S(2)}, u32[]{:S(2)}) collective-permute-start(f32[4,128,128]{2,1,0:T(8,128)S(1)} %get-tuple-element.76), channel_id=1, source_target_pairs={{0,3},{1,2},{2,1},{3,0},{4,7},{5,6},{6,5},{7,4},{8,11},{9,10},{10,... | collective-permute-start | bytes 786440 | tf_op jit(solution)/shard_map/ppermute | solution.py:477

commit v6 on v5

--- a/solution.py
+++ b/solution.py
@@ -251,21 +251,21 @@
             at = lax.rem(step * XD + plane, cells_x)
             grid_ref[at] += (high[:, :LANES] + high[:, LANES:]) + (low[:, :LANES] + low[:, LANES:])
 
-    for tile in range(doms // 2):
-        add_tile(tile, [(2 * tile, 0, 1.0), (2 * tile + 1, 0, 1.0)])
-
     reach = [live_ref[step * doms + slot] for slot in range(doms)]
     reach = [sum(reach[: slot + 1]) for slot in range(doms)]
-    for tile in range(doms // 2):
-
-        @pl.when(reach[-1] > 2 * tile)
-        def _(tile=tile):
-            chosen = []
-            for place in (2 * tile, 2 * tile + 1):
-                slot = sum((total <= place).astype(jnp.int32) for total in reach)
-                weight = jnp.where(slot < doms, 1.0, 0.0).astype(F32)
-                chosen.append((jnp.minimum(slot, doms - 1), 1, weight))
-            add_tile(doms // 2 + tile, chosen)
+    for extra in range(doms // 2 + 1):
+
+        @pl.when((reach[-1] + 1) // 2 == extra)
+        def _(extra=extra):
+            for tile in range(doms // 2):
+                add_tile(tile, [(2 * tile, 0, 1.0), (2 * tile + 1, 0, 1.0)])
+            for tile in range(extra):
+                chosen = []
+                for place in (2 * tile, 2 * tile + 1):
+                    slot = sum((total <= place).astype(jnp.int32) for total in reach)
+                    weight = jnp.where(slot < doms, 1.0, 0.0).astype(F32)
+                    chosen.append((jnp.minimum(slot, doms - 1), 1, weight))
+                add_tile(doms // 2 + tile, chosen)
 
     @pl.when(step == pl.num_programs(0) - 1)
     def _():

time: 79.2 us -> 78.5 us (level)
  Pallas kernels: 40.1 us -> 38.6 us
  waiting for transfers between devices: 7.01 us -> 5.89 us
  starting transfers between devices: 18.8 us -> 19.9 us
    pallas_call x1, Pallas kernels: 20 us -> 18.5 us  [per_device(): pl.pallas_call(forward_kernel, grid=(slabs,), in_specs=[SMEM] * 2 + [vmem...]
    ppermute x10, starting transfers between devices: 9.04 us -> 10.2 us  [swapped(): lax.ppermute(value, axis, [(i, i ^ distance) for i in range(lax.axis_size...]
    ppermute x10, waiting for transfers between devices: 1.72 us -> 0.6 us  [swapped(): lax.ppermute(value, axis, [(i, i ^ distance) for i in range(lax.axis_size...]
  transfers between devices with their start and end apart: 12 -> 12, of which waited for: 2 -> 2; matrix products, arithmetic and copies ran while one was open for 4% -> 4% of each run, Pallas kernels for 43% -> 41%
where the time goes in v6:
time: 78.5 us; the launch traced here: 78 us
  Pallas kernels  38.6 us (49%)
  starting transfers between devices  19.9 us (25%)
  blocking collectives  8.88 us (11%)
  waiting for transfers between devices  5.89 us (8%)
  local copies, waits for them, and re-layouts  2.18 us (3%)
  between operations  1.46 us (2%)
  other arithmetic  1.1 us (1%)
    pallas_call x1, Pallas kernels, per_device(): pl.pallas_call(forward_kernel, grid=(slabs,), in_specs=[SMEM] * 2 + [vmem...  18.5 us
    ppermute x10, starting transfers between devices, swapped(): lax.ppermute(value, axis, [(i, i ^ distance) for i in range(lax.axis_size...  10.2 us
    pallas_call x2, Pallas kernels, gather(): pl.pallas_call(functools.partial(gather_kernel, part * steps), grid=(step...  10.2 us
    all_to_all x1, blocking collectives, per_device(): lax.all_to_all(partial.reshape(members, atoms_local), ('slab', 'dom'), 0,...  8.88 us
    all_to_all x1, starting transfers between devices, per_device(): lax.all_to_all(atoms, ('slab', 'dom'), 0, 0, axis_index_groups=[everyone[...  8.31 us
    all_to_all x1, waiting for transfers between devices, per_device(): lax.all_to_all(atoms, ('slab', 'dom'), 0, 0, axis_index_groups=[everyone[...  5.29 us
    pallas_call x2, Pallas kernels, per_device(): pl.pallas_call(inverse_x_kernel, in_specs=[SMEM] + [vmem] * 2, out_specs=...  2.68 us
    pallas_call x1, Pallas kernels, per_device(): pl.pallas_call(functools.partial(inverse_z_kernel, doms), grid=(XD // DEP...  2.59 us
  transfers between devices with their start and end apart: 12, of which 2 were waited for; matrix products, arithmetic and copies ran while one was open for 4% of the time, Pallas kernels for 41%

profile of v6, /device:TPU:0, one launch (start us, length us, event | category | flops | bytes accessed | tf_op | source)
XLA Modules:
  0.0 78.0 jit_solution(3669655970279317759)
XLA Ops:
  1.3 1.4 %pack.1 = f32[16,8,256]{2,1,0:T(8,128)} custom-call(s32[1]{0:T(128)} %copy.12.counts_ref, s32[3,256]{1,0:T(4,128)} %cells_ref.1, f32[3,256]{1,0:T(4,128)} %offsets_ref.1, f32[1,256]{1,0:T(1,128)} %bitcast.31), custom_call_target="tpu_custom_call" | custom-call | tf_op jit(solution)/shard_map/pack/pallas_call | solution.py:500
  2.7 8.3 %all-to-all-start = ((f32[16,8,256]{2,1,0:T(8,128)}), f32[16,8,256]{2,1,0:T(8,128)S(1)}, u32[]{:S(2)}, u32[]{:S(2)}) async-start(f32[16,8,256]{2,1,0:T(8,128)} %pack.1), calls=%async_computation | async-start | bytes 262144 | tf_op jit(solution)/shard_map/all_to_all | solution.py:516
  11.0 1.3 %fusion.1 = (f32[32,32,64]{2,1,0:T(8,128)S(1)}, f32[32,32,64]{2,1,0:T(8,128)S(1)}) fusion(f32[32,64,64]{2,1,0:T(8,128)} %param.15), kind=kLoop, calls=%fused_computation.8 | loop fusion | bytes 1048576 | tf_op jit(solution)/shard_map/slice | solution.py:521
  12.4 0.7 waves.1
  13.5 5.3 %all-to-all-done.same_ref = f32[16,8,256]{2,1,0:T(8,128)S(1)} async-done(((f32[16,8,256]{2,1,0:T(8,128)}), f32[16,8,256]{2,1,0:T(8,128)S(1)}, u32[]{:S(2)}, u32[]{:S(2)}) %all-to-all-start) | async-done | bytes 131104 | tf_op jit(solution)/shard_map/all_to_all | solution.py:516
  18.8 1.4 %collective-permute-start.1 = (f32[32,32,128]{2,1,0:T(8,128)S(1)}, f32[32,32,128]{2,1,0:T(8,128)S(1)}, u32[]{:S(2)}, u32[]{:S(2)}) collective-permute-start(f32[32,32,128]{2,1,0:T(8,128)S(1)} %maximum_multiply_fusion), channel_id=1, source_target_pairs={{0,28},{4,24},{8,20},{12,16},{16,12},{20,8},{24,4},{28,0},{1,29},{... | collective-permute-start | bytes 1572872 | tf_op jit(solution)/shard_map/ppermute | solution.py:528
  21.2 18.5 %forward.1 = (f32[2,32,32,128]{3,2,1,0:T(8,128)S(1)}, f32[2,32,32,128]{3,2,1,0:T(8,128)S(1)}, f32[5,144,1024]{2,1,0:T(8,128)S(1)}, f32[5,128,1024]{2,1,0:T(8,128)S(1)}) custom-call(s32[6]{0:T(128)S(1)} %stack.27.place_ref, s32[32]{0:T(128)S(1)} %reshape.57.live_ref, f32[16,8,256]{2,1,0:T(8,128)S(1)} %all-to-all-done.same_ref, ...), custom_call_target="tpu_custom_call" | custom-call | flops 1000000 | bytes 10000 | tf_op jit(solution)/shard_map/forward/pallas_call | solution.py:535
  39.7 1.3 %inverse_x.2 = (f32[4,2,32,128]{3,2,1,0:T(8,128)S(1)}, f32[4,2,32,128]{3,2,1,0:T(8,128)S(1)}, f32[4,2,32,128]{3,2,1,0:T(8,128)S(1)}, f32[4,2,32,128]{3,2,1,0:T(8,128)S(1)}, f32[19,2,32,128]{3,2,1,0:T(8,128)S(1)}) custom-call(s32[6]{0:T(128)S(1)} %stack.27.place_ref, f32[2,32,32,128]{3,2,1,0:T(8,128)S(1)} %get-tuple-element.49.spectrum_ref, ...), custom_call_target="tpu_custom_call" | custom-call | flops 1000000 | bytes 10000 | tf_op jit(solution)/shard_map/inverse_x/pallas_call | solution.py:562
  41.0 1.4 %collective-permute-start.2 = (f32[4,64,128]{2,1,0:T(8,128)S(1)}, f32[4,64,128]{2,1,0:T(8,128)S(1)}, u32[]{:S(2)}, u32[]{:S(2)}) collective-permute-start(f32[4,64,128]{2,1,0:T(8,128)S(1)} %bitcast.27), channel_id=1, source_target_pairs={{0,4},{4,0},{8,12},{12,8},{16,20},{20,16},{24,28},{28,24},{1,5},{5... | collective-permute-start | bytes 393224 | tf_op jit(solution)/shard_map/ppermute | solution.py:477
  42.4 0.2 collective-permute-start.3
  42.6 2.0 %collective-permute-start.4 = (f32[4,64,128]{2,1,0:T(8,128)S(1)}, f32[4,64,128]{2,1,0:T(8,128)S(1)}, u32[]{:S(2)}, u32[]{:S(2)}) collective-permute-start(f32[4,64,128]{2,1,0:T(8,128)S(1)} %bitcast.25), channel_id=1, source_target_pairs={{0,12},{4,8},{8,4},{12,0},{16,28},{20,24},{24,20},{28,16},{1,13},{... | collective-permute-start | bytes 393224 | tf_op jit(solution)/shard_map/ppermute | solution.py:477
  44.6 1.3 %inverse_x.3 = (f32[4,2,32,128]{3,2,1,0:T(8,128)S(1)}, f32[4,2,32,128]{3,2,1,0:T(8,128)S(1)}, f32[4,2,32,128]{3,2,1,0:T(8,128)S(1)}, f32[4,2,32,128]{3,2,1,0:T(8,128)S(1)}, f32[19,2,32,128]{3,2,1,0:T(8,128)S(1)}) custom-call(s32[6]{0:T(128)S(1)} %stack.27.place_ref, f32[2,32,32,128]{3,2,1,0:T(8,128)S(1)} %get-tuple-element.51.spectrum_ref, ...), custom_call_target="tpu_custom_call" | custom-call | flops 1000000 | bytes 10000 | tf_op jit(solution)/shard_map/inverse_x/pallas_call | solution.py:562
  45.9 1.4 %collective-permute-start.5 = (f32[4,64,128]{2,1,0:T(8,128)S(1)}, f32[4,64,128]{2,1,0:T(8,128)S(1)}, u32[]{:S(2)}, u32[]{:S(2)}) collective-permute-start(f32[4,64,128]{2,1,0:T(8,128)S(1)} %bitcast.30), channel_id=1, source_target_pairs={{0,4},{4,0},{8,12},{12,8},{16,20},{20,16},{24,28},{28,24},{1,5},{5... | collective-permute-start | bytes 393224 | tf_op jit(solution)/shard_map/ppermute | solution.py:477
  47.3 1.0 %collective-permute-start.6 = (f32[4,64,128]{2,1,0:T(8,128)S(1)}, f32[4,64,128]{2,1,0:T(8,128)S(1)}, u32[]{:S(2)}, u32[]{:S(2)}) collective-permute-start(f32[4,64,128]{2,1,0:T(8,128)S(1)} %bitcast.29), channel_id=1, source_target_pairs={{0,8},{4,12},{8,0},{12,4},{16,24},{20,28},{24,16},{28,20},{1,9},{5... | collective-permute-start | bytes 393224 | tf_op jit(solution)/shard_map/ppermute | solution.py:477
  48.2 2.4 %collective-permute-start.7 = (f32[4,64,128]{2,1,0:T(8,128)S(1)}, f32[4,64,128]{2,1,0:T(8,128)S(1)}, u32[]{:S(2)}, u32[]{:S(2)}) collective-permute-start(f32[4,64,128]{2,1,0:T(8,128)S(1)} %bitcast.28), channel_id=1, source_target_pairs={{0,12},{4,8},{8,4},{12,0},{16,28},{20,24},{24,20},{28,16},{1,13},{... | collective-permute-start | bytes 393224 | tf_op jit(solution)/shard_map/ppermute | solution.py:477
  50.6 5.1 %gather.2 = f32[8,1,256]{2,1,0:T(1,128)S(1)} custom-call(s32[6]{0:T(128)S(1)} %stack.27.place_ref, f32[16,8,256]{2,1,0:T(8,128)S(1)} %all-to-all-done.same_ref, f32[16,8,256]{2,1,0:T(8,128)S(1)} %collective-permute-done.other_ref, f32[5,144,1024]{2,1,0:T(8,128)S(1)} %get-tuple-element.47.table_y, f32[5,128,1024]{2,1,0:T(8,128)S(1)} %get-tuple-element.48.table_z, ...), custom_call_target="tpu_custom_call" | custom-call | flops 1000000 | bytes 10000 | tf_op jit(solution)/shard_map/gather/pallas_call | solution.py:578
  55.8 0.6 collective-permute-done.7.refs_7_
  56.4 2.5 %inverse_y.1 = (f32[4,128,128]{2,1,0:T(8,128)S(1)}, f32[4,128,128]{2,1,0:T(8,128)S(1)}, f32[4,128,128]{2,1,0:T(8,128)S(1)}, f32[4,128,128]{2,1,0:T(8,128)S(1)}) custom-call(s32[6]{0:T(128)S(1)} %stack.27.place_ref, f32[4,64,128]{2,1,0:T(8,128)S(1)} %bitcast.23, f32[4,64,128]{2,1,0:T(8,128)S(1)} %collective-permute-done.2.refs_1_, ...), custom_call_target="tpu_custom_call" | custom-call | flops 1000000 | bytes 10000 | tf_op jit(solution)/shard_map/inverse_y/pallas_call | solution.py:599
  58.9 0.5 collective-permute-start.9
  59.5 1.3 %collective-permute-start.10 = (f32[4,128,128]{2,1,0:T(8,128)S(1)}, f32[4,128,128]{2,1,0:T(8,128)S(1)}, u32[]{:S(2)}, u32[]{:S(2)}) collective-permute-start(f32[4,128,128]{2,1,0:T(8,128)S(1)} %get-tuple-element.76), channel_id=1, source_target_pairs={{0,3},{1,2},{2,1},{3,0},{4,7},{5,6},{6,5},{7,4},{8,11},{9,10},{10,... | collective-permute-start | bytes 786440 | tf_op jit(solution)/shard_map/ppermute | solution.py:477
  60.8 5.1 %gather.3 = f32[8,1,256]{2,1,0:T(1,128)S(1)} custom-call(s32[6]{0:T(128)S(1)} %stack.27.place_ref, f32[16,8,256]{2,1,0:T(8,128)S(1)} %all-to-all-done.same_ref, f32[16,8,256]{2,1,0:T(8,128)S(1)} %collective-permute-done.other_ref, f32[5,144,1024]{2,1,0:T(8,128)S(1)} %get-tuple-element.47.table_y, f32[5,128,1024]{2,1,0:T(8,128)S(1)} %get-tuple-element.48.table_z, ...), custom_call_target="tpu_custom_call" | custom-call | flops 1000000 | bytes 10000 | tf_op jit(solution)/shard_map/gather/pallas_call | solution.py:578
  65.9 8.9 %all_to_all.11 = f32[16,1,256]{2,1,0:T(1,128)S(1)} all-to-all(f32[16,1,256]{2,1,0:T(1,128)S(1)} %pad_maximum_fusion), channel_id=1, replica_groups={{0,1,2,3,4,5,6,7,8,9,10,11,12,13,14,15},{16,17,18,19,20,21,22,23,24,25,..., dimensions={0} | all-to-all | bytes 32768 | tf_op jit(solution)/shard_map/all_to_all | solution.py:617
  74.8 0.6 compare_select_fusion
  75.4 2.6 %inverse_z.1 = f32[4,128,512]{2,1,0:T(8,128)} custom-call(s32[6]{0:T(128)S(1)} %stack.27.place_ref, f32[4,128,128]{2,1,0:T(8,128)S(1)} %get-tuple-element.77.refs_0_, f32[4,128,128]{2,1,0:T(8,128)S(1)} %collective-permute-done.8.refs_1_, f32[4,128,128]{2,1,0:T(8,128)S(1)} %collective-permute-done.9.refs_2_, ...), custom_call_target="tpu_custom_call" | custom-call | flops 1000000 | bytes 10000 | tf_op jit(solution)/shard_map/inverse_z/pallas_call | solution.py:629
  (35 shorter events, 1.5 us)
Async XLA Ops:
  2.7 16.1 %all-to-all-start = ((f32[16,8,256]{2,1,0:T(8,128)}), f32[16,8,256]{2,1,0:T(8,128)S(1)}, u32[]{:S(2)}, u32[]{:S(2)}) async-start(f32[16,8,256]{2,1,0:T(8,128)} %pack.1), calls=%async_computation | async-start | bytes 262144 | tf_op jit(solution)/shard_map/all_to_all | solution.py:516
  18.8 1.9 %collective-permute-start = (f32[16,8,256]{2,1,0:T(8,128)S(1)}, f32[16,8,256]{2,1,0:T(8,128)S(1)}, u32[]{:S(2)}, u32[]{:S(2)}) collective-permute-start(f32[16,8,256]{2,1,0:T(8,128)S(1)} %all-to-all-done.same_ref), channel_id=1, source_target_pairs={{0,1},{1,0},{2,3},{3,2},{4,5},{5,4},{6,7},{7,6},{8,9},{9,8},{10,11... | collective-permute-start | bytes 393224 | tf_op jit(solution)/shard_map/ppermute | solution.py:477
  18.8 25.8 %collective-permute-start.1 = (f32[32,32,128]{2,1,0:T(8,128)S(1)}, f32[32,32,128]{2,1,0:T(8,128)S(1)}, u32[]{:S(2)}, u32[]{:S(2)}) collective-permute-start(f32[32,32,128]{2,1,0:T(8,128)S(1)} %maximum_multiply_fusion), channel_id=1, source_target_pairs={{0,28},{4,24},{8,20},{12,16},{16,12},{20,8},{24,4},{28,0},{1,29},{... | collective-permute-start | bytes 1572872 | tf_op jit(solution)/shard_map/ppermute | solution.py:528
  41.0 7.2 %collective-permute-start.2 = (f32[4,64,128]{2,1,0:T(8,128)S(1)}, f32[4,64,128]{2,1,0:T(8,128)S(1)}, u32[]{:S(2)}, u32[]{:S(2)}) collective-permute-start(f32[4,64,128]{2,1,0:T(8,128)S(1)} %bitcast.27), channel_id=1, source_target_pairs={{0,4},{4,0},{8,12},{12,8},{16,20},{20,16},{24,28},{28,24},{1,5},{5... | collective-permute-start | bytes 393224 | tf_op jit(solution)/shard_map/ppermute | solution.py:477
  42.4 13.4 %collective-permute-start.3 = (f32[4,64,128]{2,1,0:T(8,128)S(1)}, f32[4,64,128]{2,1,0:T(8,128)S(1)}, u32[]{:S(2)}, u32[]{:S(2)}) collective-permute-start(f32[4,64,128]{2,1,0:T(8,128)S(1)} %bitcast.26), channel_id=1, source_target_pairs={{0,8},{4,12},{8,0},{12,4},{16,24},{20,28},{24,16},{28,20},{1,9},{5... | collective-permute-start | bytes 393224 | tf_op jit(solution)/shard_map/ppermute | solution.py:477
  42.6 13.2 %collective-permute-start.4 = (f32[4,64,128]{2,1,0:T(8,128)S(1)}, f32[4,64,128]{2,1,0:T(8,128)S(1)}, u32[]{:S(2)}, u32[]{:S(2)}) collective-permute-start(f32[4,64,128]{2,1,0:T(8,128)S(1)} %bitcast.25), channel_id=1, source_target_pairs={{0,12},{4,8},{8,4},{12,0},{16,28},{20,24},{24,20},{28,16},{1,13},{... | collective-permute-start | bytes 393224 | tf_op jit(solution)/shard_map/ppermute | solution.py:477
  45.9 9.8 %collective-permute-start.5 = (f32[4,64,128]{2,1,0:T(8,128)S(1)}, f32[4,64,128]{2,1,0:T(8,128)S(1)}, u32[]{:S(2)}, u32[]{:S(2)}) collective-permute-start(f32[4,64,128]{2,1,0:T(8,128)S(1)} %bitcast.30), channel_id=1, source_target_pairs={{0,4},{4,0},{8,12},{12,8},{16,20},{20,16},{24,28},{28,24},{1,5},{5... | collective-permute-start | bytes 393224 | tf_op jit(solution)/shard_map/ppermute | solution.py:477
  47.3 8.5 %collective-permute-start.6 = (f32[4,64,128]{2,1,0:T(8,128)S(1)}, f32[4,64,128]{2,1,0:T(8,128)S(1)}, u32[]{:S(2)}, u32[]{:S(2)}) collective-permute-start(f32[4,64,128]{2,1,0:T(8,128)S(1)} %bitcast.29), channel_id=1, source_target_pairs={{0,8},{4,12},{8,0},{12,4},{16,24},{20,28},{24,16},{28,20},{1,9},{5... | collective-permute-start | bytes 393224 | tf_op jit(solution)/shard_map/ppermute | solution.py:477
  48.2 8.1 %collective-permute-start.7 = (f32[4,64,128]{2,1,0:T(8,128)S(1)}, f32[4,64,128]{2,1,0:T(8,128)S(1)}, u32[]{:S(2)}, u32[]{:S(2)}) collective-permute-start(f32[4,64,128]{2,1,0:T(8,128)S(1)} %bitcast.28), channel_id=1, source_target_pairs={{0,12},{4,8},{8,4},{12,0},{16,28},{20,24},{24,20},{28,16},{1,13},{... | collective-permute-start | bytes 393224 | tf_op jit(solution)/shard_map/ppermute | solution.py:477
  50.6 5.7 %copy-start = (bf16[512,1024]{1,0:T(8,128)(2,1)S(1)}, bf16[512,1024]{1,0:T(8,128)(2,1)}, u32[]{:S(2)}) copy-start(bf16[512,1024]{1,0:T(8,128)(2,1)} %constant.52.clone.refs_9_) | copy-start | bytes 3145732
  50.6 5.7 %copy-start.1 = (bf16[512,1024]{1,0:T(8,128)(2,1)S(1)}, bf16[512,1024]{1,0:T(8,128)(2,1)}, u32[]{:S(2)}) copy-start(bf16[512,1024]{1,0:T(8,128)(2,1)} %constant.51.clone.refs_8_) | copy-start | bytes 3145732
  58.9 2.0 %collective-permute-start.8 = (f32[4,128,128]{2,1,0:T(8,128)S(1)}, f32[4,128,128]{2,1,0:T(8,128)S(1)}, u32[]{:S(2)}, u32[]{:S(2)}) collective-permute-start(f32[4,128,128]{2,1,0:T(8,128)S(1)} %get-tuple-element.71), channel_id=1, source_target_pairs={{0,1},{1,0},{2,3},{3,2},{4,5},{5,4},{6,7},{7,6},{8,9},{9,8},{10,11... | collective-permute-start | bytes 786440 | tf_op jit(solution)/shard_map/ppermute | solution.py:477
  58.9 16.5 %collective-permute-start.9 = (f32[4,128,128]{2,1,0:T(8,128)S(1)}, f32[4,128,128]{2,1,0:T(8,128)S(1)}, u32[]{:S(2)}, u32[]{:S(2)}) collective-permute-start(f32[4,128,128]{2,1,0:T(8,128)S(1)} %get-tuple-element.75), channel_id=1, source_target_pairs={{0,2},{1,3},{2,0},{3,1},{4,6},{5,7},{6,4},{7,5},{8,10},{9,11},{10,... | collective-permute-start | bytes 786440 | tf_op jit(solution)/shard_map/ppermute | solution.py:477
  59.5 15.4 %copy-start.4 = (f32[256]{0:T(256)S(1)}, f32[256]{0:T(256)}, u32[]{:S(2)}) copy-start(f32[256]{0:T(256)} %param.13) | copy-start | bytes 3076
  59.5 16.0 %copy-start.2 = (bf16[512,512]{1,0:T(8,128)(2,1)S(1)}, bf16[512,512]{1,0:T(8,128)(2,1)}, u32[]{:S(2)}) copy-start(bf16[512,512]{1,0:T(8,128)(2,1)} %constant.54.clone.refs_5_) | copy-start | bytes 1572868
  59.5 16.0 %copy-start.3 = (bf16[512,512]{1,0:T(8,128)(2,1)S(1)}, bf16[512,512]{1,0:T(8,128)(2,1)}, u32[]{:S(2)}) copy-start(bf16[512,512]{1,0:T(8,128)(2,1)} %constant.53.clone.refs_4_) | copy-start | bytes 1572868
  59.5 15.9 %collective-permute-start.10 = (f32[4,128,128]{2,1,0:T(8,128)S(1)}, f32[4,128,128]{2,1,0:T(8,128)S(1)}, u32[]{:S(2)}, u32[]{:S(2)}) collective-permute-start(f32[4,128,128]{2,1,0:T(8,128)S(1)} %get-tuple-element.76), channel_id=1, source_target_pairs={{0,3},{1,2},{2,1},{3,0},{4,7},{5,6},{6,5},{7,4},{8,11},{9,10},{10,... | collective-permute-start | bytes 786440 | tf_op jit(solution)/shard_map/ppermute | solution.py:477

commit v7 on v6

--- a/solution.py
+++ b/solution.py
@@ -319,26 +319,43 @@
 
 def inverse_y_kernel(sources, place_ref, *refs):
     ins, (high_ref, low_ref) = refs[: 2 * sources], refs[2 * sources : 2 * sources + 2]
-    outs, (lines_ref, turned_ref) = refs[2 * sources + 2 : -2], refs[-2:]
+    outs, (plus_ref, minus_ref, turned_ref) = refs[2 * sources + 2 : -3], refs[-3:]
+    waves = NY // 2
+    halves = half_sign()
+    minus_ref[:, pl.ds(0, 8), :] = jnp.zeros((XD, 8, LANES), F32)
     for number, in_ref in enumerate(ins):
-        source = lax.bitwise_xor(place_ref[4], number % sources)
-        half = in_ref.shape[1]
-        rows = pl.ds(half * (number // sources), half)
-        lines_ref[source, :, rows, :] = in_ref[...]
-    parts = []
+        count = in_ref.shape[1]
+        start = lax.bitwise_xor(place_ref[4], number % sources) * count
+        if number < sources:
+            plus_ref[:, pl.ds(pl.multiple_of(start, 8), count), :] = in_ref[...]
+        else:
+            minus_ref[:, pl.ds(pl.multiple_of(start + 8, 8), count), :] = in_ref[...]
+    sums = []
+    for parity in (0, 1):
+        parts = []
+        for x in range(XD):
+            plus = plus_ref[x, pl.ds(parity, waves // 2, stride=2), :]
+            minus = minus_ref[x, pl.ds(7 + parity, waves // 2, stride=2), :]
+            parts.append(split(jnp.concatenate([plus + minus, swap(plus - minus) * halves], 0)))
+        both = jnp.concatenate([value for part in parts for value in part], 1)
+        main = jnp.dot(high_ref[parity], both, preferred_element_type=F32)
+        high = jnp.concatenate([part[0] for part in parts], 1)
+        rest = jnp.dot(low_ref[parity], high, preferred_element_type=F32)
+        sums.append(
+            [
+                main[:, 2 * x * LANES : (2 * x + 1) * LANES]
+                + main[:, (2 * x + 1) * LANES : (2 * x + 2) * LANES]
+                + rest[:, x * LANES : (x + 1) * LANES]
+                for x in range(XD)
+            ]
+        )
+    row = lax.broadcasted_iota(jnp.int32, (waves, 1), 0)
+    alternate = jnp.where(row % 2 == 0, 1.0, -1.0)
+    sign = jnp.where(place_ref[3] == 1, alternate, 1.0)
     for x in range(XD):
-        lines = jnp.concatenate([lines_ref[source, x] for source in range(sources)], 0)
-        pairs = jnp.concatenate([lines, swap(lines) * half_sign()], 0)
-        parts.append(split(pairs))
-    both = jnp.concatenate([value for part in parts for value in part], 1)
-    main = jnp.dot(high_ref[...], both, preferred_element_type=F32)
-    high = jnp.concatenate([part[0] for part in parts], 1)
-    rest = jnp.dot(low_ref[...], high, preferred_element_type=F32)
-    row = lax.broadcasted_iota(jnp.int32, (NY, 1), 0)
-    sign = jnp.where((row % 2 == 1) & (place_ref[3] == 1), -1.0, 1.0)
-    for x in range(XD):
-        total = main[:, 2 * x * LANES : (2 * x + 1) * LANES] + main[:, (2 * x + 1) * LANES : (2 * x + 2) * LANES]
-        total = (total + rest[:, x * LANES : (x + 1) * LANES]) * sign
+        last = minus_ref[x, pl.ds(waves, 8), :][7:8]
+        even, odd = sums[0][x] + alternate * last, sums[1][x]
+        total = jnp.concatenate([(even + odd) * sign, (even - odd) * sign], 0)
         turned_ref[:, x] = total.reshape(len(outs), -1, LANES)
     for k in range(len(outs)):
         outs[k][...] = turned_ref[lax.bitwise_xor(place_ref[5], k)]
@@ -440,13 +457,13 @@
     return jnp.asarray(high), jnp.asarray(low)
 
 
-def inverse_y_table(slab_half, ky_local):
-    waves = []
-    for slab in range(slab_half):
-        first = slab * ky_local
-        waves += [first + i for i in range(ky_local)] + [-(first + i + 1) for i in range(ky_local)]
-    angle = 2.0 * np.pi * (np.outer(np.arange(NY), np.array(waves)) % NY) / NY
-    return bf16_pair(np.concatenate([np.cos(angle), np.sin(angle)], 1))
+def inverse_y_table():
+    tables = []
+    for parity in (0, 1):
+        waves = np.arange(parity, NY // 2, 2)
+        angle = 2.0 * np.pi * (np.outer(np.arange(NY // 2), waves) % NY) / NY
+        tables.append(np.concatenate([np.cos(angle), np.sin(angle)], 1))
+    return bf16_pair(np.stack(tables))
 
 
 def inverse_z_table(dom_count):
@@ -593,7 +610,7 @@
 
     earlier, *lines = lax.optimization_barrier((gather(0, place), *lines))
 
-    high_y, low_y = inverse_y_table(slab_half, ky_local)
+    high_y, low_y = inverse_y_table()
     high_z, low_z = inverse_z_table(doms)
 
     turned = pl.pallas_call(
@@ -602,7 +619,8 @@
         out_specs=[vmem] * doms,
         out_shape=[jax.ShapeDtypeStruct((XD, rows_local, LANES), F32)] * doms,
         scratch_shapes=[
-            pltpu.VMEM((slab_half, XD, 2 * ky_local, LANES), F32),
+            pltpu.VMEM((XD, NY // 2, LANES), F32),
+            pltpu.VMEM((XD, NY // 2 + 8, LANES), F32),
             pltpu.VMEM((doms, XD, rows_local, LANES), F32),
         ],
         compiler_params=params(32),
@@ -624,7 +642,6 @@
     )
     alive = jnp.arange(atoms_local, dtype=jnp.int32) < counts[0]
     gradient = jnp.where(alive, bias_coupling * jnp.sum(sampled, 0), 0.0)
-    gradient, *columns = lax.optimization_barrier((gradient, *columns))
 
     potential = pl.pallas_call(
         functools.partial(inverse_z_kernel, doms),

time: 78.5 us -> 76.2 us (0.971)
  blocking collectives: 8.88 us -> 0 us
  waiting for transfers between devices: 5.89 us -> 9.99 us
  starting transfers between devices: 19.9 us -> 22.3 us
    all_to_all x1 -> x0, blocking collectives: 8.88 us -> none  [per_device(): lax.all_to_all(partial.reshape(members, atoms_local), ('slab', 'dom'), 0,...]
    ppermute x10, waiting for transfers between devices: 0.6 us -> 4.58 us  [swapped(): lax.ppermute(value, axis, [(i, i ^ distance) for i in range(lax.axis_size...]
    all_to_all x0 -> x1, starting transfers between devices: none -> 3.48 us  [per_device(): lax.all_to_all(partial.reshape(members, atoms_local), ('slab', 'dom'), 0,...]
    ppermute x10, starting transfers between devices: 10.2 us -> 9.04 us  [swapped(): lax.ppermute(value, axis, [(i, i ^ distance) for i in range(lax.axis_size...]
    pallas_call x1, Pallas kernels: 2.49 us -> 1.41 us  [per_device(): pl.pallas_call(functools.partial(inverse_y_kernel, slab_half), in_specs=[...]
    pallas_call x1, Pallas kernels: 18.5 us -> 19.6 us  [per_device(): pl.pallas_call(forward_kernel, grid=(slabs,), in_specs=[SMEM] * 2 + [vmem...]
  transfers between devices with their start and end apart: 12 -> 13, of which waited for: 2 -> 4; matrix products, arithmetic and copies ran while one was open for 4% -> 4% of each run, Pallas kernels for 41% -> 47%
where the time goes in v7:
time: 76.2 us; the launch traced here: 76.1 us
  Pallas kernels  38.5 us (51%)
  starting transfers between devices  22.3 us (29%)
  waiting for transfers between devices  9.99 us (13%)
  local copies, waits for them, and re-layouts  2.18 us (3%)
  other arithmetic  1.71 us (2%)
  between operations  1.47 us (2%)
    pallas_call x1, Pallas kernels, per_device(): pl.pallas_call(forward_kernel, grid=(slabs,), in_specs=[SMEM] * 2 + [vmem...  19.6 us
    pallas_call x2, Pallas kernels, gather(): pl.pallas_call(functools.partial(gather_kernel, part * steps), grid=(step...  10.1 us
    ppermute x10, starting transfers between devices, swapped(): lax.ppermute(value, axis, [(i, i ^ distance) for i in range(lax.axis_size...  9.04 us
    all_to_all x1, starting transfers between devices, per_device(): lax.all_to_all(atoms, ('slab', 'dom'), 0, 0, axis_index_groups=[everyone[...  8.31 us
    all_to_all x1, waiting for transfers between devices, per_device(): lax.all_to_all(atoms, ('slab', 'dom'), 0, 0, axis_index_groups=[everyone[...  5.29 us
    ppermute x10, waiting for transfers between devices, swapped(): lax.ppermute(value, axis, [(i, i ^ distance) for i in range(lax.axis_size...  4.58 us
    all_to_all x1, starting transfers between devices, per_device(): lax.all_to_all(partial.reshape(members, atoms_local), ('slab', 'dom'), 0,...  3.48 us
    pallas_call x2, Pallas kernels, per_device(): pl.pallas_call(inverse_x_kernel, in_specs=[SMEM] + [vmem] * 2, out_specs=...  2.68 us
  transfers between devices with their start and end apart: 13, of which 4 were waited for; matrix products, arithmetic and copies ran while one was open for 4% of the time, Pallas kernels for 47%

profile of v7, /device:TPU:0, one launch (start us, length us, event | category | flops | bytes accessed | tf_op | source)
XLA Modules:
  0.0 76.1 jit_solution(5335723915146890324)
XLA Ops:
  1.3 1.4 %pack.1 = f32[16,8,256]{2,1,0:T(8,128)} custom-call(s32[1]{0:T(128)} %copy.12.counts_ref, s32[3,256]{1,0:T(4,128)} %cells_ref.1, f32[3,256]{1,0:T(4,128)} %offsets_ref.1, f32[1,256]{1,0:T(1,128)} %bitcast.31), custom_call_target="tpu_custom_call" | custom-call | tf_op jit(solution)/shard_map/pack/pallas_call | solution.py:517
  2.7 8.3 %all-to-all-start = ((f32[16,8,256]{2,1,0:T(8,128)}), f32[16,8,256]{2,1,0:T(8,128)S(1)}, u32[]{:S(2)}, u32[]{:S(2)}) async-start(f32[16,8,256]{2,1,0:T(8,128)} %pack.1), calls=%async_computation | async-start | bytes 262144 | tf_op jit(solution)/shard_map/all_to_all | solution.py:533
  11.0 1.3 %fusion.1 = (f32[32,32,64]{2,1,0:T(8,128)S(1)}, f32[32,32,64]{2,1,0:T(8,128)S(1)}) fusion(f32[32,64,64]{2,1,0:T(8,128)} %param.15), kind=kLoop, calls=%fused_computation.8 | loop fusion | bytes 1048576 | tf_op jit(solution)/shard_map/slice | solution.py:538
  12.4 0.7 waves.1
  13.5 5.3 %all-to-all-done.same_ref = f32[16,8,256]{2,1,0:T(8,128)S(1)} async-done(((f32[16,8,256]{2,1,0:T(8,128)}), f32[16,8,256]{2,1,0:T(8,128)S(1)}, u32[]{:S(2)}, u32[]{:S(2)}) %all-to-all-start) | async-done | bytes 131104 | tf_op jit(solution)/shard_map/all_to_all | solution.py:533
  18.8 1.4 %collective-permute-start.1 = (f32[32,32,128]{2,1,0:T(8,128)S(1)}, f32[32,32,128]{2,1,0:T(8,128)S(1)}, u32[]{:S(2)}, u32[]{:S(2)}) collective-permute-start(f32[32,32,128]{2,1,0:T(8,128)S(1)} %maximum_multiply_fusion), channel_id=1, source_target_pairs={{0,28},{4,24},{8,20},{12,16},{16,12},{20,8},{24,4},{28,0},{1,29},{... | collective-permute-start | bytes 1572872 | tf_op jit(solution)/shard_map/ppermute | solution.py:545
  21.2 19.6 %forward.1 = (f32[2,32,32,128]{3,2,1,0:T(8,128)S(1)}, f32[2,32,32,128]{3,2,1,0:T(8,128)S(1)}, f32[5,144,1024]{2,1,0:T(8,128)S(1)}, f32[5,128,1024]{2,1,0:T(8,128)S(1)}) custom-call(s32[6]{0:T(128)S(1)} %stack.27.place_ref, s32[32]{0:T(128)S(1)} %reshape.57.live_ref, f32[16,8,256]{2,1,0:T(8,128)S(1)} %all-to-all-done.same_ref, ...), custom_call_target="tpu_custom_call" | custom-call | flops 1000000 | bytes 10000 | tf_op jit(solution)/shard_map/forward/pallas_call | solution.py:552
  40.7 1.3 %inverse_x.2 = (f32[4,2,32,128]{3,2,1,0:T(8,128)S(1)}, f32[4,2,32,128]{3,2,1,0:T(8,128)S(1)}, f32[4,2,32,128]{3,2,1,0:T(8,128)S(1)}, f32[4,2,32,128]{3,2,1,0:T(8,128)S(1)}, f32[19,2,32,128]{3,2,1,0:T(8,128)S(1)}) custom-call(s32[6]{0:T(128)S(1)} %stack.27.place_ref, f32[2,32,32,128]{3,2,1,0:T(8,128)S(1)} %get-tuple-element.44.spectrum_ref, ...), custom_call_target="tpu_custom_call" | custom-call | flops 1000000 | bytes 10000 | tf_op jit(solution)/shard_map/inverse_x/pallas_call | solution.py:579
  42.1 1.3 %collective-permute-start.2 = (f32[4,64,128]{2,1,0:T(8,128)S(1)}, f32[4,64,128]{2,1,0:T(8,128)S(1)}, u32[]{:S(2)}, u32[]{:S(2)}) collective-permute-start(f32[4,64,128]{2,1,0:T(8,128)S(1)} %bitcast.27), channel_id=1, source_target_pairs={{0,4},{4,0},{8,12},{12,8},{16,20},{20,16},{24,28},{28,24},{1,5},{5... | collective-permute-start | bytes 393224 | tf_op jit(solution)/shard_map/ppermute | solution.py:494
  43.6 2.0 %collective-permute-start.4 = (f32[4,64,128]{2,1,0:T(8,128)S(1)}, f32[4,64,128]{2,1,0:T(8,128)S(1)}, u32[]{:S(2)}, u32[]{:S(2)}) collective-permute-start(f32[4,64,128]{2,1,0:T(8,128)S(1)} %bitcast.25), channel_id=1, source_target_pairs={{0,12},{4,8},{8,4},{12,0},{16,28},{20,24},{24,20},{28,16},{1,13},{... | collective-permute-start | bytes 393224 | tf_op jit(solution)/shard_map/ppermute | solution.py:494
  45.6 1.3 %inverse_x.3 = (f32[4,2,32,128]{3,2,1,0:T(8,128)S(1)}, f32[4,2,32,128]{3,2,1,0:T(8,128)S(1)}, f32[4,2,32,128]{3,2,1,0:T(8,128)S(1)}, f32[4,2,32,128]{3,2,1,0:T(8,128)S(1)}, f32[19,2,32,128]{3,2,1,0:T(8,128)S(1)}) custom-call(s32[6]{0:T(128)S(1)} %stack.27.place_ref, f32[2,32,32,128]{3,2,1,0:T(8,128)S(1)} %get-tuple-element.46.spectrum_ref, ...), custom_call_target="tpu_custom_call" | custom-call | flops 1000000 | bytes 10000 | tf_op jit(solution)/shard_map/inverse_x/pallas_call | solution.py:579
  47.0 1.3 %collective-permute-start.5 = (f32[4,64,128]{2,1,0:T(8,128)S(1)}, f32[4,64,128]{2,1,0:T(8,128)S(1)}, u32[]{:S(2)}, u32[]{:S(2)}) collective-permute-start(f32[4,64,128]{2,1,0:T(8,128)S(1)} %bitcast.30), channel_id=1, source_target_pairs={{0,4},{4,0},{8,12},{12,8},{16,20},{20,16},{24,28},{28,24},{1,5},{5... | collective-permute-start | bytes 393224 | tf_op jit(solution)/shard_map/ppermute | solution.py:494
  48.6 2.0 %collective-permute-start.7 = (f32[4,64,128]{2,1,0:T(8,128)S(1)}, f32[4,64,128]{2,1,0:T(8,128)S(1)}, u32[]{:S(2)}, u32[]{:S(2)}) collective-permute-start(f32[4,64,128]{2,1,0:T(8,128)S(1)} %bitcast.28), channel_id=1, source_target_pairs={{0,12},{4,8},{8,4},{12,0},{16,28},{20,24},{24,20},{28,16},{1,13},{... | collective-permute-start | bytes 393224 | tf_op jit(solution)/shard_map/ppermute | solution.py:494
  50.5 5.1 %gather.2 = f32[8,1,256]{2,1,0:T(1,128)S(1)} custom-call(s32[6]{0:T(128)S(1)} %stack.27.place_ref, f32[16,8,256]{2,1,0:T(8,128)S(1)} %all-to-all-done.same_ref, f32[16,8,256]{2,1,0:T(8,128)S(1)} %collective-permute-done.other_ref, f32[5,144,1024]{2,1,0:T(8,128)S(1)} %get-tuple-element.42.table_y, f32[5,128,1024]{2,1,0:T(8,128)S(1)} %get-tuple-element.43.table_z, ...), custom_call_target="tpu_custom_call" | custom-call | flops 1000000 | bytes 10000 | tf_op jit(solution)/shard_map/gather/pallas_call | solution.py:595
  55.6 1.7 %collective-permute-done.7.refs_7_ = f32[4,64,128]{2,1,0:T(8,128)S(1)} collective-permute-done((f32[4,64,128]{2,1,0:T(8,128)S(1)}, f32[4,64,128]{2,1,0:T(8,128)S(1)}, u32[]{:S(2)}, u32[]{:S(2)}) %collective-permute-start.7) | collective-permute-done | bytes 131104 | tf_op jit(solution)/shard_map/ppermute | solution.py:494
  57.4 1.4 %inverse_y.1 = (f32[4,128,128]{2,1,0:T(8,128)S(1)}, f32[4,128,128]{2,1,0:T(8,128)S(1)}, f32[4,128,128]{2,1,0:T(8,128)S(1)}, f32[4,128,128]{2,1,0:T(8,128)S(1)}) custom-call(s32[6]{0:T(128)S(1)} %stack.27.place_ref, f32[4,64,128]{2,1,0:T(8,128)S(1)} %bitcast.23, f32[4,64,128]{2,1,0:T(8,128)S(1)} %collective-permute-done.2.refs_1_, ...), custom_call_target="tpu_custom_call" | custom-call | flops 1000000 | bytes 10000 | tf_op jit(solution)/shard_map/inverse_y/pallas_call | solution.py:616
  58.9 0.5 collective-permute-start.9
  59.4 1.3 %collective-permute-start.10 = (f32[4,128,128]{2,1,0:T(8,128)S(1)}, f32[4,128,128]{2,1,0:T(8,128)S(1)}, u32[]{:S(2)}, u32[]{:S(2)}) collective-permute-start(f32[4,128,128]{2,1,0:T(8,128)S(1)} %get-tuple-element.69), channel_id=1, source_target_pairs={{0,3},{1,2},{2,1},{3,0},{4,7},{5,6},{6,5},{7,4},{8,11},{9,10},{10,... | collective-permute-start | bytes 786440 | tf_op jit(solution)/shard_map/ppermute | solution.py:494
  60.8 5.1 %gather.3 = f32[8,1,256]{2,1,0:T(1,128)S(1)} custom-call(s32[6]{0:T(128)S(1)} %stack.27.place_ref, f32[16,8,256]{2,1,0:T(8,128)S(1)} %all-to-all-done.same_ref, f32[16,8,256]{2,1,0:T(8,128)S(1)} %collective-permute-done.other_ref, f32[5,144,1024]{2,1,0:T(8,128)S(1)} %get-tuple-element.42.table_y, f32[5,128,1024]{2,1,0:T(8,128)S(1)} %get-tuple-element.43.table_z, ...), custom_call_target="tpu_custom_call" | custom-call | flops 1000000 | bytes 10000 | tf_op jit(solution)/shard_map/gather/pallas_call | solution.py:595
  65.8 0.6 pad_maximum_fusion
  66.5 3.5 %all-to-all-start.1 = ((f32[16,1,256]{2,1,0:T(1,128)}), f32[16,1,256]{2,1,0:T(1,128)S(1)}, u32[]{:S(2)}, u32[]{:S(2)}) async-start(f32[16,1,256]{2,1,0:T(1,128)} %pad_maximum_fusion), calls=%async_computation.1 | async-start | bytes 32768 | tf_op jit(solution)/shard_map/all_to_all | solution.py:635
  69.9 2.8 %collective-permute-done.10.refs_3_ = f32[4,128,128]{2,1,0:T(8,128)S(1)} collective-permute-done((f32[4,128,128]{2,1,0:T(8,128)S(1)}, f32[4,128,128]{2,1,0:T(8,128)S(1)}, u32[]{:S(2)}, u32[]{:S(2)}) %collective-permute-start.10) | collective-permute-done | bytes 262176 | tf_op jit(solution)/shard_map/ppermute | solution.py:494
  72.8 2.6 %inverse_z.1 = f32[4,128,512]{2,1,0:T(8,128)} custom-call(s32[6]{0:T(128)S(1)} %stack.27.place_ref, f32[4,128,128]{2,1,0:T(8,128)S(1)} %get-tuple-element.65.refs_0_, f32[4,128,128]{2,1,0:T(8,128)S(1)} %collective-permute-done.8.refs_1_, f32[4,128,128]{2,1,0:T(8,128)S(1)} %collective-permute-done.9.refs_2_, ...), custom_call_target="tpu_custom_call" | custom-call | flops 1000000 | bytes 10000 | tf_op jit(solution)/shard_map/inverse_z/pallas_call | solution.py:646
  75.5 0.6 compare_select_fusion
  (36 shorter events, 2.1 us)
Async XLA Ops:
  2.7 16.1 %all-to-all-start = ((f32[16,8,256]{2,1,0:T(8,128)}), f32[16,8,256]{2,1,0:T(8,128)S(1)}, u32[]{:S(2)}, u32[]{:S(2)}) async-start(f32[16,8,256]{2,1,0:T(8,128)} %pack.1), calls=%async_computation | async-start | bytes 262144 | tf_op jit(solution)/shard_map/all_to_all | solution.py:533
  18.8 1.9 %collective-permute-start = (f32[16,8,256]{2,1,0:T(8,128)S(1)}, f32[16,8,256]{2,1,0:T(8,128)S(1)}, u32[]{:S(2)}, u32[]{:S(2)}) collective-permute-start(f32[16,8,256]{2,1,0:T(8,128)S(1)} %all-to-all-done.same_ref), channel_id=1, source_target_pairs={{0,1},{1,0},{2,3},{3,2},{4,5},{5,4},{6,7},{7,6},{8,9},{9,8},{10,11... | collective-permute-start | bytes 393224 | tf_op jit(solution)/shard_map/ppermute | solution.py:494
  18.8 26.9 %collective-permute-start.1 = (f32[32,32,128]{2,1,0:T(8,128)S(1)}, f32[32,32,128]{2,1,0:T(8,128)S(1)}, u32[]{:S(2)}, u32[]{:S(2)}) collective-permute-start(f32[32,32,128]{2,1,0:T(8,128)S(1)} %maximum_multiply_fusion), channel_id=1, source_target_pairs={{0,28},{4,24},{8,20},{12,16},{16,12},{20,8},{24,4},{28,0},{1,29},{... | collective-permute-start | bytes 1572872 | tf_op jit(solution)/shard_map/ppermute | solution.py:545
  42.1 6.5 %collective-permute-start.2 = (f32[4,64,128]{2,1,0:T(8,128)S(1)}, f32[4,64,128]{2,1,0:T(8,128)S(1)}, u32[]{:S(2)}, u32[]{:S(2)}) collective-permute-start(f32[4,64,128]{2,1,0:T(8,128)S(1)} %bitcast.27), channel_id=1, source_target_pairs={{0,4},{4,0},{8,12},{12,8},{16,20},{20,16},{24,28},{28,24},{1,5},{5... | collective-permute-start | bytes 393224 | tf_op jit(solution)/shard_map/ppermute | solution.py:494
  43.4 12.2 %collective-permute-start.3 = (f32[4,64,128]{2,1,0:T(8,128)S(1)}, f32[4,64,128]{2,1,0:T(8,128)S(1)}, u32[]{:S(2)}, u32[]{:S(2)}) collective-permute-start(f32[4,64,128]{2,1,0:T(8,128)S(1)} %bitcast.26), channel_id=1, source_target_pairs={{0,8},{4,12},{8,0},{12,4},{16,24},{20,28},{24,16},{28,20},{1,9},{5... | collective-permute-start | bytes 393224 | tf_op jit(solution)/shard_map/ppermute | solution.py:494
  43.6 12.0 %collective-permute-start.4 = (f32[4,64,128]{2,1,0:T(8,128)S(1)}, f32[4,64,128]{2,1,0:T(8,128)S(1)}, u32[]{:S(2)}, u32[]{:S(2)}) collective-permute-start(f32[4,64,128]{2,1,0:T(8,128)S(1)} %bitcast.25), channel_id=1, source_target_pairs={{0,12},{4,8},{8,4},{12,0},{16,28},{20,24},{24,20},{28,16},{1,13},{... | collective-permute-start | bytes 393224 | tf_op jit(solution)/shard_map/ppermute | solution.py:494
  47.0 8.7 %collective-permute-start.5 = (f32[4,64,128]{2,1,0:T(8,128)S(1)}, f32[4,64,128]{2,1,0:T(8,128)S(1)}, u32[]{:S(2)}, u32[]{:S(2)}) collective-permute-start(f32[4,64,128]{2,1,0:T(8,128)S(1)} %bitcast.30), channel_id=1, source_target_pairs={{0,4},{4,0},{8,12},{12,8},{16,20},{20,16},{24,28},{28,24},{1,5},{5... | collective-permute-start | bytes 393224 | tf_op jit(solution)/shard_map/ppermute | solution.py:494
  48.3 7.3 %collective-permute-start.6 = (f32[4,64,128]{2,1,0:T(8,128)S(1)}, f32[4,64,128]{2,1,0:T(8,128)S(1)}, u32[]{:S(2)}, u32[]{:S(2)}) collective-permute-start(f32[4,64,128]{2,1,0:T(8,128)S(1)} %bitcast.29), channel_id=1, source_target_pairs={{0,8},{4,12},{8,0},{12,4},{16,24},{20,28},{24,16},{28,20},{1,9},{5... | collective-permute-start | bytes 393224 | tf_op jit(solution)/shard_map/ppermute | solution.py:494
  48.6 8.8 %collective-permute-start.7 = (f32[4,64,128]{2,1,0:T(8,128)S(1)}, f32[4,64,128]{2,1,0:T(8,128)S(1)}, u32[]{:S(2)}, u32[]{:S(2)}) collective-permute-start(f32[4,64,128]{2,1,0:T(8,128)S(1)} %bitcast.28), channel_id=1, source_target_pairs={{0,12},{4,8},{8,4},{12,0},{16,28},{20,24},{24,20},{28,16},{1,13},{... | collective-permute-start | bytes 393224 | tf_op jit(solution)/shard_map/ppermute | solution.py:494
  50.5 6.9 %copy-start.2 = (bf16[2,256,256]{2,1,0:T(8,128)(2,1)S(1)}, bf16[2,256,256]{2,1,0:T(8,128)(2,1)}, u32[]{:S(2)}) copy-start(bf16[2,256,256]{2,1,0:T(8,128)(2,1)} %constant.52.clone.refs_9_) | copy-start | bytes 786436
  50.5 6.9 %copy-start.3 = (bf16[2,256,256]{2,1,0:T(8,128)(2,1)S(1)}, bf16[2,256,256]{2,1,0:T(8,128)(2,1)}, u32[]{:S(2)}) copy-start(bf16[2,256,256]{2,1,0:T(8,128)(2,1)} %constant.51.clone.refs_8_) | copy-start | bytes 786436
  58.8 1.9 %collective-permute-start.8 = (f32[4,128,128]{2,1,0:T(8,128)S(1)}, f32[4,128,128]{2,1,0:T(8,128)S(1)}, u32[]{:S(2)}, u32[]{:S(2)}) collective-permute-start(f32[4,128,128]{2,1,0:T(8,128)S(1)} %get-tuple-element.66), channel_id=1, source_target_pairs={{0,1},{1,0},{2,3},{3,2},{4,5},{5,4},{6,7},{7,6},{8,9},{9,8},{10,11... | collective-permute-start | bytes 786440 | tf_op jit(solution)/shard_map/ppermute | solution.py:494
  58.9 11.1 %collective-permute-start.9 = (f32[4,128,128]{2,1,0:T(8,128)S(1)}, f32[4,128,128]{2,1,0:T(8,128)S(1)}, u32[]{:S(2)}, u32[]{:S(2)}) collective-permute-start(f32[4,128,128]{2,1,0:T(8,128)S(1)} %get-tuple-element.68), channel_id=1, source_target_pairs={{0,2},{1,3},{2,0},{3,1},{4,6},{5,7},{6,4},{7,5},{8,10},{9,11},{10,... | collective-permute-start | bytes 786440 | tf_op jit(solution)/shard_map/ppermute | solution.py:494
  59.4 13.4 %copy-start = (bf16[512,512]{1,0:T(8,128)(2,1)S(1)}, bf16[512,512]{1,0:T(8,128)(2,1)}, u32[]{:S(2)}) copy-start(bf16[512,512]{1,0:T(8,128)(2,1)} %constant.54.clone.refs_5_) | copy-start | bytes 1572868
  59.4 13.4 %copy-start.1 = (bf16[512,512]{1,0:T(8,128)(2,1)S(1)}, bf16[512,512]{1,0:T(8,128)(2,1)}, u32[]{:S(2)}) copy-start(bf16[512,512]{1,0:T(8,128)(2,1)} %constant.53.clone.refs_4_) | copy-start | bytes 1572868
  59.4 13.3 %collective-permute-start.10 = (f32[4,128,128]{2,1,0:T(8,128)S(1)}, f32[4,128,128]{2,1,0:T(8,128)S(1)}, u32[]{:S(2)}, u32[]{:S(2)}) collective-permute-start(f32[4,128,128]{2,1,0:T(8,128)S(1)} %get-tuple-element.69), channel_id=1, source_target_pairs={{0,3},{1,2},{2,1},{3,0},{4,7},{5,6},{6,5},{7,4},{8,11},{9,10},{10,... | collective-permute-start | bytes 786440 | tf_op jit(solution)/shard_map/ppermute | solution.py:494
  65.8 9.7 %copy-start.4 = (f32[256]{0:T(256)S(1)}, f32[256]{0:T(256)}, u32[]{:S(2)}) copy-start(f32[256]{0:T(256)} %param.13) | copy-start | bytes 3076
  66.5 9.0 %all-to-all-start.1 = ((f32[16,1,256]{2,1,0:T(1,128)}), f32[16,1,256]{2,1,0:T(1,128)S(1)}, u32[]{:S(2)}, u32[]{:S(2)}) async-start(f32[16,1,256]{2,1,0:T(1,128)} %pad_maximum_fusion), calls=%async_computation.1 | async-start | bytes 32768 | tf_op jit(solution)/shard_map/all_to_all | solution.py:635

commit v8 on v7

--- a/solution.py
+++ b/solution.py
@@ -208,20 +208,16 @@
     ky_local = rows - 8
     half_slot = same_ref.shape[2] // 2
     doms = table_y.shape[2] // (2 * half_slot)
-    kept = step - place_ref[2]
-    kept = jnp.where((kept >= 0) & (kept < table_y.shape[0] - 1), kept, table_y.shape[0] - 1)
-
-    @pl.when(step == 0)
-    def _():
-        grid_ref[...] = jnp.zeros_like(grid_ref)
-        digits_y[...] = jnp.zeros_like(digits_y)
-        digits_z[...] = jnp.zeros_like(digits_z)
-
-    for slot in range(doms):
-        atoms_ref[slot] = atoms_of(same_ref, other_ref, step, slot, doms)
-
-    def add_tile(tile, halves):
-        atoms = jnp.concatenate([atoms_ref[slot, :, pl.ds(part * half_slot, half_slot)] for slot, part, _ in halves], 1)
+    slabs = cells_x // XD
+
+    def kept(slab):
+        at = slab - place_ref[2]
+        return jnp.where((at >= 0) & (at < table_y.shape[0] - 1), at, table_y.shape[0] - 1)
+
+    def build_tile(tile, slab, halves):
+        lanes_of = [pl.ds(part * half_slot, half_slot) for _, part, _ in halves]
+        atoms = [atoms_ref[slab * doms + slot, :, lanes] for (slot, _, _), lanes in zip(halves, lanes_of)]
+        atoms = jnp.concatenate(atoms, 1)
         counted = jnp.concatenate([jnp.full((1, half_slot), weight) for _, _, weight in halves], 1)
         weights = spline(atoms)
         along_x = plane_weights(atoms, weights) * (atoms[6:7] * counted)
@@ -232,8 +228,8 @@
         for number, (slot, part, _) in enumerate(halves):
             lanes = slice(number * half_slot, (number + 1) * half_slot)
             start = pl.multiple_of((2 * slot + part) * half_slot, half_slot)
-            table_z[kept, :, pl.ds(start, half_slot)] = waves_z[:, lanes]
-            table_y[kept, :, pl.ds(start, half_slot)] = waves_y[:, lanes]
+            table_z[kept(slab), :, pl.ds(start, half_slot)] = waves_z[:, lanes]
+            table_y[kept(slab), :, pl.ds(start, half_slot)] = waves_y[:, lanes]
         high, low = split(waves_z)
         right_ref[tile, pl.ds(0, LANES), :] = high
         right_ref[tile, pl.ds(LANES, LANES), :] = low
@@ -242,6 +238,8 @@
             high, low = split(waves_y * along_x[plane : plane + 1])
             left_ref[tile, pl.ds(first, 2 * rows), :] = high
             left_ref[tile, pl.ds(first + 2 * rows, 2 * rows), :] = low
+
+    def add_tile(tile):
         product = lax.dot_general(
             left_ref[tile], right_ref[tile], (((1,), (1,)), ((), ())), preferred_element_type=F32
         )
@@ -251,21 +249,35 @@
             at = lax.rem(step * XD + plane, cells_x)
             grid_ref[at] += (high[:, :LANES] + high[:, LANES:]) + (low[:, :LANES] + low[:, LANES:])
 
+    @pl.when(step == 0)
+    def _():
+        grid_ref[...] = jnp.zeros_like(grid_ref)
+        digits_y[...] = jnp.zeros_like(digits_y)
+        digits_z[...] = jnp.zeros_like(digits_z)
+        for slab in range(slabs):
+            for slot in range(doms):
+                atoms_ref[slab * doms + slot] = atoms_of(same_ref, other_ref, slab, slot, doms)
+        build_tile(0, 0, [(0, 0, 1.0), (1, 0, 1.0)])
+
     reach = [live_ref[step * doms + slot] for slot in range(doms)]
     reach = [sum(reach[: slot + 1]) for slot in range(doms)]
     for extra in range(doms // 2 + 1):
 
         @pl.when((reach[-1] + 1) // 2 == extra)
         def _(extra=extra):
-            for tile in range(doms // 2):
-                add_tile(tile, [(2 * tile, 0, 1.0), (2 * tile + 1, 0, 1.0)])
+            add_tile(0)
+            for tile in range(1, doms // 2):
+                build_tile(tile, step, [(2 * tile, 0, 1.0), (2 * tile + 1, 0, 1.0)])
+                add_tile(tile)
             for tile in range(extra):
                 chosen = []
                 for place in (2 * tile, 2 * tile + 1):
                     slot = sum((total <= place).astype(jnp.int32) for total in reach)
                     weight = jnp.where(slot < doms, 1.0, 0.0).astype(F32)
                     chosen.append((jnp.minimum(slot, doms - 1), 1, weight))
-                add_tile(doms // 2 + tile, chosen)
+                build_tile(doms // 2 + tile, step, chosen)
+                add_tile(doms // 2 + tile)
+            build_tile(0, jnp.minimum(step + 1, slabs - 1), [(0, 0, 1.0), (1, 0, 1.0)])
 
     @pl.when(step == pl.num_programs(0) - 1)
     def _():
@@ -494,6 +506,11 @@
     return lax.ppermute(value, axis, [(i, i ^ distance) for i in range(lax.axis_size(axis))])
 
 
+def partners(values, axis):
+    received = [swapped(value, axis, k) for k, value in reversed(list(enumerate(values)))]
+    return received[::-1]
+
+
 def per_device(base_cells, offsets, charges, bias_coupling, counts, green):
     slabs = lax.axis_size("slab")
     doms = lax.axis_size("dom")
@@ -564,7 +581,7 @@
             pltpu.VMEM((doms, SPAN * 4 * rows, atoms_local), BF16),
             pltpu.VMEM((doms, 2 * LANES, atoms_local), BF16),
             pltpu.VMEM((cells_x, 2 * rows, LANES), F32),
-            pltpu.VMEM((doms, 8, atoms_local), F32),
+            pltpu.VMEM((slabs * doms, 8, atoms_local), F32),
             pltpu.VMEM((doms, TERMS, atoms_local), BF16),
             pltpu.VMEM((doms, TERMS, atoms_local), BF16),
         ],
@@ -587,7 +604,7 @@
             name="inverse_x",
         )(place, spectrum, influence)
         near.append(planes.reshape(near_planes, ky_local, LANES))
-        lines += [swapped(value.reshape(XD, ky_local, LANES), "slab", k) for k, value in enumerate(pieces)]
+        lines += partners([value.reshape(XD, ky_local, LANES) for value in pieces], "slab")
 
     steps = slab_half // GATHERS
 
@@ -627,7 +644,7 @@
         cost_estimate=SMALL,
         name="inverse_y",
     )(place, *lines, high_y, low_y)
-    columns = [swapped(value, "dom", k) for k, value in enumerate(turned)]
+    columns = partners(turned, "dom")
 
     columns[1], late_place = lax.optimization_barrier((columns[1], place))
     partial = jnp.concatenate([earlier] + [gather(part, late_place) for part in range(1, GATHERS)], 0)

time: 76.2 us -> 76.3 us (level)
  no operation moved by 1% of the time
where the time goes in v8:
time: 76.3 us; the launch traced here: 76.2 us
  Pallas kernels  38.6 us (51%)
  starting transfers between devices  22.3 us (29%)
  waiting for transfers between devices  9.98 us (13%)
  local copies, waits for them, and re-layouts  2.18 us (3%)
  other arithmetic  1.71 us (2%)
  between operations  1.47 us (2%)
    pallas_call x1, Pallas kernels, per_device(): pl.pallas_call(forward_kernel, grid=(slabs,), in_specs=[SMEM] * 2 + [vmem...  19.8 us
    pallas_call x2, Pallas kernels, gather(): pl.pallas_call(functools.partial(gather_kernel, part * steps), grid=(step...  10.1 us
    ppermute x10, starting transfers between devices, swapped(): lax.ppermute(value, axis, [(i, i ^ distance) for i in range(lax.axis_size...  9.04 us
    all_to_all x1, starting transfers between devices, per_device(): lax.all_to_all(atoms, ('slab', 'dom'), 0, 0, axis_index_groups=[everyone[...  8.31 us
    all_to_all x1, waiting for transfers between devices, per_device(): lax.all_to_all(atoms, ('slab', 'dom'), 0, 0, axis_index_groups=[everyone[...  5.29 us
    ppermute x10, waiting for transfers between devices, swapped(): lax.ppermute(value, axis, [(i, i ^ distance) for i in range(lax.axis_size...  4.57 us
    all_to_all x1, starting transfers between devices, per_device(): lax.all_to_all(partial.reshape(members, atoms_local), ('slab', 'dom'), 0,...  3.48 us
    pallas_call x2, Pallas kernels, per_device(): pl.pallas_call(inverse_x_kernel, in_specs=[SMEM] + [vmem] * 2, out_specs=...  2.68 us
  transfers between devices with their start and end apart: 13, of which 4 were waited for; matrix products, arithmetic and copies ran while one was open for 4% of the time, Pallas kernels for 47%

profile of v8, /device:TPU:0, one launch (start us, length us, event | category | flops | bytes accessed | tf_op | source)
XLA Modules:
  0.0 76.2 jit_solution(10816053633647593339)
XLA Ops:
  1.3 1.4 %pack.1 = f32[16,8,256]{2,1,0:T(8,128)} custom-call(s32[1]{0:T(128)} %copy.12.counts_ref, s32[3,256]{1,0:T(4,128)} %cells_ref.1, f32[3,256]{1,0:T(4,128)} %offsets_ref.1, f32[1,256]{1,0:T(1,128)} %bitcast.31), custom_call_target="tpu_custom_call" | custom-call | tf_op jit(solution)/shard_map/pack/pallas_call | solution.py:534
  2.7 8.3 %all-to-all-start = ((f32[16,8,256]{2,1,0:T(8,128)}), f32[16,8,256]{2,1,0:T(8,128)S(1)}, u32[]{:S(2)}, u32[]{:S(2)}) async-start(f32[16,8,256]{2,1,0:T(8,128)} %pack.1), calls=%async_computation | async-start | bytes 262144 | tf_op jit(solution)/shard_map/all_to_all | solution.py:550
  11.0 1.3 %fusion.1 = (f32[32,32,64]{2,1,0:T(8,128)S(1)}, f32[32,32,64]{2,1,0:T(8,128)S(1)}) fusion(f32[32,64,64]{2,1,0:T(8,128)} %param.15), kind=kLoop, calls=%fused_computation.8 | loop fusion | bytes 1048576 | tf_op jit(solution)/shard_map/slice | solution.py:555
  12.4 0.7 waves.1
  13.5 5.3 %all-to-all-done.same_ref = f32[16,8,256]{2,1,0:T(8,128)S(1)} async-done(((f32[16,8,256]{2,1,0:T(8,128)}), f32[16,8,256]{2,1,0:T(8,128)S(1)}, u32[]{:S(2)}, u32[]{:S(2)}) %all-to-all-start) | async-done | bytes 131104 | tf_op jit(solution)/shard_map/all_to_all | solution.py:550
  18.8 1.4 %collective-permute-start.1 = (f32[32,32,128]{2,1,0:T(8,128)S(1)}, f32[32,32,128]{2,1,0:T(8,128)S(1)}, u32[]{:S(2)}, u32[]{:S(2)}) collective-permute-start(f32[32,32,128]{2,1,0:T(8,128)S(1)} %maximum_multiply_fusion), channel_id=1, source_target_pairs={{0,28},{4,24},{8,20},{12,16},{16,12},{20,8},{24,4},{28,0},{1,29},{... | collective-permute-start | bytes 1572872 | tf_op jit(solution)/shard_map/ppermute | solution.py:562
  21.2 19.8 %forward.1 = (f32[2,32,32,128]{3,2,1,0:T(8,128)S(1)}, f32[2,32,32,128]{3,2,1,0:T(8,128)S(1)}, f32[5,144,1024]{2,1,0:T(8,128)S(1)}, f32[5,128,1024]{2,1,0:T(8,128)S(1)}) custom-call(s32[6]{0:T(128)S(1)} %stack.27.place_ref, s32[32]{0:T(128)S(1)} %reshape.57.live_ref, f32[16,8,256]{2,1,0:T(8,128)S(1)} %all-to-all-done.same_ref, ...), custom_call_target="tpu_custom_call" | custom-call | flops 1000000 | bytes 10000 | tf_op jit(solution)/shard_map/forward/pallas_call | solution.py:569
  40.9 1.3 %inverse_x.2 = (f32[4,2,32,128]{3,2,1,0:T(8,128)S(1)}, f32[4,2,32,128]{3,2,1,0:T(8,128)S(1)}, f32[4,2,32,128]{3,2,1,0:T(8,128)S(1)}, f32[4,2,32,128]{3,2,1,0:T(8,128)S(1)}, f32[19,2,32,128]{3,2,1,0:T(8,128)S(1)}) custom-call(s32[6]{0:T(128)S(1)} %stack.27.place_ref, f32[2,32,32,128]{3,2,1,0:T(8,128)S(1)} %get-tuple-element.44.spectrum_ref, ...), custom_call_target="tpu_custom_call" | custom-call | flops 1000000 | bytes 10000 | tf_op jit(solution)/shard_map/inverse_x/pallas_call | solution.py:596
  42.3 1.3 %collective-permute-start.2 = (f32[4,64,128]{2,1,0:T(8,128)S(1)}, f32[4,64,128]{2,1,0:T(8,128)S(1)}, u32[]{:S(2)}, u32[]{:S(2)}) collective-permute-start(f32[4,64,128]{2,1,0:T(8,128)S(1)} %bitcast.27), channel_id=1, source_target_pairs={{0,4},{4,0},{8,12},{12,8},{16,20},{20,16},{24,28},{28,24},{1,5},{5... | collective-permute-start | bytes 393224 | tf_op jit(solution)/shard_map/ppermute | solution.py:506
  43.8 2.0 %collective-permute-start.4 = (f32[4,64,128]{2,1,0:T(8,128)S(1)}, f32[4,64,128]{2,1,0:T(8,128)S(1)}, u32[]{:S(2)}, u32[]{:S(2)}) collective-permute-start(f32[4,64,128]{2,1,0:T(8,128)S(1)} %bitcast.25), channel_id=1, source_target_pairs={{0,12},{4,8},{8,4},{12,0},{16,28},{20,24},{24,20},{28,16},{1,13},{... | collective-permute-start | bytes 393224 | tf_op jit(solution)/shard_map/ppermute | solution.py:506
  45.8 1.3 %inverse_x.3 = (f32[4,2,32,128]{3,2,1,0:T(8,128)S(1)}, f32[4,2,32,128]{3,2,1,0:T(8,128)S(1)}, f32[4,2,32,128]{3,2,1,0:T(8,128)S(1)}, f32[4,2,32,128]{3,2,1,0:T(8,128)S(1)}, f32[19,2,32,128]{3,2,1,0:T(8,128)S(1)}) custom-call(s32[6]{0:T(128)S(1)} %stack.27.place_ref, f32[2,32,32,128]{3,2,1,0:T(8,128)S(1)} %get-tuple-element.46.spectrum_ref, ...), custom_call_target="tpu_custom_call" | custom-call | flops 1000000 | bytes 10000 | tf_op jit(solution)/shard_map/inverse_x/pallas_call | solution.py:596
  47.2 1.3 %collective-permute-start.5 = (f32[4,64,128]{2,1,0:T(8,128)S(1)}, f32[4,64,128]{2,1,0:T(8,128)S(1)}, u32[]{:S(2)}, u32[]{:S(2)}) collective-permute-start(f32[4,64,128]{2,1,0:T(8,128)S(1)} %bitcast.30), channel_id=1, source_target_pairs={{0,4},{4,0},{8,12},{12,8},{16,20},{20,16},{24,28},{28,24},{1,5},{5... | collective-permute-start | bytes 393224 | tf_op jit(solution)/shard_map/ppermute | solution.py:506
  48.7 2.0 %collective-permute-start.7 = (f32[4,64,128]{2,1,0:T(8,128)S(1)}, f32[4,64,128]{2,1,0:T(8,128)S(1)}, u32[]{:S(2)}, u32[]{:S(2)}) collective-permute-start(f32[4,64,128]{2,1,0:T(8,128)S(1)} %bitcast.28), channel_id=1, source_target_pairs={{0,12},{4,8},{8,4},{12,0},{16,28},{20,24},{24,20},{28,16},{1,13},{... | collective-permute-start | bytes 393224 | tf_op jit(solution)/shard_map/ppermute | solution.py:506
  50.7 5.1 %gather.2 = f32[8,1,256]{2,1,0:T(1,128)S(1)} custom-call(s32[6]{0:T(128)S(1)} %stack.27.place_ref, f32[16,8,256]{2,1,0:T(8,128)S(1)} %all-to-all-done.same_ref, f32[16,8,256]{2,1,0:T(8,128)S(1)} %collective-permute-done.other_ref, f32[5,144,1024]{2,1,0:T(8,128)S(1)} %get-tuple-element.42.table_y, f32[5,128,1024]{2,1,0:T(8,128)S(1)} %get-tuple-element.43.table_z, ...), custom_call_target="tpu_custom_call" | custom-call | flops 1000000 | bytes 10000 | tf_op jit(solution)/shard_map/gather/pallas_call | solution.py:612
  55.8 1.7 %collective-permute-done.7.refs_7_ = f32[4,64,128]{2,1,0:T(8,128)S(1)} collective-permute-done((f32[4,64,128]{2,1,0:T(8,128)S(1)}, f32[4,64,128]{2,1,0:T(8,128)S(1)}, u32[]{:S(2)}, u32[]{:S(2)}) %collective-permute-start.7) | collective-permute-done | bytes 131104 | tf_op jit(solution)/shard_map/ppermute | solution.py:506
  57.6 1.4 %inverse_y.1 = (f32[4,128,128]{2,1,0:T(8,128)S(1)}, f32[4,128,128]{2,1,0:T(8,128)S(1)}, f32[4,128,128]{2,1,0:T(8,128)S(1)}, f32[4,128,128]{2,1,0:T(8,128)S(1)}) custom-call(s32[6]{0:T(128)S(1)} %stack.27.place_ref, f32[4,64,128]{2,1,0:T(8,128)S(1)} %bitcast.23, f32[4,64,128]{2,1,0:T(8,128)S(1)} %collective-permute-done.2.refs_1_, ...), custom_call_target="tpu_custom_call" | custom-call | flops 1000000 | bytes 10000 | tf_op jit(solution)/shard_map/inverse_y/pallas_call | solution.py:633
  59.1 0.5 collective-permute-start.9
  59.6 1.3 %collective-permute-start.10 = (f32[4,128,128]{2,1,0:T(8,128)S(1)}, f32[4,128,128]{2,1,0:T(8,128)S(1)}, u32[]{:S(2)}, u32[]{:S(2)}) collective-permute-start(f32[4,128,128]{2,1,0:T(8,128)S(1)} %get-tuple-element.69), channel_id=1, source_target_pairs={{0,3},{1,2},{2,1},{3,0},{4,7},{5,6},{6,5},{7,4},{8,11},{9,10},{10,... | collective-permute-start | bytes 786440 | tf_op jit(solution)/shard_map/ppermute | solution.py:506
  60.9 5.1 %gather.3 = f32[8,1,256]{2,1,0:T(1,128)S(1)} custom-call(s32[6]{0:T(128)S(1)} %stack.27.place_ref, f32[16,8,256]{2,1,0:T(8,128)S(1)} %all-to-all-done.same_ref, f32[16,8,256]{2,1,0:T(8,128)S(1)} %collective-permute-done.other_ref, f32[5,144,1024]{2,1,0:T(8,128)S(1)} %get-tuple-element.42.table_y, f32[5,128,1024]{2,1,0:T(8,128)S(1)} %get-tuple-element.43.table_z, ...), custom_call_target="tpu_custom_call" | custom-call | flops 1000000 | bytes 10000 | tf_op jit(solution)/shard_map/gather/pallas_call | solution.py:612
  66.0 0.6 pad_maximum_fusion
  66.6 3.5 %all-to-all-start.1 = ((f32[16,1,256]{2,1,0:T(1,128)}), f32[16,1,256]{2,1,0:T(1,128)S(1)}, u32[]{:S(2)}, u32[]{:S(2)}) async-start(f32[16,1,256]{2,1,0:T(1,128)} %pad_maximum_fusion), calls=%async_computation.1 | async-start | bytes 32768 | tf_op jit(solution)/shard_map/all_to_all | solution.py:652
  70.1 2.8 %collective-permute-done.10.refs_3_ = f32[4,128,128]{2,1,0:T(8,128)S(1)} collective-permute-done((f32[4,128,128]{2,1,0:T(8,128)S(1)}, f32[4,128,128]{2,1,0:T(8,128)S(1)}, u32[]{:S(2)}, u32[]{:S(2)}) %collective-permute-start.10) | collective-permute-done | bytes 262176 | tf_op jit(solution)/shard_map/ppermute | solution.py:506
  73.0 2.6 %inverse_z.1 = f32[4,128,512]{2,1,0:T(8,128)} custom-call(s32[6]{0:T(128)S(1)} %stack.27.place_ref, f32[4,128,128]{2,1,0:T(8,128)S(1)} %get-tuple-element.65.refs_0_, f32[4,128,128]{2,1,0:T(8,128)S(1)} %collective-permute-done.8.refs_1_, f32[4,128,128]{2,1,0:T(8,128)S(1)} %collective-permute-done.9.refs_2_, ...), custom_call_target="tpu_custom_call" | custom-call | flops 1000000 | bytes 10000 | tf_op jit(solution)/shard_map/inverse_z/pallas_call | solution.py:663
  75.7 0.6 compare_select_fusion
  (36 shorter events, 2.1 us)
Async XLA Ops:
  2.7 16.1 %all-to-all-start = ((f32[16,8,256]{2,1,0:T(8,128)}), f32[16,8,256]{2,1,0:T(8,128)S(1)}, u32[]{:S(2)}, u32[]{:S(2)}) async-start(f32[16,8,256]{2,1,0:T(8,128)} %pack.1), calls=%async_computation | async-start | bytes 262144 | tf_op jit(solution)/shard_map/all_to_all | solution.py:550
  18.8 1.9 %collective-permute-start = (f32[16,8,256]{2,1,0:T(8,128)S(1)}, f32[16,8,256]{2,1,0:T(8,128)S(1)}, u32[]{:S(2)}, u32[]{:S(2)}) collective-permute-start(f32[16,8,256]{2,1,0:T(8,128)S(1)} %all-to-all-done.same_ref), channel_id=1, source_target_pairs={{0,1},{1,0},{2,3},{3,2},{4,5},{5,4},{6,7},{7,6},{8,9},{9,8},{10,11... | collective-permute-start | bytes 393224 | tf_op jit(solution)/shard_map/ppermute | solution.py:506
  18.8 27.0 %collective-permute-start.1 = (f32[32,32,128]{2,1,0:T(8,128)S(1)}, f32[32,32,128]{2,1,0:T(8,128)S(1)}, u32[]{:S(2)}, u32[]{:S(2)}) collective-permute-start(f32[32,32,128]{2,1,0:T(8,128)S(1)} %maximum_multiply_fusion), channel_id=1, source_target_pairs={{0,28},{4,24},{8,20},{12,16},{16,12},{20,8},{24,4},{28,0},{1,29},{... | collective-permute-start | bytes 1572872 | tf_op jit(solution)/shard_map/ppermute | solution.py:562
  42.3 6.5 %collective-permute-start.2 = (f32[4,64,128]{2,1,0:T(8,128)S(1)}, f32[4,64,128]{2,1,0:T(8,128)S(1)}, u32[]{:S(2)}, u32[]{:S(2)}) collective-permute-start(f32[4,64,128]{2,1,0:T(8,128)S(1)} %bitcast.27), channel_id=1, source_target_pairs={{0,4},{4,0},{8,12},{12,8},{16,20},{20,16},{24,28},{28,24},{1,5},{5... | collective-permute-start | bytes 393224 | tf_op jit(solution)/shard_map/ppermute | solution.py:506
  43.6 12.2 %collective-permute-start.3 = (f32[4,64,128]{2,1,0:T(8,128)S(1)}, f32[4,64,128]{2,1,0:T(8,128)S(1)}, u32[]{:S(2)}, u32[]{:S(2)}) collective-permute-start(f32[4,64,128]{2,1,0:T(8,128)S(1)} %bitcast.26), channel_id=1, source_target_pairs={{0,8},{4,12},{8,0},{12,4},{16,24},{20,28},{24,16},{28,20},{1,9},{5... | collective-permute-start | bytes 393224 | tf_op jit(solution)/shard_map/ppermute | solution.py:506
  43.8 12.0 %collective-permute-start.4 = (f32[4,64,128]{2,1,0:T(8,128)S(1)}, f32[4,64,128]{2,1,0:T(8,128)S(1)}, u32[]{:S(2)}, u32[]{:S(2)}) collective-permute-start(f32[4,64,128]{2,1,0:T(8,128)S(1)} %bitcast.25), channel_id=1, source_target_pairs={{0,12},{4,8},{8,4},{12,0},{16,28},{20,24},{24,20},{28,16},{1,13},{... | collective-permute-start | bytes 393224 | tf_op jit(solution)/shard_map/ppermute | solution.py:506
  47.2 8.7 %collective-permute-start.5 = (f32[4,64,128]{2,1,0:T(8,128)S(1)}, f32[4,64,128]{2,1,0:T(8,128)S(1)}, u32[]{:S(2)}, u32[]{:S(2)}) collective-permute-start(f32[4,64,128]{2,1,0:T(8,128)S(1)} %bitcast.30), channel_id=1, source_target_pairs={{0,4},{4,0},{8,12},{12,8},{16,20},{20,16},{24,28},{28,24},{1,5},{5... | collective-permute-start | bytes 393224 | tf_op jit(solution)/shard_map/ppermute | solution.py:506
  48.5 7.3 %collective-permute-start.6 = (f32[4,64,128]{2,1,0:T(8,128)S(1)}, f32[4,64,128]{2,1,0:T(8,128)S(1)}, u32[]{:S(2)}, u32[]{:S(2)}) collective-permute-start(f32[4,64,128]{2,1,0:T(8,128)S(1)} %bitcast.29), channel_id=1, source_target_pairs={{0,8},{4,12},{8,0},{12,4},{16,24},{20,28},{24,16},{28,20},{1,9},{5... | collective-permute-start | bytes 393224 | tf_op jit(solution)/shard_map/ppermute | solution.py:506
  48.7 8.8 %collective-permute-start.7 = (f32[4,64,128]{2,1,0:T(8,128)S(1)}, f32[4,64,128]{2,1,0:T(8,128)S(1)}, u32[]{:S(2)}, u32[]{:S(2)}) collective-permute-start(f32[4,64,128]{2,1,0:T(8,128)S(1)} %bitcast.28), channel_id=1, source_target_pairs={{0,12},{4,8},{8,4},{12,0},{16,28},{20,24},{24,20},{28,16},{1,13},{... | collective-permute-start | bytes 393224 | tf_op jit(solution)/shard_map/ppermute | solution.py:506
  50.7 6.8 %copy-start.2 = (bf16[2,256,256]{2,1,0:T(8,128)(2,1)S(1)}, bf16[2,256,256]{2,1,0:T(8,128)(2,1)}, u32[]{:S(2)}) copy-start(bf16[2,256,256]{2,1,0:T(8,128)(2,1)} %constant.52.clone.refs_9_) | copy-start | bytes 786436
  50.7 6.8 %copy-start.3 = (bf16[2,256,256]{2,1,0:T(8,128)(2,1)S(1)}, bf16[2,256,256]{2,1,0:T(8,128)(2,1)}, u32[]{:S(2)}) copy-start(bf16[2,256,256]{2,1,0:T(8,128)(2,1)} %constant.51.clone.refs_8_) | copy-start | bytes 786436
  59.0 1.9 %collective-permute-start.8 = (f32[4,128,128]{2,1,0:T(8,128)S(1)}, f32[4,128,128]{2,1,0:T(8,128)S(1)}, u32[]{:S(2)}, u32[]{:S(2)}) collective-permute-start(f32[4,128,128]{2,1,0:T(8,128)S(1)} %get-tuple-element.66), channel_id=1, source_target_pairs={{0,1},{1,0},{2,3},{3,2},{4,5},{5,4},{6,7},{7,6},{8,9},{9,8},{10,11... | collective-permute-start | bytes 786440 | tf_op jit(solution)/shard_map/ppermute | solution.py:506
  59.1 11.1 %collective-permute-start.9 = (f32[4,128,128]{2,1,0:T(8,128)S(1)}, f32[4,128,128]{2,1,0:T(8,128)S(1)}, u32[]{:S(2)}, u32[]{:S(2)}) collective-permute-start(f32[4,128,128]{2,1,0:T(8,128)S(1)} %get-tuple-element.68), channel_id=1, source_target_pairs={{0,2},{1,3},{2,0},{3,1},{4,6},{5,7},{6,4},{7,5},{8,10},{9,11},{10,... | collective-permute-start | bytes 786440 | tf_op jit(solution)/shard_map/ppermute | solution.py:506
  59.6 13.3 %copy-start = (bf16[512,512]{1,0:T(8,128)(2,1)S(1)}, bf16[512,512]{1,0:T(8,128)(2,1)}, u32[]{:S(2)}) copy-start(bf16[512,512]{1,0:T(8,128)(2,1)} %constant.54.clone.refs_5_) | copy-start | bytes 1572868
  59.6 13.3 %copy-start.1 = (bf16[512,512]{1,0:T(8,128)(2,1)S(1)}, bf16[512,512]{1,0:T(8,128)(2,1)}, u32[]{:S(2)}) copy-start(bf16[512,512]{1,0:T(8,128)(2,1)} %constant.53.clone.refs_4_) | copy-start | bytes 1572868
  59.6 13.3 %collective-permute-start.10 = (f32[4,128,128]{2,1,0:T(8,128)S(1)}, f32[4,128,128]{2,1,0:T(8,128)S(1)}, u32[]{:S(2)}, u32[]{:S(2)}) collective-permute-start(f32[4,128,128]{2,1,0:T(8,128)S(1)} %get-tuple-element.69), channel_id=1, source_target_pairs={{0,3},{1,2},{2,1},{3,0},{4,7},{5,6},{6,5},{7,4},{8,11},{9,10},{10,... | collective-permute-start | bytes 786440 | tf_op jit(solution)/shard_map/ppermute | solution.py:506
  66.0 9.7 %copy-start.4 = (f32[256]{0:T(256)S(1)}, f32[256]{0:T(256)}, u32[]{:S(2)}) copy-start(f32[256]{0:T(256)} %param.13) | copy-start | bytes 3076
  66.6 9.0 %all-to-all-start.1 = ((f32[16,1,256]{2,1,0:T(1,128)}), f32[16,1,256]{2,1,0:T(1,128)S(1)}, u32[]{:S(2)}, u32[]{:S(2)}) async-start(f32[16,1,256]{2,1,0:T(1,128)} %pad_maximum_fusion), calls=%async_computation.1 | async-start | bytes 32768 | tf_op jit(solution)/shard_map/all_to_all | solution.py:652

commit v9 on v7

--- a/solution.py
+++ b/solution.py
@@ -186,7 +186,8 @@
 
 def forward_kernel(
     place_ref,
-    live_ref,
+    same_reach,
+    other_reach,
     same_ref,
     other_ref,
     factors_y,
@@ -251,7 +252,9 @@
             at = lax.rem(step * XD + plane, cells_x)
             grid_ref[at] += (high[:, :LANES] + high[:, LANES:]) + (low[:, :LANES] + low[:, LANES:])
 
-    reach = [live_ref[step * doms + slot] for slot in range(doms)]
+    reach = [
+        (same_reach, other_reach)[2 * slot // doms][step * (doms // 2) + slot % (doms // 2)] for slot in range(doms)
+    ]
     reach = [sum(reach[: slot + 1]) for slot in range(doms)]
     for extra in range(doms // 2 + 1):
 
@@ -325,7 +328,7 @@
     minus_ref[:, pl.ds(0, 8), :] = jnp.zeros((XD, 8, LANES), F32)
     for number, in_ref in enumerate(ins):
         count = in_ref.shape[1]
-        start = lax.bitwise_xor(place_ref[4], number % sources) * count
+        start = lax.bitwise_xor(place_ref[4], sources - 1 - number % sources) * count
         if number < sources:
             plus_ref[:, pl.ds(pl.multiple_of(start, 8), count), :] = in_ref[...]
         else:
@@ -361,24 +364,29 @@
         outs[k][...] = turned_ref[lax.bitwise_xor(place_ref[5], k)]
 
 
-def inverse_z_kernel(sources, place_ref, *refs):
-    ins, (high_ref, low_ref) = refs[:sources], refs[sources : sources + 2]
-    out_ref, lines_ref = refs[-2:]
-    first = pl.program_id(0) * DEPTH
-    for k in range(sources):
-        lines_ref[lax.bitwise_xor(place_ref[5], k)] = ins[k][pl.ds(first, DEPTH)]
-    rows = DEPTH * lines_ref.shape[2]
-    lines = jnp.concatenate([lines_ref[source].reshape(rows, LANES) for source in range(sources)], 1)
-    high, low = split(lines)
-    total = jnp.dot(high, high_ref[...], preferred_element_type=F32)
-    total += jnp.dot(low, high_ref[...], preferred_element_type=F32)
-    total += jnp.dot(high, low_ref[...], preferred_element_type=F32)
-    out_ref[...] = total.reshape(out_ref.shape)
-
-
-def gather_kernel(
-    first, place_ref, same_ref, other_ref, table_y, table_z, plus_ref, minus_ref, out_ref, shift_ref, fields_ref, stack_ref
-):
+def inverse_z_kernel(distances, place_ref, *refs):
+    count = len(distances)
+    ins, (high_ref, low_ref), (*total_refs, out_ref) = refs[:count], refs[count : count + 2], refs[count + 2 :]
+    planes, rows, depth = out_ref.shape
+    span = pl.ds(pl.program_id(0) * planes, planes)
+    lines, tables = [], []
+    for in_ref, distance in zip(ins, distances):
+        lines.append(in_ref[span].reshape(planes * rows, LANES))
+        start = pl.multiple_of(lax.bitwise_xor(place_ref[5], distance) * LANES, LANES)
+        tables.append((high_ref[pl.ds(start, LANES), :], low_ref[pl.ds(start, LANES), :]))
+    high, low = split(jnp.concatenate(lines, 1))
+    table_high, table_low = (jnp.concatenate([pair[part] for pair in tables], 0) for part in (0, 1))
+    total = jnp.dot(high, table_high, preferred_element_type=F32)
+    total += jnp.dot(low, table_high, preferred_element_type=F32)
+    total += jnp.dot(high, table_low, preferred_element_type=F32)
+    total = total.reshape(planes, rows, depth)
+    for total_ref in total_refs:
+        total += total_ref[span]
+    out_ref[...] = total
+
+
+def gather_kernel(first, place_ref, same_ref, other_ref, table_y, table_z, plus_ref, minus_ref, *refs):
+    *earlier, out_ref, shift_ref, fields_ref, stack_ref = refs
     step = pl.program_id(0)
     half = LANES // 2
     rows = table_y.shape[1] // 2
@@ -390,6 +398,8 @@
 
     @pl.when(step == 0)
     def _():
+        for earlier_ref in earlier:
+            out_ref[pl.ds(0, first * doms)] = earlier_ref[...]
         stack_ref[...] = jnp.zeros_like(stack_ref)
         shift_ref[...] = jnp.zeros_like(shift_ref)
         row = lax.broadcasted_iota(jnp.int32, (8, LANES), 0)
@@ -448,7 +458,7 @@
         waves = total * table_z[first + step, :, lanes]
         sampled = jnp.sum((waves[:half] - waves[half:]) * twice, axis=0, keepdims=True)
         core = place_ref[5] % 2 if slot < doms // 2 else 1 - place_ref[5] % 2
-        out_ref[step * doms + 2 * (slot % (doms // 2)) + core] = sampled
+        out_ref[(first + step) * doms + 2 * (slot % (doms // 2)) + core] = sampled
 
 
 def bf16_pair(table):
@@ -544,15 +554,14 @@
     other = swapped(same, "dom", 1)
     mirrored = lax.ppermute(flipped, "slab", [(s, slabs - 1 - s) for s in range(slabs)])
 
-    reaches = [value[:, 7, 0].reshape(slabs, doms // 2) for value in (same, other)]
-    live = (jnp.concatenate(reaches, 1).reshape(-1) > atoms_local // 2).astype(jnp.int32)
+    reaches = [(value[:, 7, 0] > atoms_local // 2).astype(jnp.int32) for value in (same, other)]
     atoms_slab = doms * atoms_local
     table_bytes = 4 * (slab_half + 1) * (2 * rows + LANES) * atoms_slab
     spectrum_bytes = 16 * cells_x * max(8, quarter_rows) * LANES
     plus, minus, table_y, table_z = pl.pallas_call(
         forward_kernel,
         grid=(slabs,),
-        in_specs=[SMEM] * 2 + [vmem] * 4,
+        in_specs=[SMEM] * 3 + [vmem] * 4,
         out_specs=[vmem] * 4,
         out_shape=[
             jax.ShapeDtypeStruct((2, cells_x, quarter_rows, LANES), F32),
@@ -571,7 +580,7 @@
         compiler_params=params(16 + (table_bytes + spectrum_bytes) // MIB),
         cost_estimate=SMALL,
         name="forward",
-    )(place, live, same, other, factors_y, factors_z)
+    )(place, *reaches, same, other, factors_y, factors_z)
 
     near_planes = cells_x // 2 + 3
     lines, near = [], []
@@ -587,17 +596,17 @@
             name="inverse_x",
         )(place, spectrum, influence)
         near.append(planes.reshape(near_planes, ky_local, LANES))
-        lines += [swapped(value.reshape(XD, ky_local, LANES), "slab", k) for k, value in enumerate(pieces)]
+        lines += [swapped(value.reshape(XD, ky_local, LANES), "slab", k) for k, value in enumerate(pieces)][::-1]
 
     steps = slab_half // GATHERS
 
-    def gather(part, place):
+    def gather(part, place, *earlier):
         return pl.pallas_call(
             functools.partial(gather_kernel, part * steps),
             grid=(steps,),
-            in_specs=[SMEM] + [vmem] * 6,
+            in_specs=[SMEM] + [vmem] * (6 + len(earlier)),
             out_specs=vmem,
-            out_shape=jax.ShapeDtypeStruct((steps * doms, 1, atoms_local), F32),
+            out_shape=jax.ShapeDtypeStruct(((part + 1) * steps * doms, 1, atoms_local), F32),
             scratch_shapes=[
                 pltpu.VMEM((rows, LANES), F32),
                 pltpu.VMEM((steps * XD + 3, LANES, 4 * LANES), BF16),
@@ -606,9 +615,9 @@
             compiler_params=params(12 + (table_bytes + 8 * near_planes * LANES * LANES) // MIB),
             cost_estimate=SMALL,
             name="gather",
-        )(place, same, other, table_y, table_z, *near)
-
-    earlier, *lines = lax.optimization_barrier((gather(0, place), *lines))
+        )(place, same, other, table_y, table_z, *near, *earlier)
+
+    partial, *lines = lax.optimization_barrier((gather(0, place), *lines))
 
     high_y, low_y = inverse_y_table()
     high_z, low_z = inverse_z_table(doms)
@@ -630,7 +639,9 @@
     columns = [swapped(value, "dom", k) for k, value in enumerate(turned)]
 
     columns[1], late_place = lax.optimization_barrier((columns[1], place))
-    partial = jnp.concatenate([earlier] + [gather(part, late_place) for part in range(1, GATHERS)], 0)
+    for part in range(1, GATHERS):
+        partial = gather(part, late_place, partial)
+    partial, columns[0] = lax.optimization_barrier((partial, columns[0]))
     members = slab_half * doms
     sampled = lax.all_to_all(
         partial.reshape(members, atoms_local),
@@ -643,17 +654,22 @@
     alive = jnp.arange(atoms_local, dtype=jnp.int32) < counts[0]
     gradient = jnp.where(alive, bias_coupling * jnp.sum(sampled, 0), 0.0)
 
-    potential = pl.pallas_call(
-        functools.partial(inverse_z_kernel, doms),
-        grid=(XD // DEPTH,),
-        in_specs=[SMEM] + [vmem] * (doms + 2),
-        out_specs=pl.BlockSpec((DEPTH, rows_local, NZ), lambda step: (step, 0, 0)),
-        out_shape=jax.ShapeDtypeStruct((XD, rows_local, NZ), F32),
-        scratch_shapes=[pltpu.VMEM((doms, DEPTH, rows_local, LANES), F32)],
-        compiler_params=params(24),
-        cost_estimate=SMALL,
-        name="inverse_z",
-    )(place, *columns, high_z, low_z)
+    total = []
+    for distances in (range(doms // 2), range(doms - 1, doms // 2 - 1, -1)):
+        last = len(total) == 1
+        total = [
+            pl.pallas_call(
+                functools.partial(inverse_z_kernel, distances),
+                grid=(XD // DEPTH if last else 1,),
+                in_specs=[SMEM] + [vmem] * (len(distances) + 2 + len(total)),
+                out_specs=pl.BlockSpec((DEPTH, rows_local, NZ), lambda step: (step, 0, 0)) if last else vmem,
+                out_shape=jax.ShapeDtypeStruct((XD, rows_local, NZ), F32),
+                compiler_params=params(24),
+                cost_estimate=SMALL,
+                name="inverse_z",
+            )(place, *[columns[k] for k in distances], high_z, low_z, *total)
+        ]
+    potential = total[0]
     return (potential, gradient)
 
 

time: 76.2 us -> 74.9 us (0.983)
  Pallas kernels: 38.5 us -> 37.7 us
    pallas_call x2 -> x3, Pallas kernels: 22.1 us -> 20.7 us  [the longest x1 17.4 us: per_device(): pl.pallas_call(forward_kernel, grid=(slabs,), in_specs=[SMEM] * 3 + [vmem...]
    ppermute x10, waiting for transfers between devices: 4.58 us -> 3.76 us  [swapped(): lax.ppermute(value, axis, [(i, i ^ distance) for i in range(lax.axis_size...]
  transfers between devices with their start and end apart: 13 -> 13, of which waited for: 4 -> 6; matrix products, arithmetic and copies ran while one was open for 4% -> 4% of each run, Pallas kernels for 47% -> 47%
where the time goes in v9:
time: 74.9 us; the launch traced here: 74.6 us
  Pallas kernels  37.7 us (50%)
  starting transfers between devices  22.7 us (30%)
  waiting for transfers between devices  9.5 us (13%)
  other arithmetic  1.76 us (2%)
  local copies, waits for them, and re-layouts  1.53 us (2%)
  between operations  1.47 us (2%)
    pallas_call x1, Pallas kernels, per_device(): pl.pallas_call(forward_kernel, grid=(slabs,), in_specs=[SMEM] * 3 + [vmem...  17.4 us
    pallas_call x2, Pallas kernels, gather(): pl.pallas_call(functools.partial(gather_kernel, part * steps), grid=(step...  10.8 us
    ppermute x10, starting transfers between devices, swapped(): lax.ppermute(value, axis, [(i, i ^ distance) for i in range(lax.axis_size...  9.45 us
    all_to_all x1, starting transfers between devices, per_device(): lax.all_to_all(atoms, ('slab', 'dom'), 0, 0, axis_index_groups=[everyone[...  8.31 us
    all_to_all x1, waiting for transfers between devices, per_device(): lax.all_to_all(atoms, ('slab', 'dom'), 0, 0, axis_index_groups=[everyone[...  5.29 us
    ppermute x10, waiting for transfers between devices, swapped(): lax.ppermute(value, axis, [(i, i ^ distance) for i in range(lax.axis_size...  3.76 us
    all_to_all x1, starting transfers between devices, per_device(): lax.all_to_all(partial.reshape(members, atoms_local), ('slab', 'dom'), 0,...  3.48 us
    pallas_call x2, Pallas kernels, per_device(): pl.pallas_call(functools.partial(inverse_z_kernel, distances), grid=(XD /...  3.23 us
  transfers between devices with their start and end apart: 13, of which 6 were waited for; matrix products, arithmetic and copies ran while one was open for 4% of the time, Pallas kernels for 47%

profile of v9, /device:TPU:0, one launch (start us, length us, event | category | flops | bytes accessed | tf_op | source)
XLA Modules:
  0.0 74.6 jit_solution(1923997568845341495)
XLA Ops:
  1.3 1.4 %pack.1 = f32[16,8,256]{2,1,0:T(8,128)} custom-call(s32[1]{0:T(128)} %copy.12.counts_ref, s32[3,256]{1,0:T(4,128)} %cells_ref.1, f32[3,256]{1,0:T(4,128)} %offsets_ref.1, f32[1,256]{1,0:T(1,128)} %bitcast.31), custom_call_target="tpu_custom_call" | custom-call | tf_op jit(solution)/shard_map/pack/pallas_call | solution.py:527
  2.7 8.3 %all-to-all-start = ((f32[16,8,256]{2,1,0:T(8,128)}), f32[16,8,256]{2,1,0:T(8,128)S(1)}, u32[]{:S(2)}, u32[]{:S(2)}) async-start(f32[16,8,256]{2,1,0:T(8,128)} %pack.1), calls=%async_computation | async-start | bytes 262144 | tf_op jit(solution)/shard_map/all_to_all | solution.py:543
  11.0 1.3 %fusion.2 = (f32[32,32,64]{2,1,0:T(8,128)S(1)}, f32[32,32,64]{2,1,0:T(8,128)S(1)}) fusion(f32[32,64,64]{2,1,0:T(8,128)} %param.15), kind=kLoop, calls=%fused_computation.7 | loop fusion | bytes 1048576 | tf_op jit(solution)/shard_map/slice | solution.py:548
  13.5 5.3 %all-to-all-done.same_ref = f32[16,8,256]{2,1,0:T(8,128)S(1)} async-done(((f32[16,8,256]{2,1,0:T(8,128)}), f32[16,8,256]{2,1,0:T(8,128)S(1)}, u32[]{:S(2)}, u32[]{:S(2)}) %all-to-all-start) | async-done | bytes 131104 | tf_op jit(solution)/shard_map/all_to_all | solution.py:543
  18.8 1.4 %collective-permute-start.1 = (f32[32,32,128]{2,1,0:T(8,128)S(1)}, f32[32,32,128]{2,1,0:T(8,128)S(1)}, u32[]{:S(2)}, u32[]{:S(2)}) collective-permute-start(f32[32,32,128]{2,1,0:T(8,128)S(1)} %maximum_multiply_fusion), channel_id=1, source_target_pairs={{0,28},{4,24},{8,20},{12,16},{16,12},{20,8},{24,4},{28,0},{1,29},{... | collective-permute-start | bytes 1572872 | tf_op jit(solution)/shard_map/ppermute | solution.py:555
  20.8 0.8 %collective-permute-done.other_ref = f32[16,8,256]{2,1,0:T(8,128)S(1)} collective-permute-done((f32[16,8,256]{2,1,0:T(8,128)S(1)}, f32[16,8,256]{2,1,0:T(8,128)S(1)}, u32[]{:S(2)}, u32[]{:S(2)}) %collective-permute-start) | collective-permute-done | bytes 131104 | tf_op jit(solution)/shard_map/ppermute | solution.py:504
  21.9 17.4 %forward.1 = (f32[2,32,32,128]{3,2,1,0:T(8,128)S(1)}, f32[2,32,32,128]{3,2,1,0:T(8,128)S(1)}, f32[5,144,1024]{2,1,0:T(8,128)S(1)}, f32[5,128,1024]{2,1,0:T(8,128)S(1)}) custom-call(s32[6]{0:T(128)S(1)} %stack.27.place_ref, s32[16]{0:T(128)S(1)} %fusion.same_reach, s32[16]{0:T(128)S(1)} %fusion.1.other_reach, f32[16,8,256]{2,1,0:T(8,128)S(1)} %all-to-all-done.same_ref, ...), custom_call_target="tpu_custom_call" | custom-call | flops 1000000 | bytes 10000 | tf_op jit(solution)/shard_map/forward/pallas_call | solution.py:561
  39.4 1.3 %inverse_x.2 = (f32[4,2,32,128]{3,2,1,0:T(8,128)S(1)}, f32[4,2,32,128]{3,2,1,0:T(8,128)S(1)}, f32[4,2,32,128]{3,2,1,0:T(8,128)S(1)}, f32[4,2,32,128]{3,2,1,0:T(8,128)S(1)}, f32[19,2,32,128]{3,2,1,0:T(8,128)S(1)}) custom-call(s32[6]{0:T(128)S(1)} %stack.27.place_ref, f32[2,32,32,128]{3,2,1,0:T(8,128)S(1)} %get-tuple-element.46.spectrum_ref, ...), custom_call_target="tpu_custom_call" | custom-call | flops 1000000 | bytes 10000 | tf_op jit(solution)/shard_map/inverse_x/pallas_call | solution.py:588
  40.7 1.0 %collective-permute-start.2 = (f32[4,64,128]{2,1,0:T(8,128)S(1)}, f32[4,64,128]{2,1,0:T(8,128)S(1)}, u32[]{:S(2)}, u32[]{:S(2)}) collective-permute-start(f32[4,64,128]{2,1,0:T(8,128)S(1)} %bitcast.27), channel_id=1, source_target_pairs={{0,12},{4,8},{8,4},{12,0},{16,28},{20,24},{24,20},{28,16},{1,13},{... | collective-permute-start | bytes 393224 | tf_op jit(solution)/shard_map/ppermute | solution.py:504
  41.7 1.8 %collective-permute-start.3 = (f32[4,64,128]{2,1,0:T(8,128)S(1)}, f32[4,64,128]{2,1,0:T(8,128)S(1)}, u32[]{:S(2)}, u32[]{:S(2)}) collective-permute-start(f32[4,64,128]{2,1,0:T(8,128)S(1)} %bitcast.26), channel_id=1, source_target_pairs={{0,8},{4,12},{8,0},{12,4},{16,24},{20,28},{24,16},{28,20},{1,9},{5... | collective-permute-start | bytes 393224 | tf_op jit(solution)/shard_map/ppermute | solution.py:504
  43.5 0.7 collective-permute-start.4
  44.3 1.3 %inverse_x.3 = (f32[4,2,32,128]{3,2,1,0:T(8,128)S(1)}, f32[4,2,32,128]{3,2,1,0:T(8,128)S(1)}, f32[4,2,32,128]{3,2,1,0:T(8,128)S(1)}, f32[4,2,32,128]{3,2,1,0:T(8,128)S(1)}, f32[19,2,32,128]{3,2,1,0:T(8,128)S(1)}) custom-call(s32[6]{0:T(128)S(1)} %stack.27.place_ref, f32[2,32,32,128]{3,2,1,0:T(8,128)S(1)} %get-tuple-element.48.spectrum_ref, ...), custom_call_target="tpu_custom_call" | custom-call | flops 1000000 | bytes 10000 | tf_op jit(solution)/shard_map/inverse_x/pallas_call | solution.py:588
  45.6 1.0 %collective-permute-start.5 = (f32[4,64,128]{2,1,0:T(8,128)S(1)}, f32[4,64,128]{2,1,0:T(8,128)S(1)}, u32[]{:S(2)}, u32[]{:S(2)}) collective-permute-start(f32[4,64,128]{2,1,0:T(8,128)S(1)} %bitcast.30), channel_id=1, source_target_pairs={{0,12},{4,8},{8,4},{12,0},{16,28},{20,24},{24,20},{28,16},{1,13},{... | collective-permute-start | bytes 393224 | tf_op jit(solution)/shard_map/ppermute | solution.py:504
  46.6 1.8 %collective-permute-start.6 = (f32[4,64,128]{2,1,0:T(8,128)S(1)}, f32[4,64,128]{2,1,0:T(8,128)S(1)}, u32[]{:S(2)}, u32[]{:S(2)}) collective-permute-start(f32[4,64,128]{2,1,0:T(8,128)S(1)} %bitcast.29), channel_id=1, source_target_pairs={{0,8},{4,12},{8,0},{12,4},{16,24},{20,28},{24,16},{28,20},{1,9},{5... | collective-permute-start | bytes 393224 | tf_op jit(solution)/shard_map/ppermute | solution.py:504
  48.4 0.9 %collective-permute-start.7 = (f32[4,64,128]{2,1,0:T(8,128)S(1)}, f32[4,64,128]{2,1,0:T(8,128)S(1)}, u32[]{:S(2)}, u32[]{:S(2)}) collective-permute-start(f32[4,64,128]{2,1,0:T(8,128)S(1)} %bitcast.28), channel_id=1, source_target_pairs={{0,4},{4,0},{8,12},{12,8},{16,20},{20,16},{24,28},{28,24},{1,5},{5... | collective-permute-start | bytes 393224 | tf_op jit(solution)/shard_map/ppermute | solution.py:504
  49.3 5.1 %gather.2.refs_0_ = f32[8,1,256]{2,1,0:T(1,128)S(1)} custom-call(s32[6]{0:T(128)S(1)} %stack.27.place_ref, f32[16,8,256]{2,1,0:T(8,128)S(1)} %all-to-all-done.same_ref, f32[16,8,256]{2,1,0:T(8,128)S(1)} %collective-permute-done.other_ref, f32[5,144,1024]{2,1,0:T(8,128)S(1)} %get-tuple-element.44.table_y, f32[5,128,1024]{2,1,0:T(8,128)S(1)} %get-tuple-element.45.table_z, ...), custom_call_target="tpu_custom_call" | custom-call | flops 1000000 | bytes 10000 | tf_op jit(solution)/shard_map/gather/pallas_call | solution.py:604
  54.5 1.1 %collective-permute-done.6.refs_5_ = f32[4,64,128]{2,1,0:T(8,128)S(1)} collective-permute-done((f32[4,64,128]{2,1,0:T(8,128)S(1)}, f32[4,64,128]{2,1,0:T(8,128)S(1)}, u32[]{:S(2)}, u32[]{:S(2)}) %collective-permute-start.6) | collective-permute-done | bytes 131104 | tf_op jit(solution)/shard_map/ppermute | solution.py:504
  55.7 1.4 %inverse_y.1 = (f32[4,128,128]{2,1,0:T(8,128)S(1)}, f32[4,128,128]{2,1,0:T(8,128)S(1)}, f32[4,128,128]{2,1,0:T(8,128)S(1)}, f32[4,128,128]{2,1,0:T(8,128)S(1)}) custom-call(s32[6]{0:T(128)S(1)} %stack.27.place_ref, f32[4,64,128]{2,1,0:T(8,128)S(1)} %collective-permute-done.2.refs_0_, f32[4,64,128]{2,1,0:T(8,128)S(1)} %collective-permute-done.3.refs_1_, ...), custom_call_target="tpu_custom_call" | custom-call | flops 1000000 | bytes 10000 | tf_op jit(solution)/shard_map/inverse_y/pallas_call | solution.py:625
  57.7 1.6 %collective-permute-start.9 = (f32[4,128,128]{2,1,0:T(8,128)S(1)}, f32[4,128,128]{2,1,0:T(8,128)S(1)}, u32[]{:S(2)}, u32[]{:S(2)}) collective-permute-start(f32[4,128,128]{2,1,0:T(8,128)S(1)} %get-tuple-element.68), channel_id=1, source_target_pairs={{0,2},{1,3},{2,0},{3,1},{4,6},{5,7},{6,4},{7,5},{8,10},{9,11},{10,... | collective-permute-start | bytes 786440 | tf_op jit(solution)/shard_map/ppermute | solution.py:504
  59.3 5.7 %gather.3 = f32[16,1,256]{2,1,0:T(1,128)} custom-call(s32[6]{0:T(128)S(1)} %stack.27.place_ref, f32[16,8,256]{2,1,0:T(8,128)S(1)} %all-to-all-done.same_ref, f32[16,8,256]{2,1,0:T(8,128)S(1)} %collective-permute-done.other_ref, f32[5,144,1024]{2,1,0:T(8,128)S(1)} %get-tuple-element.44.table_y, f32[5,128,1024]{2,1,0:T(8,128)S(1)} %get-tuple-element.45.table_z, ...), custom_call_target="tpu_custom_call" | custom-call | flops 1000000 | bytes 10000 | tf_op jit(solution)/shard_map/gather/pallas_call | solution.py:604
  65.0 3.5 %all-to-all-start.1 = ((f32[16,1,256]{2,1,0:T(1,128)}), f32[16,1,256]{2,1,0:T(1,128)S(1)}, u32[]{:S(2)}, u32[]{:S(2)}) async-start(f32[16,1,256]{2,1,0:T(1,128)} %gather.3), calls=%async_computation.1 | async-start | bytes 32768 | tf_op jit(solution)/shard_map/all_to_all | solution.py:646
  68.5 1.1 %inverse_z.2.refs_4_ = f32[4,128,512]{2,1,0:T(8,128)S(1)} custom-call(s32[6]{0:T(128)S(1)} %stack.27.place_ref, f32[4,128,128]{2,1,0:T(8,128)S(1)} %get-tuple-element.73.refs_0_, f32[4,128,128]{2,1,0:T(8,128)S(1)} %collective-permute-done.10.refs_1_, bf16[512,512]{1,0:T(8,128)(2,1)S(1)} %copy-done.1, bf16[512,512]{1,0:T(8,128)(2,1)S(1)} %copy-done), custom_call_target="tpu_custom_call" | custom-call | flops 1000000 | bytes 10000 | tf_op jit(solution)/shard_map/inverse_z/pallas_call | solution.py:661
  69.7 1.8 %collective-permute-done.9.refs_1_ = f32[4,128,128]{2,1,0:T(8,128)S(1)} collective-permute-done((f32[4,128,128]{2,1,0:T(8,128)S(1)}, f32[4,128,128]{2,1,0:T(8,128)S(1)}, u32[]{:S(2)}, u32[]{:S(2)}) %collective-permute-start.9) | collective-permute-done | bytes 262176 | tf_op jit(solution)/shard_map/ppermute | solution.py:504
  71.4 2.1 %inverse_z.3 = f32[4,128,512]{2,1,0:T(8,128)} custom-call(s32[6]{0:T(128)S(1)} %stack.27.place_ref, f32[4,128,128]{2,1,0:T(8,128)S(1)} %collective-permute-done.8.refs_0_, f32[4,128,128]{2,1,0:T(8,128)S(1)} %collective-permute-done.9.refs_1_, bf16[512,512]{1,0:T(8,128)(2,1)S(1)} %copy-done.1, bf16[512,512]{1,0:T(8,128)(2,1)S(1)} %copy-done, ...), custom_call_target="tpu_custom_call" | custom-call | flops 1000000 | bytes 10000 | tf_op jit(solution)/shard_map/inverse_z/pallas_call | solution.py:661
  (32 shorter events, 4.0 us)
Async XLA Ops:
  2.7 16.1 %all-to-all-start = ((f32[16,8,256]{2,1,0:T(8,128)}), f32[16,8,256]{2,1,0:T(8,128)S(1)}, u32[]{:S(2)}, u32[]{:S(2)}) async-start(f32[16,8,256]{2,1,0:T(8,128)} %pack.1), calls=%async_computation | async-start | bytes 262144 | tf_op jit(solution)/shard_map/all_to_all | solution.py:543
  18.8 25.5 %collective-permute-start.1 = (f32[32,32,128]{2,1,0:T(8,128)S(1)}, f32[32,32,128]{2,1,0:T(8,128)S(1)}, u32[]{:S(2)}, u32[]{:S(2)}) collective-permute-start(f32[32,32,128]{2,1,0:T(8,128)S(1)} %maximum_multiply_fusion), channel_id=1, source_target_pairs={{0,28},{4,24},{8,20},{12,16},{16,12},{20,8},{24,4},{28,0},{1,29},{... | collective-permute-start | bytes 1572872 | tf_op jit(solution)/shard_map/ppermute | solution.py:555
  20.2 1.3 %collective-permute-start = (f32[16,8,256]{2,1,0:T(8,128)S(1)}, f32[16,8,256]{2,1,0:T(8,128)S(1)}, u32[]{:S(2)}, u32[]{:S(2)}) collective-permute-start(f32[16,8,256]{2,1,0:T(8,128)S(1)} %all-to-all-done.same_ref), channel_id=1, source_target_pairs={{0,1},{1,0},{2,3},{3,2},{4,5},{5,4},{6,7},{7,6},{8,9},{9,8},{10,11... | collective-permute-start | bytes 393224 | tf_op jit(solution)/shard_map/ppermute | solution.py:504
  40.7 7.7 %collective-permute-start.2 = (f32[4,64,128]{2,1,0:T(8,128)S(1)}, f32[4,64,128]{2,1,0:T(8,128)S(1)}, u32[]{:S(2)}, u32[]{:S(2)}) collective-permute-start(f32[4,64,128]{2,1,0:T(8,128)S(1)} %bitcast.27), channel_id=1, source_target_pairs={{0,12},{4,8},{8,4},{12,0},{16,28},{20,24},{24,20},{28,16},{1,13},{... | collective-permute-start | bytes 393224 | tf_op jit(solution)/shard_map/ppermute | solution.py:504
  41.7 12.7 %collective-permute-start.3 = (f32[4,64,128]{2,1,0:T(8,128)S(1)}, f32[4,64,128]{2,1,0:T(8,128)S(1)}, u32[]{:S(2)}, u32[]{:S(2)}) collective-permute-start(f32[4,64,128]{2,1,0:T(8,128)S(1)} %bitcast.26), channel_id=1, source_target_pairs={{0,8},{4,12},{8,0},{12,4},{16,24},{20,28},{24,16},{28,20},{1,9},{5... | collective-permute-start | bytes 393224 | tf_op jit(solution)/shard_map/ppermute | solution.py:504
  43.5 10.9 %collective-permute-start.4 = (f32[4,64,128]{2,1,0:T(8,128)S(1)}, f32[4,64,128]{2,1,0:T(8,128)S(1)}, u32[]{:S(2)}, u32[]{:S(2)}) collective-permute-start(f32[4,64,128]{2,1,0:T(8,128)S(1)} %bitcast.25), channel_id=1, source_target_pairs={{0,4},{4,0},{8,12},{12,8},{16,20},{20,16},{24,28},{28,24},{1,5},{5... | collective-permute-start | bytes 393224 | tf_op jit(solution)/shard_map/ppermute | solution.py:504
  45.6 8.8 %collective-permute-start.5 = (f32[4,64,128]{2,1,0:T(8,128)S(1)}, f32[4,64,128]{2,1,0:T(8,128)S(1)}, u32[]{:S(2)}, u32[]{:S(2)}) collective-permute-start(f32[4,64,128]{2,1,0:T(8,128)S(1)} %bitcast.30), channel_id=1, source_target_pairs={{0,12},{4,8},{8,4},{12,0},{16,28},{20,24},{24,20},{28,16},{1,13},{... | collective-permute-start | bytes 393224 | tf_op jit(solution)/shard_map/ppermute | solution.py:504
  46.6 8.9 %collective-permute-start.6 = (f32[4,64,128]{2,1,0:T(8,128)S(1)}, f32[4,64,128]{2,1,0:T(8,128)S(1)}, u32[]{:S(2)}, u32[]{:S(2)}) collective-permute-start(f32[4,64,128]{2,1,0:T(8,128)S(1)} %bitcast.29), channel_id=1, source_target_pairs={{0,8},{4,12},{8,0},{12,4},{16,24},{20,28},{24,16},{28,20},{1,9},{5... | collective-permute-start | bytes 393224 | tf_op jit(solution)/shard_map/ppermute | solution.py:504
  48.4 7.2 %collective-permute-start.7 = (f32[4,64,128]{2,1,0:T(8,128)S(1)}, f32[4,64,128]{2,1,0:T(8,128)S(1)}, u32[]{:S(2)}, u32[]{:S(2)}) collective-permute-start(f32[4,64,128]{2,1,0:T(8,128)S(1)} %bitcast.28), channel_id=1, source_target_pairs={{0,4},{4,0},{8,12},{12,8},{16,20},{20,16},{24,28},{28,24},{1,5},{5... | collective-permute-start | bytes 393224 | tf_op jit(solution)/shard_map/ppermute | solution.py:504
  49.3 6.3 %copy-start.2 = (bf16[2,256,256]{2,1,0:T(8,128)(2,1)S(1)}, bf16[2,256,256]{2,1,0:T(8,128)(2,1)}, u32[]{:S(2)}) copy-start(bf16[2,256,256]{2,1,0:T(8,128)(2,1)} %constant.52.clone.refs_9_) | copy-start | bytes 786436
  49.3 6.3 %copy-start.3 = (bf16[2,256,256]{2,1,0:T(8,128)(2,1)S(1)}, bf16[2,256,256]{2,1,0:T(8,128)(2,1)}, u32[]{:S(2)}) copy-start(bf16[2,256,256]{2,1,0:T(8,128)(2,1)} %constant.51.clone.refs_8_) | copy-start | bytes 786436
  57.1 2.2 %collective-permute-start.10 = (f32[4,128,128]{2,1,0:T(8,128)S(1)}, f32[4,128,128]{2,1,0:T(8,128)S(1)}, u32[]{:S(2)}, u32[]{:S(2)}) collective-permute-start(f32[4,128,128]{2,1,0:T(8,128)S(1)} %get-tuple-element.69), channel_id=1, source_target_pairs={{0,1},{1,0},{2,3},{3,2},{4,5},{5,4},{6,7},{7,6},{8,9},{9,8},{10,11... | collective-permute-start | bytes 786440 | tf_op jit(solution)/shard_map/ppermute | solution.py:504
  57.2 12.5 %collective-permute-start.8 = (f32[4,128,128]{2,1,0:T(8,128)S(1)}, f32[4,128,128]{2,1,0:T(8,128)S(1)}, u32[]{:S(2)}, u32[]{:S(2)}) collective-permute-start(f32[4,128,128]{2,1,0:T(8,128)S(1)} %get-tuple-element.67), channel_id=1, source_target_pairs={{0,3},{1,2},{2,1},{3,0},{4,7},{5,6},{6,5},{7,4},{8,11},{9,10},{10,... | collective-permute-start | bytes 786440 | tf_op jit(solution)/shard_map/ppermute | solution.py:504
  57.7 10.7 %copy-start = (bf16[512,512]{1,0:T(8,128)(2,1)S(1)}, bf16[512,512]{1,0:T(8,128)(2,1)}, u32[]{:S(2)}) copy-start(bf16[512,512]{1,0:T(8,128)(2,1)} %constant.54.clone.refs_3_) | copy-start | bytes 1572868
  57.7 10.8 %copy-start.1 = (bf16[512,512]{1,0:T(8,128)(2,1)S(1)}, bf16[512,512]{1,0:T(8,128)(2,1)}, u32[]{:S(2)}) copy-start(bf16[512,512]{1,0:T(8,128)(2,1)} %constant.53.clone.refs_2_) | copy-start | bytes 1572868
  57.7 13.7 %collective-permute-start.9 = (f32[4,128,128]{2,1,0:T(8,128)S(1)}, f32[4,128,128]{2,1,0:T(8,128)S(1)}, u32[]{:S(2)}, u32[]{:S(2)}) collective-permute-start(f32[4,128,128]{2,1,0:T(8,128)S(1)} %get-tuple-element.68), channel_id=1, source_target_pairs={{0,2},{1,3},{2,0},{3,1},{4,6},{5,7},{6,4},{7,5},{8,10},{9,11},{10,... | collective-permute-start | bytes 786440 | tf_op jit(solution)/shard_map/ppermute | solution.py:504
  65.0 9.0 %all-to-all-start.1 = ((f32[16,1,256]{2,1,0:T(1,128)}), f32[16,1,256]{2,1,0:T(1,128)S(1)}, u32[]{:S(2)}, u32[]{:S(2)}) async-start(f32[16,1,256]{2,1,0:T(1,128)} %gather.3), calls=%async_computation.1 | async-start | bytes 32768 | tf_op jit(solution)/shard_map/all_to_all | solution.py:646
  68.5 5.5 %copy-start.4 = (f32[256]{0:T(256)S(1)}, f32[256]{0:T(256)}, u32[]{:S(2)}) copy-start(f32[256]{0:T(256)} %param.13) | copy-start | bytes 3076

commit v10 on v9

--- a/solution.py
+++ b/solution.py
@@ -186,8 +186,7 @@
 
 def forward_kernel(
     place_ref,
-    same_reach,
-    other_reach,
+    live_ref,
     same_ref,
     other_ref,
     factors_y,
@@ -239,22 +238,21 @@
         right_ref[tile, pl.ds(0, LANES), :] = high
         right_ref[tile, pl.ds(LANES, LANES), :] = low
         for plane in range(SPAN):
-            first = 4 * rows * plane
             high, low = split(waves_y * along_x[plane : plane + 1])
-            left_ref[tile, pl.ds(first, 2 * rows), :] = high
-            left_ref[tile, pl.ds(first + 2 * rows, 2 * rows), :] = low
-        product = lax.dot_general(
-            left_ref[tile], right_ref[tile], (((1,), (1,)), ((), ())), preferred_element_type=F32
+            left_ref[tile, 0, pl.ds(2 * rows * plane, 2 * rows), :] = high
+            left_ref[tile, 1, pl.ds(2 * rows * plane, 2 * rows), :] = low
+        across = (((1,), (1,)), ((), ()))
+        high = lax.dot_general(left_ref[tile, 0], right_ref[tile], across, preferred_element_type=F32)
+        low = lax.dot_general(
+            left_ref[tile, 1], right_ref[tile, pl.ds(0, LANES), :], across, preferred_element_type=F32
         )
         for plane in range(SPAN):
-            first = 4 * rows * plane
-            high, low = product[first : first + 2 * rows], product[first + 2 * rows : first + 4 * rows]
+            span = slice(2 * rows * plane, 2 * rows * (plane + 1))
             at = lax.rem(step * XD + plane, cells_x)
-            grid_ref[at] += (high[:, :LANES] + high[:, LANES:]) + (low[:, :LANES] + low[:, LANES:])
-
-    reach = [
-        (same_reach, other_reach)[2 * slot // doms][step * (doms // 2) + slot % (doms // 2)] for slot in range(doms)
-    ]
+            grid_ref[at] += (high[span, :LANES] + high[span, LANES:]) + low[span]
+
+    slabs, pairs = cells_x // XD, doms // 2
+    reach = [live_ref[(slot // pairs * slabs + step) * pairs + slot % pairs] for slot in range(doms)]
     reach = [sum(reach[: slot + 1]) for slot in range(doms)]
     for extra in range(doms // 2 + 1):
 
@@ -548,20 +546,21 @@
         return jnp.concatenate([value[:, :quarter_rows], value[:, quarter_rows:]], 2) * normalize
 
     own = halves_beside(green)
-    same, flipped, factors_y, factors_z = lax.optimization_barrier(
-        (same, halves_beside(green[:, ::-1]), factors_y, factors_z)
+    same, own, flipped, factors_y, factors_z = lax.optimization_barrier(
+        (same, own, halves_beside(green[:, ::-1]), factors_y, factors_z)
     )
     other = swapped(same, "dom", 1)
     mirrored = lax.ppermute(flipped, "slab", [(s, slabs - 1 - s) for s in range(slabs)])
 
-    reaches = [(value[:, 7, 0] > atoms_local // 2).astype(jnp.int32) for value in (same, other)]
+    live = jnp.concatenate([same[:, 7, 0], other[:, 7, 0]])
+    live = (live > atoms_local // 2).astype(jnp.int32)
     atoms_slab = doms * atoms_local
     table_bytes = 4 * (slab_half + 1) * (2 * rows + LANES) * atoms_slab
     spectrum_bytes = 16 * cells_x * max(8, quarter_rows) * LANES
     plus, minus, table_y, table_z = pl.pallas_call(
         forward_kernel,
         grid=(slabs,),
-        in_specs=[SMEM] * 3 + [vmem] * 4,
+        in_specs=[SMEM] * 2 + [vmem] * 4,
         out_specs=[vmem] * 4,
         out_shape=[
             jax.ShapeDtypeStruct((2, cells_x, quarter_rows, LANES), F32),
@@ -570,7 +569,7 @@
             jax.ShapeDtypeStruct((slab_half + 1, LANES, atoms_slab), F32),
         ],
         scratch_shapes=[
-            pltpu.VMEM((doms, SPAN * 4 * rows, atoms_local), BF16),
+            pltpu.VMEM((doms, 2, SPAN * 2 * rows, atoms_local), BF16),
             pltpu.VMEM((doms, 2 * LANES, atoms_local), BF16),
             pltpu.VMEM((cells_x, 2 * rows, LANES), F32),
             pltpu.VMEM((doms, 8, atoms_local), F32),
@@ -580,7 +579,7 @@
         compiler_params=params(16 + (table_bytes + spectrum_bytes) // MIB),
         cost_estimate=SMALL,
         name="forward",
-    )(place, *reaches, same, other, factors_y, factors_z)
+    )(place, live, same, other, factors_y, factors_z)
 
     near_planes = cells_x // 2 + 3
     lines, near = [], []

time: 74.9 us -> 77.5 us (1.035)
  Pallas kernels: 37.7 us -> 40.3 us
    pallas_call x1, Pallas kernels: 17.4 us -> 20 us  [per_device(): pl.pallas_call(forward_kernel, grid=(slabs,), in_specs=[SMEM] * 2 + [vmem...]
    all_to_all x1, waiting for transfers between devices: 5.29 us -> 4.38 us  [per_device(): lax.all_to_all(atoms, ('slab', 'dom'), 0, 0, axis_index_groups=[everyone[...]
  transfers between devices with their start and end apart: 13 -> 13, of which waited for: 6 -> 6; matrix products, arithmetic and copies ran while one was open for 4% -> 4% of each run, Pallas kernels for 47% -> 49%
where the time goes in v10:
time: 77.5 us; the launch traced here: 77.1 us
  Pallas kernels  40.3 us (52%)
  starting transfers between devices  22.7 us (29%)
  waiting for transfers between devices  9 us (12%)
  local copies, waits for them, and re-layouts  1.93 us (2%)
  other arithmetic  1.8 us (2%)
  between operations  1.46 us (2%)
    pallas_call x1, Pallas kernels, per_device(): pl.pallas_call(forward_kernel, grid=(slabs,), in_specs=[SMEM] * 2 + [vmem...  20 us
    pallas_call x2, Pallas kernels, gather(): pl.pallas_call(functools.partial(gather_kernel, part * steps), grid=(step...  10.8 us
    ppermute x10, starting transfers between devices, swapped(): lax.ppermute(value, axis, [(i, i ^ distance) for i in range(lax.axis_size...  9.45 us
    all_to_all x1, starting transfers between devices, per_device(): lax.all_to_all(atoms, ('slab', 'dom'), 0, 0, axis_index_groups=[everyone[...  8.31 us
    all_to_all x1, waiting for transfers between devices, per_device(): lax.all_to_all(atoms, ('slab', 'dom'), 0, 0, axis_index_groups=[everyone[...  4.38 us
    ppermute x10, waiting for transfers between devices, swapped(): lax.ppermute(value, axis, [(i, i ^ distance) for i in range(lax.axis_size...  4.15 us
    all_to_all x1, starting transfers between devices, per_device(): lax.all_to_all(partial.reshape(members, atoms_local), ('slab', 'dom'), 0,...  3.49 us
    pallas_call x2, Pallas kernels, per_device(): pl.pallas_call(functools.partial(inverse_z_kernel, distances), grid=(XD /...  3.22 us
  transfers between devices with their start and end apart: 13, of which 6 were waited for; matrix products, arithmetic and copies ran while one was open for 4% of the time, Pallas kernels for 49%

profile of v10, /device:TPU:0, one launch (start us, length us, event | category | flops | bytes accessed | tf_op | source)
XLA Modules:
  0.0 77.1 jit_solution(1158004859907392168)
XLA Ops:
  1.3 1.4 %pack.1 = f32[16,8,256]{2,1,0:T(8,128)} custom-call(s32[1]{0:T(128)} %copy.12.counts_ref, s32[3,256]{1,0:T(4,128)} %cells_ref.1, f32[3,256]{1,0:T(4,128)} %offsets_ref.1, f32[1,256]{1,0:T(1,128)} %bitcast.31), custom_call_target="tpu_custom_call" | custom-call | tf_op jit(solution)/shard_map/pack/pallas_call | solution.py:525
  2.7 8.3 %all-to-all-start = ((f32[16,8,256]{2,1,0:T(8,128)}), f32[16,8,256]{2,1,0:T(8,128)S(1)}, u32[]{:S(2)}, u32[]{:S(2)}) async-start(f32[16,8,256]{2,1,0:T(8,128)} %pack.1), calls=%async_computation | async-start | bytes 262144 | tf_op jit(solution)/shard_map/all_to_all | solution.py:541
  11.0 1.3 %fusion = (f32[32,32,64]{2,1,0:T(8,128)S(1)}, f32[32,32,64]{2,1,0:T(8,128)S(1)}) fusion(f32[32,64,64]{2,1,0:T(8,128)} %param.15), kind=kLoop, calls=%fused_computation.6 | loop fusion | bytes 1048576 | tf_op jit(solution)/shard_map/slice | solution.py:546
  13.3 1.1 %maximum_multiply_fusion = (f32[32,32,128]{2,1,0:T(8,128)S(1)}, f32[32,32,128]{2,1,0:T(8,128)}) fusion(f32[32,32,64]{2,1,0:T(8,128)S(1)} %get-tuple-element.79, f32[32,32,64]{2,1,0:T(8,128)S(1)} %get-tuple-element.78, f32[32,32,64]{2,1,0:T(8,128)S(1)} %slice.23, f32[32,32,64]{2,1,0:T(8,128)S(1)} %slice.22), kind=kLoop, calls=%fused_computation | loop fusion | flops 524288 | bytes 2097152 | tf_op jit(solution)/shard_map/mul | solution.py:546
  14.4 4.4 %all-to-all-done.same_ref = f32[16,8,256]{2,1,0:T(8,128)S(1)} async-done(((f32[16,8,256]{2,1,0:T(8,128)}), f32[16,8,256]{2,1,0:T(8,128)S(1)}, u32[]{:S(2)}, u32[]{:S(2)}) %all-to-all-start) | async-done | bytes 131104 | tf_op jit(solution)/shard_map/all_to_all | solution.py:541
  18.8 1.4 %collective-permute-start.1 = (f32[32,32,128]{2,1,0:T(8,128)}, f32[32,32,128]{2,1,0:T(8,128)S(1)}, u32[]{:S(2)}, u32[]{:S(2)}) collective-permute-start(f32[32,32,128]{2,1,0:T(8,128)} %get-tuple-element.51), channel_id=1, source_target_pairs={{0,28},{4,24},{8,20},{12,16},{16,12},{20,8},{24,4},{28,0},{1,29},{... | collective-permute-start | bytes 1572872 | tf_op jit(solution)/shard_map/ppermute | solution.py:553
  20.4 1.1 %collective-permute-done.other_ref = f32[16,8,256]{2,1,0:T(8,128)S(1)} collective-permute-done((f32[16,8,256]{2,1,0:T(8,128)S(1)}, f32[16,8,256]{2,1,0:T(8,128)S(1)}, u32[]{:S(2)}, u32[]{:S(2)}) %collective-permute-start) | collective-permute-done | bytes 131104 | tf_op jit(solution)/shard_map/ppermute | solution.py:502
  21.9 20.0 %forward.1 = (f32[2,32,32,128]{3,2,1,0:T(8,128)S(1)}, f32[2,32,32,128]{3,2,1,0:T(8,128)S(1)}, f32[5,144,1024]{2,1,0:T(8,128)S(1)}, f32[5,128,1024]{2,1,0:T(8,128)S(1)}) custom-call(s32[6]{0:T(128)S(1)} %stack.27.place_ref, s32[32]{0:T(128)S(1)} %compare_convert_fusion.live_ref, f32[16,8,256]{2,1,0:T(8,128)S(1)} %all-to-all-done.same_ref, ...), custom_call_target="tpu_custom_call" | custom-call | flops 1000000 | bytes 10000 | tf_op jit(solution)/shard_map/forward/pallas_call | solution.py:560
  41.9 1.3 %inverse_x.2 = (f32[4,2,32,128]{3,2,1,0:T(8,128)S(1)}, f32[4,2,32,128]{3,2,1,0:T(8,128)S(1)}, f32[4,2,32,128]{3,2,1,0:T(8,128)S(1)}, f32[4,2,32,128]{3,2,1,0:T(8,128)S(1)}, f32[19,2,32,128]{3,2,1,0:T(8,128)S(1)}) custom-call(s32[6]{0:T(128)S(1)} %stack.27.place_ref, f32[2,32,32,128]{3,2,1,0:T(8,128)S(1)} %get-tuple-element.47.spectrum_ref, ...), custom_call_target="tpu_custom_call" | custom-call | flops 1000000 | bytes 10000 | tf_op jit(solution)/shard_map/inverse_x/pallas_call | solution.py:587
  43.2 1.0 %collective-permute-start.2 = (f32[4,64,128]{2,1,0:T(8,128)S(1)}, f32[4,64,128]{2,1,0:T(8,128)S(1)}, u32[]{:S(2)}, u32[]{:S(2)}) collective-permute-start(f32[4,64,128]{2,1,0:T(8,128)S(1)} %bitcast.27), channel_id=1, source_target_pairs={{0,12},{4,8},{8,4},{12,0},{16,28},{20,24},{24,20},{28,16},{1,13},{... | collective-permute-start | bytes 393224 | tf_op jit(solution)/shard_map/ppermute | solution.py:502
  44.2 1.8 %collective-permute-start.3 = (f32[4,64,128]{2,1,0:T(8,128)S(1)}, f32[4,64,128]{2,1,0:T(8,128)S(1)}, u32[]{:S(2)}, u32[]{:S(2)}) collective-permute-start(f32[4,64,128]{2,1,0:T(8,128)S(1)} %bitcast.26), channel_id=1, source_target_pairs={{0,8},{4,12},{8,0},{12,4},{16,24},{20,28},{24,16},{28,20},{1,9},{5... | collective-permute-start | bytes 393224 | tf_op jit(solution)/shard_map/ppermute | solution.py:502
  46.8 1.3 %inverse_x.3 = (f32[4,2,32,128]{3,2,1,0:T(8,128)S(1)}, f32[4,2,32,128]{3,2,1,0:T(8,128)S(1)}, f32[4,2,32,128]{3,2,1,0:T(8,128)S(1)}, f32[4,2,32,128]{3,2,1,0:T(8,128)S(1)}, f32[19,2,32,128]{3,2,1,0:T(8,128)S(1)}) custom-call(s32[6]{0:T(128)S(1)} %stack.27.place_ref, f32[2,32,32,128]{3,2,1,0:T(8,128)S(1)} %get-tuple-element.50.spectrum_ref, ...), custom_call_target="tpu_custom_call" | custom-call | flops 1000000 | bytes 10000 | tf_op jit(solution)/shard_map/inverse_x/pallas_call | solution.py:587
  48.1 1.0 %collective-permute-start.5 = (f32[4,64,128]{2,1,0:T(8,128)S(1)}, f32[4,64,128]{2,1,0:T(8,128)S(1)}, u32[]{:S(2)}, u32[]{:S(2)}) collective-permute-start(f32[4,64,128]{2,1,0:T(8,128)S(1)} %bitcast.30), channel_id=1, source_target_pairs={{0,12},{4,8},{8,4},{12,0},{16,28},{20,24},{24,20},{28,16},{1,13},{... | collective-permute-start | bytes 393224 | tf_op jit(solution)/shard_map/ppermute | solution.py:502
  49.1 1.8 %collective-permute-start.6 = (f32[4,64,128]{2,1,0:T(8,128)S(1)}, f32[4,64,128]{2,1,0:T(8,128)S(1)}, u32[]{:S(2)}, u32[]{:S(2)}) collective-permute-start(f32[4,64,128]{2,1,0:T(8,128)S(1)} %bitcast.29), channel_id=1, source_target_pairs={{0,8},{4,12},{8,0},{12,4},{16,24},{20,28},{24,16},{28,20},{1,9},{5... | collective-permute-start | bytes 393224 | tf_op jit(solution)/shard_map/ppermute | solution.py:502
  50.9 0.9 %collective-permute-start.7 = (f32[4,64,128]{2,1,0:T(8,128)S(1)}, f32[4,64,128]{2,1,0:T(8,128)S(1)}, u32[]{:S(2)}, u32[]{:S(2)}) collective-permute-start(f32[4,64,128]{2,1,0:T(8,128)S(1)} %bitcast.28), channel_id=1, source_target_pairs={{0,4},{4,0},{8,12},{12,8},{16,20},{20,16},{24,28},{28,24},{1,5},{5... | collective-permute-start | bytes 393224 | tf_op jit(solution)/shard_map/ppermute | solution.py:502
  51.8 5.1 %gather.2.refs_0_ = f32[8,1,256]{2,1,0:T(1,128)S(1)} custom-call(s32[6]{0:T(128)S(1)} %stack.27.place_ref, f32[16,8,256]{2,1,0:T(8,128)S(1)} %all-to-all-done.same_ref, f32[16,8,256]{2,1,0:T(8,128)S(1)} %collective-permute-done.other_ref, f32[5,144,1024]{2,1,0:T(8,128)S(1)} %get-tuple-element.45.table_y, f32[5,128,1024]{2,1,0:T(8,128)S(1)} %get-tuple-element.46.table_z, ...), custom_call_target="tpu_custom_call" | custom-call | flops 1000000 | bytes 10000 | tf_op jit(solution)/shard_map/gather/pallas_call | solution.py:603
  57.0 1.1 %collective-permute-done.6.refs_5_ = f32[4,64,128]{2,1,0:T(8,128)S(1)} collective-permute-done((f32[4,64,128]{2,1,0:T(8,128)S(1)}, f32[4,64,128]{2,1,0:T(8,128)S(1)}, u32[]{:S(2)}, u32[]{:S(2)}) %collective-permute-start.6) | collective-permute-done | bytes 131104 | tf_op jit(solution)/shard_map/ppermute | solution.py:502
  58.2 1.4 %inverse_y.1 = (f32[4,128,128]{2,1,0:T(8,128)S(1)}, f32[4,128,128]{2,1,0:T(8,128)S(1)}, f32[4,128,128]{2,1,0:T(8,128)S(1)}, f32[4,128,128]{2,1,0:T(8,128)S(1)}) custom-call(s32[6]{0:T(128)S(1)} %stack.27.place_ref, f32[4,64,128]{2,1,0:T(8,128)S(1)} %collective-permute-done.2.refs_0_, f32[4,64,128]{2,1,0:T(8,128)S(1)} %collective-permute-done.3.refs_1_, ...), custom_call_target="tpu_custom_call" | custom-call | flops 1000000 | bytes 10000 | tf_op jit(solution)/shard_map/inverse_y/pallas_call | solution.py:624
  60.3 1.6 %collective-permute-start.9 = (f32[4,128,128]{2,1,0:T(8,128)S(1)}, f32[4,128,128]{2,1,0:T(8,128)S(1)}, u32[]{:S(2)}, u32[]{:S(2)}) collective-permute-start(f32[4,128,128]{2,1,0:T(8,128)S(1)} %get-tuple-element.70), channel_id=1, source_target_pairs={{0,2},{1,3},{2,0},{3,1},{4,6},{5,7},{6,4},{7,5},{8,10},{9,11},{10,... | collective-permute-start | bytes 786440 | tf_op jit(solution)/shard_map/ppermute | solution.py:502
  61.8 5.7 %gather.3 = f32[16,1,256]{2,1,0:T(1,128)} custom-call(s32[6]{0:T(128)S(1)} %stack.27.place_ref, f32[16,8,256]{2,1,0:T(8,128)S(1)} %all-to-all-done.same_ref, f32[16,8,256]{2,1,0:T(8,128)S(1)} %collective-permute-done.other_ref, f32[5,144,1024]{2,1,0:T(8,128)S(1)} %get-tuple-element.45.table_y, f32[5,128,1024]{2,1,0:T(8,128)S(1)} %get-tuple-element.46.table_z, ...), custom_call_target="tpu_custom_call" | custom-call | flops 1000000 | bytes 10000 | tf_op jit(solution)/shard_map/gather/pallas_call | solution.py:603
  67.5 3.5 %all-to-all-start.1 = ((f32[16,1,256]{2,1,0:T(1,128)}), f32[16,1,256]{2,1,0:T(1,128)S(1)}, u32[]{:S(2)}, u32[]{:S(2)}) async-start(f32[16,1,256]{2,1,0:T(1,128)} %gather.3), calls=%async_computation.1 | async-start | bytes 32768 | tf_op jit(solution)/shard_map/all_to_all | solution.py:645
  71.1 1.1 %inverse_z.2.refs_4_ = f32[4,128,512]{2,1,0:T(8,128)S(1)} custom-call(s32[6]{0:T(128)S(1)} %stack.27.place_ref, f32[4,128,128]{2,1,0:T(8,128)S(1)} %get-tuple-element.75.refs_0_, f32[4,128,128]{2,1,0:T(8,128)S(1)} %collective-permute-done.10.refs_1_, bf16[512,512]{1,0:T(8,128)(2,1)S(1)} %copy-done.1, bf16[512,512]{1,0:T(8,128)(2,1)S(1)} %copy-done), custom_call_target="tpu_custom_call" | custom-call | flops 1000000 | bytes 10000 | tf_op jit(solution)/shard_map/inverse_z/pallas_call | solution.py:660
  72.2 1.8 %collective-permute-done.9.refs_1_ = f32[4,128,128]{2,1,0:T(8,128)S(1)} collective-permute-done((f32[4,128,128]{2,1,0:T(8,128)S(1)}, f32[4,128,128]{2,1,0:T(8,128)S(1)}, u32[]{:S(2)}, u32[]{:S(2)}) %collective-permute-start.9) | collective-permute-done | bytes 262176 | tf_op jit(solution)/shard_map/ppermute | solution.py:502
  74.0 2.1 %inverse_z.3 = f32[4,128,512]{2,1,0:T(8,128)} custom-call(s32[6]{0:T(128)S(1)} %stack.27.place_ref, f32[4,128,128]{2,1,0:T(8,128)S(1)} %collective-permute-done.8.refs_0_, f32[4,128,128]{2,1,0:T(8,128)S(1)} %collective-permute-done.9.refs_1_, bf16[512,512]{1,0:T(8,128)(2,1)S(1)} %copy-done.1, bf16[512,512]{1,0:T(8,128)(2,1)S(1)} %copy-done, ...), custom_call_target="tpu_custom_call" | custom-call | flops 1000000 | bytes 10000 | tf_op jit(solution)/shard_map/inverse_z/pallas_call | solution.py:660
  (32 shorter events, 4.1 us)
Async XLA Ops:
  2.7 16.1 %all-to-all-start = ((f32[16,8,256]{2,1,0:T(8,128)}), f32[16,8,256]{2,1,0:T(8,128)S(1)}, u32[]{:S(2)}, u32[]{:S(2)}) async-start(f32[16,8,256]{2,1,0:T(8,128)} %pack.1), calls=%async_computation | async-start | bytes 262144 | tf_op jit(solution)/shard_map/all_to_all | solution.py:541
  18.8 28.0 %collective-permute-start.1 = (f32[32,32,128]{2,1,0:T(8,128)}, f32[32,32,128]{2,1,0:T(8,128)S(1)}, u32[]{:S(2)}, u32[]{:S(2)}) collective-permute-start(f32[32,32,128]{2,1,0:T(8,128)} %get-tuple-element.51), channel_id=1, source_target_pairs={{0,28},{4,24},{8,20},{12,16},{16,12},{20,8},{24,4},{28,0},{1,29},{... | collective-permute-start | bytes 1572872 | tf_op jit(solution)/shard_map/ppermute | solution.py:553
  20.2 1.3 %collective-permute-start = (f32[16,8,256]{2,1,0:T(8,128)S(1)}, f32[16,8,256]{2,1,0:T(8,128)S(1)}, u32[]{:S(2)}, u32[]{:S(2)}) collective-permute-start(f32[16,8,256]{2,1,0:T(8,128)S(1)} %all-to-all-done.same_ref), channel_id=1, source_target_pairs={{0,1},{1,0},{2,3},{3,2},{4,5},{5,4},{6,7},{7,6},{8,9},{9,8},{10,11... | collective-permute-start | bytes 393224 | tf_op jit(solution)/shard_map/ppermute | solution.py:502
  43.2 7.7 %collective-permute-start.2 = (f32[4,64,128]{2,1,0:T(8,128)S(1)}, f32[4,64,128]{2,1,0:T(8,128)S(1)}, u32[]{:S(2)}, u32[]{:S(2)}) collective-permute-start(f32[4,64,128]{2,1,0:T(8,128)S(1)} %bitcast.27), channel_id=1, source_target_pairs={{0,12},{4,8},{8,4},{12,0},{16,28},{20,24},{24,20},{28,16},{1,13},{... | collective-permute-start | bytes 393224 | tf_op jit(solution)/shard_map/ppermute | solution.py:502
  44.2 12.7 %collective-permute-start.3 = (f32[4,64,128]{2,1,0:T(8,128)S(1)}, f32[4,64,128]{2,1,0:T(8,128)S(1)}, u32[]{:S(2)}, u32[]{:S(2)}) collective-permute-start(f32[4,64,128]{2,1,0:T(8,128)S(1)} %bitcast.26), channel_id=1, source_target_pairs={{0,8},{4,12},{8,0},{12,4},{16,24},{20,28},{24,16},{28,20},{1,9},{5... | collective-permute-start | bytes 393224 | tf_op jit(solution)/shard_map/ppermute | solution.py:502
  46.0 10.9 %collective-permute-start.4 = (f32[4,64,128]{2,1,0:T(8,128)S(1)}, f32[4,64,128]{2,1,0:T(8,128)S(1)}, u32[]{:S(2)}, u32[]{:S(2)}) collective-permute-start(f32[4,64,128]{2,1,0:T(8,128)S(1)} %bitcast.25), channel_id=1, source_target_pairs={{0,4},{4,0},{8,12},{12,8},{16,20},{20,16},{24,28},{28,24},{1,5},{5... | collective-permute-start | bytes 393224 | tf_op jit(solution)/shard_map/ppermute | solution.py:502
  48.1 8.8 %collective-permute-start.5 = (f32[4,64,128]{2,1,0:T(8,128)S(1)}, f32[4,64,128]{2,1,0:T(8,128)S(1)}, u32[]{:S(2)}, u32[]{:S(2)}) collective-permute-start(f32[4,64,128]{2,1,0:T(8,128)S(1)} %bitcast.30), channel_id=1, source_target_pairs={{0,12},{4,8},{8,4},{12,0},{16,28},{20,24},{24,20},{28,16},{1,13},{... | collective-permute-start | bytes 393224 | tf_op jit(solution)/shard_map/ppermute | solution.py:502
  49.1 8.9 %collective-permute-start.6 = (f32[4,64,128]{2,1,0:T(8,128)S(1)}, f32[4,64,128]{2,1,0:T(8,128)S(1)}, u32[]{:S(2)}, u32[]{:S(2)}) collective-permute-start(f32[4,64,128]{2,1,0:T(8,128)S(1)} %bitcast.29), channel_id=1, source_target_pairs={{0,8},{4,12},{8,0},{12,4},{16,24},{20,28},{24,16},{28,20},{1,9},{5... | collective-permute-start | bytes 393224 | tf_op jit(solution)/shard_map/ppermute | solution.py:502
  50.9 7.2 %collective-permute-start.7 = (f32[4,64,128]{2,1,0:T(8,128)S(1)}, f32[4,64,128]{2,1,0:T(8,128)S(1)}, u32[]{:S(2)}, u32[]{:S(2)}) collective-permute-start(f32[4,64,128]{2,1,0:T(8,128)S(1)} %bitcast.28), channel_id=1, source_target_pairs={{0,4},{4,0},{8,12},{12,8},{16,20},{20,16},{24,28},{28,24},{1,5},{5... | collective-permute-start | bytes 393224 | tf_op jit(solution)/shard_map/ppermute | solution.py:502
  51.8 6.4 %copy-start.2 = (bf16[2,256,256]{2,1,0:T(8,128)(2,1)S(1)}, bf16[2,256,256]{2,1,0:T(8,128)(2,1)}, u32[]{:S(2)}) copy-start(bf16[2,256,256]{2,1,0:T(8,128)(2,1)} %constant.52.clone.refs_9_) | copy-start | bytes 786436
  51.8 6.4 %copy-start.3 = (bf16[2,256,256]{2,1,0:T(8,128)(2,1)S(1)}, bf16[2,256,256]{2,1,0:T(8,128)(2,1)}, u32[]{:S(2)}) copy-start(bf16[2,256,256]{2,1,0:T(8,128)(2,1)} %constant.51.clone.refs_8_) | copy-start | bytes 786436
  59.6 2.2 %collective-permute-start.10 = (f32[4,128,128]{2,1,0:T(8,128)S(1)}, f32[4,128,128]{2,1,0:T(8,128)S(1)}, u32[]{:S(2)}, u32[]{:S(2)}) collective-permute-start(f32[4,128,128]{2,1,0:T(8,128)S(1)} %get-tuple-element.71), channel_id=1, source_target_pairs={{0,1},{1,0},{2,3},{3,2},{4,5},{5,4},{6,7},{7,6},{8,9},{9,8},{10,11... | collective-permute-start | bytes 786440 | tf_op jit(solution)/shard_map/ppermute | solution.py:502
  59.7 12.5 %collective-permute-start.8 = (f32[4,128,128]{2,1,0:T(8,128)S(1)}, f32[4,128,128]{2,1,0:T(8,128)S(1)}, u32[]{:S(2)}, u32[]{:S(2)}) collective-permute-start(f32[4,128,128]{2,1,0:T(8,128)S(1)} %get-tuple-element.69), channel_id=1, source_target_pairs={{0,3},{1,2},{2,1},{3,0},{4,7},{5,6},{6,5},{7,4},{8,11},{9,10},{10,... | collective-permute-start | bytes 786440 | tf_op jit(solution)/shard_map/ppermute | solution.py:502
  60.3 10.8 %copy-start = (bf16[512,512]{1,0:T(8,128)(2,1)S(1)}, bf16[512,512]{1,0:T(8,128)(2,1)}, u32[]{:S(2)}) copy-start(bf16[512,512]{1,0:T(8,128)(2,1)} %constant.54.clone.refs_3_) | copy-start | bytes 1572868
  60.3 10.8 %copy-start.1 = (bf16[512,512]{1,0:T(8,128)(2,1)S(1)}, bf16[512,512]{1,0:T(8,128)(2,1)}, u32[]{:S(2)}) copy-start(bf16[512,512]{1,0:T(8,128)(2,1)} %constant.53.clone.refs_2_) | copy-start | bytes 1572868
  60.3 13.7 %collective-permute-start.9 = (f32[4,128,128]{2,1,0:T(8,128)S(1)}, f32[4,128,128]{2,1,0:T(8,128)S(1)}, u32[]{:S(2)}, u32[]{:S(2)}) collective-permute-start(f32[4,128,128]{2,1,0:T(8,128)S(1)} %get-tuple-element.70), channel_id=1, source_target_pairs={{0,2},{1,3},{2,0},{3,1},{4,6},{5,7},{6,4},{7,5},{8,10},{9,11},{10,... | collective-permute-start | bytes 786440 | tf_op jit(solution)/shard_map/ppermute | solution.py:502
  67.5 9.0 %all-to-all-start.1 = ((f32[16,1,256]{2,1,0:T(1,128)}), f32[16,1,256]{2,1,0:T(1,128)S(1)}, u32[]{:S(2)}, u32[]{:S(2)}) async-start(f32[16,1,256]{2,1,0:T(1,128)} %gather.3), calls=%async_computation.1 | async-start | bytes 32768 | tf_op jit(solution)/shard_map/all_to_all | solution.py:645
  71.0 5.5 %copy-start.4 = (f32[256]{0:T(256)S(1)}, f32[256]{0:T(256)}, u32[]{:S(2)}) copy-start(f32[256]{0:T(256)} %param.13) | copy-start | bytes 3076

commit v11 on v10

--- a/solution.py
+++ b/solution.py
@@ -220,7 +220,7 @@
     for slot in range(doms):
         atoms_ref[slot] = atoms_of(same_ref, other_ref, step, slot, doms)
 
-    def add_tile(tile, halves):
+    def build_tile(tile, halves):
         atoms = jnp.concatenate([atoms_ref[slot, :, pl.ds(part * half_slot, half_slot)] for slot, part, _ in halves], 1)
         counted = jnp.concatenate([jnp.full((1, half_slot), weight) for _, _, weight in halves], 1)
         weights = spline(atoms)
@@ -235,21 +235,25 @@
             table_z[kept, :, pl.ds(start, half_slot)] = waves_z[:, lanes]
             table_y[kept, :, pl.ds(start, half_slot)] = waves_y[:, lanes]
         high, low = split(waves_z)
-        right_ref[tile, pl.ds(0, LANES), :] = high
-        right_ref[tile, pl.ds(LANES, LANES), :] = low
+        lanes = pl.ds(2 * half_slot * tile, 2 * half_slot)
+        right_ref[pl.ds(0, LANES), lanes] = high
+        right_ref[pl.ds(LANES, LANES), lanes] = low
         for plane in range(SPAN):
+            first = 4 * rows * plane
             high, low = split(waves_y * along_x[plane : plane + 1])
-            left_ref[tile, 0, pl.ds(2 * rows * plane, 2 * rows), :] = high
-            left_ref[tile, 1, pl.ds(2 * rows * plane, 2 * rows), :] = low
-        across = (((1,), (1,)), ((), ()))
-        high = lax.dot_general(left_ref[tile, 0], right_ref[tile], across, preferred_element_type=F32)
-        low = lax.dot_general(
-            left_ref[tile, 1], right_ref[tile, pl.ds(0, LANES), :], across, preferred_element_type=F32
+            left_ref[pl.ds(first, 2 * rows), lanes] = high
+            left_ref[pl.ds(first + 2 * rows, 2 * rows), lanes] = low
+
+    def add_tiles(count):
+        lanes = pl.ds(0, 2 * half_slot * count)
+        product = lax.dot_general(
+            left_ref[:, lanes], right_ref[:, lanes], (((1,), (1,)), ((), ())), preferred_element_type=F32
         )
         for plane in range(SPAN):
-            span = slice(2 * rows * plane, 2 * rows * (plane + 1))
+            first = 4 * rows * plane
+            high, low = product[first : first + 2 * rows], product[first + 2 * rows : first + 4 * rows]
             at = lax.rem(step * XD + plane, cells_x)
-            grid_ref[at] += (high[span, :LANES] + high[span, LANES:]) + low[span]
+            grid_ref[at] += (high[:, :LANES] + high[:, LANES:]) + (low[:, :LANES] + low[:, LANES:])
 
     slabs, pairs = cells_x // XD, doms // 2
     reach = [live_ref[(slot // pairs * slabs + step) * pairs + slot % pairs] for slot in range(doms)]
@@ -259,14 +263,15 @@
         @pl.when((reach[-1] + 1) // 2 == extra)
         def _(extra=extra):
             for tile in range(doms // 2):
-                add_tile(tile, [(2 * tile, 0, 1.0), (2 * tile + 1, 0, 1.0)])
+                build_tile(tile, [(2 * tile, 0, 1.0), (2 * tile + 1, 0, 1.0)])
             for tile in range(extra):
                 chosen = []
                 for place in (2 * tile, 2 * tile + 1):
                     slot = sum((total <= place).astype(jnp.int32) for total in reach)
                     weight = jnp.where(slot < doms, 1.0, 0.0).astype(F32)
                     chosen.append((jnp.minimum(slot, doms - 1), 1, weight))
-                add_tile(doms // 2 + tile, chosen)
+                build_tile(doms // 2 + tile, chosen)
+            add_tiles(doms // 2 + extra)
 
     @pl.when(step == pl.num_programs(0) - 1)
     def _():
@@ -569,8 +574,8 @@
             jax.ShapeDtypeStruct((slab_half + 1, LANES, atoms_slab), F32),
         ],
         scratch_shapes=[
-            pltpu.VMEM((doms, 2, SPAN * 2 * rows, atoms_local), BF16),
-            pltpu.VMEM((doms, 2 * LANES, atoms_local), BF16),
+            pltpu.VMEM((SPAN * 4 * rows, atoms_slab), BF16),
+            pltpu.VMEM((2 * LANES, atoms_slab), BF16),
             pltpu.VMEM((cells_x, 2 * rows, LANES), F32),
             pltpu.VMEM((doms, 8, atoms_local), F32),
             pltpu.VMEM((doms, TERMS, atoms_local), BF16),

time: 77.5 us -> 73.9 us (0.954)
  Pallas kernels: 40.3 us -> 37 us
    pallas_call x1, Pallas kernels: 20 us -> 16.7 us  [per_device(): pl.pallas_call(forward_kernel, grid=(slabs,), in_specs=[SMEM] * 2 + [vmem...]
  transfers between devices with their start and end apart: 13 -> 13, of which waited for: 6 -> 6; matrix products, arithmetic and copies ran while one was open for 4% -> 4% of each run, Pallas kernels for 49% -> 46%
where the time goes in v11:
time: 73.9 us; the launch traced here: 73.8 us
  Pallas kernels  37 us (50%)
  starting transfers between devices  22.7 us (31%)
  waiting for transfers between devices  8.99 us (12%)
  local copies, waits for them, and re-layouts  1.93 us (3%)
  other arithmetic  1.8 us (2%)
  between operations  1.46 us (2%)
    pallas_call x1, Pallas kernels, per_device(): pl.pallas_call(forward_kernel, grid=(slabs,), in_specs=[SMEM] * 2 + [vmem...  16.7 us
    pallas_call x2, Pallas kernels, gather(): pl.pallas_call(functools.partial(gather_kernel, part * steps), grid=(step...  10.8 us
    ppermute x10, starting transfers between devices, swapped(): lax.ppermute(value, axis, [(i, i ^ distance) for i in range(lax.axis_size...  9.44 us
    all_to_all x1, starting transfers between devices, per_device(): lax.all_to_all(atoms, ('slab', 'dom'), 0, 0, axis_index_groups=[everyone[...  8.31 us
    all_to_all x1, waiting for transfers between devices, per_device(): lax.all_to_all(atoms, ('slab', 'dom'), 0, 0, axis_index_groups=[everyone[...  4.38 us
    ppermute x10, waiting for transfers between devices, swapped(): lax.ppermute(value, axis, [(i, i ^ distance) for i in range(lax.axis_size...  4.15 us
    all_to_all x1, starting transfers between devices, per_device(): lax.all_to_all(partial.reshape(members, atoms_local), ('slab', 'dom'), 0,...  3.49 us
    pallas_call x2, Pallas kernels, per_device(): pl.pallas_call(functools.partial(inverse_z_kernel, distances), grid=(XD /...  3.23 us
  transfers between devices with their start and end apart: 13, of which 6 were waited for; matrix products, arithmetic and copies ran while one was open for 4% of the time, Pallas kernels for 46%

profile of v11, /device:TPU:0, one launch (start us, length us, event | category | flops | bytes accessed | tf_op | source)
XLA Modules:
  0.0 73.8 jit_solution(1233340721343306182)
XLA Ops:
  1.3 1.4 %pack.1 = f32[16,8,256]{2,1,0:T(8,128)} custom-call(s32[1]{0:T(128)} %copy.12.counts_ref, s32[3,256]{1,0:T(4,128)} %cells_ref.1, f32[3,256]{1,0:T(4,128)} %offsets_ref.1, f32[1,256]{1,0:T(1,128)} %bitcast.31), custom_call_target="tpu_custom_call" | custom-call | tf_op jit(solution)/shard_map/pack/pallas_call | solution.py:530
  2.7 8.3 %all-to-all-start = ((f32[16,8,256]{2,1,0:T(8,128)}), f32[16,8,256]{2,1,0:T(8,128)S(1)}, u32[]{:S(2)}, u32[]{:S(2)}) async-start(f32[16,8,256]{2,1,0:T(8,128)} %pack.1), calls=%async_computation | async-start | bytes 262144 | tf_op jit(solution)/shard_map/all_to_all | solution.py:546
  11.0 1.3 %fusion = (f32[32,32,64]{2,1,0:T(8,128)S(1)}, f32[32,32,64]{2,1,0:T(8,128)S(1)}) fusion(f32[32,64,64]{2,1,0:T(8,128)} %param.15), kind=kLoop, calls=%fused_computation.6 | loop fusion | bytes 1048576 | tf_op jit(solution)/shard_map/slice | solution.py:551
  13.3 1.1 %maximum_multiply_fusion = (f32[32,32,128]{2,1,0:T(8,128)S(1)}, f32[32,32,128]{2,1,0:T(8,128)}) fusion(f32[32,32,64]{2,1,0:T(8,128)S(1)} %get-tuple-element.79, f32[32,32,64]{2,1,0:T(8,128)S(1)} %get-tuple-element.78, f32[32,32,64]{2,1,0:T(8,128)S(1)} %slice.23, f32[32,32,64]{2,1,0:T(8,128)S(1)} %slice.22), kind=kLoop, calls=%fused_computation | loop fusion | flops 524288 | bytes 2097152 | tf_op jit(solution)/shard_map/mul | solution.py:551
  14.4 4.4 %all-to-all-done.same_ref = f32[16,8,256]{2,1,0:T(8,128)S(1)} async-done(((f32[16,8,256]{2,1,0:T(8,128)}), f32[16,8,256]{2,1,0:T(8,128)S(1)}, u32[]{:S(2)}, u32[]{:S(2)}) %all-to-all-start) | async-done | bytes 131104 | tf_op jit(solution)/shard_map/all_to_all | solution.py:546
  18.8 1.4 %collective-permute-start.1 = (f32[32,32,128]{2,1,0:T(8,128)}, f32[32,32,128]{2,1,0:T(8,128)S(1)}, u32[]{:S(2)}, u32[]{:S(2)}) collective-permute-start(f32[32,32,128]{2,1,0:T(8,128)} %get-tuple-element.51), channel_id=1, source_target_pairs={{0,28},{4,24},{8,20},{12,16},{16,12},{20,8},{24,4},{28,0},{1,29},{... | collective-permute-start | bytes 1572872 | tf_op jit(solution)/shard_map/ppermute | solution.py:558
  20.4 1.1 %collective-permute-done.other_ref = f32[16,8,256]{2,1,0:T(8,128)S(1)} collective-permute-done((f32[16,8,256]{2,1,0:T(8,128)S(1)}, f32[16,8,256]{2,1,0:T(8,128)S(1)}, u32[]{:S(2)}, u32[]{:S(2)}) %collective-permute-start) | collective-permute-done | bytes 131104 | tf_op jit(solution)/shard_map/ppermute | solution.py:507
  21.9 16.7 %forward.1 = (f32[2,32,32,128]{3,2,1,0:T(8,128)S(1)}, f32[2,32,32,128]{3,2,1,0:T(8,128)S(1)}, f32[5,144,1024]{2,1,0:T(8,128)S(1)}, f32[5,128,1024]{2,1,0:T(8,128)S(1)}) custom-call(s32[6]{0:T(128)S(1)} %stack.27.place_ref, s32[32]{0:T(128)S(1)} %compare_convert_fusion.live_ref, f32[16,8,256]{2,1,0:T(8,128)S(1)} %all-to-all-done.same_ref, ...), custom_call_target="tpu_custom_call" | custom-call | flops 1000000 | bytes 10000 | tf_op jit(solution)/shard_map/forward/pallas_call | solution.py:565
  38.6 1.3 %inverse_x.2 = (f32[4,2,32,128]{3,2,1,0:T(8,128)S(1)}, f32[4,2,32,128]{3,2,1,0:T(8,128)S(1)}, f32[4,2,32,128]{3,2,1,0:T(8,128)S(1)}, f32[4,2,32,128]{3,2,1,0:T(8,128)S(1)}, f32[19,2,32,128]{3,2,1,0:T(8,128)S(1)}) custom-call(s32[6]{0:T(128)S(1)} %stack.27.place_ref, f32[2,32,32,128]{3,2,1,0:T(8,128)S(1)} %get-tuple-element.47.spectrum_ref, ...), custom_call_target="tpu_custom_call" | custom-call | flops 1000000 | bytes 10000 | tf_op jit(solution)/shard_map/inverse_x/pallas_call | solution.py:592
  39.9 1.0 %collective-permute-start.2 = (f32[4,64,128]{2,1,0:T(8,128)S(1)}, f32[4,64,128]{2,1,0:T(8,128)S(1)}, u32[]{:S(2)}, u32[]{:S(2)}) collective-permute-start(f32[4,64,128]{2,1,0:T(8,128)S(1)} %bitcast.27), channel_id=1, source_target_pairs={{0,12},{4,8},{8,4},{12,0},{16,28},{20,24},{24,20},{28,16},{1,13},{... | collective-permute-start | bytes 393224 | tf_op jit(solution)/shard_map/ppermute | solution.py:507
  40.9 1.8 %collective-permute-start.3 = (f32[4,64,128]{2,1,0:T(8,128)S(1)}, f32[4,64,128]{2,1,0:T(8,128)S(1)}, u32[]{:S(2)}, u32[]{:S(2)}) collective-permute-start(f32[4,64,128]{2,1,0:T(8,128)S(1)} %bitcast.26), channel_id=1, source_target_pairs={{0,8},{4,12},{8,0},{12,4},{16,24},{20,28},{24,16},{28,20},{1,9},{5... | collective-permute-start | bytes 393224 | tf_op jit(solution)/shard_map/ppermute | solution.py:507
  43.5 1.3 %inverse_x.3 = (f32[4,2,32,128]{3,2,1,0:T(8,128)S(1)}, f32[4,2,32,128]{3,2,1,0:T(8,128)S(1)}, f32[4,2,32,128]{3,2,1,0:T(8,128)S(1)}, f32[4,2,32,128]{3,2,1,0:T(8,128)S(1)}, f32[19,2,32,128]{3,2,1,0:T(8,128)S(1)}) custom-call(s32[6]{0:T(128)S(1)} %stack.27.place_ref, f32[2,32,32,128]{3,2,1,0:T(8,128)S(1)} %get-tuple-element.50.spectrum_ref, ...), custom_call_target="tpu_custom_call" | custom-call | flops 1000000 | bytes 10000 | tf_op jit(solution)/shard_map/inverse_x/pallas_call | solution.py:592
  44.8 1.1 %collective-permute-start.5 = (f32[4,64,128]{2,1,0:T(8,128)S(1)}, f32[4,64,128]{2,1,0:T(8,128)S(1)}, u32[]{:S(2)}, u32[]{:S(2)}) collective-permute-start(f32[4,64,128]{2,1,0:T(8,128)S(1)} %bitcast.30), channel_id=1, source_target_pairs={{0,12},{4,8},{8,4},{12,0},{16,28},{20,24},{24,20},{28,16},{1,13},{... | collective-permute-start | bytes 393224 | tf_op jit(solution)/shard_map/ppermute | solution.py:507
  45.9 1.7 %collective-permute-start.6 = (f32[4,64,128]{2,1,0:T(8,128)S(1)}, f32[4,64,128]{2,1,0:T(8,128)S(1)}, u32[]{:S(2)}, u32[]{:S(2)}) collective-permute-start(f32[4,64,128]{2,1,0:T(8,128)S(1)} %bitcast.29), channel_id=1, source_target_pairs={{0,8},{4,12},{8,0},{12,4},{16,24},{20,28},{24,16},{28,20},{1,9},{5... | collective-permute-start | bytes 393224 | tf_op jit(solution)/shard_map/ppermute | solution.py:507
  47.6 0.9 %collective-permute-start.7 = (f32[4,64,128]{2,1,0:T(8,128)S(1)}, f32[4,64,128]{2,1,0:T(8,128)S(1)}, u32[]{:S(2)}, u32[]{:S(2)}) collective-permute-start(f32[4,64,128]{2,1,0:T(8,128)S(1)} %bitcast.28), channel_id=1, source_target_pairs={{0,4},{4,0},{8,12},{12,8},{16,20},{20,16},{24,28},{28,24},{1,5},{5... | collective-permute-start | bytes 393224 | tf_op jit(solution)/shard_map/ppermute | solution.py:507
  48.5 5.1 %gather.2.refs_0_ = f32[8,1,256]{2,1,0:T(1,128)S(1)} custom-call(s32[6]{0:T(128)S(1)} %stack.27.place_ref, f32[16,8,256]{2,1,0:T(8,128)S(1)} %all-to-all-done.same_ref, f32[16,8,256]{2,1,0:T(8,128)S(1)} %collective-permute-done.other_ref, f32[5,144,1024]{2,1,0:T(8,128)S(1)} %get-tuple-element.45.table_y, f32[5,128,1024]{2,1,0:T(8,128)S(1)} %get-tuple-element.46.table_z, ...), custom_call_target="tpu_custom_call" | custom-call | flops 1000000 | bytes 10000 | tf_op jit(solution)/shard_map/gather/pallas_call | solution.py:608
  53.6 1.1 %collective-permute-done.6.refs_5_ = f32[4,64,128]{2,1,0:T(8,128)S(1)} collective-permute-done((f32[4,64,128]{2,1,0:T(8,128)S(1)}, f32[4,64,128]{2,1,0:T(8,128)S(1)}, u32[]{:S(2)}, u32[]{:S(2)}) %collective-permute-start.6) | collective-permute-done | bytes 131104 | tf_op jit(solution)/shard_map/ppermute | solution.py:507
  54.9 1.4 %inverse_y.1 = (f32[4,128,128]{2,1,0:T(8,128)S(1)}, f32[4,128,128]{2,1,0:T(8,128)S(1)}, f32[4,128,128]{2,1,0:T(8,128)S(1)}, f32[4,128,128]{2,1,0:T(8,128)S(1)}) custom-call(s32[6]{0:T(128)S(1)} %stack.27.place_ref, f32[4,64,128]{2,1,0:T(8,128)S(1)} %collective-permute-done.2.refs_0_, f32[4,64,128]{2,1,0:T(8,128)S(1)} %collective-permute-done.3.refs_1_, ...), custom_call_target="tpu_custom_call" | custom-call | flops 1000000 | bytes 10000 | tf_op jit(solution)/shard_map/inverse_y/pallas_call | solution.py:629
  56.9 1.5 %collective-permute-start.9 = (f32[4,128,128]{2,1,0:T(8,128)S(1)}, f32[4,128,128]{2,1,0:T(8,128)S(1)}, u32[]{:S(2)}, u32[]{:S(2)}) collective-permute-start(f32[4,128,128]{2,1,0:T(8,128)S(1)} %get-tuple-element.70), channel_id=1, source_target_pairs={{0,2},{1,3},{2,0},{3,1},{4,6},{5,7},{6,4},{7,5},{8,10},{9,11},{10,... | collective-permute-start | bytes 786440 | tf_op jit(solution)/shard_map/ppermute | solution.py:507
  58.5 5.7 %gather.3 = f32[16,1,256]{2,1,0:T(1,128)} custom-call(s32[6]{0:T(128)S(1)} %stack.27.place_ref, f32[16,8,256]{2,1,0:T(8,128)S(1)} %all-to-all-done.same_ref, f32[16,8,256]{2,1,0:T(8,128)S(1)} %collective-permute-done.other_ref, f32[5,144,1024]{2,1,0:T(8,128)S(1)} %get-tuple-element.45.table_y, f32[5,128,1024]{2,1,0:T(8,128)S(1)} %get-tuple-element.46.table_z, ...), custom_call_target="tpu_custom_call" | custom-call | flops 1000000 | bytes 10000 | tf_op jit(solution)/shard_map/gather/pallas_call | solution.py:608
  64.2 3.5 %all-to-all-start.1 = ((f32[16,1,256]{2,1,0:T(1,128)}), f32[16,1,256]{2,1,0:T(1,128)S(1)}, u32[]{:S(2)}, u32[]{:S(2)}) async-start(f32[16,1,256]{2,1,0:T(1,128)} %gather.3), calls=%async_computation.1 | async-start | bytes 32768 | tf_op jit(solution)/shard_map/all_to_all | solution.py:650
  67.7 1.1 %inverse_z.2.refs_4_ = f32[4,128,512]{2,1,0:T(8,128)S(1)} custom-call(s32[6]{0:T(128)S(1)} %stack.27.place_ref, f32[4,128,128]{2,1,0:T(8,128)S(1)} %get-tuple-element.75.refs_0_, f32[4,128,128]{2,1,0:T(8,128)S(1)} %collective-permute-done.10.refs_1_, bf16[512,512]{1,0:T(8,128)(2,1)S(1)} %copy-done.1, bf16[512,512]{1,0:T(8,128)(2,1)S(1)} %copy-done), custom_call_target="tpu_custom_call" | custom-call | flops 1000000 | bytes 10000 | tf_op jit(solution)/shard_map/inverse_z/pallas_call | solution.py:665
  68.9 1.8 %collective-permute-done.9.refs_1_ = f32[4,128,128]{2,1,0:T(8,128)S(1)} collective-permute-done((f32[4,128,128]{2,1,0:T(8,128)S(1)}, f32[4,128,128]{2,1,0:T(8,128)S(1)}, u32[]{:S(2)}, u32[]{:S(2)}) %collective-permute-start.9) | collective-permute-done | bytes 262176 | tf_op jit(solution)/shard_map/ppermute | solution.py:507
  70.6 2.1 %inverse_z.3 = f32[4,128,512]{2,1,0:T(8,128)} custom-call(s32[6]{0:T(128)S(1)} %stack.27.place_ref, f32[4,128,128]{2,1,0:T(8,128)S(1)} %collective-permute-done.8.refs_0_, f32[4,128,128]{2,1,0:T(8,128)S(1)} %collective-permute-done.9.refs_1_, bf16[512,512]{1,0:T(8,128)(2,1)S(1)} %copy-done.1, bf16[512,512]{1,0:T(8,128)(2,1)S(1)} %copy-done, ...), custom_call_target="tpu_custom_call" | custom-call | flops 1000000 | bytes 10000 | tf_op jit(solution)/shard_map/inverse_z/pallas_call | solution.py:665
  (32 shorter events, 4.1 us)
Async XLA Ops:
  2.7 16.1 %all-to-all-start = ((f32[16,8,256]{2,1,0:T(8,128)}), f32[16,8,256]{2,1,0:T(8,128)S(1)}, u32[]{:S(2)}, u32[]{:S(2)}) async-start(f32[16,8,256]{2,1,0:T(8,128)} %pack.1), calls=%async_computation | async-start | bytes 262144 | tf_op jit(solution)/shard_map/all_to_all | solution.py:546
  18.8 24.7 %collective-permute-start.1 = (f32[32,32,128]{2,1,0:T(8,128)}, f32[32,32,128]{2,1,0:T(8,128)S(1)}, u32[]{:S(2)}, u32[]{:S(2)}) collective-permute-start(f32[32,32,128]{2,1,0:T(8,128)} %get-tuple-element.51), channel_id=1, source_target_pairs={{0,28},{4,24},{8,20},{12,16},{16,12},{20,8},{24,4},{28,0},{1,29},{... | collective-permute-start | bytes 1572872 | tf_op jit(solution)/shard_map/ppermute | solution.py:558
  20.2 1.3 %collective-permute-start = (f32[16,8,256]{2,1,0:T(8,128)S(1)}, f32[16,8,256]{2,1,0:T(8,128)S(1)}, u32[]{:S(2)}, u32[]{:S(2)}) collective-permute-start(f32[16,8,256]{2,1,0:T(8,128)S(1)} %all-to-all-done.same_ref), channel_id=1, source_target_pairs={{0,1},{1,0},{2,3},{3,2},{4,5},{5,4},{6,7},{7,6},{8,9},{9,8},{10,11... | collective-permute-start | bytes 393224 | tf_op jit(solution)/shard_map/ppermute | solution.py:507
  39.9 7.7 %collective-permute-start.2 = (f32[4,64,128]{2,1,0:T(8,128)S(1)}, f32[4,64,128]{2,1,0:T(8,128)S(1)}, u32[]{:S(2)}, u32[]{:S(2)}) collective-permute-start(f32[4,64,128]{2,1,0:T(8,128)S(1)} %bitcast.27), channel_id=1, source_target_pairs={{0,12},{4,8},{8,4},{12,0},{16,28},{20,24},{24,20},{28,16},{1,13},{... | collective-permute-start | bytes 393224 | tf_op jit(solution)/shard_map/ppermute | solution.py:507
  40.9 12.7 %collective-permute-start.3 = (f32[4,64,128]{2,1,0:T(8,128)S(1)}, f32[4,64,128]{2,1,0:T(8,128)S(1)}, u32[]{:S(2)}, u32[]{:S(2)}) collective-permute-start(f32[4,64,128]{2,1,0:T(8,128)S(1)} %bitcast.26), channel_id=1, source_target_pairs={{0,8},{4,12},{8,0},{12,4},{16,24},{20,28},{24,16},{28,20},{1,9},{5... | collective-permute-start | bytes 393224 | tf_op jit(solution)/shard_map/ppermute | solution.py:507
  42.7 10.9 %collective-permute-start.4 = (f32[4,64,128]{2,1,0:T(8,128)S(1)}, f32[4,64,128]{2,1,0:T(8,128)S(1)}, u32[]{:S(2)}, u32[]{:S(2)}) collective-permute-start(f32[4,64,128]{2,1,0:T(8,128)S(1)} %bitcast.25), channel_id=1, source_target_pairs={{0,4},{4,0},{8,12},{12,8},{16,20},{20,16},{24,28},{28,24},{1,5},{5... | collective-permute-start | bytes 393224 | tf_op jit(solution)/shard_map/ppermute | solution.py:507
  44.8 8.8 %collective-permute-start.5 = (f32[4,64,128]{2,1,0:T(8,128)S(1)}, f32[4,64,128]{2,1,0:T(8,128)S(1)}, u32[]{:S(2)}, u32[]{:S(2)}) collective-permute-start(f32[4,64,128]{2,1,0:T(8,128)S(1)} %bitcast.30), channel_id=1, source_target_pairs={{0,12},{4,8},{8,4},{12,0},{16,28},{20,24},{24,20},{28,16},{1,13},{... | collective-permute-start | bytes 393224 | tf_op jit(solution)/shard_map/ppermute | solution.py:507
  45.9 8.8 %collective-permute-start.6 = (f32[4,64,128]{2,1,0:T(8,128)S(1)}, f32[4,64,128]{2,1,0:T(8,128)S(1)}, u32[]{:S(2)}, u32[]{:S(2)}) collective-permute-start(f32[4,64,128]{2,1,0:T(8,128)S(1)} %bitcast.29), channel_id=1, source_target_pairs={{0,8},{4,12},{8,0},{12,4},{16,24},{20,28},{24,16},{28,20},{1,9},{5... | collective-permute-start | bytes 393224 | tf_op jit(solution)/shard_map/ppermute | solution.py:507
  47.6 7.2 %collective-permute-start.7 = (f32[4,64,128]{2,1,0:T(8,128)S(1)}, f32[4,64,128]{2,1,0:T(8,128)S(1)}, u32[]{:S(2)}, u32[]{:S(2)}) collective-permute-start(f32[4,64,128]{2,1,0:T(8,128)S(1)} %bitcast.28), channel_id=1, source_target_pairs={{0,4},{4,0},{8,12},{12,8},{16,20},{20,16},{24,28},{28,24},{1,5},{5... | collective-permute-start | bytes 393224 | tf_op jit(solution)/shard_map/ppermute | solution.py:507
  48.5 6.4 %copy-start.2 = (bf16[2,256,256]{2,1,0:T(8,128)(2,1)S(1)}, bf16[2,256,256]{2,1,0:T(8,128)(2,1)}, u32[]{:S(2)}) copy-start(bf16[2,256,256]{2,1,0:T(8,128)(2,1)} %constant.52.clone.refs_9_) | copy-start | bytes 786436
  48.5 6.4 %copy-start.3 = (bf16[2,256,256]{2,1,0:T(8,128)(2,1)S(1)}, bf16[2,256,256]{2,1,0:T(8,128)(2,1)}, u32[]{:S(2)}) copy-start(bf16[2,256,256]{2,1,0:T(8,128)(2,1)} %constant.51.clone.refs_8_) | copy-start | bytes 786436
  56.3 2.2 %collective-permute-start.10 = (f32[4,128,128]{2,1,0:T(8,128)S(1)}, f32[4,128,128]{2,1,0:T(8,128)S(1)}, u32[]{:S(2)}, u32[]{:S(2)}) collective-permute-start(f32[4,128,128]{2,1,0:T(8,128)S(1)} %get-tuple-element.71), channel_id=1, source_target_pairs={{0,1},{1,0},{2,3},{3,2},{4,5},{5,4},{6,7},{7,6},{8,9},{9,8},{10,11... | collective-permute-start | bytes 786440 | tf_op jit(solution)/shard_map/ppermute | solution.py:507
  56.3 12.5 %collective-permute-start.8 = (f32[4,128,128]{2,1,0:T(8,128)S(1)}, f32[4,128,128]{2,1,0:T(8,128)S(1)}, u32[]{:S(2)}, u32[]{:S(2)}) collective-permute-start(f32[4,128,128]{2,1,0:T(8,128)S(1)} %get-tuple-element.69), channel_id=1, source_target_pairs={{0,3},{1,2},{2,1},{3,0},{4,7},{5,6},{6,5},{7,4},{8,11},{9,10},{10,... | collective-permute-start | bytes 786440 | tf_op jit(solution)/shard_map/ppermute | solution.py:507
  56.9 10.8 %copy-start = (bf16[512,512]{1,0:T(8,128)(2,1)S(1)}, bf16[512,512]{1,0:T(8,128)(2,1)}, u32[]{:S(2)}) copy-start(bf16[512,512]{1,0:T(8,128)(2,1)} %constant.54.clone.refs_3_) | copy-start | bytes 1572868
  56.9 10.8 %copy-start.1 = (bf16[512,512]{1,0:T(8,128)(2,1)S(1)}, bf16[512,512]{1,0:T(8,128)(2,1)}, u32[]{:S(2)}) copy-start(bf16[512,512]{1,0:T(8,128)(2,1)} %constant.53.clone.refs_2_) | copy-start | bytes 1572868
  56.9 13.7 %collective-permute-start.9 = (f32[4,128,128]{2,1,0:T(8,128)S(1)}, f32[4,128,128]{2,1,0:T(8,128)S(1)}, u32[]{:S(2)}, u32[]{:S(2)}) collective-permute-start(f32[4,128,128]{2,1,0:T(8,128)S(1)} %get-tuple-element.70), channel_id=1, source_target_pairs={{0,2},{1,3},{2,0},{3,1},{4,6},{5,7},{6,4},{7,5},{8,10},{9,11},{10,... | collective-permute-start | bytes 786440 | tf_op jit(solution)/shard_map/ppermute | solution.py:507
  64.2 9.0 %all-to-all-start.1 = ((f32[16,1,256]{2,1,0:T(1,128)}), f32[16,1,256]{2,1,0:T(1,128)S(1)}, u32[]{:S(2)}, u32[]{:S(2)}) async-start(f32[16,1,256]{2,1,0:T(1,128)} %gather.3), calls=%async_computation.1 | async-start | bytes 32768 | tf_op jit(solution)/shard_map/all_to_all | solution.py:650
  67.7 5.5 %copy-start.4 = (f32[256]{0:T(256)S(1)}, f32[256]{0:T(256)}, u32[]{:S(2)}) copy-start(f32[256]{0:T(256)} %param.13) | copy-start | bytes 3076

commit v12 on v11

--- a/solution.py
+++ b/solution.py
@@ -343,18 +343,10 @@
             plus = plus_ref[x, pl.ds(parity, waves // 2, stride=2), :]
             minus = minus_ref[x, pl.ds(7 + parity, waves // 2, stride=2), :]
             parts.append(split(jnp.concatenate([plus + minus, swap(plus - minus) * halves], 0)))
-        both = jnp.concatenate([value for part in parts for value in part], 1)
-        main = jnp.dot(high_ref[parity], both, preferred_element_type=F32)
-        high = jnp.concatenate([part[0] for part in parts], 1)
-        rest = jnp.dot(low_ref[parity], high, preferred_element_type=F32)
-        sums.append(
-            [
-                main[:, 2 * x * LANES : (2 * x + 1) * LANES]
-                + main[:, (2 * x + 1) * LANES : (2 * x + 2) * LANES]
-                + rest[:, x * LANES : (x + 1) * LANES]
-                for x in range(XD)
-            ]
-        )
+        high, low = (jnp.concatenate([part[i] for part in parts], 1) for i in (0, 1))
+        left = jnp.concatenate([high_ref[parity], high_ref[parity], low_ref[parity]], 1)
+        total = jnp.dot(left, jnp.concatenate([high, low, high], 0), preferred_element_type=F32)
+        sums.append([total[:, x * LANES : (x + 1) * LANES] for x in range(XD)])
     row = lax.broadcasted_iota(jnp.int32, (waves, 1), 0)
     alternate = jnp.where(row % 2 == 0, 1.0, -1.0)
     sign = jnp.where(place_ref[3] == 1, alternate, 1.0)
@@ -379,10 +371,8 @@
         tables.append((high_ref[pl.ds(start, LANES), :], low_ref[pl.ds(start, LANES), :]))
     high, low = split(jnp.concatenate(lines, 1))
     table_high, table_low = (jnp.concatenate([pair[part] for pair in tables], 0) for part in (0, 1))
-    total = jnp.dot(high, table_high, preferred_element_type=F32)
-    total += jnp.dot(low, table_high, preferred_element_type=F32)
-    total += jnp.dot(high, table_low, preferred_element_type=F32)
-    total = total.reshape(planes, rows, depth)
+    left, right = jnp.concatenate([high, low, high], 1), jnp.concatenate([table_high, table_high, table_low], 0)
+    total = jnp.dot(left, right, preferred_element_type=F32).reshape(planes, rows, depth)
     for total_ref in total_refs:
         total += total_ref[span]
     out_ref[...] = total
@@ -446,10 +436,7 @@
         rest_high = rest.astype(BF16).astype(F32)
         rest = jnp.where(row < 4, rest_high, jnp.where(row < 6, rest - rest_high, 0.0))
         stack_ref[pl.ds(3 * LANES, 16), lanes] = rest.astype(BF16)
-    product = sum(
-        jnp.dot(fields[:, part : part + 2 * LANES], stack_ref[pl.ds(part, 2 * LANES), :], preferred_element_type=F32)
-        for part in (0, 2 * LANES)
-    )
+    product = jnp.dot(fields, stack_ref[...], preferred_element_type=F32)
     for slot in range(doms):
         atoms = atoms_of(same_ref, other_ref, place_ref[2] + first + step, slot, doms)
         along_x = plane_weights(atoms, spline(atoms))

time: 73.9 us -> 73.9 us (level)
  no operation moved by 1% of the time
where the time goes in v12:
time: 73.9 us; the launch traced here: 73.3 us
  Pallas kernels  36.3 us (49%)
  starting transfers between devices  22.7 us (31%)
  waiting for transfers between devices  9.09 us (12%)
  local copies, waits for them, and re-layouts  1.93 us (3%)
  other arithmetic  1.8 us (2%)
  between operations  1.46 us (2%)
    pallas_call x1, Pallas kernels, per_device(): pl.pallas_call(forward_kernel, grid=(slabs,), in_specs=[SMEM] * 2 + [vmem...  16.2 us
    pallas_call x2, Pallas kernels, gather(): pl.pallas_call(functools.partial(gather_kernel, part * steps), grid=(step...  10.6 us
    ppermute x10, starting transfers between devices, swapped(): lax.ppermute(value, axis, [(i, i ^ distance) for i in range(lax.axis_size...  9.46 us
    all_to_all x1, starting transfers between devices, per_device(): lax.all_to_all(atoms, ('slab', 'dom'), 0, 0, axis_index_groups=[everyone[...  8.31 us
    all_to_all x1, waiting for transfers between devices, per_device(): lax.all_to_all(atoms, ('slab', 'dom'), 0, 0, axis_index_groups=[everyone[...  4.38 us
    ppermute x10, waiting for transfers between devices, swapped(): lax.ppermute(value, axis, [(i, i ^ distance) for i in range(lax.axis_size...  4.33 us
    all_to_all x1, starting transfers between devices, per_device(): lax.all_to_all(partial.reshape(members, atoms_local), ('slab', 'dom'), 0,...  3.49 us
    pallas_call x2, Pallas kernels, per_device(): pl.pallas_call(functools.partial(inverse_z_kernel, distances), grid=(XD /...  3.23 us
  transfers between devices with their start and end apart: 13, of which 6 were waited for; matrix products, arithmetic and copies ran while one was open for 4% of the time, Pallas kernels for 46%

profile of v12, /device:TPU:0, one launch (start us, length us, event | category | flops | bytes accessed | tf_op | source)
XLA Modules:
  0.0 73.3 jit_solution(8603493503139884275)
XLA Ops:
  1.3 1.4 %pack.1 = f32[16,8,256]{2,1,0:T(8,128)} custom-call(s32[1]{0:T(128)} %copy.12.counts_ref, s32[3,256]{1,0:T(4,128)} %cells_ref.1, f32[3,256]{1,0:T(4,128)} %offsets_ref.1, f32[1,256]{1,0:T(1,128)} %bitcast.31), custom_call_target="tpu_custom_call" | custom-call | tf_op jit(solution)/shard_map/pack/pallas_call | solution.py:517
  2.7 8.3 %all-to-all-start = ((f32[16,8,256]{2,1,0:T(8,128)}), f32[16,8,256]{2,1,0:T(8,128)S(1)}, u32[]{:S(2)}, u32[]{:S(2)}) async-start(f32[16,8,256]{2,1,0:T(8,128)} %pack.1), calls=%async_computation | async-start | bytes 262144 | tf_op jit(solution)/shard_map/all_to_all | solution.py:533
  11.0 1.3 %fusion = (f32[32,32,64]{2,1,0:T(8,128)S(1)}, f32[32,32,64]{2,1,0:T(8,128)S(1)}) fusion(f32[32,64,64]{2,1,0:T(8,128)} %param.15), kind=kLoop, calls=%fused_computation.6 | loop fusion | bytes 1048576 | tf_op jit(solution)/shard_map/slice | solution.py:538
  13.3 1.1 %maximum_multiply_fusion = (f32[32,32,128]{2,1,0:T(8,128)S(1)}, f32[32,32,128]{2,1,0:T(8,128)}) fusion(f32[32,32,64]{2,1,0:T(8,128)S(1)} %get-tuple-element.79, f32[32,32,64]{2,1,0:T(8,128)S(1)} %get-tuple-element.78, f32[32,32,64]{2,1,0:T(8,128)S(1)} %slice.23, f32[32,32,64]{2,1,0:T(8,128)S(1)} %slice.22), kind=kLoop, calls=%fused_computation | loop fusion | flops 524288 | bytes 2097152 | tf_op jit(solution)/shard_map/mul | solution.py:538
  14.4 4.4 %all-to-all-done.same_ref = f32[16,8,256]{2,1,0:T(8,128)S(1)} async-done(((f32[16,8,256]{2,1,0:T(8,128)}), f32[16,8,256]{2,1,0:T(8,128)S(1)}, u32[]{:S(2)}, u32[]{:S(2)}) %all-to-all-start) | async-done | bytes 131104 | tf_op jit(solution)/shard_map/all_to_all | solution.py:533
  18.8 1.4 %collective-permute-start.1 = (f32[32,32,128]{2,1,0:T(8,128)}, f32[32,32,128]{2,1,0:T(8,128)S(1)}, u32[]{:S(2)}, u32[]{:S(2)}) collective-permute-start(f32[32,32,128]{2,1,0:T(8,128)} %get-tuple-element.51), channel_id=1, source_target_pairs={{0,28},{4,24},{8,20},{12,16},{16,12},{20,8},{24,4},{28,0},{1,29},{... | collective-permute-start | bytes 1572872 | tf_op jit(solution)/shard_map/ppermute | solution.py:545
  20.4 1.1 %collective-permute-done.other_ref = f32[16,8,256]{2,1,0:T(8,128)S(1)} collective-permute-done((f32[16,8,256]{2,1,0:T(8,128)S(1)}, f32[16,8,256]{2,1,0:T(8,128)S(1)}, u32[]{:S(2)}, u32[]{:S(2)}) %collective-permute-start) | collective-permute-done | bytes 131104 | tf_op jit(solution)/shard_map/ppermute | solution.py:494
  21.9 16.2 %forward.1 = (f32[2,32,32,128]{3,2,1,0:T(8,128)S(1)}, f32[2,32,32,128]{3,2,1,0:T(8,128)S(1)}, f32[5,144,1024]{2,1,0:T(8,128)S(1)}, f32[5,128,1024]{2,1,0:T(8,128)S(1)}) custom-call(s32[6]{0:T(128)S(1)} %stack.27.place_ref, s32[32]{0:T(128)S(1)} %compare_convert_fusion.live_ref, f32[16,8,256]{2,1,0:T(8,128)S(1)} %all-to-all-done.same_ref, ...), custom_call_target="tpu_custom_call" | custom-call | flops 1000000 | bytes 10000 | tf_op jit(solution)/shard_map/forward/pallas_call | solution.py:552
  38.1 1.3 %inverse_x.2 = (f32[4,2,32,128]{3,2,1,0:T(8,128)S(1)}, f32[4,2,32,128]{3,2,1,0:T(8,128)S(1)}, f32[4,2,32,128]{3,2,1,0:T(8,128)S(1)}, f32[4,2,32,128]{3,2,1,0:T(8,128)S(1)}, f32[19,2,32,128]{3,2,1,0:T(8,128)S(1)}) custom-call(s32[6]{0:T(128)S(1)} %stack.27.place_ref, f32[2,32,32,128]{3,2,1,0:T(8,128)S(1)} %get-tuple-element.47.spectrum_ref, ...), custom_call_target="tpu_custom_call" | custom-call | flops 1000000 | bytes 10000 | tf_op jit(solution)/shard_map/inverse_x/pallas_call | solution.py:579
  39.5 1.0 %collective-permute-start.2 = (f32[4,64,128]{2,1,0:T(8,128)S(1)}, f32[4,64,128]{2,1,0:T(8,128)S(1)}, u32[]{:S(2)}, u32[]{:S(2)}) collective-permute-start(f32[4,64,128]{2,1,0:T(8,128)S(1)} %bitcast.27), channel_id=1, source_target_pairs={{0,12},{4,8},{8,4},{12,0},{16,28},{20,24},{24,20},{28,16},{1,13},{... | collective-permute-start | bytes 393224 | tf_op jit(solution)/shard_map/ppermute | solution.py:494
  40.5 1.8 %collective-permute-start.3 = (f32[4,64,128]{2,1,0:T(8,128)S(1)}, f32[4,64,128]{2,1,0:T(8,128)S(1)}, u32[]{:S(2)}, u32[]{:S(2)}) collective-permute-start(f32[4,64,128]{2,1,0:T(8,128)S(1)} %bitcast.26), channel_id=1, source_target_pairs={{0,8},{4,12},{8,0},{12,4},{16,24},{20,28},{24,16},{28,20},{1,9},{5... | collective-permute-start | bytes 393224 | tf_op jit(solution)/shard_map/ppermute | solution.py:494
  43.0 1.3 %inverse_x.3 = (f32[4,2,32,128]{3,2,1,0:T(8,128)S(1)}, f32[4,2,32,128]{3,2,1,0:T(8,128)S(1)}, f32[4,2,32,128]{3,2,1,0:T(8,128)S(1)}, f32[4,2,32,128]{3,2,1,0:T(8,128)S(1)}, f32[19,2,32,128]{3,2,1,0:T(8,128)S(1)}) custom-call(s32[6]{0:T(128)S(1)} %stack.27.place_ref, f32[2,32,32,128]{3,2,1,0:T(8,128)S(1)} %get-tuple-element.50.spectrum_ref, ...), custom_call_target="tpu_custom_call" | custom-call | flops 1000000 | bytes 10000 | tf_op jit(solution)/shard_map/inverse_x/pallas_call | solution.py:579
  44.4 1.9 %collective-permute-start.5 = (f32[4,64,128]{2,1,0:T(8,128)S(1)}, f32[4,64,128]{2,1,0:T(8,128)S(1)}, u32[]{:S(2)}, u32[]{:S(2)}) collective-permute-start(f32[4,64,128]{2,1,0:T(8,128)S(1)} %bitcast.30), channel_id=1, source_target_pairs={{0,12},{4,8},{8,4},{12,0},{16,28},{20,24},{24,20},{28,16},{1,13},{... | collective-permute-start | bytes 393224 | tf_op jit(solution)/shard_map/ppermute | solution.py:494
  46.3 0.9 %collective-permute-start.6 = (f32[4,64,128]{2,1,0:T(8,128)S(1)}, f32[4,64,128]{2,1,0:T(8,128)S(1)}, u32[]{:S(2)}, u32[]{:S(2)}) collective-permute-start(f32[4,64,128]{2,1,0:T(8,128)S(1)} %bitcast.29), channel_id=1, source_target_pairs={{0,8},{4,12},{8,0},{12,4},{16,24},{20,28},{24,16},{28,20},{1,9},{5... | collective-permute-start | bytes 393224 | tf_op jit(solution)/shard_map/ppermute | solution.py:494
  47.2 0.9 %collective-permute-start.7 = (f32[4,64,128]{2,1,0:T(8,128)S(1)}, f32[4,64,128]{2,1,0:T(8,128)S(1)}, u32[]{:S(2)}, u32[]{:S(2)}) collective-permute-start(f32[4,64,128]{2,1,0:T(8,128)S(1)} %bitcast.28), channel_id=1, source_target_pairs={{0,4},{4,0},{8,12},{12,8},{16,20},{20,16},{24,28},{28,24},{1,5},{5... | collective-permute-start | bytes 393224 | tf_op jit(solution)/shard_map/ppermute | solution.py:494
  48.1 5.0 %gather.2.refs_0_ = f32[8,1,256]{2,1,0:T(1,128)S(1)} custom-call(s32[6]{0:T(128)S(1)} %stack.27.place_ref, f32[16,8,256]{2,1,0:T(8,128)S(1)} %all-to-all-done.same_ref, f32[16,8,256]{2,1,0:T(8,128)S(1)} %collective-permute-done.other_ref, f32[5,144,1024]{2,1,0:T(8,128)S(1)} %get-tuple-element.45.table_y, f32[5,128,1024]{2,1,0:T(8,128)S(1)} %get-tuple-element.46.table_z, ...), custom_call_target="tpu_custom_call" | custom-call | flops 1000000 | bytes 10000 | tf_op jit(solution)/shard_map/gather/pallas_call | solution.py:595
  53.1 1.2 %collective-permute-done.6.refs_5_ = f32[4,64,128]{2,1,0:T(8,128)S(1)} collective-permute-done((f32[4,64,128]{2,1,0:T(8,128)S(1)}, f32[4,64,128]{2,1,0:T(8,128)S(1)}, u32[]{:S(2)}, u32[]{:S(2)}) %collective-permute-start.6) | collective-permute-done | bytes 131104 | tf_op jit(solution)/shard_map/ppermute | solution.py:494
  54.4 1.4 %inverse_y.1 = (f32[4,128,128]{2,1,0:T(8,128)S(1)}, f32[4,128,128]{2,1,0:T(8,128)S(1)}, f32[4,128,128]{2,1,0:T(8,128)S(1)}, f32[4,128,128]{2,1,0:T(8,128)S(1)}) custom-call(s32[6]{0:T(128)S(1)} %stack.27.place_ref, f32[4,64,128]{2,1,0:T(8,128)S(1)} %collective-permute-done.2.refs_0_, f32[4,64,128]{2,1,0:T(8,128)S(1)} %collective-permute-done.3.refs_1_, ...), custom_call_target="tpu_custom_call" | custom-call | flops 1000000 | bytes 10000 | tf_op jit(solution)/shard_map/inverse_y/pallas_call | solution.py:616
  56.5 1.6 %collective-permute-start.9 = (f32[4,128,128]{2,1,0:T(8,128)S(1)}, f32[4,128,128]{2,1,0:T(8,128)S(1)}, u32[]{:S(2)}, u32[]{:S(2)}) collective-permute-start(f32[4,128,128]{2,1,0:T(8,128)S(1)} %get-tuple-element.70), channel_id=1, source_target_pairs={{0,2},{1,3},{2,0},{3,1},{4,6},{5,7},{6,4},{7,5},{8,10},{9,11},{10,... | collective-permute-start | bytes 786440 | tf_op jit(solution)/shard_map/ppermute | solution.py:494
  58.1 5.6 %gather.3 = f32[16,1,256]{2,1,0:T(1,128)} custom-call(s32[6]{0:T(128)S(1)} %stack.27.place_ref, f32[16,8,256]{2,1,0:T(8,128)S(1)} %all-to-all-done.same_ref, f32[16,8,256]{2,1,0:T(8,128)S(1)} %collective-permute-done.other_ref, f32[5,144,1024]{2,1,0:T(8,128)S(1)} %get-tuple-element.45.table_y, f32[5,128,1024]{2,1,0:T(8,128)S(1)} %get-tuple-element.46.table_z, ...), custom_call_target="tpu_custom_call" | custom-call | flops 1000000 | bytes 10000 | tf_op jit(solution)/shard_map/gather/pallas_call | solution.py:595
  63.7 3.5 %all-to-all-start.1 = ((f32[16,1,256]{2,1,0:T(1,128)}), f32[16,1,256]{2,1,0:T(1,128)S(1)}, u32[]{:S(2)}, u32[]{:S(2)}) async-start(f32[16,1,256]{2,1,0:T(1,128)} %gather.3), calls=%async_computation.1 | async-start | bytes 32768 | tf_op jit(solution)/shard_map/all_to_all | solution.py:637
  67.2 1.1 %inverse_z.2.refs_4_ = f32[4,128,512]{2,1,0:T(8,128)S(1)} custom-call(s32[6]{0:T(128)S(1)} %stack.27.place_ref, f32[4,128,128]{2,1,0:T(8,128)S(1)} %get-tuple-element.75.refs_0_, f32[4,128,128]{2,1,0:T(8,128)S(1)} %collective-permute-done.10.refs_1_, bf16[512,512]{1,0:T(8,128)(2,1)S(1)} %copy-done.1, bf16[512,512]{1,0:T(8,128)(2,1)S(1)} %copy-done), custom_call_target="tpu_custom_call" | custom-call | flops 1000000 | bytes 10000 | tf_op jit(solution)/shard_map/inverse_z/pallas_call | solution.py:652
  68.4 1.9 %collective-permute-done.9.refs_1_ = f32[4,128,128]{2,1,0:T(8,128)S(1)} collective-permute-done((f32[4,128,128]{2,1,0:T(8,128)S(1)}, f32[4,128,128]{2,1,0:T(8,128)S(1)}, u32[]{:S(2)}, u32[]{:S(2)}) %collective-permute-start.9) | collective-permute-done | bytes 262176 | tf_op jit(solution)/shard_map/ppermute | solution.py:494
  70.2 2.1 %inverse_z.3 = f32[4,128,512]{2,1,0:T(8,128)} custom-call(s32[6]{0:T(128)S(1)} %stack.27.place_ref, f32[4,128,128]{2,1,0:T(8,128)S(1)} %collective-permute-done.8.refs_0_, f32[4,128,128]{2,1,0:T(8,128)S(1)} %collective-permute-done.9.refs_1_, bf16[512,512]{1,0:T(8,128)(2,1)S(1)} %copy-done.1, bf16[512,512]{1,0:T(8,128)(2,1)S(1)} %copy-done, ...), custom_call_target="tpu_custom_call" | custom-call | flops 1000000 | bytes 10000 | tf_op jit(solution)/shard_map/inverse_z/pallas_call | solution.py:652
  (32 shorter events, 4.0 us)
Async XLA Ops:
  2.7 16.1 %all-to-all-start = ((f32[16,8,256]{2,1,0:T(8,128)}), f32[16,8,256]{2,1,0:T(8,128)S(1)}, u32[]{:S(2)}, u32[]{:S(2)}) async-start(f32[16,8,256]{2,1,0:T(8,128)} %pack.1), calls=%async_computation | async-start | bytes 262144 | tf_op jit(solution)/shard_map/all_to_all | solution.py:533
  18.8 24.2 %collective-permute-start.1 = (f32[32,32,128]{2,1,0:T(8,128)}, f32[32,32,128]{2,1,0:T(8,128)S(1)}, u32[]{:S(2)}, u32[]{:S(2)}) collective-permute-start(f32[32,32,128]{2,1,0:T(8,128)} %get-tuple-element.51), channel_id=1, source_target_pairs={{0,28},{4,24},{8,20},{12,16},{16,12},{20,8},{24,4},{28,0},{1,29},{... | collective-permute-start | bytes 1572872 | tf_op jit(solution)/shard_map/ppermute | solution.py:545
  20.2 1.3 %collective-permute-start = (f32[16,8,256]{2,1,0:T(8,128)S(1)}, f32[16,8,256]{2,1,0:T(8,128)S(1)}, u32[]{:S(2)}, u32[]{:S(2)}) collective-permute-start(f32[16,8,256]{2,1,0:T(8,128)S(1)} %all-to-all-done.same_ref), channel_id=1, source_target_pairs={{0,1},{1,0},{2,3},{3,2},{4,5},{5,4},{6,7},{7,6},{8,9},{9,8},{10,11... | collective-permute-start | bytes 393224 | tf_op jit(solution)/shard_map/ppermute | solution.py:494
  39.5 7.7 %collective-permute-start.2 = (f32[4,64,128]{2,1,0:T(8,128)S(1)}, f32[4,64,128]{2,1,0:T(8,128)S(1)}, u32[]{:S(2)}, u32[]{:S(2)}) collective-permute-start(f32[4,64,128]{2,1,0:T(8,128)S(1)} %bitcast.27), channel_id=1, source_target_pairs={{0,12},{4,8},{8,4},{12,0},{16,28},{20,24},{24,20},{28,16},{1,13},{... | collective-permute-start | bytes 393224 | tf_op jit(solution)/shard_map/ppermute | solution.py:494
  40.5 12.6 %collective-permute-start.3 = (f32[4,64,128]{2,1,0:T(8,128)S(1)}, f32[4,64,128]{2,1,0:T(8,128)S(1)}, u32[]{:S(2)}, u32[]{:S(2)}) collective-permute-start(f32[4,64,128]{2,1,0:T(8,128)S(1)} %bitcast.26), channel_id=1, source_target_pairs={{0,8},{4,12},{8,0},{12,4},{16,24},{20,28},{24,16},{28,20},{1,9},{5... | collective-permute-start | bytes 393224 | tf_op jit(solution)/shard_map/ppermute | solution.py:494
  42.3 10.8 %collective-permute-start.4 = (f32[4,64,128]{2,1,0:T(8,128)S(1)}, f32[4,64,128]{2,1,0:T(8,128)S(1)}, u32[]{:S(2)}, u32[]{:S(2)}) collective-permute-start(f32[4,64,128]{2,1,0:T(8,128)S(1)} %bitcast.25), channel_id=1, source_target_pairs={{0,4},{4,0},{8,12},{12,8},{16,20},{20,16},{24,28},{28,24},{1,5},{5... | collective-permute-start | bytes 393224 | tf_op jit(solution)/shard_map/ppermute | solution.py:494
  44.4 8.7 %collective-permute-start.5 = (f32[4,64,128]{2,1,0:T(8,128)S(1)}, f32[4,64,128]{2,1,0:T(8,128)S(1)}, u32[]{:S(2)}, u32[]{:S(2)}) collective-permute-start(f32[4,64,128]{2,1,0:T(8,128)S(1)} %bitcast.30), channel_id=1, source_target_pairs={{0,12},{4,8},{8,4},{12,0},{16,28},{20,24},{24,20},{28,16},{1,13},{... | collective-permute-start | bytes 393224 | tf_op jit(solution)/shard_map/ppermute | solution.py:494
  46.3 8.0 %collective-permute-start.6 = (f32[4,64,128]{2,1,0:T(8,128)S(1)}, f32[4,64,128]{2,1,0:T(8,128)S(1)}, u32[]{:S(2)}, u32[]{:S(2)}) collective-permute-start(f32[4,64,128]{2,1,0:T(8,128)S(1)} %bitcast.29), channel_id=1, source_target_pairs={{0,8},{4,12},{8,0},{12,4},{16,24},{20,28},{24,16},{28,20},{1,9},{5... | collective-permute-start | bytes 393224 | tf_op jit(solution)/shard_map/ppermute | solution.py:494
  47.2 7.2 %collective-permute-start.7 = (f32[4,64,128]{2,1,0:T(8,128)S(1)}, f32[4,64,128]{2,1,0:T(8,128)S(1)}, u32[]{:S(2)}, u32[]{:S(2)}) collective-permute-start(f32[4,64,128]{2,1,0:T(8,128)S(1)} %bitcast.28), channel_id=1, source_target_pairs={{0,4},{4,0},{8,12},{12,8},{16,20},{20,16},{24,28},{28,24},{1,5},{5... | collective-permute-start | bytes 393224 | tf_op jit(solution)/shard_map/ppermute | solution.py:494
  48.0 6.4 %copy-start.2 = (bf16[2,256,256]{2,1,0:T(8,128)(2,1)S(1)}, bf16[2,256,256]{2,1,0:T(8,128)(2,1)}, u32[]{:S(2)}) copy-start(bf16[2,256,256]{2,1,0:T(8,128)(2,1)} %constant.52.clone.refs_9_) | copy-start | bytes 786436
  48.0 6.4 %copy-start.3 = (bf16[2,256,256]{2,1,0:T(8,128)(2,1)S(1)}, bf16[2,256,256]{2,1,0:T(8,128)(2,1)}, u32[]{:S(2)}) copy-start(bf16[2,256,256]{2,1,0:T(8,128)(2,1)} %constant.51.clone.refs_8_) | copy-start | bytes 786436
  55.8 2.2 %collective-permute-start.10 = (f32[4,128,128]{2,1,0:T(8,128)S(1)}, f32[4,128,128]{2,1,0:T(8,128)S(1)}, u32[]{:S(2)}, u32[]{:S(2)}) collective-permute-start(f32[4,128,128]{2,1,0:T(8,128)S(1)} %get-tuple-element.71), channel_id=1, source_target_pairs={{0,1},{1,0},{2,3},{3,2},{4,5},{5,4},{6,7},{7,6},{8,9},{9,8},{10,11... | collective-permute-start | bytes 786440 | tf_op jit(solution)/shard_map/ppermute | solution.py:494
  55.9 12.4 %collective-permute-start.8 = (f32[4,128,128]{2,1,0:T(8,128)S(1)}, f32[4,128,128]{2,1,0:T(8,128)S(1)}, u32[]{:S(2)}, u32[]{:S(2)}) collective-permute-start(f32[4,128,128]{2,1,0:T(8,128)S(1)} %get-tuple-element.69), channel_id=1, source_target_pairs={{0,3},{1,2},{2,1},{3,0},{4,7},{5,6},{6,5},{7,4},{8,11},{9,10},{10,... | collective-permute-start | bytes 786440 | tf_op jit(solution)/shard_map/ppermute | solution.py:494
  56.5 10.7 %copy-start = (bf16[512,512]{1,0:T(8,128)(2,1)S(1)}, bf16[512,512]{1,0:T(8,128)(2,1)}, u32[]{:S(2)}) copy-start(bf16[512,512]{1,0:T(8,128)(2,1)} %constant.54.clone.refs_3_) | copy-start | bytes 1572868
  56.5 10.7 %copy-start.1 = (bf16[512,512]{1,0:T(8,128)(2,1)S(1)}, bf16[512,512]{1,0:T(8,128)(2,1)}, u32[]{:S(2)}) copy-start(bf16[512,512]{1,0:T(8,128)(2,1)} %constant.53.clone.refs_2_) | copy-start | bytes 1572868
  56.5 13.7 %collective-permute-start.9 = (f32[4,128,128]{2,1,0:T(8,128)S(1)}, f32[4,128,128]{2,1,0:T(8,128)S(1)}, u32[]{:S(2)}, u32[]{:S(2)}) collective-permute-start(f32[4,128,128]{2,1,0:T(8,128)S(1)} %get-tuple-element.70), channel_id=1, source_target_pairs={{0,2},{1,3},{2,0},{3,1},{4,6},{5,7},{6,4},{7,5},{8,10},{9,11},{10,... | collective-permute-start | bytes 786440 | tf_op jit(solution)/shard_map/ppermute | solution.py:494
  63.7 9.0 %all-to-all-start.1 = ((f32[16,1,256]{2,1,0:T(1,128)}), f32[16,1,256]{2,1,0:T(1,128)S(1)}, u32[]{:S(2)}, u32[]{:S(2)}) async-start(f32[16,1,256]{2,1,0:T(1,128)} %gather.3), calls=%async_computation.1 | async-start | bytes 32768 | tf_op jit(solution)/shard_map/all_to_all | solution.py:637
  67.2 5.5 %copy-start.4 = (f32[256]{0:T(256)S(1)}, f32[256]{0:T(256)}, u32[]{:S(2)}) copy-start(f32[256]{0:T(256)} %param.13) | copy-start | bytes 3076
